TPU v7x, 32 devices: a whole 2x2x4 slice. The times are simulated.
32 devices in a mesh: gx: 4 (over x, core), gy: 8 (over z, y).
Axes of the slice: x: 2, y: 2, z: 4, core: 2. Of those that a mesh axis runs over, the one named last changes fastest.
Arguments:
- fields: bfloat16 [672, 672, 1536], P('gx', 'gy'), may hold values from -16 to 16
- x_factor: bfloat16 [672, 336], replicated, may hold values from -0.00030517578 to 0.00030517578
- running_r: float32 [672, 672], replicated, as said below
Outputs:
- new_r: float32 [672, 672], P('gy', 'gx')
Inputs may be any that keep to these rules, and one draw needn't show every extreme that they name: `running_r`: upper triangular with a positive diagonal.
All inputs are finite; a program needn't handle non-finite values.
Results may differ from a plain program's by a relative error of at most 0.0003.
Values may be sent and summed in bfloat16 or wider, within the bound.
No kernel may reach another device: no remote copies, remote signals or barrier semaphores. Data moves between devices by JAX's collectives and lax.ppermute only.
A program may use at most 256 MiB of HBM per device.

v0:
```python
import jax
import jax.numpy as jnp
from jax import lax
from jax.sharding import PartitionSpec as P


def fibre_gram(fibres):
    local_gram = lax.dot_general(
        fibres, fibres, (((0, 2), (0, 2)), ((), ())), preferred_element_type=jnp.float32
    )
    return lax.psum(local_gram, ("gx", "gy"))


def project_local(x_factor, block):
    full_x = block.shape[0]
    middle = block.shape[1]
    part_cells = block.shape[2]
    product = lax.dot_general(
        x_factor,
        block.reshape(full_x, middle * part_cells),
        (((0,), (0,)), ((), ())),
        preferred_element_type=jnp.float32,
    )
    return product.astype(jnp.bfloat16).reshape(x_factor.shape[1], middle, part_cells)


def on_device(fields, x_factor, running_r):
    full_y = running_r.shape[0]
    exchanged = lax.all_to_all(fields, "gx", split_axis=2, concat_axis=0, tiled=True)
    projected = project_local(x_factor, exchanged)
    fibres = lax.all_to_all(projected, "gy", split_axis=2, concat_axis=1, tiled=True)
    gram_sum = fibre_gram(fibres)
    total = (
        jnp.dot(
            running_r.T,
            running_r,
            precision=lax.Precision.HIGHEST,
            preferred_element_type=jnp.float32,
        )
        + gram_sum
    )
    upper_r = jnp.linalg.cholesky(total).T
    row_block = full_y // lax.axis_size("gy")
    col_block = full_y // lax.axis_size("gx")
    return lax.dynamic_slice(
        upper_r,
        (lax.axis_index("gy") * row_block, lax.axis_index("gx") * col_block),
        (row_block, col_block),
    )


def solution(mesh):
    in_specs = (P("gx", "gy", None), P(), P())
    out_specs = P("gy", "gx")
    return jax.shard_map(
        on_device, mesh=mesh, in_specs=in_specs, out_specs=out_specs, check_vma=False
    )
```

profile of v0, /device:TPU:0, one launch (start us, length us, event | category | flops | bytes accessed | tf_op | source)
XLA Modules:
  0.0 1956.4 jit_solution(15579727666196647956)
XLA Ops:
  6.5 81.1 %copy.27 = bf16[168,84,1536]{1,0,2:T(8,128)(2,1)} copy(bf16[168,84,1536]{2,0,1:T(8,128)(2,1)} %param.3) | data formatting | bytes 86704128 | tf_op args[0]
  87.7 743.7 %all_to_all.33 = bf16[168,84,1536]{1,0,2:T(8,128)(2,1)} all-to-all(bf16[168,84,1536]{1,0,2:T(8,128)(2,1)} %copy.27), channel_id=1, replica_groups=mesh['gx'=4,'gy'=8] {'gx'}, dimensions={2} | all-to-all | bytes 86704128 | tf_op jit(solution)/shard_map/all_to_all | solution.py:29
  831.3 85.0 %copy.28 = bf16[168,84,4,384]{3,1,0,2:T(8,128)(2,1)} copy(bf16[168,84,4,384]{1,0,3,2:T(8,128)(2,1)} %bitcast.49) | data formatting | bytes 86704128 | tf_op jit(solution)/shard_map/all_to_all | solution.py:29
  916.3 30.2 %copy.41 = bf16[84,8,84,384]{3,1,2,0:T(8,128)(2,1)} copy(bf16[84,8,84,384]{3,2,1,0:T(8,128)(2,1)} %bitcast.50) | data formatting | bytes 86704128
  946.5 29.6 %convolution_convert_fusion = bf16[336,32256]{1,0:T(8,128)(2,1)} fusion(bf16[672,336]{1,0:T(8,128)(2,1)S(1)} %copy-done.2, bf16[672,32256]{1,0:T(8,128)(2,1)} %bitcast.52), kind=kOutput, calls=%fused_computation | convolution fusion | flops 14577131520 | bytes 65479680 | tf_op jit(solution)/shard_map/dot_general | solution.py:18
  976.1 33.7 %reshape.47 = bf16[336,84,384]{2,1,0:T(8,128)(2,1)} reshape(bf16[336,32256]{1,0:T(8,128)(2,1)} %convolution_convert_fusion) | data formatting | bytes 43352064 | tf_op jit(solution)/shard_map/reshape | solution.py:24
  1009.8 35.7 %copy.29 = bf16[336,84,384]{0,1,2:T(8,128)(2,1)} copy(bf16[336,84,384]{2,1,0:T(8,128)(2,1)} %reshape.47) | data formatting | bytes 43352064 | tf_op jit(solution)/shard_map/reshape | solution.py:24
  1045.5 566.8 %all_to_all.34 = bf16[336,84,384]{0,1,2:T(8,128)(2,1)S(1)} all-to-all(bf16[336,84,384]{0,1,2:T(8,128)(2,1)} %copy.29), channel_id=1, replica_groups=mesh['gx'=4,'gy'=8] {'gy'}, dimensions={2} | all-to-all | bytes 43352064 | tf_op jit(solution)/shard_map/all_to_all | solution.py:31
  1612.3 10.4 copy.31
  1622.8 34.1 %fusion.3 = f32[672,672]{0,1:T(8,128)} fusion(bf16[336,672,48]{0,2,1:T(8,128)(2,1)} %bitcast.53), kind=kOutput, calls=%fused_computation.6 | convolution fusion | flops 14566293504 | bytes 23482368 | tf_op jit(solution)/shard_map/dot_general | solution.py:8
  1656.9 131.1 %all-reduce.3.cloned.1.call-done = f32[672,672]{0,1:T(8,128)} async-done(((f32[672,672]{0,1:T(8,128)}), f32[672,672]{0,1:T(8,128)}) %all-reduce.3.cloned.1.call-update) | async-done | bytes 1806352 | tf_op jit(solution)/shard_map/psum | solution.py:11
  1788.0 8.2 convolution_add_fusion
  1796.3 11.4 copy.36
  1807.7 2.5 fusion.2
  1811.5 11.7 cholesky.166
  1823.3 9.8 custom-call.43
  1833.1 1.4 cholesky.342
  1834.5 2.1 constant_dynamic-update-slice_fusion.4
  1836.6 1.3 convolution_subtract_fusion
  1837.9 11.7 cholesky.189
  1850.3 10.0 custom-call.44
  1861.3 1.6 convolution_subtract_fusion.1
  1863.0 11.7 cholesky.356
  1876.0 9.8 custom-call.45
  1886.8 1.7 convolution_subtract_fusion.2
  1888.5 11.9 cholesky.375
  1901.7 9.8 custom-call.46
  1912.4 1.5 convolution_subtract_fusion.3
  1913.9 11.7 cholesky.394
  1927.0 9.8 custom-call.47
  1938.7 2.9 cholesky.415
  1947.5 1.7 fusion.17
  (29 shorter events, 12.8 us)
Async XLA Ops:
  6.5 1781.5 %copy-start = (f32[672,672]{1,0:T(8,128)S(1)}, f32[672,672]{1,0:T(8,128)}, u32[]{:S(2)}) copy-start(f32[672,672]{1,0:T(8,128)} %param.5) | copy-start | bytes 5419012
  6.5 1781.5 %all-reduce.3.cloned.1.call-start = ((), (), s32[]{:S(2)}) async-start(), calls=%async_computation.2 | async-start | bytes 4128768 | tf_op jit(solution)/shard_map/psum | solution.py:11
  916.3 30.2 %copy-start.2 = (bf16[672,336]{1,0:T(8,128)(2,1)S(1)}, bf16[672,336]{1,0:T(8,128)(2,1)}, u32[]{:S(2)}) copy-start(bf16[672,336]{1,0:T(8,128)(2,1)} %param.4) | copy-start | bytes 1354756
  1810.2 1.3 copy-start.1
Sparse Core Ops, SparseCore 0:
  1657.0 130.9 all-reduce.2
where the time goes:
time: 1970 us; the launch traced here: 1960 us
  blocking collectives  1310 us (66%)
  local copies, waits for them, and re-layouts  290 us (15%)
  waiting for transfers between devices  131 us (7%)
  other arithmetic  122 us (6%)
  matrix products  84.9 us (4%)
    all_to_all x1, blocking collectives, on_device(): lax.all_to_all(fields, 'gx', split_axis=2, concat_axis=0, tiled=True)  744 us
    all_to_all x1, blocking collectives, on_device(): lax.all_to_all(projected, 'gy', split_axis=2, concat_axis=1, tiled=True)  567 us
    psum x1, waiting for transfers between devices, fibre_gram(): return lax.psum(local_gram, ('gx', 'gy'))  131 us
    another operation x22, other arithmetic, on_device(): upper_r = jnp.linalg.cholesky(total).T  118 us
    unnamed x8, local copies, waits for them, and re-layouts  113 us
    all_to_all x1, local copies, waits for them, and re-layouts, on_device(): lax.all_to_all(fields, 'gx', split_axis=2, concat_axis=0, tiled=True)  85 us
    reshape x2, local copies, waits for them, and re-layouts, project_local(): product.astype(jnp.bfloat16).reshape(x_factor.shape[1], middle, part_cells)  69.4 us
  transfers between devices with their start and end apart: 1, of which 1 were waited for; matrix products, arithmetic and copies ran while one was open for 0% of the time, Pallas kernels for 0%

commit v1 on v0

v1 whole, which is shorter than its diff:
```python
import functools

import jax
import jax.numpy as jnp
from jax import lax
from jax.experimental import pallas as pl
from jax.experimental.pallas import tpu as pltpu
from jax.sharding import PartitionSpec as P

LANES = 128
PITCH = 96
VMEM_BYTES = 56 * 1024 * 1024


def y_pieces(rows):
    leftover = rows % 16
    main = rows - leftover
    pieces = []
    start = 0
    while start < main:
        size = min(32, main - start)
        pieces.append([start, size, 0])
        start += size
    pieces[-1][2] = leftover
    return [tuple(p) for p in pieces]


def project_kernel(start, main, left, rank, share, scalars, fields, got, factor, outs, own, wide, sem):
    rows = main + left
    column = pl.multiple_of(scalars[0], LANES)
    copy = pltpu.make_async_copy(
        fields.at[pl.ds(start, rows), :, pl.ds(column, LANES)], own, sem
    )
    copy.start()
    copy.wait()
    blocks = [own] + list(got)

    def one_pair(pair, _):
        y = pair * 2
        total = None
        for index, block in enumerate(blocks):
            right = jnp.concatenate([block[y], block[y + 1]], axis=1)
            term = jnp.dot(factor[index], right, preferred_element_type=jnp.float32)
            total = term if total is None else total + term
        at = pl.multiple_of(y * rank, 8)
        wide[pl.ds(at, rank), :] = total[:, :LANES]
        wide[pl.ds(at + rank, rank), :] = total[:, LANES:]
        return 0

    lax.fori_loop(0, rows // 2, one_pair, 0)

    for part, out in enumerate(outs):
        first = scalars[1 + part]

        def one_row(i, _):
            picked = wide[pl.ds(first + i, main, stride=rank), :]
            out[pl.ds(pl.multiple_of(i * main, 16), main), :] = picked.astype(jnp.bfloat16)
            return 0

        lax.fori_loop(0, share, one_row, 0)
        if left:
            per = 16 // left
            for group in range(0, share, per):
                count = min(per, share - group)
                tile = [
                    wide[pl.ds(main * rank + first + group + k, left, stride=rank), :]
                    for k in range(count)
                ]
                tile = jnp.concatenate(tile, axis=0).astype(jnp.bfloat16)
                at = share * main + group * left
                out[at : at + count * left, :] = tile


def project(fields, got, factor, scalars, piece, share):
    start, main, left = piece
    rows = main + left
    rank = factor.shape[1]
    depth = fields.shape[1]
    parts = scalars.shape[0] - 1
    n_got = len(got)

    def body(scalars, fields, *rest):
        got = rest[:n_got]
        factor = rest[n_got]
        outs = rest[n_got + 1 : n_got + 1 + parts]
        own, wide, sem = rest[n_got + 1 + parts :]
        project_kernel(
            start, main, left, rank, share, scalars, fields, got, factor, outs, own, wide, sem
        )

    vmem = pl.BlockSpec(memory_space=pltpu.VMEM)
    out_rows = share * rows
    return pl.pallas_call(
        body,
        out_shape=[jax.ShapeDtypeStruct((out_rows, LANES), jnp.bfloat16)] * parts,
        in_specs=[pl.BlockSpec(memory_space=pltpu.SMEM), pl.BlockSpec(memory_space=pl.ANY)]
        + [vmem] * (n_got + 1),
        out_specs=[vmem] * parts,
        scratch_shapes=[
            pltpu.VMEM((rows, depth, LANES), jnp.bfloat16),
            pltpu.VMEM((rows * rank, LANES), jnp.float32),
            pltpu.SemaphoreType.DMA,
        ],
        compiler_params=pltpu.CompilerParams(vmem_limit_bytes=VMEM_BYTES),
        cost_estimate=pl.CostEstimate(
            flops=2 * rows * LANES * rank * depth * (n_got + 1),
            bytes_accessed=2 * rows * LANES * (depth * (n_got + 1) + rank),
            transcendentals=0,
        ),
        name="project",
    )(scalars, fields, *got, factor)


def gram_kernel(pieces, share, sources, blocks, carried, out, fibres):
    n_pieces = len(pieces)
    parts = len(blocks) // n_pieces
    whole = fibres.shape[0]

    for part in range(parts):
        base = pl.multiple_of(sources[part] * PITCH, 16)

        def one_row(i, _):
            at = pl.multiple_of(i * LANES, LANES)
            for index, (start, main, _left) in enumerate(pieces):
                block = blocks[part * n_pieces + index]
                fibres[pl.ds(base + start, main), pl.ds(at, LANES)] = block[
                    pl.ds(pl.multiple_of(i * main, 16), main), :
                ]
            return 0

        lax.fori_loop(0, share, one_row, 0)
        for index, (start, main, left) in enumerate(pieces):
            if not left:
                continue
            block = blocks[part * n_pieces + index]
            per = 16 // left
            for group in range(0, share, per):
                count = min(per, share - group)
                at = share * main + group * left
                tile = block[at : at + count * left, :].astype(jnp.float32)
                for k in range(count):
                    rows = tile[k * left : (k + 1) * left, :]
                    rows = jnp.concatenate(
                        [rows, jnp.zeros((16 - left, LANES), jnp.float32)], axis=0
                    )
                    fibres[
                        pl.ds(base + start + main, 16), (group + k) * LANES : (group + k + 1) * LANES
                    ] = rows.astype(jnp.bfloat16)

    step = 256
    for i in range(0, whole, step):
        for j in range(0, whole, step):
            if j < i:
                out[i : i + step, j : j + step] = jnp.zeros((step, step), jnp.float32)
                continue
            product = lax.dot_general(
                fibres[i : i + step, :],
                fibres[j : j + step, :],
                (((1,), (1,)), ((), ())),
                preferred_element_type=jnp.float32,
            )
            if carried is not None:
                product = product + carried[i : i + step, j : j + step]
            out[i : i + step, j : j + step] = product


def gram(blocks, carried, sources, pieces, share):
    parts = sources.shape[0]
    whole = parts * PITCH
    n_blocks = len(blocks)

    def body(sources, *rest):
        blocks = rest[:n_blocks]
        if carried is None:
            out, fibres = rest[n_blocks:]
            before = None
        else:
            before, out, fibres = rest[n_blocks:]
        gram_kernel(pieces, share, sources, blocks, before, out, fibres)

    vmem = pl.BlockSpec(memory_space=pltpu.VMEM)
    extra = [] if carried is None else [carried]
    return pl.pallas_call(
        body,
        out_shape=jax.ShapeDtypeStruct((whole, whole), jnp.float32),
        in_specs=[pl.BlockSpec(memory_space=pltpu.SMEM)] + [vmem] * (n_blocks + len(extra)),
        out_specs=vmem,
        scratch_shapes=[pltpu.VMEM((whole, share * LANES), jnp.bfloat16)],
        compiler_params=pltpu.CompilerParams(vmem_limit_bytes=VMEM_BYTES),
        cost_estimate=pl.CostEstimate(
            flops=2 * whole * whole * share * LANES,
            bytes_accessed=2 * whole * share * LANES + 8 * whole * whole,
            transcendentals=0,
        ),
        name="gram",
    )(sources, *blocks, *extra)


def slice_out(upper_r):
    row_block = upper_r.shape[0] // lax.axis_size("gy")
    col_block = upper_r.shape[1] // lax.axis_size("gx")
    return lax.dynamic_slice(
        upper_r,
        (lax.axis_index("gy") * row_block, lax.axis_index("gx") * col_block),
        (row_block, col_block),
    )


def finish(gram_sum, running_r):
    total = (
        jnp.dot(
            running_r.T,
            running_r,
            precision=lax.Precision.HIGHEST,
            preferred_element_type=jnp.float32,
        )
        + gram_sum
    )
    return slice_out(lax.linalg.cholesky(total.T, symmetrize_input=False).T)


def plain(fields, x_factor, running_r):
    exchanged = lax.all_to_all(fields, "gx", split_axis=2, concat_axis=0, tiled=True)
    full_x, middle, part_cells = exchanged.shape
    product = lax.dot_general(
        x_factor,
        exchanged.reshape(full_x, middle * part_cells),
        (((0,), (0,)), ((), ())),
        preferred_element_type=jnp.float32,
    )
    projected = product.astype(jnp.bfloat16).reshape(x_factor.shape[1], middle, part_cells)
    fibres = lax.all_to_all(projected, "gy", split_axis=2, concat_axis=1, tiled=True)
    local_gram = lax.dot_general(
        fibres, fibres, (((0, 2), (0, 2)), ((), ())), preferred_element_type=jnp.float32
    )
    return finish(lax.psum(local_gram, ("gx", "gy")), running_r)


def pipelined(fields, x_factor, running_r):
    n_x, n_y = lax.axis_size("gx"), lax.axis_size("gy")
    me_x, me_y = lax.axis_index("gx"), lax.axis_index("gy")
    depth, rows, cells = fields.shape
    rank = x_factor.shape[1]
    share = rank // n_y
    cells_part = cells // n_x
    pieces = y_pieces(rows)
    by_y = jnp.transpose(fields, (1, 0, 2))

    factor = jnp.stack(
        [
            lax.dynamic_slice(x_factor, ((me_x ^ d) * depth, 0), (depth, rank)).T
            for d in range(n_x)
        ]
    )
    slow = n_y // 2
    shifts = [(dz, dy) for dz in range(slow) for dy in range(2)]

    def to(index, shift):
        return (index // 2 + shift[0]) % slow * 2 + (index % 2 + shift[1]) % 2

    def back(index, shift):
        return (index // 2 + slow - shift[0]) % slow * 2 + (index % 2 + shift[1]) % 2

    sends = jnp.stack([to(me_y, s) * share for s in shifts]).astype(jnp.int32)
    sources = jnp.stack([back(me_y, s) for s in shifts]).astype(jnp.int32)

    carried = None
    for k in range(cells_part // LANES):
        scalars = jnp.concatenate(
            [(me_x * cells_part + k * LANES).astype(jnp.int32)[None], sends]
        )
        blocks = [None] * (len(shifts) * len(pieces))
        for index, piece in enumerate(pieces):
            start, main, left = piece
            got = []
            for d in range(1, n_x):
                block = lax.dynamic_slice(
                    by_y,
                    (start, 0, (me_x ^ d) * cells_part + k * LANES),
                    (main + left, depth, LANES),
                )
                got.append(lax.ppermute(block, "gx", [(i, i ^ d) for i in range(n_x)]))
            outs = project(by_y, got, factor, scalars, piece, share)
            for part, shift in enumerate(shifts):
                block = outs[part]
                if shift != (0, 0):
                    block = lax.ppermute(block, "gy", [(i, to(i, shift)) for i in range(n_y)])
                blocks[part * len(pieces) + index] = block
        carried = gram(blocks, carried, sources, pieces, share)

    parts = n_y
    gram_sum = carried.reshape(parts, PITCH, parts, PITCH)[:, :rows, :, :rows]
    gram_sum = lax.psum(gram_sum.reshape(parts * rows, parts * rows), ("gx", "gy"))
    return finish(gram_sum, running_r)


def on_device(fields, x_factor, running_r):
    n_x, n_y = lax.axis_size("gx"), lax.axis_size("gy")
    depth, rows, cells = fields.shape
    rank = x_factor.shape[1]
    fits = (
        cells % (n_x * LANES) == 0
        and rank % (2 * n_y) == 0
        and depth % 8 == 0
        and 16 <= rows <= PITCH
        and rows % 16 in (0, 4, 8)
        and n_x & (n_x - 1) == 0
        and n_y % 2 == 0
        and n_y * PITCH % 256 == 0
    )
    if fits:
        return pipelined(fields, x_factor, running_r)
    return plain(fields, x_factor, running_r)


def solution(mesh):
    in_specs = (P("gx", "gy", None), P(), P())
    out_specs = P("gy", "gx")
    return jax.shard_map(
        on_device, mesh=mesh, in_specs=in_specs, out_specs=out_specs, check_vma=False
    )
```

time: 1970 us -> 1230 us (0.62)
  blocking collectives: 1310 us -> 0 us
  waiting for transfers between devices: 131 us -> 591 us
  starting transfers between devices: 0.01 us -> 244 us
  local copies, waits for them, and re-layouts: 290 us -> 57.8 us
  Pallas kernels: 0 us -> 167 us
  matrix products: 84.9 us -> 20.6 us
    all_to_all x2 -> x0, blocking collectives: 1310 us -> none  [the longest x1 744 us: on_device(): lax.all_to_all(fields, 'gx', split_axis=2, concat_axis=0, tiled=True)]
    ppermute x0 -> x90, waiting for transfers between devices: none -> 451 us  [the longest x27 316 us: pipelined(): got.append(lax.ppermute(block, 'gx', [(i, i ^ d) for i in range(n_x)]))]
    ppermute x0 -> x90, starting transfers between devices: none -> 244 us  [the longest x63 225 us: pipelined(): block = lax.ppermute(block, 'gy', [(i, to(i, shift)) for i in range(n_y)])]
    pallas_call x0 -> x12, Pallas kernels: none -> 167 us  [the longest x9 126 us: project(): pl.pallas_call(body, out_shape=[jax.ShapeDtypeStruct((out_rows, LANES), j...]
    unnamed x8 -> x172, local copies, waits for them, and re-layouts: 113 us -> 14.5 us
    all_to_all x2 -> x0, local copies, waits for them, and re-layouts: 95.4 us -> none  [the longest x1 85 us: on_device(): lax.all_to_all(fields, 'gx', split_axis=2, concat_axis=0, tiled=True)]
    dot_general x3 -> x1, matrix products: 71.9 us -> 7.32 us  [finish(): jnp.dot(running_r.T, running_r, precision=lax.Precision.HIGHEST, preferre...]
    reshape x2 -> x3, local copies, waits for them, and re-layouts: 69.4 us -> 11.2 us  [the longest x2 6.81 us: pipelined(): gram_sum.reshape(parts * rows, parts * rows)]
  transfers between devices with their start and end apart: 1 -> 91, of which waited for: 1 -> 31; matrix products, arithmetic and copies ran while one was open for 0% -> 2% of each run, Pallas kernels for 0% -> 13%
where the time goes in v1:
time: 1230 us; the launch traced here: 1220 us
  waiting for transfers between devices  591 us (48%)
  starting transfers between devices  244 us (20%)
  Pallas kernels  167 us (14%)
  other arithmetic  121 us (10%)
  local copies, waits for them, and re-layouts  57.8 us (5%)
  matrix products  20.6 us (2%)
  between operations  18.4 us (1%)
    ppermute x27, waiting for transfers between devices, pipelined(): got.append(lax.ppermute(block, 'gx', [(i, i ^ d) for i in range(n_x)]))  316 us
    ppermute x63, starting transfers between devices, pipelined(): block = lax.ppermute(block, 'gy', [(i, to(i, shift)) for i in range(n_y)])  225 us
    psum x1, waiting for transfers between devices, pipelined(): lax.psum(gram_sum.reshape(parts * rows, parts * rows), ('gx', 'gy'))  140 us
    ppermute x63, waiting for transfers between devices, pipelined(): block = lax.ppermute(block, 'gy', [(i, to(i, shift)) for i in range(n_y)])  135 us
    pallas_call x9, Pallas kernels, project(): pl.pallas_call(body, out_shape=[jax.ShapeDtypeStruct((out_rows, LANES), j...  126 us
    another operation x22, other arithmetic, finish(): return slice_out(lax.linalg.cholesky(total.T, symmetrize_input=False).T)  118 us
    pallas_call x3, Pallas kernels, gram(): pl.pallas_call(body, out_shape=jax.ShapeDtypeStruct((whole, whole), jnp.f...  41.7 us
  transfers between devices with their start and end apart: 91, of which 31 were waited for; matrix products, arithmetic and copies ran while one was open for 2% of the time, Pallas kernels for 13%

profile of v1, /device:TPU:0, one launch (start us, length us, event | category | flops | bytes accessed | tf_op | source)
XLA Modules:
  0.0 1220.5 jit_solution(18222296513805972333)
XLA Ops:
  17.8 17.8 %collective-permute-done.67.rest_1_ = bf16[20,168,128]{2,1,0:T(8,128)(2,1)S(1)} collective-permute-done((bf16[20,168,128]{2,1,0:T(8,128)(2,1)S(1)}, bf16[20,168,128]{2,1,0:T(8,128)(2,1)S(1)}, u32[]{:S(2)}, u32[]{:S(2)}) %collective-permute-start.67) | collective-permute-done | bytes 860192 | tf_op jit(solution)/shard_map/ppermute | solution.py:282
  36.5 17.3 %collective-permute-done.68.rest_2_ = bf16[20,168,128]{2,1,0:T(8,128)(2,1)} collective-permute-done((bf16[20,168,128]{2,1,0:T(8,128)(2,1)S(1)}, bf16[20,168,128]{2,1,0:T(8,128)(2,1)}, u32[]{:S(2)}, u32[]{:S(2)}) %collective-permute-start.68) | collective-permute-done | bytes 860192 | tf_op jit(solution)/shard_map/ppermute | solution.py:282
  76.7 13.9 %collective-permute-done.38.rest_2_ = bf16[20,168,128]{2,1,0:T(8,128)(2,1)} collective-permute-done((bf16[20,168,128]{2,1,0:T(8,128)(2,1)}, bf16[20,168,128]{2,1,0:T(8,128)(2,1)}, u32[]{:S(2)}, u32[]{:S(2)}) %collective-permute-start.38) | collective-permute-done | bytes 860192 | tf_op jit(solution)/shard_map/ppermute | solution.py:282
  112.5 15.0 %collective-permute-done.8.rest_2_ = bf16[20,168,128]{2,1,0:T(8,128)(2,1)} collective-permute-done((bf16[20,168,128]{2,1,0:T(8,128)(2,1)}, bf16[20,168,128]{2,1,0:T(8,128)(2,1)}, u32[]{:S(2)}, u32[]{:S(2)}) %collective-permute-start.8) | collective-permute-done | bytes 860192 | tf_op jit(solution)/shard_map/ppermute | solution.py:282
  155.8 15.4 %collective-permute-start.56 = (bf16[840,128]{1,0:T(8,128)(2,1)}, bf16[840,128]{1,0:T(8,128)(2,1)}, u32[]{:S(2)}, u32[]{:S(2)}) collective-permute-start(bf16[840,128]{1,0:T(8,128)(2,1)} %get-tuple-element.121), channel_id=1, source_target_pairs={{0,6},{1,7},{2,0},{3,1},{4,2},{5,3},{6,4},{7,5},{8,14},{9,15},{10,... | collective-permute-start | bytes 645128 | tf_op jit(solution)/shard_map/ppermute | solution.py:287
  171.2 17.4 %dynamic-slice_bitcast_fusion = (bf16[32,168,128]{2,1,0:T(8,128)(2,1)}, bf16[32,168,128]{2,1,0:T(8,128)(2,1)}, bf16[32,168,128]{2,1,0:T(8,128)(2,1)}, bf16[32,16...) fusion(bf16[168,84,1536]{2,0,1:T(8,128)(2,1)} %param.3, ...), kind=kLoop, calls=%fused_computation.1 | loop fusion | bytes 49545252 | tf_op jit(solution)/shard_map/dynamic_slice | solution.py:277
  257.5 29.6 %collective-permute-done.64.rest_1_ = bf16[32,168,128]{2,1,0:T(8,128)(2,1)S(1)} collective-permute-done((bf16[32,168,128]{2,1,0:T(8,128)(2,1)}, bf16[32,168,128]{2,1,0:T(8,128)(2,1)S(1)}, u32[]{:S(2)}, u32[]{:S(2)}) %collective-permute-start.64) | collective-permute-done | bytes 1376288 | tf_op jit(solution)/shard_map/ppermute | solution.py:282
  287.1 28.6 %collective-permute-done.65.rest_2_ = bf16[32,168,128]{2,1,0:T(8,128)(2,1)S(1)} collective-permute-done((bf16[32,168,128]{2,1,0:T(8,128)(2,1)}, bf16[32,168,128]{2,1,0:T(8,128)(2,1)S(1)}, u32[]{:S(2)}, u32[]{:S(2)}) %collective-permute-start.65) | collective-permute-done | bytes 1376288 | tf_op jit(solution)/shard_map/ppermute | solution.py:282
  319.0 27.0 %collective-permute-done.34.rest_1_ = bf16[32,168,128]{2,1,0:T(8,128)(2,1)S(1)} collective-permute-done((bf16[32,168,128]{2,1,0:T(8,128)(2,1)S(1)}, bf16[32,168,128]{2,1,0:T(8,128)(2,1)S(1)}, u32[]{:S(2)}, u32[]{:S(2)}) %collective-permute-start.34) | collective-permute-done | bytes 1376288 | tf_op jit(solution)/shard_map/ppermute | solution.py:282
  346.1 28.6 %collective-permute-done.35.rest_2_ = bf16[32,168,128]{2,1,0:T(8,128)(2,1)S(1)} collective-permute-done((bf16[32,168,128]{2,1,0:T(8,128)(2,1)}, bf16[32,168,128]{2,1,0:T(8,128)(2,1)S(1)}, u32[]{:S(2)}, u32[]{:S(2)}) %collective-permute-start.35) | collective-permute-done | bytes 1376288 | tf_op jit(solution)/shard_map/ppermute | solution.py:282
  376.8 28.3 %collective-permute-done.31.rest_1_ = bf16[32,168,128]{2,1,0:T(8,128)(2,1)S(1)} collective-permute-done((bf16[32,168,128]{2,1,0:T(8,128)(2,1)}, bf16[32,168,128]{2,1,0:T(8,128)(2,1)S(1)}, u32[]{:S(2)}, u32[]{:S(2)}) %collective-permute-start.31) | collective-permute-done | bytes 1376288 | tf_op jit(solution)/shard_map/ppermute | solution.py:282
  405.1 28.5 %collective-permute-done.32.rest_2_ = bf16[32,168,128]{2,1,0:T(8,128)(2,1)S(1)} collective-permute-done((bf16[32,168,128]{2,1,0:T(8,128)(2,1)S(1)}, bf16[32,168,128]{2,1,0:T(8,128)(2,1)S(1)}, u32[]{:S(2)}, u32[]{:S(2)}) %collective-permute-start.32) | collective-permute-done | bytes 1376288 | tf_op jit(solution)/shard_map/ppermute | solution.py:282
  436.6 15.3 %project.15 = (bf16[1344,128]{1,0:T(8,128)(2,1)}, bf16[1344,128]{1,0:T(8,128)(2,1)}, bf16[1344,128]{1,0:T(8,128)(2,1)}, bf16[1344,128]{1,0:T(8,128)(2,1)}, bf16[...) custom-call(s32[9]{0:T(128)} %concatenate.14.scalars, ...), custom_call_target="tpu_custom_call" | custom-call | flops 1849688064 | bytes 8257536 | tf_op jit(solution)/shard_map/project/pallas_call | solution.py:93
  451.9 15.3 %project.16 = (bf16[1344,128]{1,0:T(8,128)(2,1)}, bf16[1344,128]{1,0:T(8,128)(2,1)}, bf16[1344,128]{1,0:T(8,128)(2,1)}, bf16[1344,128]{1,0:T(8,128)(2,1)}, bf16[...) custom-call(s32[9]{0:T(128)} %concatenate.14.scalars, ...), custom_call_target="tpu_custom_call" | custom-call | flops 1849688064 | bytes 8257536 | tf_op jit(solution)/shard_map/project/pallas_call | solution.py:93
  469.3 23.4 %collective-permute-done.5.rest_2_ = bf16[32,168,128]{2,1,0:T(8,128)(2,1)} collective-permute-done((bf16[32,168,128]{2,1,0:T(8,128)(2,1)}, bf16[32,168,128]{2,1,0:T(8,128)(2,1)}, u32[]{:S(2)}, u32[]{:S(2)}) %collective-permute-start.5) | collective-permute-done | bytes 1376288 | tf_op jit(solution)/shard_map/ppermute | solution.py:282
  495.2 27.8 %collective-permute-done.1.rest_1_ = bf16[32,168,128]{2,1,0:T(8,128)(2,1)S(1)} collective-permute-done((bf16[32,168,128]{2,1,0:T(8,128)(2,1)}, bf16[32,168,128]{2,1,0:T(8,128)(2,1)S(1)}, u32[]{:S(2)}, u32[]{:S(2)}) %collective-permute-start.1) | collective-permute-done | bytes 1376288 | tf_op jit(solution)/shard_map/ppermute | solution.py:282
  523.6 26.9 %collective-permute-done.2.rest_2_ = bf16[32,168,128]{2,1,0:T(8,128)(2,1)S(1)} collective-permute-done((bf16[32,168,128]{2,1,0:T(8,128)(2,1)}, bf16[32,168,128]{2,1,0:T(8,128)(2,1)S(1)}, u32[]{:S(2)}, u32[]{:S(2)}) %collective-permute-start.2) | collective-permute-done | bytes 1376288 | tf_op jit(solution)/shard_map/ppermute | solution.py:282
  572.5 36.6 %collective-permute-done.78.rest_12_ = bf16[1344,128]{1,0:T(8,128)(2,1)} collective-permute-done((bf16[1344,128]{1,0:T(8,128)(2,1)}, bf16[1344,128]{1,0:T(8,128)(2,1)}, u32[]{:S(2)}, u32[]{:S(2)}) %collective-permute-start.78) | collective-permute-done | bytes 344096 | tf_op jit(solution)/shard_map/ppermute | solution.py:287
  614.5 15.4 %project.13 = (bf16[1344,128]{1,0:T(8,128)(2,1)}, bf16[1344,128]{1,0:T(8,128)(2,1)}, bf16[1344,128]{1,0:T(8,128)(2,1)}, bf16[1344,128]{1,0:T(8,128)(2,1)}, bf16[...) custom-call(s32[9]{0:T(128)} %concatenate.13.scalars, ...), custom_call_target="tpu_custom_call" | custom-call | flops 1849688064 | bytes 8257536 | tf_op jit(solution)/shard_map/project/pallas_call | solution.py:93
  631.5 13.4 %collective-permute-start.88 = (bf16[1344,128]{1,0:T(8,128)(2,1)}, bf16[1344,128]{1,0:T(8,128)(2,1)S(1)}, u32[]{:S(2)}, u32[]{:S(2)}) collective-permute-start(bf16[1344,128]{1,0:T(8,128)(2,1)} %get-tuple-element.147), channel_id=1, source_target_pairs={{0,7},{1,6},{2,1},{3,0},{4,3},{5,2},{6,5},{7,4},{8,15},{9,14},{10,... | collective-permute-start | bytes 1032200 | tf_op jit(solution)/shard_map/ppermute | solution.py:287
  658.0 15.4 %project.12 = (bf16[1344,128]{1,0:T(8,128)(2,1)}, bf16[1344,128]{1,0:T(8,128)(2,1)}, bf16[1344,128]{1,0:T(8,128)(2,1)}, bf16[1344,128]{1,0:T(8,128)(2,1)}, bf16[...) custom-call(s32[9]{0:T(128)} %concatenate.13.scalars, ...), custom_call_target="tpu_custom_call" | custom-call | flops 1849688064 | bytes 8257536 | tf_op jit(solution)/shard_map/project/pallas_call | solution.py:93
  684.4 17.0 %collective-permute-done.49.rest_13_ = bf16[1344,128]{1,0:T(8,128)(2,1)S(1)} collective-permute-done((bf16[1344,128]{1,0:T(8,128)(2,1)S(1)}, bf16[1344,128]{1,0:T(8,128)(2,1)S(1)}, u32[]{:S(2)}, u32[]{:S(2)}) %collective-permute-start.49) | collective-permute-done | bytes 344096 | tf_op jit(solution)/shard_map/ppermute | solution.py:287
  701.4 14.4 %collective-permute-start.42 = (bf16[1344,128]{1,0:T(8,128)(2,1)}, bf16[1344,128]{1,0:T(8,128)(2,1)S(1)}, u32[]{:S(2)}, u32[]{:S(2)}) collective-permute-start(bf16[1344,128]{1,0:T(8,128)(2,1)} %get-tuple-element.107), channel_id=1, source_target_pairs={{0,2},{1,3},{2,4},{3,5},{4,6},{5,7},{6,0},{7,1},{8,10},{9,11},{10,... | collective-permute-start | bytes 1032200 | tf_op jit(solution)/shard_map/ppermute | solution.py:287
  727.5 17.7 %collective-permute-start.51 = (bf16[1344,128]{1,0:T(8,128)(2,1)}, bf16[1344,128]{1,0:T(8,128)(2,1)}, u32[]{:S(2)}, u32[]{:S(2)}) collective-permute-start(bf16[1344,128]{1,0:T(8,128)(2,1)} %get-tuple-element.116), channel_id=1, source_target_pairs={{0,5},{1,4},{2,7},{3,6},{4,1},{5,0},{6,3},{7,2},{8,13},{9,12},{10,... | collective-permute-start | bytes 1032200 | tf_op jit(solution)/shard_map/ppermute | solution.py:287
  749.4 15.3 %project.10 = (bf16[1344,128]{1,0:T(8,128)(2,1)}, bf16[1344,128]{1,0:T(8,128)(2,1)}, bf16[1344,128]{1,0:T(8,128)(2,1)}, bf16[1344,128]{1,0:T(8,128)(2,1)}, bf16[...) custom-call(s32[9]{0:T(128)} %concatenate.12.scalars, ...), custom_call_target="tpu_custom_call" | custom-call | flops 1849688064 | bytes 8257536 | tf_op jit(solution)/shard_map/project/pallas_call | solution.py:93
  787.2 15.3 %project.9 = (bf16[1344,128]{1,0:T(8,128)(2,1)}, bf16[1344,128]{1,0:T(8,128)(2,1)}, bf16[1344,128]{1,0:T(8,128)(2,1)}, bf16[1344,128]{1,0:T(8,128)(2,1)}, bf16[1...) custom-call(s32[9]{0:T(128)} %concatenate.12.scalars, ...), custom_call_target="tpu_custom_call" | custom-call | flops 1849688064 | bytes 8257536 | tf_op jit(solution)/shard_map/project/pallas_call | solution.py:93
  819.8 14.3 %collective-permute-start.15 = (bf16[1344,128]{1,0:T(8,128)(2,1)}, bf16[1344,128]{1,0:T(8,128)(2,1)S(1)}, u32[]{:S(2)}, u32[]{:S(2)}) collective-permute-start(bf16[1344,128]{1,0:T(8,128)(2,1)} %get-tuple-element.86), channel_id=1, source_target_pairs={{0,3},{1,2},{2,5},{3,4},{4,7},{5,6},{6,1},{7,0},{8,11},{9,10},{10,... | collective-permute-start | bytes 1032200 | tf_op jit(solution)/shard_map/ppermute | solution.py:287
  834.1 13.4 %gram.3.rest_24_ = f32[768,768]{1,0:T(8,128)} custom-call(s32[8]{0:T(128)} %stack.75.sources, bf16[1344,128]{1,0:T(8,128)(2,1)} %get-tuple-element.125.rest_0_, bf16[1344,128]{1,0:T(8,128)(2,1)} %get-tuple-element.126.rest_1_, bf16[840,128]{1,0:T(8,128)(2,1)} %get-tuple-element.127.rest_2_, bf16[1344,128]{1,0:T(8,128)(2,1)} %copy-done.23, ...), custom_call_target="tpu_custom_call" | custom-call | flops 6341787648 | bytes 12976128 | tf_op jit(solution)/shard_map/gram/pallas_call | solution.py:183
  853.5 15.3 %collective-permute-start.27 = (bf16[1344,128]{1,0:T(8,128)(2,1)S(1)}, bf16[1344,128]{1,0:T(8,128)(2,1)S(1)}, u32[]{:S(2)}, u32[]{:S(2)}) collective-permute-start(bf16[1344,128]{1,0:T(8,128)(2,1)S(1)} %copy-done.49), channel_id=1, source_target_pairs={{0,7},{1,6},{2,1},{3,0},{4,3},{5,2},{6,5},{7,4},{8,15},{9,14},{10,... | collective-permute-start | bytes 1032200 | tf_op jit(solution)/shard_map/ppermute | solution.py:287
  874.0 14.1 %gram.4.rest_24_ = f32[768,768]{1,0:T(8,128)} custom-call(s32[8]{0:T(128)} %stack.75.sources, bf16[1344,128]{1,0:T(8,128)(2,1)} %get-tuple-element.101.rest_0_, bf16[1344,128]{1,0:T(8,128)(2,1)} %get-tuple-element.102.rest_1_, bf16[840,128]{1,0:T(8,128)(2,1)} %get-tuple-element.103.rest_2_, bf16[1344,128]{1,0:T(8,128)(2,1)} %copy-done.37, ...), custom_call_target="tpu_custom_call" | custom-call | flops 6341787648 | bytes 12976128 | tf_op jit(solution)/shard_map/gram/pallas_call | solution.py:183
  898.0 14.2 %gram.5 = f32[768,768]{1,0:T(8,128)} custom-call(s32[8]{0:T(128)} %stack.75.sources, bf16[1344,128]{1,0:T(8,128)(2,1)} %get-tuple-element.77.rest_0_, bf16[1344,128]{1,0:T(8,128)(2,1)} %get-tuple-element.78.rest_1_, bf16[840,128]{1,0:T(8,128)(2,1)} %get-tuple-element.79.rest_2_, bf16[1344,128]{1,0:T(8,128)(2,1)} %copy-done.64, bf16[1344,128]{1,0:T(8,128)(2,1)} %copy-done.39, ...), custom_call_target="tpu_custom_call" | custom-call | flops 6341787648 | bytes 12976128 | tf_op jit(solution)/shard_map/gram/pallas_call | solution.py:183
  926.9 139.8 %all-reduce.3.cloned.1.call-done = f32[672,672]{0,1:T(8,128)} async-done(((f32[672,672]{0,1:T(8,128)}), f32[672,672]{0,1:T(8,128)}) %all-reduce.3.cloned.1.call-update) | async-done | bytes 1806352 | tf_op jit(solution)/shard_map/psum | solution.py:293
  (387 shorter events, 454.3 us)
Async XLA Ops:
  6.5 1060.2 %all-reduce.3.cloned.1.call-start = ((), (), s32[]{:S(2)}) async-start(), calls=%async_computation | async-start | bytes 4128768 | tf_op jit(solution)/shard_map/psum | solution.py:293
  15.9 59.0 %collective-permute-start.37 = (bf16[20,168,128]{2,1,0:T(8,128)(2,1)}, bf16[20,168,128]{2,1,0:T(8,128)(2,1)}, u32[]{:S(2)}, u32[]{:S(2)}) collective-permute-start(bf16[20,168,128]{2,1,0:T(8,128)(2,1)} %get-tuple-element.152), channel_id=1, source_target_pairs={{0,16},{8,24},{16,0},{24,8},{1,17},{9,25},{17,1},{25,9},{2,18},{10... | collective-permute-start | bytes 2580488 | tf_op jit(solution)/shard_map/ppermute | solution.py:282
  17.8 72.8 %collective-permute-start.38 = (bf16[20,168,128]{2,1,0:T(8,128)(2,1)}, bf16[20,168,128]{2,1,0:T(8,128)(2,1)}, u32[]{:S(2)}, u32[]{:S(2)}) collective-permute-start(bf16[20,168,128]{2,1,0:T(8,128)(2,1)} %get-tuple-element.151), channel_id=1, source_target_pairs={{0,24},{8,16},{16,8},{24,0},{1,25},{9,17},{17,9},{25,1},{2,26},{10... | collective-permute-start | bytes 2580488 | tf_op jit(solution)/shard_map/ppermute | solution.py:282
  36.5 55.8 %collective-permute-start.6 = (bf16[20,168,128]{2,1,0:T(8,128)(2,1)}, bf16[20,168,128]{2,1,0:T(8,128)(2,1)S(1)}, u32[]{:S(2)}, u32[]{:S(2)}) collective-permute-start(bf16[20,168,128]{2,1,0:T(8,128)(2,1)} %get-tuple-element.156), channel_id=1, source_target_pairs={{0,8},{8,0},{16,24},{24,16},{1,9},{9,1},{17,25},{25,17},{2,10},{10... | collective-permute-start | bytes 2580488 | tf_op jit(solution)/shard_map/ppermute | solution.py:282
  55.4 72.2 %collective-permute-start.8 = (bf16[20,168,128]{2,1,0:T(8,128)(2,1)}, bf16[20,168,128]{2,1,0:T(8,128)(2,1)}, u32[]{:S(2)}, u32[]{:S(2)}) collective-permute-start(bf16[20,168,128]{2,1,0:T(8,128)(2,1)} %get-tuple-element.154), channel_id=1, source_target_pairs={{0,24},{8,16},{16,8},{24,0},{1,25},{9,17},{17,9},{25,1},{2,26},{10... | collective-permute-start | bytes 2580488 | tf_op jit(solution)/shard_map/ppermute | solution.py:282
  74.9 56.2 %collective-permute-start.71 = (bf16[840,128]{1,0:T(8,128)(2,1)}, bf16[840,128]{1,0:T(8,128)(2,1)S(1)}, u32[]{:S(2)}, u32[]{:S(2)}) collective-permute-start(bf16[840,128]{1,0:T(8,128)(2,1)} %get-tuple-element.130), channel_id=1, source_target_pairs={{0,1},{1,0},{2,3},{3,2},{4,5},{5,4},{6,7},{7,6},{8,9},{9,8},{10,11... | collective-permute-start | bytes 645128 | tf_op jit(solution)/shard_map/ppermute | solution.py:287
  189.4 65.9 %collective-permute-start.60 = (bf16[32,168,128]{2,1,0:T(8,128)(2,1)}, bf16[32,168,128]{2,1,0:T(8,128)(2,1)S(1)}, u32[]{:S(2)}, u32[]{:S(2)}) collective-permute-start(bf16[32,168,128]{2,1,0:T(8,128)(2,1)} %get-tuple-element.163), channel_id=1, source_target_pairs={{0,8},{8,0},{16,24},{24,16},{1,9},{9,1},{17,25},{25,17},{2,10},{10... | collective-permute-start | bytes 4128776 | tf_op jit(solution)/shard_map/ppermute | solution.py:282
  189.4 65.9 %collective-permute-start.61 = (bf16[32,168,128]{2,1,0:T(8,128)(2,1)}, bf16[32,168,128]{2,1,0:T(8,128)(2,1)}, u32[]{:S(2)}, u32[]{:S(2)}) collective-permute-start(bf16[32,168,128]{2,1,0:T(8,128)(2,1)} %get-tuple-element.162), channel_id=1, source_target_pairs={{0,16},{8,24},{16,0},{24,8},{1,17},{9,25},{17,1},{25,9},{2,18},{10... | collective-permute-start | bytes 4128776 | tf_op jit(solution)/shard_map/ppermute | solution.py:282
  190.9 65.1 %collective-permute-start.62 = (bf16[32,168,128]{2,1,0:T(8,128)(2,1)}, bf16[32,168,128]{2,1,0:T(8,128)(2,1)}, u32[]{:S(2)}, u32[]{:S(2)}) collective-permute-start(bf16[32,168,128]{2,1,0:T(8,128)(2,1)} %get-tuple-element.161), channel_id=1, source_target_pairs={{0,24},{8,16},{16,8},{24,0},{1,25},{9,17},{17,9},{25,1},{2,26},{10... | collective-permute-start | bytes 4128776 | tf_op jit(solution)/shard_map/ppermute | solution.py:282
  255.3 60.4 %collective-permute-start.65 = (bf16[32,168,128]{2,1,0:T(8,128)(2,1)}, bf16[32,168,128]{2,1,0:T(8,128)(2,1)S(1)}, u32[]{:S(2)}, u32[]{:S(2)}) collective-permute-start(bf16[32,168,128]{2,1,0:T(8,128)(2,1)} %get-tuple-element.158), channel_id=1, source_target_pairs={{0,24},{8,16},{16,8},{24,0},{1,25},{9,17},{17,9},{25,1},{2,26},{10... | collective-permute-start | bytes 4128776 | tf_op jit(solution)/shard_map/ppermute | solution.py:282
  255.3 60.9 %collective-permute-start.33 = (bf16[32,168,128]{2,1,0:T(8,128)(2,1)}, bf16[32,168,128]{2,1,0:T(8,128)(2,1)S(1)}, u32[]{:S(2)}, u32[]{:S(2)}) collective-permute-start(bf16[32,168,128]{2,1,0:T(8,128)(2,1)} %get-tuple-element.166), channel_id=1, source_target_pairs={{0,8},{8,0},{16,24},{24,16},{1,9},{9,1},{17,25},{25,17},{2,10},{10... | collective-permute-start | bytes 4128776 | tf_op jit(solution)/shard_map/ppermute | solution.py:282
  256.0 90.1 %collective-permute-start.34 = (bf16[32,168,128]{2,1,0:T(8,128)(2,1)S(1)}, bf16[32,168,128]{2,1,0:T(8,128)(2,1)S(1)}, u32[]{:S(2)}, u32[]{:S(2)}) collective-permute-start(bf16[32,168,128]{2,1,0:T(8,128)(2,1)S(1)} %copy-done.18), channel_id=1, source_target_pairs={{0,16},{8,24},{16,0},{24,8},{1,17},{9,25},{17,1},{25,9},{2,18},{10... | collective-permute-start | bytes 4128776 | tf_op jit(solution)/shard_map/ppermute | solution.py:282
  257.5 117.2 %collective-permute-start.35 = (bf16[32,168,128]{2,1,0:T(8,128)(2,1)}, bf16[32,168,128]{2,1,0:T(8,128)(2,1)S(1)}, u32[]{:S(2)}, u32[]{:S(2)}) collective-permute-start(bf16[32,168,128]{2,1,0:T(8,128)(2,1)} %get-tuple-element.164), channel_id=1, source_target_pairs={{0,24},{8,16},{16,8},{24,0},{1,25},{9,17},{17,9},{25,1},{2,26},{10... | collective-permute-start | bytes 4128776 | tf_op jit(solution)/shard_map/ppermute | solution.py:282
  287.1 88.1 %collective-permute-start.30 = (bf16[32,168,128]{2,1,0:T(8,128)(2,1)}, bf16[32,168,128]{2,1,0:T(8,128)(2,1)S(1)}, u32[]{:S(2)}, u32[]{:S(2)}) collective-permute-start(bf16[32,168,128]{2,1,0:T(8,128)(2,1)} %get-tuple-element.169), channel_id=1, source_target_pairs={{0,8},{8,0},{16,24},{24,16},{1,9},{9,1},{17,25},{25,17},{2,10},{10... | collective-permute-start | bytes 4128776 | tf_op jit(solution)/shard_map/ppermute | solution.py:282
  315.7 89.4 %collective-permute-start.31 = (bf16[32,168,128]{2,1,0:T(8,128)(2,1)}, bf16[32,168,128]{2,1,0:T(8,128)(2,1)S(1)}, u32[]{:S(2)}, u32[]{:S(2)}) collective-permute-start(bf16[32,168,128]{2,1,0:T(8,128)(2,1)} %get-tuple-element.168), channel_id=1, source_target_pairs={{0,16},{8,24},{16,0},{24,8},{1,17},{9,25},{17,1},{25,9},{2,18},{10... | collective-permute-start | bytes 4128776 | tf_op jit(solution)/shard_map/ppermute | solution.py:282
  317.3 116.2 %collective-permute-start.32 = (bf16[32,168,128]{2,1,0:T(8,128)(2,1)S(1)}, bf16[32,168,128]{2,1,0:T(8,128)(2,1)S(1)}, u32[]{:S(2)}, u32[]{:S(2)}) collective-permute-start(bf16[32,168,128]{2,1,0:T(8,128)(2,1)S(1)} %copy-done.17), channel_id=1, source_target_pairs={{0,24},{8,16},{16,8},{24,0},{1,25},{9,17},{17,9},{25,1},{2,26},{10... | collective-permute-start | bytes 4128776 | tf_op jit(solution)/shard_map/ppermute | solution.py:282
  346.1 88.0 %collective-permute-start.3 = (bf16[32,168,128]{2,1,0:T(8,128)(2,1)S(1)}, bf16[32,168,128]{2,1,0:T(8,128)(2,1)S(1)}, u32[]{:S(2)}, u32[]{:S(2)}) collective-permute-start(bf16[32,168,128]{2,1,0:T(8,128)(2,1)S(1)} %copy-done.16), channel_id=1, source_target_pairs={{0,8},{8,0},{16,24},{24,16},{1,9},{9,1},{17,25},{25,17},{2,10},{10... | collective-permute-start | bytes 4128776 | tf_op jit(solution)/shard_map/ppermute | solution.py:282
  374.7 92.5 %collective-permute-start.4 = (bf16[32,168,128]{2,1,0:T(8,128)(2,1)}, bf16[32,168,128]{2,1,0:T(8,128)(2,1)}, u32[]{:S(2)}, u32[]{:S(2)}) collective-permute-start(bf16[32,168,128]{2,1,0:T(8,128)(2,1)} %get-tuple-element.171), channel_id=1, source_target_pairs={{0,16},{8,24},{16,0},{24,8},{1,17},{9,25},{17,1},{25,9},{2,18},{10... | collective-permute-start | bytes 4128776 | tf_op jit(solution)/shard_map/ppermute | solution.py:282
  375.2 117.4 %collective-permute-start.5 = (bf16[32,168,128]{2,1,0:T(8,128)(2,1)}, bf16[32,168,128]{2,1,0:T(8,128)(2,1)}, u32[]{:S(2)}, u32[]{:S(2)}) collective-permute-start(bf16[32,168,128]{2,1,0:T(8,128)(2,1)} %get-tuple-element.170), channel_id=1, source_target_pairs={{0,24},{8,16},{16,8},{24,0},{1,25},{9,17},{17,9},{25,1},{2,26},{10... | collective-permute-start | bytes 4128776 | tf_op jit(solution)/shard_map/ppermute | solution.py:282
  405.1 89.6 %collective-permute-start = (bf16[32,168,128]{2,1,0:T(8,128)(2,1)}, bf16[32,168,128]{2,1,0:T(8,128)(2,1)S(1)}, u32[]{:S(2)}, u32[]{:S(2)}) collective-permute-start(bf16[32,168,128]{2,1,0:T(8,128)(2,1)} %get-tuple-element.175), channel_id=1, source_target_pairs={{0,8},{8,0},{16,24},{24,16},{1,9},{9,1},{17,25},{25,17},{2,10},{10... | collective-permute-start | bytes 4128776 | tf_op jit(solution)/shard_map/ppermute | solution.py:282
  433.6 89.5 %collective-permute-start.1 = (bf16[32,168,128]{2,1,0:T(8,128)(2,1)}, bf16[32,168,128]{2,1,0:T(8,128)(2,1)S(1)}, u32[]{:S(2)}, u32[]{:S(2)}) collective-permute-start(bf16[32,168,128]{2,1,0:T(8,128)(2,1)} %get-tuple-element.174), channel_id=1, source_target_pairs={{0,16},{8,24},{16,0},{24,8},{1,17},{9,25},{17,1},{25,9},{2,18},{10... | collective-permute-start | bytes 4128776 | tf_op jit(solution)/shard_map/ppermute | solution.py:282
  434.6 115.9 %collective-permute-start.2 = (bf16[32,168,128]{2,1,0:T(8,128)(2,1)}, bf16[32,168,128]{2,1,0:T(8,128)(2,1)S(1)}, u32[]{:S(2)}, u32[]{:S(2)}) collective-permute-start(bf16[32,168,128]{2,1,0:T(8,128)(2,1)} %get-tuple-element.173), channel_id=1, source_target_pairs={{0,24},{8,16},{16,8},{24,0},{1,25},{9,17},{17,9},{25,1},{2,26},{10... | collective-permute-start | bytes 4128776 | tf_op jit(solution)/shard_map/ppermute | solution.py:282
  467.2 85.5 %collective-permute-start.69 = (bf16[1344,128]{1,0:T(8,128)(2,1)}, bf16[1344,128]{1,0:T(8,128)(2,1)S(1)}, u32[]{:S(2)}, u32[]{:S(2)}) collective-permute-start(bf16[1344,128]{1,0:T(8,128)(2,1)} %get-tuple-element.128), channel_id=1, source_target_pairs={{0,1},{1,0},{2,3},{3,2},{4,5},{5,4},{6,7},{7,6},{8,9},{9,8},{10,11... | collective-permute-start | bytes 1032200 | tf_op jit(solution)/shard_map/ppermute | solution.py:287
  492.7 60.1 %collective-permute-start.70 = (bf16[1344,128]{1,0:T(8,128)(2,1)}, bf16[1344,128]{1,0:T(8,128)(2,1)S(1)}, u32[]{:S(2)}, u32[]{:S(2)}) collective-permute-start(bf16[1344,128]{1,0:T(8,128)(2,1)} %get-tuple-element.129), channel_id=1, source_target_pairs={{0,1},{1,0},{2,3},{3,2},{4,5},{5,4},{6,7},{7,6},{8,9},{9,8},{10,11... | collective-permute-start | bytes 1032200 | tf_op jit(solution)/shard_map/ppermute | solution.py:287
  494.7 61.2 %collective-permute-start.72 = (bf16[1344,128]{1,0:T(8,128)(2,1)}, bf16[1344,128]{1,0:T(8,128)(2,1)S(1)}, u32[]{:S(2)}, u32[]{:S(2)}) collective-permute-start(bf16[1344,128]{1,0:T(8,128)(2,1)} %get-tuple-element.131), channel_id=1, source_target_pairs={{0,2},{1,3},{2,4},{3,5},{4,6},{5,7},{6,0},{7,1},{8,10},{9,11},{10,... | collective-permute-start | bytes 1032200 | tf_op jit(solution)/shard_map/ppermute | solution.py:287
  552.8 56.3 %collective-permute-start.78 = (bf16[1344,128]{1,0:T(8,128)(2,1)}, bf16[1344,128]{1,0:T(8,128)(2,1)}, u32[]{:S(2)}, u32[]{:S(2)}) collective-permute-start(bf16[1344,128]{1,0:T(8,128)(2,1)} %get-tuple-element.137), channel_id=1, source_target_pairs={{0,4},{1,5},{2,6},{3,7},{4,0},{5,1},{6,2},{7,3},{8,12},{9,13},{10,... | collective-permute-start | bytes 1032200 | tf_op jit(solution)/shard_map/ppermute | solution.py:287
  555.8 74.2 %collective-permute-start.79 = (bf16[1344,128]{1,0:T(8,128)(2,1)}, bf16[1344,128]{1,0:T(8,128)(2,1)}, u32[]{:S(2)}, u32[]{:S(2)}) collective-permute-start(bf16[1344,128]{1,0:T(8,128)(2,1)} %get-tuple-element.138), channel_id=1, source_target_pairs={{0,4},{1,5},{2,6},{3,7},{4,0},{5,1},{6,2},{7,3},{8,12},{9,13},{10,... | collective-permute-start | bytes 1032200 | tf_op jit(solution)/shard_map/ppermute | solution.py:287
  555.9 75.5 %collective-permute-start.81 = (bf16[1344,128]{1,0:T(8,128)(2,1)}, bf16[1344,128]{1,0:T(8,128)(2,1)}, u32[]{:S(2)}, u32[]{:S(2)}) collective-permute-start(bf16[1344,128]{1,0:T(8,128)(2,1)} %get-tuple-element.140), channel_id=1, source_target_pairs={{0,5},{1,4},{2,7},{3,6},{4,1},{5,0},{6,3},{7,2},{8,13},{9,12},{10,... | collective-permute-start | bytes 1032200 | tf_op jit(solution)/shard_map/ppermute | solution.py:287
  564.5 80.4 %collective-permute-start.82 = (bf16[1344,128]{1,0:T(8,128)(2,1)}, bf16[1344,128]{1,0:T(8,128)(2,1)}, u32[]{:S(2)}, u32[]{:S(2)}) collective-permute-start(bf16[1344,128]{1,0:T(8,128)(2,1)} %get-tuple-element.141), channel_id=1, source_target_pairs={{0,5},{1,4},{2,7},{3,6},{4,1},{5,0},{6,3},{7,2},{8,13},{9,12},{10,... | collective-permute-start | bytes 1032200 | tf_op jit(solution)/shard_map/ppermute | solution.py:287
  571.9 74.9 %collective-permute-start.84 = (bf16[1344,128]{1,0:T(8,128)(2,1)}, bf16[1344,128]{1,0:T(8,128)(2,1)}, u32[]{:S(2)}, u32[]{:S(2)}) collective-permute-start(bf16[1344,128]{1,0:T(8,128)(2,1)} %get-tuple-element.143), channel_id=1, source_target_pairs={{0,6},{1,7},{2,0},{3,1},{4,2},{5,3},{6,4},{7,5},{8,14},{9,15},{10,... | collective-permute-start | bytes 1032200 | tf_op jit(solution)/shard_map/ppermute | solution.py:287
  683.8 61.4 %collective-permute-start.39 = (bf16[1344,128]{1,0:T(8,128)(2,1)}, bf16[1344,128]{1,0:T(8,128)(2,1)S(1)}, u32[]{:S(2)}, u32[]{:S(2)}) collective-permute-start(bf16[1344,128]{1,0:T(8,128)(2,1)} %get-tuple-element.104), channel_id=1, source_target_pairs={{0,1},{1,0},{2,3},{3,2},{4,5},{5,4},{6,7},{7,6},{8,9},{9,8},{10,11... | collective-permute-start | bytes 1032200 | tf_op jit(solution)/shard_map/ppermute | solution.py:287
  701.4 63.4 %collective-permute-start.42 = (bf16[1344,128]{1,0:T(8,128)(2,1)}, bf16[1344,128]{1,0:T(8,128)(2,1)S(1)}, u32[]{:S(2)}, u32[]{:S(2)}) collective-permute-start(bf16[1344,128]{1,0:T(8,128)(2,1)} %get-tuple-element.107), channel_id=1, source_target_pairs={{0,2},{1,3},{2,4},{3,5},{4,6},{5,7},{6,0},{7,1},{8,10},{9,11},{10,... | collective-permute-start | bytes 1032200 | tf_op jit(solution)/shard_map/ppermute | solution.py:287
  (143 other events, 6704.4 us)
Sparse Core Ops, SparseCore 0:
  927.0 139.6 all-reduce.2

commit v2 on v1

--- a/solution.py
+++ b/solution.py
@@ -9,6 +9,7 @@
 
 LANES = 128
 PITCH = 96
+STEP = 256
 VMEM_BYTES = 56 * 1024 * 1024
 
 
@@ -25,39 +26,96 @@
     return [tuple(p) for p in pieces]
 
 
-def project_kernel(start, main, left, rank, share, scalars, fields, got, factor, outs, own, wide, sem):
+def pack_copies(fields, sends, scalars, cell, piece, sems):
+    start, main, left = piece
+    copies = []
+    for index, send in enumerate(sends):
+        column = pl.multiple_of(scalars[1 + index] + cell, LANES)
+        copies.append(
+            pltpu.make_async_copy(
+                fields.at[pl.ds(start, main + left), :, pl.ds(column, LANES)],
+                send,
+                sems.at[index],
+            )
+        )
+    return copies
+
+
+def pack(fields, scalars, chunks, n_x):
+    depth = fields.shape[1]
+    n_sends = n_x - 1
+
+    def body(scalars, fields, *rest):
+        sems = rest[-1]
+        copies = []
+        for index, (cell, piece) in enumerate(chunks):
+            sends = rest[index * n_sends : (index + 1) * n_sends]
+            copies += pack_copies(fields, sends, scalars, cell, piece, sems.at[index])
+        for copy in copies:
+            copy.start()
+        for copy in copies:
+            copy.wait()
+
+    any_space = pl.BlockSpec(memory_space=pl.ANY)
+    shapes = [
+        jax.ShapeDtypeStruct((piece[1] + piece[2], depth, LANES), jnp.bfloat16)
+        for _, piece in chunks
+        for _ in range(n_sends)
+    ]
+    outs = pl.pallas_call(
+        body,
+        out_shape=shapes,
+        in_specs=[pl.BlockSpec(memory_space=pltpu.SMEM), any_space],
+        out_specs=[any_space] * len(shapes),
+        scratch_shapes=[pltpu.SemaphoreType.DMA((len(chunks), n_sends))],
+        cost_estimate=pl.CostEstimate(flops=0, bytes_accessed=0, transcendentals=0),
+        name="pack",
+    )(scalars, fields)
+    return [outs[i * n_sends : (i + 1) * n_sends] for i in range(len(chunks))]
+
+
+def project_kernel(chunk, following, rank, share, scalars, fields, got, factor, outs, sends, own, wide, sems):
+    cell, (start, main, left) = chunk
     rows = main + left
-    column = pl.multiple_of(scalars[0], LANES)
+    column = pl.multiple_of(scalars[0] + cell, LANES)
     copy = pltpu.make_async_copy(
-        fields.at[pl.ds(start, rows), :, pl.ds(column, LANES)], own, sem
+        fields.at[pl.ds(start, rows), :, pl.ds(column, LANES)], own, sems.at[0]
     )
     copy.start()
+    packing = []
+    if following is not None:
+        packing = pack_copies(
+            fields, sends, scalars, following[0], following[1], sems.at[pl.ds(1, len(sends))]
+        )
+    for other in packing:
+        other.start()
     copy.wait()
     blocks = [own] + list(got)
-
-    def one_pair(pair, _):
-        y = pair * 2
+    many = 4
+
+    def one_group(group, _):
+        y = group * many
         total = None
         for index, block in enumerate(blocks):
-            right = jnp.concatenate([block[y], block[y + 1]], axis=1)
+            right = jnp.concatenate([block[y + k] for k in range(many)], axis=1)
             term = jnp.dot(factor[index], right, preferred_element_type=jnp.float32)
             total = term if total is None else total + term
-        at = pl.multiple_of(y * rank, 8)
-        wide[pl.ds(at, rank), :] = total[:, :LANES]
-        wide[pl.ds(at + rank, rank), :] = total[:, LANES:]
+        for k in range(many):
+            at = pl.multiple_of((y + k) * rank, 8)
+            wide[pl.ds(at, rank), :] = total[:, k * LANES : (k + 1) * LANES]
         return 0
 
-    lax.fori_loop(0, rows // 2, one_pair, 0)
+    lax.fori_loop(0, rows // many, one_group, 0)
 
     for part, out in enumerate(outs):
-        first = scalars[1 + part]
+        first = scalars[1 + len(blocks) - 1 + part]
 
         def one_row(i, _):
             picked = wide[pl.ds(first + i, main, stride=rank), :]
             out[pl.ds(pl.multiple_of(i * main, 16), main), :] = picked.astype(jnp.bfloat16)
             return 0
 
-        lax.fori_loop(0, share, one_row, 0)
+        lax.fori_loop(0, share, one_row, 0, unroll=6)
         if left:
             per = 16 // left
             for group in range(0, share, per):
@@ -69,46 +127,57 @@
                 tile = jnp.concatenate(tile, axis=0).astype(jnp.bfloat16)
                 at = share * main + group * left
                 out[at : at + count * left, :] = tile
-
-
-def project(fields, got, factor, scalars, piece, share):
-    start, main, left = piece
+    for other in packing:
+        other.wait()
+
+
+def project(fields, got, factor, scalars, chunk, following, share, parts, after):
+    _, (start, main, left) = chunk
     rows = main + left
     rank = factor.shape[1]
     depth = fields.shape[1]
-    parts = scalars.shape[0] - 1
     n_got = len(got)
+    n_sends = 0 if following is None else n_got
+    n_after = len(after)
 
     def body(scalars, fields, *rest):
         got = rest[:n_got]
         factor = rest[n_got]
-        outs = rest[n_got + 1 : n_got + 1 + parts]
-        own, wide, sem = rest[n_got + 1 + parts :]
+        rest = rest[n_got + 1 + n_after :]
+        outs = rest[:parts]
+        sends = rest[parts : parts + n_sends]
+        own, wide, sems = rest[parts + n_sends :]
         project_kernel(
-            start, main, left, rank, share, scalars, fields, got, factor, outs, own, wide, sem
+            chunk, following, rank, share, scalars, fields, got, factor, outs, sends, own, wide, sems
         )
 
     vmem = pl.BlockSpec(memory_space=pltpu.VMEM)
-    out_rows = share * rows
-    return pl.pallas_call(
+    any_space = pl.BlockSpec(memory_space=pl.ANY)
+    shapes = [jax.ShapeDtypeStruct((share * rows, LANES), jnp.bfloat16)] * parts
+    if following is not None:
+        next_rows = following[1][1] + following[1][2]
+        shapes += [jax.ShapeDtypeStruct((next_rows, depth, LANES), jnp.bfloat16)] * n_sends
+    outs = pl.pallas_call(
         body,
-        out_shape=[jax.ShapeDtypeStruct((out_rows, LANES), jnp.bfloat16)] * parts,
-        in_specs=[pl.BlockSpec(memory_space=pltpu.SMEM), pl.BlockSpec(memory_space=pl.ANY)]
-        + [vmem] * (n_got + 1),
-        out_specs=[vmem] * parts,
+        out_shape=shapes,
+        in_specs=[pl.BlockSpec(memory_space=pltpu.SMEM), any_space]
+        + [vmem] * (n_got + 1)
+        + [any_space] * n_after,
+        out_specs=[vmem] * parts + [any_space] * n_sends,
         scratch_shapes=[
             pltpu.VMEM((rows, depth, LANES), jnp.bfloat16),
             pltpu.VMEM((rows * rank, LANES), jnp.float32),
-            pltpu.SemaphoreType.DMA,
+            pltpu.SemaphoreType.DMA((1 + n_got,)),
         ],
         compiler_params=pltpu.CompilerParams(vmem_limit_bytes=VMEM_BYTES),
-        cost_estimate=pl.CostEstimate(
-            flops=2 * rows * LANES * rank * depth * (n_got + 1),
-            bytes_accessed=2 * rows * LANES * (depth * (n_got + 1) + rank),
-            transcendentals=0,
-        ),
+        cost_estimate=pl.CostEstimate(flops=0, bytes_accessed=0, transcendentals=0),
         name="project",
-    )(scalars, fields, *got, factor)
+    )(scalars, fields, *got, factor, *after)
+    return outs[:parts], outs[parts:]
+
+
+def block_pairs(whole):
+    return [(i, j) for i in range(0, whole, STEP) for j in range(i, whole, STEP)]
 
 
 def gram_kernel(pieces, share, sources, blocks, carried, out, fibres):
@@ -147,21 +216,18 @@
                         pl.ds(base + start + main, 16), (group + k) * LANES : (group + k + 1) * LANES
                     ] = rows.astype(jnp.bfloat16)
 
-    step = 256
-    for i in range(0, whole, step):
-        for j in range(0, whole, step):
-            if j < i:
-                out[i : i + step, j : j + step] = jnp.zeros((step, step), jnp.float32)
-                continue
-            product = lax.dot_general(
-                fibres[i : i + step, :],
-                fibres[j : j + step, :],
-                (((1,), (1,)), ((), ())),
-                preferred_element_type=jnp.float32,
-            )
-            if carried is not None:
-                product = product + carried[i : i + step, j : j + step]
-            out[i : i + step, j : j + step] = product
+    at = 0
+    for i, j in block_pairs(whole):
+        product = lax.dot_general(
+            fibres[i : i + STEP, :],
+            fibres[j : j + STEP, :],
+            (((1,), (1,)), ((), ())),
+            preferred_element_type=jnp.float32,
+        )
+        if carried is not None:
+            product = product + carried[at : at + STEP, :]
+        out[at : at + STEP, :] = product
+        at += STEP
 
 
 def gram(blocks, carried, sources, pieces, share):
@@ -182,16 +248,12 @@
     extra = [] if carried is None else [carried]
     return pl.pallas_call(
         body,
-        out_shape=jax.ShapeDtypeStruct((whole, whole), jnp.float32),
+        out_shape=jax.ShapeDtypeStruct((len(block_pairs(whole)) * STEP, STEP), jnp.float32),
         in_specs=[pl.BlockSpec(memory_space=pltpu.SMEM)] + [vmem] * (n_blocks + len(extra)),
         out_specs=vmem,
         scratch_shapes=[pltpu.VMEM((whole, share * LANES), jnp.bfloat16)],
         compiler_params=pltpu.CompilerParams(vmem_limit_bytes=VMEM_BYTES),
-        cost_estimate=pl.CostEstimate(
-            flops=2 * whole * whole * share * LANES,
-            bytes_accessed=2 * whole * share * LANES + 8 * whole * whole,
-            transcendentals=0,
-        ),
+        cost_estimate=pl.CostEstimate(flops=0, bytes_accessed=0, transcendentals=0),
         name="gram",
     )(sources, *blocks, *extra)
 
@@ -234,6 +296,63 @@
         fibres, fibres, (((0, 2), (0, 2)), ((), ())), preferred_element_type=jnp.float32
     )
     return finish(lax.psum(local_gram, ("gx", "gy")), running_r)
+
+
+def bit_of(axis, bit):
+    return (lax.axis_index(axis) >> bit) & 1
+
+
+def swap(value, axis, bit):
+    flips = [(i, i ^ (1 << bit)) for i in range(lax.axis_size(axis))]
+    return lax.ppermute(value, axis, flips)
+
+
+def halve(value, axis, bit):
+    halves = value.reshape(2, value.shape[0] // 2, value.shape[1])
+    mine = bit_of(axis, bit)
+    keep = lax.dynamic_index_in_dim(halves, mine, 0, keepdims=False)
+    give = lax.dynamic_index_in_dim(halves, 1 - mine, 0, keepdims=False)
+    return keep + swap(give, axis, bit)
+
+
+def double(value, axis, bit):
+    other = swap(value, axis, bit)
+    return jnp.where(
+        bit_of(axis, bit) == 0,
+        jnp.concatenate([value, other]),
+        jnp.concatenate([other, value]),
+    )
+
+
+def shift_slow(value, step, slow):
+    n = slow * 2
+    return lax.ppermute(value, "gy", [(i, (i + 2 * step) % n) for i in range(n)])
+
+
+def sum_over_all(value):
+    n_x, n_y = lax.axis_size("gx"), lax.axis_size("gy")
+    bits = n_x.bit_length() - 1
+    slow = n_y // 2
+    mine = lax.axis_index("gy") // 2
+    for bit in range(bits):
+        value = halve(value, "gx", bit)
+    value = halve(value, "gy", 0)
+    rows, width = value.shape[0] // slow, value.shape[1]
+    quarters = value.reshape(slow, rows, width)
+    total = lax.dynamic_index_in_dim(quarters, mine, 0, keepdims=False)
+    for step in range(1, slow):
+        give = lax.dynamic_index_in_dim(quarters, (mine + step) % slow, 0, keepdims=False)
+        total = total + shift_slow(give, step, slow)
+    whole = jnp.zeros((slow, rows, width), value.dtype)
+    whole = lax.dynamic_update_index_in_dim(whole, total, mine, 0)
+    for step in range(1, slow):
+        got = shift_slow(total, step, slow)
+        whole = lax.dynamic_update_index_in_dim(whole, got, (mine + slow - step) % slow, 0)
+    value = whole.reshape(slow * rows, width)
+    value = double(value, "gy", 0)
+    for bit in reversed(range(bits)):
+        value = double(value, "gx", bit)
+    return value
 
 
 def pipelined(fields, x_factor, running_r):
@@ -261,37 +380,62 @@
     def back(index, shift):
         return (index // 2 + slow - shift[0]) % slow * 2 + (index % 2 + shift[1]) % 2
 
-    sends = jnp.stack([to(me_y, s) * share for s in shifts]).astype(jnp.int32)
+    scalars = jnp.stack(
+        [(me_x ^ d) * cells_part for d in range(n_x)] + [to(me_y, s) * share for s in shifts]
+    ).astype(jnp.int32)
     sources = jnp.stack([back(me_y, s) for s in shifts]).astype(jnp.int32)
 
+    chunks = [(cell, piece) for cell in range(0, cells_part, LANES) for piece in pieces]
+    per_gram = len(pieces)
+
+    def exchange_x(sends):
+        return [
+            lax.ppermute(send, "gx", [(i, i ^ (d + 1)) for i in range(n_x)])
+            for d, send in enumerate(sends)
+        ]
+
+    ahead = 2
+    moving = [exchange_x(sends) for sends in pack(by_y, scalars, chunks[:ahead], n_x)]
+    arrived = []
     carried = None
-    for k in range(cells_part // LANES):
-        scalars = jnp.concatenate(
-            [(me_x * cells_part + k * LANES).astype(jnp.int32)[None], sends]
-        )
-        blocks = [None] * (len(shifts) * len(pieces))
-        for index, piece in enumerate(pieces):
-            start, main, left = piece
-            got = []
-            for d in range(1, n_x):
-                block = lax.dynamic_slice(
-                    by_y,
-                    (start, 0, (me_x ^ d) * cells_part + k * LANES),
-                    (main + left, depth, LANES),
-                )
-                got.append(lax.ppermute(block, "gx", [(i, i ^ d) for i in range(n_x)]))
-            outs = project(by_y, got, factor, scalars, piece, share)
-            for part, shift in enumerate(shifts):
-                block = outs[part]
-                if shift != (0, 0):
-                    block = lax.ppermute(block, "gy", [(i, to(i, shift)) for i in range(n_y)])
-                blocks[part * len(pieces) + index] = block
-        carried = gram(blocks, carried, sources, pieces, share)
-
-    parts = n_y
-    gram_sum = carried.reshape(parts, PITCH, parts, PITCH)[:, :rows, :, :rows]
-    gram_sum = lax.psum(gram_sum.reshape(parts * rows, parts * rows), ("gx", "gy"))
-    return finish(gram_sum, running_r)
+    for k, chunk in enumerate(chunks):
+        following = chunks[k + ahead] if k + ahead < len(chunks) else None
+        after = []
+        if k >= 2:
+            after += arrived[k - 2][1:]
+        if k >= per_gram + 2 and (k - 2) % per_gram == 0:
+            after.append(carried)
+        outs, sends = project(
+            by_y, moving[k], factor, scalars, chunk, following, share, len(shifts), after
+        )
+        if following is not None:
+            moving.append(exchange_x(sends))
+        arrived.append(
+            [
+                out
+                if shift == (0, 0)
+                else lax.ppermute(out, "gy", [(i, to(i, shift)) for i in range(n_y)])
+                for out, shift in zip(outs, shifts)
+            ]
+        )
+        if (k + 1) % per_gram == 0:
+            group = arrived[k + 1 - per_gram :]
+            blocks = [group[index][part] for part in range(n_y) for index in range(per_gram)]
+            carried = gram(blocks, carried, sources, pieces, share)
+
+    summed = sum_over_all(carried)
+    whole = n_y * PITCH
+    blocks = {
+        pair: summed[index * STEP : (index + 1) * STEP]
+        for index, pair in enumerate(block_pairs(whole))
+    }
+    none = jnp.zeros((STEP, STEP), jnp.float32)
+    starts = range(0, whole, STEP)
+    upper = jnp.concatenate(
+        [jnp.concatenate([blocks.get((i, j), none) for j in starts], axis=1) for i in starts]
+    )
+    gram_sum = upper.reshape(n_y, PITCH, n_y, PITCH)[:, :rows, :, :rows]
+    return finish(gram_sum.reshape(n_y * rows, n_y * rows), running_r)
 
 
 def on_device(fields, x_factor, running_r):
@@ -306,7 +450,8 @@
         and rows % 16 in (0, 4, 8)
         and n_x & (n_x - 1) == 0
         and n_y % 2 == 0
-        and n_y * PITCH % 256 == 0
+        and n_y * PITCH % STEP == 0
+        and len(block_pairs(n_y * PITCH)) * STEP % (8 * n_x * n_y) == 0
     )
     if fits:
         return pipelined(fields, x_factor, running_r)

time: 1230 us -> 1840 us (1.50)
  Pallas kernels: 167 us -> 1080 us
  waiting for transfers between devices: 591 us -> 316 us
  local copies, waits for them, and re-layouts: 57.8 us -> 35.7 us
    pallas_call x12 -> x13, Pallas kernels: 167 us -> 1080 us  [the longest x9 789 us: project(): pl.pallas_call(body, out_shape=shapes, in_specs=[pl.BlockSpec(memory_spac...]
    psum x1 -> x0, waiting for transfers between devices: 140 us -> none  [pipelined(): lax.psum(gram_sum.reshape(parts * rows, parts * rows), ('gx', 'gy'))]
    ppermute x90 -> x102, waiting for transfers between devices: 451 us -> 316 us  [the longest x63 202 us: pipelined(): lax.ppermute(out, 'gy', [(i, to(i, shift)) for i in range(n_y)])]
    dynamic_slice x2 -> x0, local copies, waits for them, and re-layouts: 23.6 us -> none  [pipelined(): lax.dynamic_slice(by_y, (start, 0, (me_x ^ d) * cells_part + k * LANES),...]
    ppermute x90 -> x102, starting transfers between devices: 244 us -> 246 us  [the longest x63 212 us: pipelined(): lax.ppermute(out, 'gy', [(i, to(i, shift)) for i in range(n_y)])]
  transfers between devices with their start and end apart: 91 -> 102, of which waited for: 31 -> 52; matrix products, arithmetic and copies ran while one was open for 2% -> 1% of each run, Pallas kernels for 13% -> 44%
where the time goes in v2:
time: 1840 us; the launch traced here: 1830 us
  Pallas kernels  1080 us (59%)
  waiting for transfers between devices  316 us (17%)
  starting transfers between devices  246 us (13%)
  other arithmetic  128 us (7%)
  local copies, waits for them, and re-layouts  35.7 us (2%)
  matrix products  20.7 us (1%)
    pallas_call x9, Pallas kernels, project(): pl.pallas_call(body, out_shape=shapes, in_specs=[pl.BlockSpec(memory_spac...  789 us
    pallas_call x1, Pallas kernels, pack(): pl.pallas_call(body, out_shape=shapes, in_specs=[pl.BlockSpec(memory_spac...  252 us
    ppermute x63, starting transfers between devices, pipelined(): lax.ppermute(out, 'gy', [(i, to(i, shift)) for i in range(n_y)])  212 us
    ppermute x63, waiting for transfers between devices, pipelined(): lax.ppermute(out, 'gy', [(i, to(i, shift)) for i in range(n_y)])  202 us
    another operation x22, other arithmetic, finish(): return slice_out(lax.linalg.cholesky(total.T, symmetrize_input=False).T)  118 us
    ppermute x27, waiting for transfers between devices, exchange_x(): lax.ppermute(send, 'gx', [(i, i ^ d + 1) for i in range(n_x)])  77.5 us
    pallas_call x3, Pallas kernels, gram(): pl.pallas_call(body, out_shape=jax.ShapeDtypeStruct((len(block_pairs(whol...  40.1 us
  transfers between devices with their start and end apart: 102, of which 52 were waited for; matrix products, arithmetic and copies ran while one was open for 1% of the time, Pallas kernels for 44%

profile of v2, /device:TPU:0, one launch (start us, length us, event | category | flops | bytes accessed | tf_op | source)
XLA Modules:
  0.0 1832.6 jit_solution(10869365989281984571)
XLA Ops:
  0.6 252.0 %pack.1 = (bf16[32,168,128]{2,1,0:T(8,128)(2,1)}, bf16[32,168,128]{2,1,0:T(8,128)(2,1)}, bf16[32,168,128]{2,1,0:T(8,128)(2,1)}, bf16[32,168,128]{2,1,0:T(8,128)(...) custom-call(s32[12]{0:T(128)} %stack.102.scalars, bf16[84,168,1536]{2,1,0:T(8,128)(2,1)} %bitcast.107), custom_call_target="tpu_custom_call" | custom-call | tf_op jit(solution)/shard_map/pack/pallas_call | solution.py:65
  269.7 17.3 collective-permute-done.1.rest_1_
  287.0 29.0 %collective-permute-done.2.rest_2_ = bf16[32,168,128]{2,1,0:T(8,128)(2,1)} collective-permute-done((bf16[32,168,128]{2,1,0:T(8,128)(2,1)}, bf16[32,168,128]{2,1,0:T(8,128)(2,1)}, u32[]{:S(2)}, u32[]{:S(2)}) %collective-permute-start.2) | collective-permute-done | bytes 1376288 | tf_op jit(solution)/shard_map/ppermute | solution.py:393
  316.0 83.2 %project.9 = (bf16[1344,128]{1,0:T(8,128)(2,1)}, bf16[1344,128]{1,0:T(8,128)(2,1)}, bf16[1344,128]{1,0:T(8,128)(2,1)}, bf16[1344,128]{1,0:T(8,128)(2,1)}, bf16[1...) custom-call(s32[12]{0:T(128)} %stack.102.scalars, ...), custom_call_target="tpu_custom_call" | custom-call | tf_op jit(solution)/shard_map/project/pallas_call | solution.py:160
  423.5 130.1 %project.13 = (bf16[1344,128]{1,0:T(8,128)(2,1)}, bf16[1344,128]{1,0:T(8,128)(2,1)}, bf16[1344,128]{1,0:T(8,128)(2,1)}, bf16[1344,128]{1,0:T(8,128)(2,1)}, bf16[...) custom-call(s32[12]{0:T(128)} %stack.102.scalars, ...), custom_call_target="tpu_custom_call" | custom-call | tf_op jit(solution)/shard_map/project/pallas_call | solution.py:160
  554.3 26.1 %collective-permute-start.40 = (bf16[1344,128]{1,0:T(8,128)(2,1)}, bf16[1344,128]{1,0:T(8,128)(2,1)S(1)}, u32[]{:S(2)}, u32[]{:S(2)}) collective-permute-start(bf16[1344,128]{1,0:T(8,128)(2,1)} %get-tuple-element.145), channel_id=1, source_target_pairs={{0,2},{1,3},{2,4},{3,5},{4,6},{5,7},{6,0},{7,1},{8,10},{9,11},{10,... | collective-permute-start | bytes 1032200 | tf_op jit(solution)/shard_map/ppermute | solution.py:417
  594.7 10.0 collective-permute-done.42.rest_7_.rest_13_
  619.1 129.4 %project.10 = (bf16[840,128]{1,0:T(8,128)(2,1)}, bf16[840,128]{1,0:T(8,128)(2,1)}, bf16[840,128]{1,0:T(8,128)(2,1)}, bf16[840,128]{1,0:T(8,128)(2,1)}, bf16[840,...) custom-call(s32[12]{0:T(128)} %stack.102.scalars, ...), custom_call_target="tpu_custom_call" | custom-call | tf_op jit(solution)/shard_map/project/pallas_call | solution.py:160
  773.8 83.2 %project.14 = (bf16[1344,128]{1,0:T(8,128)(2,1)}, bf16[1344,128]{1,0:T(8,128)(2,1)}, bf16[1344,128]{1,0:T(8,128)(2,1)}, bf16[1344,128]{1,0:T(8,128)(2,1)}, bf16[...) custom-call(s32[12]{0:T(128)} %stack.102.scalars, ...), custom_call_target="tpu_custom_call" | custom-call | tf_op jit(solution)/shard_map/project/pallas_call | solution.py:160
  884.1 11.4 collective-permute-start.53
  915.8 130.1 %project.11 = (bf16[1344,128]{1,0:T(8,128)(2,1)}, bf16[1344,128]{1,0:T(8,128)(2,1)}, bf16[1344,128]{1,0:T(8,128)(2,1)}, bf16[1344,128]{1,0:T(8,128)(2,1)}, bf16[...) custom-call(s32[12]{0:T(128)} %stack.102.scalars, ...), custom_call_target="tpu_custom_call" | custom-call | tf_op jit(solution)/shard_map/project/pallas_call | solution.py:160
  1047.3 13.0 gram.3.rest_11_.rest_24_
  1060.4 129.6 %project.15 = (bf16[840,128]{1,0:T(8,128)(2,1)}, bf16[840,128]{1,0:T(8,128)(2,1)}, bf16[840,128]{1,0:T(8,128)(2,1)}, bf16[840,128]{1,0:T(8,128)(2,1)}, bf16[840,...) custom-call(s32[12]{0:T(128)} %stack.102.scalars, ...), custom_call_target="tpu_custom_call" | custom-call | tf_op jit(solution)/shard_map/project/pallas_call | solution.py:160
  1214.0 12.9 collective-permute-done.62.rest_7_.rest_14_
  1241.3 20.2 %collective-permute-done.29.rest_7_.rest_13_ = bf16[1344,128]{1,0:T(8,128)(2,1)S(1)} collective-permute-done((bf16[1344,128]{1,0:T(8,128)(2,1)S(1)}, bf16[1344,128]{1,0:T(8,128)(2,1)S(1)}, u32[]{:S(2)}, u32[]{:S(2)}) %collective-permute-start.29) | collective-permute-done | bytes 344096 | tf_op jit(solution)/shard_map/ppermute | solution.py:417
  1279.2 15.7 collective-permute-done.24.rest_1_
  1294.9 16.1 collective-permute-start.64
  1311.0 12.0 collective-permute-done.25.rest_2_
  1323.0 17.4 collective-permute-start.65
  1340.4 83.2 %project.12 = (bf16[1344,128]{1,0:T(8,128)(2,1)}, bf16[1344,128]{1,0:T(8,128)(2,1)}, bf16[1344,128]{1,0:T(8,128)(2,1)}, bf16[1344,128]{1,0:T(8,128)(2,1)}, bf16[...) custom-call(s32[12]{0:T(128)} %stack.102.scalars, ...), custom_call_target="tpu_custom_call" | custom-call | tf_op jit(solution)/shard_map/project/pallas_call | solution.py:160
  1445.6 20.5 %collective-permute-done.72.rest_7_.rest_12_ = bf16[1344,128]{1,0:T(8,128)(2,1)S(1)} collective-permute-done((bf16[1344,128]{1,0:T(8,128)(2,1)}, bf16[1344,128]{1,0:T(8,128)(2,1)S(1)}, u32[]{:S(2)}, u32[]{:S(2)}) %collective-permute-start.72) | collective-permute-done | bytes 344096 | tf_op jit(solution)/shard_map/ppermute | solution.py:417
  1475.2 11.4 project.16
  1518.8 13.6 gram.4.rest_11_.rest_24_
  1541.1 10.6 collective-permute-start.79
  1563.5 12.5 collective-permute-start.85
  1594.8 13.6 gram.5
  1694.3 11.7 cholesky.166
  1721.0 11.7 cholesky.189
  1745.8 11.7 cholesky.356
  1758.9 10.2 custom-call.34
  1771.8 11.7 cholesky.375
  1797.1 11.9 cholesky.394
  (393 shorter events, 454.8 us)
Async XLA Ops:
  255.7 60.3 %collective-permute-start.2 = (bf16[32,168,128]{2,1,0:T(8,128)(2,1)}, bf16[32,168,128]{2,1,0:T(8,128)(2,1)}, u32[]{:S(2)}, u32[]{:S(2)}) collective-permute-start(bf16[32,168,128]{2,1,0:T(8,128)(2,1)} %get-tuple-element.106), channel_id=1, source_target_pairs={{0,24},{8,16},{16,8},{24,0},{1,25},{9,17},{17,9},{25,1},{2,26},{10... | collective-permute-start | bytes 4128776 | tf_op jit(solution)/shard_map/ppermute | solution.py:393
  255.8 146.7 %collective-permute-start.33 = (bf16[32,168,128]{2,1,0:T(8,128)(2,1)}, bf16[32,168,128]{2,1,0:T(8,128)(2,1)S(1)}, u32[]{:S(2)}, u32[]{:S(2)}) collective-permute-start(bf16[32,168,128]{2,1,0:T(8,128)(2,1)} %get-tuple-element.138), channel_id=1, source_target_pairs={{0,8},{8,0},{16,24},{24,16},{1,9},{9,1},{17,25},{25,17},{2,10},{10... | collective-permute-start | bytes 4128776 | tf_op jit(solution)/shard_map/ppermute | solution.py:393
  255.9 148.1 %collective-permute-start.34 = (bf16[32,168,128]{2,1,0:T(8,128)(2,1)}, bf16[32,168,128]{2,1,0:T(8,128)(2,1)}, u32[]{:S(2)}, u32[]{:S(2)}) collective-permute-start(bf16[32,168,128]{2,1,0:T(8,128)(2,1)} %get-tuple-element.139), channel_id=1, source_target_pairs={{0,16},{8,24},{16,0},{24,8},{1,17},{9,25},{17,1},{25,9},{2,18},{10... | collective-permute-start | bytes 4128776 | tf_op jit(solution)/shard_map/ppermute | solution.py:393
  257.8 147.3 %collective-permute-start.35 = (bf16[32,168,128]{2,1,0:T(8,128)(2,1)}, bf16[32,168,128]{2,1,0:T(8,128)(2,1)}, u32[]{:S(2)}, u32[]{:S(2)}) collective-permute-start(bf16[32,168,128]{2,1,0:T(8,128)(2,1)} %get-tuple-element.140), channel_id=1, source_target_pairs={{0,24},{8,16},{16,8},{24,0},{1,25},{9,17},{17,9},{25,1},{2,26},{10... | collective-permute-start | bytes 4128776 | tf_op jit(solution)/shard_map/ppermute | solution.py:393
  404.0 149.7 %collective-permute-start.9 = (bf16[1344,128]{1,0:T(8,128)(2,1)}, bf16[1344,128]{1,0:T(8,128)(2,1)S(1)}, u32[]{:S(2)}, u32[]{:S(2)}) collective-permute-start(bf16[1344,128]{1,0:T(8,128)(2,1)} %get-tuple-element.113), channel_id=1, source_target_pairs={{0,4},{1,5},{2,6},{3,7},{4,0},{5,1},{6,2},{7,3},{8,12},{9,13},{10,... | collective-permute-start | bytes 1032200 | tf_op jit(solution)/shard_map/ppermute | solution.py:417
  405.1 149.1 %collective-permute-start.10 = (bf16[1344,128]{1,0:T(8,128)(2,1)}, bf16[1344,128]{1,0:T(8,128)(2,1)S(1)}, u32[]{:S(2)}, u32[]{:S(2)}) collective-permute-start(bf16[1344,128]{1,0:T(8,128)(2,1)} %get-tuple-element.114), channel_id=1, source_target_pairs={{0,5},{1,4},{2,7},{3,6},{4,1},{5,0},{6,3},{7,2},{8,13},{9,12},{10,... | collective-permute-start | bytes 1032200 | tf_op jit(solution)/shard_map/ppermute | solution.py:417
  410.0 170.3 %collective-permute-start.11 = (bf16[1344,128]{1,0:T(8,128)(2,1)}, bf16[1344,128]{1,0:T(8,128)(2,1)S(1)}, u32[]{:S(2)}, u32[]{:S(2)}) collective-permute-start(bf16[1344,128]{1,0:T(8,128)(2,1)} %get-tuple-element.115), channel_id=1, source_target_pairs={{0,6},{1,7},{2,0},{3,1},{4,2},{5,3},{6,4},{7,5},{8,14},{9,15},{10,... | collective-permute-start | bytes 1032200 | tf_op jit(solution)/shard_map/ppermute | solution.py:417
  413.9 197.7 %collective-permute-start.3 = (bf16[20,168,128]{2,1,0:T(8,128)(2,1)}, bf16[20,168,128]{2,1,0:T(8,128)(2,1)}, u32[]{:S(2)}, u32[]{:S(2)}) collective-permute-start(bf16[20,168,128]{2,1,0:T(8,128)(2,1)} %get-tuple-element.107), channel_id=1, source_target_pairs={{0,8},{8,0},{16,24},{24,16},{1,9},{9,1},{17,25},{25,17},{2,10},{10... | collective-permute-start | bytes 2580488 | tf_op jit(solution)/shard_map/ppermute | solution.py:393
  421.1 162.6 %collective-permute-start.12 = (bf16[1344,128]{1,0:T(8,128)(2,1)}, bf16[1344,128]{1,0:T(8,128)(2,1)S(1)}, u32[]{:S(2)}, u32[]{:S(2)}) collective-permute-start(bf16[1344,128]{1,0:T(8,128)(2,1)} %get-tuple-element.116), channel_id=1, source_target_pairs={{0,7},{1,6},{2,1},{3,0},{4,3},{5,2},{6,5},{7,4},{8,15},{9,14},{10,... | collective-permute-start | bytes 1032200 | tf_op jit(solution)/shard_map/ppermute | solution.py:417
  605.4 163.6 %collective-permute-start.36 = (bf16[32,168,128]{2,1,0:T(8,128)(2,1)}, bf16[32,168,128]{2,1,0:T(8,128)(2,1)S(1)}, u32[]{:S(2)}, u32[]{:S(2)}) collective-permute-start(bf16[32,168,128]{2,1,0:T(8,128)(2,1)} %get-tuple-element.141), channel_id=1, source_target_pairs={{0,8},{8,0},{16,24},{24,16},{1,9},{9,1},{17,25},{25,17},{2,10},{10... | collective-permute-start | bytes 4128776 | tf_op jit(solution)/shard_map/ppermute | solution.py:393
  610.1 161.8 %collective-permute-start.37 = (bf16[32,168,128]{2,1,0:T(8,128)(2,1)}, bf16[32,168,128]{2,1,0:T(8,128)(2,1)S(1)}, u32[]{:S(2)}, u32[]{:S(2)}) collective-permute-start(bf16[32,168,128]{2,1,0:T(8,128)(2,1)} %get-tuple-element.142), channel_id=1, source_target_pairs={{0,16},{8,24},{16,0},{24,8},{1,17},{9,25},{17,1},{25,9},{2,18},{10... | collective-permute-start | bytes 4128776 | tf_op jit(solution)/shard_map/ppermute | solution.py:393
  611.6 160.3 %collective-permute-start.38 = (bf16[32,168,128]{2,1,0:T(8,128)(2,1)}, bf16[32,168,128]{2,1,0:T(8,128)(2,1)}, u32[]{:S(2)}, u32[]{:S(2)}) collective-permute-start(bf16[32,168,128]{2,1,0:T(8,128)(2,1)} %get-tuple-element.143), channel_id=1, source_target_pairs={{0,24},{8,16},{16,8},{24,0},{1,25},{9,17},{17,9},{25,1},{2,26},{10... | collective-permute-start | bytes 4128776 | tf_op jit(solution)/shard_map/ppermute | solution.py:393
  611.6 136.9 %collective-permute-start.44 = (bf16[1344,128]{1,0:T(8,128)(2,1)}, bf16[1344,128]{1,0:T(8,128)(2,1)S(1)}, u32[]{:S(2)}, u32[]{:S(2)}) collective-permute-start(bf16[1344,128]{1,0:T(8,128)(2,1)} %get-tuple-element.149), channel_id=1, source_target_pairs={{0,6},{1,7},{2,0},{3,1},{4,2},{5,3},{6,4},{7,5},{8,14},{9,15},{10,... | collective-permute-start | bytes 1032200 | tf_op jit(solution)/shard_map/ppermute | solution.py:417
  617.2 133.0 %collective-permute-start.45 = (bf16[1344,128]{1,0:T(8,128)(2,1)}, bf16[1344,128]{1,0:T(8,128)(2,1)S(1)}, u32[]{:S(2)}, u32[]{:S(2)}) collective-permute-start(bf16[1344,128]{1,0:T(8,128)(2,1)} %get-tuple-element.150), channel_id=1, source_target_pairs={{0,7},{1,6},{2,1},{3,0},{4,3},{5,2},{6,5},{7,4},{8,15},{9,14},{10,... | collective-permute-start | bytes 1032200 | tf_op jit(solution)/shard_map/ppermute | solution.py:417
  761.8 152.0 %collective-permute-start.13 = (bf16[32,168,128]{2,1,0:T(8,128)(2,1)}, bf16[32,168,128]{2,1,0:T(8,128)(2,1)S(1)}, u32[]{:S(2)}, u32[]{:S(2)}) collective-permute-start(bf16[32,168,128]{2,1,0:T(8,128)(2,1)} %get-tuple-element.117), channel_id=1, source_target_pairs={{0,8},{8,0},{16,24},{24,16},{1,9},{9,1},{17,25},{25,17},{2,10},{10... | collective-permute-start | bytes 4128776 | tf_op jit(solution)/shard_map/ppermute | solution.py:393
  768.1 88.9 %collective-permute-start.19 = (bf16[840,128]{1,0:T(8,128)(2,1)}, bf16[840,128]{1,0:T(8,128)(2,1)}, u32[]{:S(2)}, u32[]{:S(2)}) collective-permute-start(bf16[840,128]{1,0:T(8,128)(2,1)} %get-tuple-element.123), channel_id=1, source_target_pairs={{0,4},{1,5},{2,6},{3,7},{4,0},{5,1},{6,2},{7,3},{8,12},{9,13},{10,... | collective-permute-start | bytes 645128 | tf_op jit(solution)/shard_map/ppermute | solution.py:417
  769.0 89.5 %collective-permute-start.20 = (bf16[840,128]{1,0:T(8,128)(2,1)}, bf16[840,128]{1,0:T(8,128)(2,1)}, u32[]{:S(2)}, u32[]{:S(2)}) collective-permute-start(bf16[840,128]{1,0:T(8,128)(2,1)} %get-tuple-element.124), channel_id=1, source_target_pairs={{0,5},{1,4},{2,7},{3,6},{4,1},{5,0},{6,3},{7,2},{8,13},{9,12},{10,... | collective-permute-start | bytes 645128 | tf_op jit(solution)/shard_map/ppermute | solution.py:417
  771.9 141.9 %collective-permute-start.14 = (bf16[32,168,128]{2,1,0:T(8,128)(2,1)}, bf16[32,168,128]{2,1,0:T(8,128)(2,1)S(1)}, u32[]{:S(2)}, u32[]{:S(2)}) collective-permute-start(bf16[32,168,128]{2,1,0:T(8,128)(2,1)} %get-tuple-element.118), channel_id=1, source_target_pairs={{0,16},{8,24},{16,0},{24,8},{1,17},{9,25},{17,1},{25,9},{2,18},{10... | collective-permute-start | bytes 4128776 | tf_op jit(solution)/shard_map/ppermute | solution.py:393
  771.9 87.7 %collective-permute-start.21 = (bf16[840,128]{1,0:T(8,128)(2,1)}, bf16[840,128]{1,0:T(8,128)(2,1)}, u32[]{:S(2)}, u32[]{:S(2)}) collective-permute-start(bf16[840,128]{1,0:T(8,128)(2,1)} %get-tuple-element.125), channel_id=1, source_target_pairs={{0,6},{1,7},{2,0},{3,1},{4,2},{5,3},{6,4},{7,5},{8,14},{9,15},{10,... | collective-permute-start | bytes 645128 | tf_op jit(solution)/shard_map/ppermute | solution.py:417
  859.6 54.3 %collective-permute-start.15 = (bf16[32,168,128]{2,1,0:T(8,128)(2,1)}, bf16[32,168,128]{2,1,0:T(8,128)(2,1)S(1)}, u32[]{:S(2)}, u32[]{:S(2)}) collective-permute-start(bf16[32,168,128]{2,1,0:T(8,128)(2,1)} %get-tuple-element.119), channel_id=1, source_target_pairs={{0,24},{8,16},{16,8},{24,0},{1,25},{9,17},{17,9},{25,1},{2,26},{10... | collective-permute-start | bytes 4128776 | tf_op jit(solution)/shard_map/ppermute | solution.py:393
  904.5 155.9 %collective-permute-start.46 = (bf16[20,168,128]{2,1,0:T(8,128)(2,1)}, bf16[20,168,128]{2,1,0:T(8,128)(2,1)}, u32[]{:S(2)}, u32[]{:S(2)}) collective-permute-start(bf16[20,168,128]{2,1,0:T(8,128)(2,1)} %get-tuple-element.151), channel_id=1, source_target_pairs={{0,8},{8,0},{16,24},{24,16},{1,9},{9,1},{17,25},{25,17},{2,10},{10... | collective-permute-start | bytes 2580488 | tf_op jit(solution)/shard_map/ppermute | solution.py:393
  911.8 148.6 %collective-permute-start.47 = (bf16[20,168,128]{2,1,0:T(8,128)(2,1)}, bf16[20,168,128]{2,1,0:T(8,128)(2,1)}, u32[]{:S(2)}, u32[]{:S(2)}) collective-permute-start(bf16[20,168,128]{2,1,0:T(8,128)(2,1)} %get-tuple-element.152), channel_id=1, source_target_pairs={{0,16},{8,24},{16,0},{24,8},{1,17},{9,25},{17,1},{25,9},{2,18},{10... | collective-permute-start | bytes 2580488 | tf_op jit(solution)/shard_map/ppermute | solution.py:393
  913.8 146.7 %collective-permute-start.48 = (bf16[20,168,128]{2,1,0:T(8,128)(2,1)}, bf16[20,168,128]{2,1,0:T(8,128)(2,1)}, u32[]{:S(2)}, u32[]{:S(2)}) collective-permute-start(bf16[20,168,128]{2,1,0:T(8,128)(2,1)} %get-tuple-element.153), channel_id=1, source_target_pairs={{0,24},{8,16},{16,8},{24,0},{1,25},{9,17},{17,9},{25,1},{2,26},{10... | collective-permute-start | bytes 2580488 | tf_op jit(solution)/shard_map/ppermute | solution.py:393
  913.8 132.1 %collective-permute-start.54 = (bf16[1344,128]{1,0:T(8,128)(2,1)}, bf16[1344,128]{1,0:T(8,128)(2,1)S(1)}, u32[]{:S(2)}, u32[]{:S(2)}) collective-permute-start(bf16[1344,128]{1,0:T(8,128)(2,1)} %get-tuple-element.159), channel_id=1, source_target_pairs={{0,6},{1,7},{2,0},{3,1},{4,2},{5,3},{6,4},{7,5},{8,14},{9,15},{10,... | collective-permute-start | bytes 1032200 | tf_op jit(solution)/shard_map/ppermute | solution.py:417
  913.9 146.5 %collective-permute-start.55 = (bf16[1344,128]{1,0:T(8,128)(2,1)}, bf16[1344,128]{1,0:T(8,128)(2,1)}, u32[]{:S(2)}, u32[]{:S(2)}) collective-permute-start(bf16[1344,128]{1,0:T(8,128)(2,1)} %get-tuple-element.160), channel_id=1, source_target_pairs={{0,7},{1,6},{2,1},{3,0},{4,3},{5,2},{6,5},{7,4},{8,15},{9,14},{10,... | collective-permute-start | bytes 1032200 | tf_op jit(solution)/shard_map/ppermute | solution.py:417
  1046.6 232.2 %collective-permute-start.23 = (bf16[32,168,128]{2,1,0:T(8,128)(2,1)}, bf16[32,168,128]{2,1,0:T(8,128)(2,1)S(1)}, u32[]{:S(2)}, u32[]{:S(2)}) collective-permute-start(bf16[32,168,128]{2,1,0:T(8,128)(2,1)} %get-tuple-element.127), channel_id=1, source_target_pairs={{0,8},{8,0},{16,24},{24,16},{1,9},{9,1},{17,25},{25,17},{2,10},{10... | collective-permute-start | bytes 4128776 | tf_op jit(solution)/shard_map/ppermute | solution.py:393
  1270.4 153.9 %collective-permute-start.56 = (bf16[32,168,128]{2,1,0:T(8,128)(2,1)}, bf16[32,168,128]{2,1,0:T(8,128)(2,1)S(1)}, u32[]{:S(2)}, u32[]{:S(2)}) collective-permute-start(bf16[32,168,128]{2,1,0:T(8,128)(2,1)} %get-tuple-element.164), channel_id=1, source_target_pairs={{0,8},{8,0},{16,24},{24,16},{1,9},{9,1},{17,25},{25,17},{2,10},{10... | collective-permute-start | bytes 4128776 | tf_op jit(solution)/shard_map/ppermute | solution.py:393
  1277.7 146.7 %collective-permute-start.57 = (bf16[32,168,128]{2,1,0:T(8,128)(2,1)}, bf16[32,168,128]{2,1,0:T(8,128)(2,1)S(1)}, u32[]{:S(2)}, u32[]{:S(2)}) collective-permute-start(bf16[32,168,128]{2,1,0:T(8,128)(2,1)} %get-tuple-element.165), channel_id=1, source_target_pairs={{0,16},{8,24},{16,0},{24,8},{1,17},{9,25},{17,1},{25,9},{2,18},{10... | collective-permute-start | bytes 4128776 | tf_op jit(solution)/shard_map/ppermute | solution.py:393
  1278.9 150.7 %collective-permute-start.58 = (bf16[32,168,128]{2,1,0:T(8,128)(2,1)}, bf16[32,168,128]{2,1,0:T(8,128)(2,1)S(1)}, u32[]{:S(2)}, u32[]{:S(2)}) collective-permute-start(bf16[32,168,128]{2,1,0:T(8,128)(2,1)} %get-tuple-element.166), channel_id=1, source_target_pairs={{0,24},{8,16},{16,8},{24,0},{1,25},{9,17},{17,9},{25,1},{2,26},{10... | collective-permute-start | bytes 4128776 | tf_op jit(solution)/shard_map/ppermute | solution.py:393
  1294.9 128.8 %collective-permute-start.64 = (bf16[840,128]{1,0:T(8,128)(2,1)}, bf16[840,128]{1,0:T(8,128)(2,1)}, u32[]{:S(2)}, u32[]{:S(2)}) collective-permute-start(bf16[840,128]{1,0:T(8,128)(2,1)} %get-tuple-element.172), channel_id=1, source_target_pairs={{0,6},{1,7},{2,0},{3,1},{4,2},{5,3},{6,4},{7,5},{8,14},{9,15},{10,... | collective-permute-start | bytes 645128 | tf_op jit(solution)/shard_map/ppermute | solution.py:417
  1323.0 101.3 %collective-permute-start.65 = (bf16[840,128]{1,0:T(8,128)(2,1)}, bf16[840,128]{1,0:T(8,128)(2,1)}, u32[]{:S(2)}, u32[]{:S(2)}) collective-permute-start(bf16[840,128]{1,0:T(8,128)(2,1)} %get-tuple-element.173), channel_id=1, source_target_pairs={{0,7},{1,6},{2,1},{3,0},{4,3},{5,2},{6,5},{7,4},{8,15},{9,14},{10,... | collective-permute-start | bytes 645128 | tf_op jit(solution)/shard_map/ppermute | solution.py:417
  1445.6 64.6 %collective-permute-start.66 = (bf16[20,168,128]{2,1,0:T(8,128)(2,1)}, bf16[20,168,128]{2,1,0:T(8,128)(2,1)}, u32[]{:S(2)}, u32[]{:S(2)}) collective-permute-start(bf16[20,168,128]{2,1,0:T(8,128)(2,1)} %get-tuple-element.175), channel_id=1, source_target_pairs={{0,8},{8,0},{16,24},{24,16},{1,9},{9,1},{17,25},{25,17},{2,10},{10... | collective-permute-start | bytes 2580488 | tf_op jit(solution)/shard_map/ppermute | solution.py:393
  (139 other events, 7133.1 us)

commit v3 on v2

--- a/solution.py
+++ b/solution.py
@@ -10,6 +10,8 @@
 LANES = 128
 PITCH = 96
 STEP = 256
+WINDOW = {"gx": 3, "gy": 2}
+AHEAD = 3
 VMEM_BYTES = 56 * 1024 * 1024
 
 
@@ -26,55 +28,57 @@
     return [tuple(p) for p in pieces]
 
 
-def pack_copies(fields, sends, scalars, cell, piece, sems):
-    start, main, left = piece
+def send_list(chunk, n_x):
+    _, (_, main, left) = chunk
+    rows = main + left
+    return [(partner, 0, rows) for partner in list(range(2, n_x)) + [1]]
+
+
+def pack_copies(fields, outs, scalars, chunk, n_x, sems):
+    cell, (start, _, _) = chunk
     copies = []
-    for index, send in enumerate(sends):
-        column = pl.multiple_of(scalars[1 + index] + cell, LANES)
+    for index, (partner, at, size) in enumerate(send_list(chunk, n_x)):
+        column = pl.multiple_of(scalars[partner] + cell, LANES)
         copies.append(
             pltpu.make_async_copy(
-                fields.at[pl.ds(start, main + left), :, pl.ds(column, LANES)],
-                send,
+                fields.at[pl.ds(start + at, size), :, pl.ds(column, LANES)],
+                outs[index],
                 sems.at[index],
             )
         )
     return copies
 
 
-def pack(fields, scalars, chunks, n_x):
-    depth = fields.shape[1]
-    n_sends = n_x - 1
+def send_shapes(chunk, n_x, depth):
+    return [
+        jax.ShapeDtypeStruct((size, depth, LANES), jnp.bfloat16)
+        for _, _, size in send_list(chunk, n_x)
+    ]
+
+
+def pack(fields, scalars, chunk, n_x):
+    shapes = send_shapes(chunk, n_x, fields.shape[1])
 
     def body(scalars, fields, *rest):
-        sems = rest[-1]
-        copies = []
-        for index, (cell, piece) in enumerate(chunks):
-            sends = rest[index * n_sends : (index + 1) * n_sends]
-            copies += pack_copies(fields, sends, scalars, cell, piece, sems.at[index])
+        copies = pack_copies(fields, rest[:-1], scalars, chunk, n_x, rest[-1])
         for copy in copies:
             copy.start()
         for copy in copies:
             copy.wait()
 
-    any_space = pl.BlockSpec(memory_space=pl.ANY)
-    shapes = [
-        jax.ShapeDtypeStruct((piece[1] + piece[2], depth, LANES), jnp.bfloat16)
-        for _, piece in chunks
-        for _ in range(n_sends)
-    ]
-    outs = pl.pallas_call(
+    return pl.pallas_call(
         body,
         out_shape=shapes,
-        in_specs=[pl.BlockSpec(memory_space=pltpu.SMEM), any_space],
-        out_specs=[any_space] * len(shapes),
-        scratch_shapes=[pltpu.SemaphoreType.DMA((len(chunks), n_sends))],
+        in_specs=[pl.BlockSpec(memory_space=pltpu.SMEM), pl.BlockSpec(memory_space=pl.ANY)],
+        out_specs=[pl.BlockSpec(memory_space=pltpu.VMEM)] * len(shapes),
+        scratch_shapes=[pltpu.SemaphoreType.DMA((len(shapes),))],
+        compiler_params=pltpu.CompilerParams(vmem_limit_bytes=VMEM_BYTES),
         cost_estimate=pl.CostEstimate(flops=0, bytes_accessed=0, transcendentals=0),
         name="pack",
     )(scalars, fields)
-    return [outs[i * n_sends : (i + 1) * n_sends] for i in range(len(chunks))]
-
-
-def project_kernel(chunk, following, rank, share, scalars, fields, got, factor, outs, sends, own, wide, sems):
+
+
+def project_kernel(chunk, following, n_x, rank, share, scalars, fields, got, factor, outs, sends, own, wide, sems):
     cell, (start, main, left) = chunk
     rows = main + left
     column = pl.multiple_of(scalars[0] + cell, LANES)
@@ -85,30 +89,36 @@
     packing = []
     if following is not None:
         packing = pack_copies(
-            fields, sends, scalars, following[0], following[1], sems.at[pl.ds(1, len(sends))]
+            fields, sends, scalars, following, n_x, sems.at[pl.ds(1, len(sends))]
         )
     for other in packing:
         other.start()
     copy.wait()
-    blocks = [own] + list(got)
     many = 4
-
-    def one_group(group, _):
-        y = group * many
-        total = None
-        for index, block in enumerate(blocks):
-            right = jnp.concatenate([block[y + k] for k in range(many)], axis=1)
-            term = jnp.dot(factor[index], right, preferred_element_type=jnp.float32)
-            total = term if total is None else total + term
-        for k in range(many):
-            at = pl.multiple_of((y + k) * rank, 8)
-            wide[pl.ds(at, rank), :] = total[:, k * LANES : (k + 1) * LANES]
-        return 0
-
-    lax.fori_loop(0, rows // many, one_group, 0)
+    arrays = list(zip(send_list(chunk, n_x), got))
+
+    for start_row, size in sorted({(at, size) for (p, at, size), _ in arrays if p > 1}):
+        blocks = [(0, own, 0)]
+        for (partner, at, _), block in arrays:
+            if partner == 1 or at == start_row:
+                blocks.append((partner, block, at))
+
+        def one_group(group, _):
+            y = start_row + group * many
+            total = None
+            for partner, block, at in blocks:
+                right = jnp.concatenate([block[y - at + k] for k in range(many)], axis=1)
+                term = jnp.dot(factor[partner], right, preferred_element_type=jnp.float32)
+                total = term if total is None else total + term
+            for k in range(many):
+                at = pl.multiple_of((y + k) * rank, 8)
+                wide[pl.ds(at, rank), :] = total[:, k * LANES : (k + 1) * LANES]
+            return 0
+
+        lax.fori_loop(0, size // many, one_group, 0)
 
     for part, out in enumerate(outs):
-        first = scalars[1 + len(blocks) - 1 + part]
+        first = scalars[n_x + part]
 
         def one_row(i, _):
             picked = wide[pl.ds(first + i, main, stride=rank), :]
@@ -131,13 +141,15 @@
         other.wait()
 
 
-def project(fields, got, factor, scalars, chunk, following, share, parts, after):
+def project(fields, got, factor, scalars, chunk, following, n_x, share, parts, after):
     _, (start, main, left) = chunk
     rows = main + left
     rank = factor.shape[1]
     depth = fields.shape[1]
     n_got = len(got)
     n_sends = 0 if following is None else n_got
+    vmem = pl.BlockSpec(memory_space=pltpu.VMEM)
+    any_space = pl.BlockSpec(memory_space=pl.ANY)
     n_after = len(after)
 
     def body(scalars, fields, *rest):
@@ -148,22 +160,19 @@
         sends = rest[parts : parts + n_sends]
         own, wide, sems = rest[parts + n_sends :]
         project_kernel(
-            chunk, following, rank, share, scalars, fields, got, factor, outs, sends, own, wide, sems
-        )
-
-    vmem = pl.BlockSpec(memory_space=pltpu.VMEM)
-    any_space = pl.BlockSpec(memory_space=pl.ANY)
+            chunk, following, n_x, rank, share, scalars, fields, got, factor, outs, sends, own, wide, sems
+        )
+
     shapes = [jax.ShapeDtypeStruct((share * rows, LANES), jnp.bfloat16)] * parts
     if following is not None:
-        next_rows = following[1][1] + following[1][2]
-        shapes += [jax.ShapeDtypeStruct((next_rows, depth, LANES), jnp.bfloat16)] * n_sends
+        shapes += send_shapes(following, n_x, depth)
     outs = pl.pallas_call(
         body,
         out_shape=shapes,
         in_specs=[pl.BlockSpec(memory_space=pltpu.SMEM), any_space]
         + [vmem] * (n_got + 1)
         + [any_space] * n_after,
-        out_specs=[vmem] * parts + [any_space] * n_sends,
+        out_specs=[vmem] * (parts + n_sends),
         scratch_shapes=[
             pltpu.VMEM((rows, depth, LANES), jnp.bfloat16),
             pltpu.VMEM((rows * rank, LANES), jnp.float32),
@@ -388,40 +397,70 @@
     chunks = [(cell, piece) for cell in range(0, cells_part, LANES) for piece in pieces]
     per_gram = len(pieces)
 
-    def exchange_x(sends):
+    flown = []
+    lanes = {"gx": [], "gy": []}
+
+    def start(operand, axis, pairs):
+        lane = lanes[axis]
+        if len(lane) >= WINDOW[axis]:
+            slot = lane[-WINDOW[axis]]
+            operand, flown[slot] = lax.optimization_barrier((operand, flown[slot]))
+        lane.append(len(flown))
+        flown.append(lax.ppermute(operand, axis, pairs))
+        return lane[-1]
+
+    def start_x(chunk, sends):
         return [
-            lax.ppermute(send, "gx", [(i, i ^ (d + 1)) for i in range(n_x)])
-            for d, send in enumerate(sends)
+            functools.partial(start, send, "gx", [(i, i ^ partner) for i in range(n_x)])
+            for (partner, _, _), send in zip(send_list(chunk, n_x), sends)
         ]
 
-    ahead = 2
-    moving = [exchange_x(sends) for sends in pack(by_y, scalars, chunks[:ahead], n_x)]
+    def start_y(outs):
+        return [
+            functools.partial(start, out, "gy", [(i, to(i, shift)) for i in range(n_y)])
+            for out, shift in zip(outs, shifts)
+            if shift != (0, 0)
+        ]
+
+    moving = []
+    for chunk in chunks[:AHEAD]:
+        moving.append([begin() for begin in start_x(chunk, pack(by_y, scalars, chunk, n_x))])
     arrived = []
     carried = None
+
+    def add_gram(carried, group):
+        blocks = []
+        for part in range(n_y):
+            for own, slots in group:
+                blocks.append(own if part == 0 else flown[slots[part - 1]])
+        return gram(blocks, carried, sources, pieces, share)
+
     for k, chunk in enumerate(chunks):
-        following = chunks[k + ahead] if k + ahead < len(chunks) else None
+        following = chunks[k + AHEAD] if k + AHEAD < len(chunks) else None
         after = []
-        if k >= 2:
-            after += arrived[k - 2][1:]
         if k >= per_gram + 2 and (k - 2) % per_gram == 0:
+            done = k - 2 - per_gram
+            carried = add_gram(carried, arrived[done : done + per_gram])
             after.append(carried)
+        got = [flown[slot] for slot in moving[k]]
         outs, sends = project(
-            by_y, moving[k], factor, scalars, chunk, following, share, len(shifts), after
-        )
+            by_y, got, factor, scalars, chunk, following, n_x, share, len(shifts), after
+        )
+        to_y = start_y(outs)
+        to_x = [] if following is None else start_x(following, sends)
+        order = sorted(
+            [((i + 0.5) / len(to_y), 0, i) for i in range(len(to_y))]
+            + [((i + 0.25) / len(to_x), 1, i) for i in range(len(to_x))]
+        )
+        slots = [[None] * len(to_y), [None] * len(to_x)]
+        for _, which, i in order:
+            slots[which][i] = (to_y, to_x)[which][i]()
+        arrived.append((outs[0], slots[0]))
         if following is not None:
-            moving.append(exchange_x(sends))
-        arrived.append(
-            [
-                out
-                if shift == (0, 0)
-                else lax.ppermute(out, "gy", [(i, to(i, shift)) for i in range(n_y)])
-                for out, shift in zip(outs, shifts)
-            ]
-        )
-        if (k + 1) % per_gram == 0:
-            group = arrived[k + 1 - per_gram :]
-            blocks = [group[index][part] for part in range(n_y) for index in range(per_gram)]
-            carried = gram(blocks, carried, sources, pieces, share)
+            moving.append(slots[1])
+    for done in range(0, len(chunks), per_gram):
+        if done + per_gram + 2 >= len(chunks):
+            carried = add_gram(carried, arrived[done : done + per_gram])
 
     summed = sum_over_all(carried)
     whole = n_y * PITCH

time: 1840 us -> 945 us (0.51)
  Pallas kernels: 1080 us -> 154 us
  waiting for transfers between devices: 316 us -> 460 us
  starting transfers between devices: 246 us -> 132 us
    pallas_call x9, Pallas kernels: 789 us -> 99.9 us  [project(): pl.pallas_call(body, out_shape=shapes, in_specs=[pl.BlockSpec(memory_spac...]
    pallas_call x1 -> x3, Pallas kernels: 252 us -> 13.8 us  [pack(): pl.pallas_call(body, out_shape=shapes, in_specs=[pl.BlockSpec(memory_spac...]
    ppermute x90, waiting for transfers between devices: 279 us -> 422 us  [start(): flown.append(lax.ppermute(operand, axis, pairs))]
    ppermute x90, starting transfers between devices: 229 us -> 119 us  [start(): flown.append(lax.ppermute(operand, axis, pairs))]
  transfers between devices with their start and end apart: 102 -> 102, of which waited for: 52 -> 56; matrix products, arithmetic and copies ran while one was open for 1% -> 1% of each run, Pallas kernels for 44% -> 14%
where the time goes in v3:
time: 945 us; the launch traced here: 937 us
  waiting for transfers between devices  460 us (49%)
  Pallas kernels  154 us (16%)
  starting transfers between devices  132 us (14%)
  other arithmetic  128 us (14%)
  local copies, waits for them, and re-layouts  37.5 us (4%)
  matrix products  20.6 us (2%)
    ppermute x90, waiting for transfers between devices, start(): flown.append(lax.ppermute(operand, axis, pairs))  422 us
    ppermute x90, starting transfers between devices, start(): flown.append(lax.ppermute(operand, axis, pairs))  119 us
    another operation x22, other arithmetic, finish(): return slice_out(lax.linalg.cholesky(total.T, symmetrize_input=False).T)  118 us
    pallas_call x9, Pallas kernels, project(): pl.pallas_call(body, out_shape=shapes, in_specs=[pl.BlockSpec(memory_spac...  99.9 us
    pallas_call x3, Pallas kernels, gram(): pl.pallas_call(body, out_shape=jax.ShapeDtypeStruct((len(block_pairs(whol...  40.3 us
    ppermute x6, waiting for transfers between devices, swap(): return lax.ppermute(value, axis, flips)  32 us
  transfers between devices with their start and end apart: 102, of which 56 were waited for; matrix products, arithmetic and copies ran while one was open for 1% of the time, Pallas kernels for 14%

profile of v3, /device:TPU:0, one launch (start us, length us, event | category | flops | bytes accessed | tf_op | source)
XLA Modules:
  0.0 937.3 jit_solution(12820768018944011201)
XLA Ops:
  14.9 24.7 %collective-permute-done.1.rest_1_ = bf16[32,168,128]{2,1,0:T(8,128)(2,1)} collective-permute-done((bf16[32,168,128]{2,1,0:T(8,128)(2,1)}, bf16[32,168,128]{2,1,0:T(8,128)(2,1)}, u32[]{:S(2)}, u32[]{:S(2)}) %collective-permute-start.1) | collective-permute-done | bytes 1376288 | tf_op jit(solution)/shard_map/ppermute | solution.py:409
  41.5 28.0 %collective-permute-done.rest_0_ = bf16[32,168,128]{2,1,0:T(8,128)(2,1)} collective-permute-done((bf16[32,168,128]{2,1,0:T(8,128)(2,1)}, bf16[32,168,128]{2,1,0:T(8,128)(2,1)}, u32[]{:S(2)}, u32[]{:S(2)}) %collective-permute-start) | collective-permute-done | bytes 1376288 | tf_op jit(solution)/shard_map/ppermute | solution.py:409
  82.4 12.6 %project.9 = (bf16[1344,128]{1,0:T(8,128)(2,1)}, bf16[1344,128]{1,0:T(8,128)(2,1)}, bf16[1344,128]{1,0:T(8,128)(2,1)}, bf16[1344,128]{1,0:T(8,128)(2,1)}, bf16[1...) custom-call(s32[12]{0:T(128)} %stack.102.scalars, ...), custom_call_target="tpu_custom_call" | custom-call | tf_op jit(solution)/shard_map/project/pallas_call | solution.py:169
  111.3 17.2 %collective-permute-done.3.rest_0_ = bf16[32,168,128]{2,1,0:T(8,128)(2,1)} collective-permute-done((bf16[32,168,128]{2,1,0:T(8,128)(2,1)}, bf16[32,168,128]{2,1,0:T(8,128)(2,1)}, u32[]{:S(2)}, u32[]{:S(2)}) %collective-permute-start.3) | collective-permute-done | bytes 1376288 | tf_op jit(solution)/shard_map/ppermute | solution.py:409
  134.6 21.5 %collective-permute-done.23.rest_12_ = bf16[1344,128]{1,0:T(8,128)(2,1)S(1)} collective-permute-done((bf16[1344,128]{1,0:T(8,128)(2,1)S(1)}, bf16[1344,128]{1,0:T(8,128)(2,1)S(1)}, u32[]{:S(2)}, u32[]{:S(2)}) %collective-permute-start.23) | collective-permute-done | bytes 344096 | tf_op jit(solution)/shard_map/ppermute | solution.py:409
  178.1 12.9 %project.11 = (bf16[1344,128]{1,0:T(8,128)(2,1)}, bf16[1344,128]{1,0:T(8,128)(2,1)}, bf16[1344,128]{1,0:T(8,128)(2,1)}, bf16[1344,128]{1,0:T(8,128)(2,1)}, bf16[...) custom-call(s32[12]{0:T(128)} %stack.102.scalars, ...), custom_call_target="tpu_custom_call" | custom-call | tf_op jit(solution)/shard_map/project/pallas_call | solution.py:169
  204.2 11.1 %collective-permute-done.33.rest_10_ = bf16[1344,128]{1,0:T(8,128)(2,1)} collective-permute-done((bf16[1344,128]{1,0:T(8,128)(2,1)}, bf16[1344,128]{1,0:T(8,128)(2,1)}, u32[]{:S(2)}, u32[]{:S(2)}) %collective-permute-start.33) | collective-permute-done | bytes 344096 | tf_op jit(solution)/shard_map/ppermute | solution.py:409
  215.3 20.0 %collective-permute-done.30.rest_13_ = bf16[1344,128]{1,0:T(8,128)(2,1)} collective-permute-done((bf16[1344,128]{1,0:T(8,128)(2,1)}, bf16[1344,128]{1,0:T(8,128)(2,1)}, u32[]{:S(2)}, u32[]{:S(2)}) %collective-permute-start.30) | collective-permute-done | bytes 344096 | tf_op jit(solution)/shard_map/ppermute | solution.py:409
  263.4 10.4 %collective-permute-done.37.rest_11_ = bf16[840,128]{1,0:T(8,128)(2,1)} collective-permute-done((bf16[840,128]{1,0:T(8,128)(2,1)}, bf16[840,128]{1,0:T(8,128)(2,1)}, u32[]{:S(2)}, u32[]{:S(2)}) %collective-permute-start.37) | collective-permute-done | bytes 215072 | tf_op jit(solution)/shard_map/ppermute | solution.py:409
  276.4 12.7 %collective-permute-done.39.rest_17_ = bf16[840,128]{1,0:T(8,128)(2,1)} collective-permute-done((bf16[840,128]{1,0:T(8,128)(2,1)}, bf16[840,128]{1,0:T(8,128)(2,1)}, u32[]{:S(2)}, u32[]{:S(2)}) %collective-permute-start.39) | collective-permute-done | bytes 215072 | tf_op jit(solution)/shard_map/ppermute | solution.py:409
  293.4 12.6 %project.13 = (bf16[1344,128]{1,0:T(8,128)(2,1)}, bf16[1344,128]{1,0:T(8,128)(2,1)}, bf16[1344,128]{1,0:T(8,128)(2,1)}, bf16[1344,128]{1,0:T(8,128)(2,1)}, bf16[...) custom-call(s32[12]{0:T(128)} %stack.102.scalars, ...), custom_call_target="tpu_custom_call" | custom-call | tf_op jit(solution)/shard_map/project/pallas_call | solution.py:169
  318.8 23.2 %collective-permute-done.50.rest_12_ = bf16[1344,128]{1,0:T(8,128)(2,1)S(1)} collective-permute-done((bf16[1344,128]{1,0:T(8,128)(2,1)}, bf16[1344,128]{1,0:T(8,128)(2,1)S(1)}, u32[]{:S(2)}, u32[]{:S(2)}) %collective-permute-start.50) | collective-permute-done | bytes 344096 | tf_op jit(solution)/shard_map/ppermute | solution.py:409
  344.8 12.6 %project.12 = (bf16[1344,128]{1,0:T(8,128)(2,1)}, bf16[1344,128]{1,0:T(8,128)(2,1)}, bf16[1344,128]{1,0:T(8,128)(2,1)}, bf16[1344,128]{1,0:T(8,128)(2,1)}, bf16[...) custom-call(s32[12]{0:T(128)} %stack.102.scalars, ...), custom_call_target="tpu_custom_call" | custom-call | tf_op jit(solution)/shard_map/project/pallas_call | solution.py:169
  383.6 10.3 %collective-permute-done.60.rest_10_ = bf16[1344,128]{1,0:T(8,128)(2,1)} collective-permute-done((bf16[1344,128]{1,0:T(8,128)(2,1)}, bf16[1344,128]{1,0:T(8,128)(2,1)}, u32[]{:S(2)}, u32[]{:S(2)}) %collective-permute-start.60) | collective-permute-done | bytes 344096 | tf_op jit(solution)/shard_map/ppermute | solution.py:409
  401.4 21.5 %collective-permute-done.61.rest_16_ = bf16[1344,128]{1,0:T(8,128)(2,1)} collective-permute-done((bf16[1344,128]{1,0:T(8,128)(2,1)}, bf16[1344,128]{1,0:T(8,128)(2,1)}, u32[]{:S(2)}, u32[]{:S(2)}) %collective-permute-start.61) | collective-permute-done | bytes 344096 | tf_op jit(solution)/shard_map/ppermute | solution.py:409
  440.5 13.0 %gram.3.rest_4_.rest_24_ = f32[1536,256]{1,0:T(8,128)} custom-call(s32[8]{0:T(128)} %stack.89.sources, bf16[1344,128]{1,0:T(8,128)(2,1)} %get-tuple-element.338.rest_0_, bf16[1344,128]{1,0:T(8,128)(2,1)} %get-tuple-element.339.rest_1_, bf16[840,128]{1,0:T(8,128)(2,1)} %get-tuple-element.340.rest_2_, bf16[1344,128]{1,0:T(8,128)(2,1)} %collective-permute-done.21.rest_3_, ...), custom_call_target="tpu_custom_call" | custom-call | tf_op jit(solution)/shard_map/gram/pallas_call | solution.py:258
  471.8 14.2 %collective-permute-done.65.rest_14_ = bf16[840,128]{1,0:T(8,128)(2,1)S(1)} collective-permute-done((bf16[840,128]{1,0:T(8,128)(2,1)}, bf16[840,128]{1,0:T(8,128)(2,1)S(1)}, u32[]{:S(2)}, u32[]{:S(2)}) %collective-permute-start.65) | collective-permute-done | bytes 215072 | tf_op jit(solution)/shard_map/ppermute | solution.py:409
  491.3 11.3 %project.14 = (bf16[1344,128]{1,0:T(8,128)(2,1)}, bf16[1344,128]{1,0:T(8,128)(2,1)}, bf16[1344,128]{1,0:T(8,128)(2,1)}, bf16[1344,128]{1,0:T(8,128)(2,1)}, bf16[...) custom-call(s32[12]{0:T(128)} %stack.102.scalars, ...), custom_call_target="tpu_custom_call" | custom-call | tf_op jit(solution)/shard_map/project/pallas_call | solution.py:169
  531.4 10.6 %collective-permute-start.75 = (bf16[1344,128]{1,0:T(8,128)(2,1)}, bf16[1344,128]{1,0:T(8,128)(2,1)S(1)}, u32[]{:S(2)}, u32[]{:S(2)}) collective-permute-start(bf16[1344,128]{1,0:T(8,128)(2,1)} %get-tuple-element.504), channel_id=1, source_target_pairs={{0,5},{1,4},{2,7},{3,6},{4,1},{5,0},{6,3},{7,2},{8,13},{9,12},{10,... | collective-permute-start | bytes 1032200 | tf_op jit(solution)/shard_map/ppermute | solution.py:409
  542.0 10.0 %collective-permute-done.71.rest_12_ = bf16[1344,128]{1,0:T(8,128)(2,1)S(1)} collective-permute-done((bf16[1344,128]{1,0:T(8,128)(2,1)}, bf16[1344,128]{1,0:T(8,128)(2,1)S(1)}, u32[]{:S(2)}, u32[]{:S(2)}) %collective-permute-start.71) | collective-permute-done | bytes 344096 | tf_op jit(solution)/shard_map/ppermute | solution.py:409
  569.5 11.3 %project.16 = (bf16[1344,128]{1,0:T(8,128)(2,1)}, bf16[1344,128]{1,0:T(8,128)(2,1)}, bf16[1344,128]{1,0:T(8,128)(2,1)}, bf16[1344,128]{1,0:T(8,128)(2,1)}, bf16[...) custom-call(s32[12]{0:T(128)} %stack.102.scalars, ...), custom_call_target="tpu_custom_call" | custom-call | tf_op jit(solution)/shard_map/project/pallas_call | solution.py:169
  592.3 11.4 %collective-permute-done.81.rest_10_ = bf16[1344,128]{1,0:T(8,128)(2,1)S(1)} collective-permute-done((bf16[1344,128]{1,0:T(8,128)(2,1)}, bf16[1344,128]{1,0:T(8,128)(2,1)S(1)}, u32[]{:S(2)}, u32[]{:S(2)}) %collective-permute-start.81) | collective-permute-done | bytes 344096 | tf_op jit(solution)/shard_map/ppermute | solution.py:409
  603.7 18.5 %collective-permute-done.78.rest_13_ = bf16[1344,128]{1,0:T(8,128)(2,1)S(1)} collective-permute-done((bf16[1344,128]{1,0:T(8,128)(2,1)}, bf16[1344,128]{1,0:T(8,128)(2,1)S(1)}, u32[]{:S(2)}, u32[]{:S(2)}) %collective-permute-start.78) | collective-permute-done | bytes 344096 | tf_op jit(solution)/shard_map/ppermute | solution.py:409
  629.9 13.7 %gram.4.rest_4_.rest_24_ = f32[1536,256]{1,0:T(8,128)} custom-call(s32[8]{0:T(128)} %stack.89.sources, bf16[1344,128]{1,0:T(8,128)(2,1)} %get-tuple-element.417.rest_0_, bf16[1344,128]{1,0:T(8,128)(2,1)} %get-tuple-element.418.rest_1_, bf16[840,128]{1,0:T(8,128)(2,1)} %get-tuple-element.419.rest_2_, bf16[1344,128]{1,0:T(8,128)(2,1)} %copy-done.26, ...), custom_call_target="tpu_custom_call" | custom-call | tf_op jit(solution)/shard_map/gram/pallas_call | solution.py:258
  702.8 13.6 %gram.5 = f32[1536,256]{1,0:T(8,128)} custom-call(s32[8]{0:T(128)} %stack.89.sources, bf16[1344,128]{1,0:T(8,128)(2,1)} %get-tuple-element.334.rest_0_, bf16[1344,128]{1,0:T(8,128)(2,1)} %get-tuple-element.413.rest_1_, bf16[840,128]{1,0:T(8,128)(2,1)} %get-tuple-element.483.rest_2_, bf16[1344,128]{1,0:T(8,128)(2,1)} %copy-done.33, ...), custom_call_target="tpu_custom_call" | custom-call | tf_op jit(solution)/shard_map/gram/pallas_call | solution.py:258
  722.7 10.2 %collective-permute-done.91 = f32[384,256]{1,0:T(8,128)} collective-permute-done((f32[384,256]{1,0:T(8,128)S(1)}, f32[384,256]{1,0:T(8,128)}, u32[]{:S(2)}, u32[]{:S(2)}) %collective-permute-start.91) | collective-permute-done | bytes 393248 | tf_op jit(solution)/shard_map/ppermute | solution.py:316
  799.1 11.7 %cholesky.166 = f32[128,128]{1,0:T(8,128)S(1)} custom-call(f32[128,128]{1,0:T(8,128)S(1)} %cholesky.430), custom_call_target="Cholesky" | custom-call | tf_op jit(solution)/shard_map/cholesky | solution.py:290
  825.8 11.7 %cholesky.189 = f32[128,128]{1,0:T(8,128)S(1)} custom-call(f32[128,128]{1,0:T(8,128)S(1)} %cholesky.434), custom_call_target="Cholesky" | custom-call | tf_op jit(solution)/shard_map/cholesky | solution.py:290
  850.6 11.7 %cholesky.356 = f32[128,128]{1,0:T(8,128)S(1)} custom-call(f32[128,128]{1,0:T(8,128)S(1)} %cholesky.439), custom_call_target="Cholesky" | custom-call | tf_op jit(solution)/shard_map/cholesky | solution.py:290
  863.7 10.2 %custom-call.34 = f32[1,128,128]{1,2,0:T(8,128)S(1)} custom-call(f32[1,128,128]{2,1,0:T(8,128)S(1)} %get-tuple-element.565), custom_call_target="InvertDiagBlocksLowerTriangular" | custom-call | tf_op jit(solution)/shard_map/cholesky | solution.py:290
  876.5 11.7 %cholesky.375 = f32[128,128]{1,0:T(8,128)S(1)} custom-call(f32[128,128]{1,0:T(8,128)S(1)} %cholesky.444), custom_call_target="Cholesky" | custom-call | tf_op jit(solution)/shard_map/cholesky | solution.py:290
  901.7 11.9 %cholesky.394 = f32[128,128]{1,0:T(8,128)S(1)} custom-call(f32[128,128]{1,0:T(8,128)S(1)} %cholesky.449), custom_call_target="Cholesky" | custom-call | tf_op jit(solution)/shard_map/cholesky | solution.py:290
  (377 shorter events, 474.0 us)
Async XLA Ops:
  6.2 33.5 %collective-permute-start.1 = (bf16[32,168,128]{2,1,0:T(8,128)(2,1)}, bf16[32,168,128]{2,1,0:T(8,128)(2,1)}, u32[]{:S(2)}, u32[]{:S(2)}) collective-permute-start(bf16[32,168,128]{2,1,0:T(8,128)(2,1)} %get-tuple-element.278), channel_id=1, source_target_pairs={{0,24},{8,16},{16,8},{24,0},{1,25},{9,17},{17,9},{25,1},{2,26},{10... | collective-permute-start | bytes 4128776 | tf_op jit(solution)/shard_map/ppermute | solution.py:409
  8.8 60.8 %collective-permute-start = (bf16[32,168,128]{2,1,0:T(8,128)(2,1)}, bf16[32,168,128]{2,1,0:T(8,128)(2,1)}, u32[]{:S(2)}, u32[]{:S(2)}) collective-permute-start(bf16[32,168,128]{2,1,0:T(8,128)(2,1)} %get-tuple-element.275), channel_id=1, source_target_pairs={{0,16},{8,24},{16,0},{24,8},{1,17},{9,25},{17,1},{25,9},{2,18},{10... | collective-permute-start | bytes 4128776 | tf_op jit(solution)/shard_map/ppermute | solution.py:409
  14.8 95.8 %collective-permute-start.7 = (bf16[32,168,128]{2,1,0:T(8,128)(2,1)}, bf16[32,168,128]{2,1,0:T(8,128)(2,1)S(1)}, u32[]{:S(2)}, u32[]{:S(2)}) collective-permute-start(bf16[32,168,128]{2,1,0:T(8,128)(2,1)} %get-tuple-element.295), channel_id=1, source_target_pairs={{0,8},{8,0},{16,24},{24,16},{1,9},{9,1},{17,25},{25,17},{2,10},{10... | collective-permute-start | bytes 4128776 | tf_op jit(solution)/shard_map/ppermute | solution.py:409
  39.6 71.0 %collective-permute-start.5 = (bf16[32,168,128]{2,1,0:T(8,128)(2,1)}, bf16[32,168,128]{2,1,0:T(8,128)(2,1)}, u32[]{:S(2)}, u32[]{:S(2)}) collective-permute-start(bf16[32,168,128]{2,1,0:T(8,128)(2,1)} %get-tuple-element.290), channel_id=1, source_target_pairs={{0,24},{8,16},{16,8},{24,0},{1,25},{9,17},{17,9},{25,1},{2,26},{10... | collective-permute-start | bytes 4128776 | tf_op jit(solution)/shard_map/ppermute | solution.py:409
  69.6 59.0 %collective-permute-start.3 = (bf16[32,168,128]{2,1,0:T(8,128)(2,1)}, bf16[32,168,128]{2,1,0:T(8,128)(2,1)}, u32[]{:S(2)}, u32[]{:S(2)}) collective-permute-start(bf16[32,168,128]{2,1,0:T(8,128)(2,1)} %get-tuple-element.285), channel_id=1, source_target_pairs={{0,16},{8,24},{16,0},{24,8},{1,17},{9,25},{17,1},{25,9},{2,18},{10... | collective-permute-start | bytes 4128776 | tf_op jit(solution)/shard_map/ppermute | solution.py:409
  96.6 33.9 %collective-permute-start.22 = (bf16[1344,128]{1,0:T(8,128)(2,1)}, bf16[1344,128]{1,0:T(8,128)(2,1)S(1)}, u32[]{:S(2)}, u32[]{:S(2)}) collective-permute-start(bf16[1344,128]{1,0:T(8,128)(2,1)} %get-tuple-element.348), channel_id=1, source_target_pairs={{0,2},{1,3},{2,4},{3,5},{4,6},{5,7},{6,0},{7,1},{8,10},{9,11},{10,... | collective-permute-start | bytes 1032200 | tf_op jit(solution)/shard_map/ppermute | solution.py:409
  110.6 63.5 %collective-permute-start.8 = (bf16[20,168,128]{2,1,0:T(8,128)(2,1)}, bf16[20,168,128]{2,1,0:T(8,128)(2,1)S(1)}, u32[]{:S(2)}, u32[]{:S(2)}) collective-permute-start(bf16[20,168,128]{2,1,0:T(8,128)(2,1)} %get-tuple-element.296), channel_id=1, source_target_pairs={{0,8},{8,0},{16,24},{24,16},{1,9},{9,1},{17,25},{25,17},{2,10},{10... | collective-permute-start | bytes 2580488 | tf_op jit(solution)/shard_map/ppermute | solution.py:409
  110.7 63.4 %collective-permute-start.6 = (bf16[20,168,128]{2,1,0:T(8,128)(2,1)}, bf16[20,168,128]{2,1,0:T(8,128)(2,1)S(1)}, u32[]{:S(2)}, u32[]{:S(2)}) collective-permute-start(bf16[20,168,128]{2,1,0:T(8,128)(2,1)} %get-tuple-element.291), channel_id=1, source_target_pairs={{0,24},{8,16},{16,8},{24,0},{1,25},{9,17},{17,9},{25,1},{2,26},{10... | collective-permute-start | bytes 2580488 | tf_op jit(solution)/shard_map/ppermute | solution.py:409
  128.5 47.1 %collective-permute-start.4 = (bf16[20,168,128]{2,1,0:T(8,128)(2,1)}, bf16[20,168,128]{2,1,0:T(8,128)(2,1)S(1)}, u32[]{:S(2)}, u32[]{:S(2)}) collective-permute-start(bf16[20,168,128]{2,1,0:T(8,128)(2,1)} %get-tuple-element.286), channel_id=1, source_target_pairs={{0,16},{8,24},{16,0},{24,8},{1,17},{9,25},{17,1},{25,9},{2,18},{10... | collective-permute-start | bytes 2580488 | tf_op jit(solution)/shard_map/ppermute | solution.py:409
  156.1 34.9 %collective-permute-start.24 = (bf16[1344,128]{1,0:T(8,128)(2,1)}, bf16[1344,128]{1,0:T(8,128)(2,1)}, u32[]{:S(2)}, u32[]{:S(2)}) collective-permute-start(bf16[1344,128]{1,0:T(8,128)(2,1)} %get-tuple-element.350), channel_id=1, source_target_pairs={{0,6},{1,7},{2,0},{3,1},{4,2},{5,3},{6,4},{7,5},{8,14},{9,15},{10,... | collective-permute-start | bytes 1032200 | tf_op jit(solution)/shard_map/ppermute | solution.py:409
  174.1 84.3 %collective-permute-start.13 = (bf16[32,168,128]{2,1,0:T(8,128)(2,1)}, bf16[32,168,128]{2,1,0:T(8,128)(2,1)S(1)}, u32[]{:S(2)}, u32[]{:S(2)}) collective-permute-start(bf16[32,168,128]{2,1,0:T(8,128)(2,1)} %get-tuple-element.313), channel_id=1, source_target_pairs={{0,8},{8,0},{16,24},{24,16},{1,9},{9,1},{17,25},{25,17},{2,10},{10... | collective-permute-start | bytes 4128776 | tf_op jit(solution)/shard_map/ppermute | solution.py:409
  175.1 83.4 %collective-permute-start.11 = (bf16[32,168,128]{2,1,0:T(8,128)(2,1)}, bf16[32,168,128]{2,1,0:T(8,128)(2,1)S(1)}, u32[]{:S(2)}, u32[]{:S(2)}) collective-permute-start(bf16[32,168,128]{2,1,0:T(8,128)(2,1)} %get-tuple-element.308), channel_id=1, source_target_pairs={{0,24},{8,16},{16,8},{24,0},{1,25},{9,17},{17,9},{25,1},{2,26},{10... | collective-permute-start | bytes 4128776 | tf_op jit(solution)/shard_map/ppermute | solution.py:409
  176.6 82.5 %collective-permute-start.9 = (bf16[32,168,128]{2,1,0:T(8,128)(2,1)}, bf16[32,168,128]{2,1,0:T(8,128)(2,1)S(1)}, u32[]{:S(2)}, u32[]{:S(2)}) collective-permute-start(bf16[32,168,128]{2,1,0:T(8,128)(2,1)} %get-tuple-element.303), channel_id=1, source_target_pairs={{0,16},{8,24},{16,0},{24,8},{1,17},{9,25},{17,1},{25,9},{2,18},{10... | collective-permute-start | bytes 4128776 | tf_op jit(solution)/shard_map/ppermute | solution.py:409
  258.4 84.2 %collective-permute-start.14 = (bf16[32,168,128]{2,1,0:T(8,128)(2,1)}, bf16[32,168,128]{2,1,0:T(8,128)(2,1)S(1)}, u32[]{:S(2)}, u32[]{:S(2)}) collective-permute-start(bf16[32,168,128]{2,1,0:T(8,128)(2,1)} %get-tuple-element.314), channel_id=1, source_target_pairs={{0,8},{8,0},{16,24},{24,16},{1,9},{9,1},{17,25},{25,17},{2,10},{10... | collective-permute-start | bytes 4128776 | tf_op jit(solution)/shard_map/ppermute | solution.py:409
  258.5 84.2 %collective-permute-start.12 = (bf16[32,168,128]{2,1,0:T(8,128)(2,1)}, bf16[32,168,128]{2,1,0:T(8,128)(2,1)}, u32[]{:S(2)}, u32[]{:S(2)}) collective-permute-start(bf16[32,168,128]{2,1,0:T(8,128)(2,1)} %get-tuple-element.309), channel_id=1, source_target_pairs={{0,24},{8,16},{16,8},{24,0},{1,25},{9,17},{17,9},{25,1},{2,26},{10... | collective-permute-start | bytes 4128776 | tf_op jit(solution)/shard_map/ppermute | solution.py:409
  259.1 84.2 %collective-permute-start.10 = (bf16[32,168,128]{2,1,0:T(8,128)(2,1)}, bf16[32,168,128]{2,1,0:T(8,128)(2,1)}, u32[]{:S(2)}, u32[]{:S(2)}) collective-permute-start(bf16[32,168,128]{2,1,0:T(8,128)(2,1)} %get-tuple-element.304), channel_id=1, source_target_pairs={{0,16},{8,24},{16,0},{24,8},{1,17},{9,25},{17,1},{25,9},{2,18},{10... | collective-permute-start | bytes 4128776 | tf_op jit(solution)/shard_map/ppermute | solution.py:409
  342.5 37.6 %collective-permute-start.19 = (bf16[20,168,128]{2,1,0:T(8,128)(2,1)}, bf16[20,168,128]{2,1,0:T(8,128)(2,1)S(1)}, u32[]{:S(2)}, u32[]{:S(2)}) collective-permute-start(bf16[20,168,128]{2,1,0:T(8,128)(2,1)} %get-tuple-element.331), channel_id=1, source_target_pairs={{0,8},{8,0},{16,24},{24,16},{1,9},{9,1},{17,25},{25,17},{2,10},{10... | collective-permute-start | bytes 2580488 | tf_op jit(solution)/shard_map/ppermute | solution.py:409
  342.8 38.4 %collective-permute-start.17 = (bf16[20,168,128]{2,1,0:T(8,128)(2,1)}, bf16[20,168,128]{2,1,0:T(8,128)(2,1)}, u32[]{:S(2)}, u32[]{:S(2)}) collective-permute-start(bf16[20,168,128]{2,1,0:T(8,128)(2,1)} %get-tuple-element.326), channel_id=1, source_target_pairs={{0,24},{8,16},{16,8},{24,0},{1,25},{9,17},{17,9},{25,1},{2,26},{10... | collective-permute-start | bytes 2580488 | tf_op jit(solution)/shard_map/ppermute | solution.py:409
  343.4 39.6 %collective-permute-start.15 = (bf16[20,168,128]{2,1,0:T(8,128)(2,1)}, bf16[20,168,128]{2,1,0:T(8,128)(2,1)}, u32[]{:S(2)}, u32[]{:S(2)}) collective-permute-start(bf16[20,168,128]{2,1,0:T(8,128)(2,1)} %get-tuple-element.321), channel_id=1, source_target_pairs={{0,16},{8,24},{16,0},{24,8},{1,17},{9,25},{17,1},{25,9},{2,18},{10... | collective-permute-start | bytes 2580488 | tf_op jit(solution)/shard_map/ppermute | solution.py:409
  381.1 107.8 %collective-permute-start.20 = (bf16[32,168,128]{2,1,0:T(8,128)(2,1)}, bf16[32,168,128]{2,1,0:T(8,128)(2,1)S(1)}, u32[]{:S(2)}, u32[]{:S(2)}) collective-permute-start(bf16[32,168,128]{2,1,0:T(8,128)(2,1)} %get-tuple-element.332), channel_id=1, source_target_pairs={{0,8},{8,0},{16,24},{24,16},{1,9},{9,1},{17,25},{25,17},{2,10},{10... | collective-permute-start | bytes 4128776 | tf_op jit(solution)/shard_map/ppermute | solution.py:409
  381.3 107.7 %collective-permute-start.18 = (bf16[32,168,128]{2,1,0:T(8,128)(2,1)}, bf16[32,168,128]{2,1,0:T(8,128)(2,1)}, u32[]{:S(2)}, u32[]{:S(2)}) collective-permute-start(bf16[32,168,128]{2,1,0:T(8,128)(2,1)} %get-tuple-element.327), channel_id=1, source_target_pairs={{0,24},{8,16},{16,8},{24,0},{1,25},{9,17},{17,9},{25,1},{2,26},{10... | collective-permute-start | bytes 4128776 | tf_op jit(solution)/shard_map/ppermute | solution.py:409
  383.0 106.8 %collective-permute-start.16 = (bf16[32,168,128]{2,1,0:T(8,128)(2,1)}, bf16[32,168,128]{2,1,0:T(8,128)(2,1)}, u32[]{:S(2)}, u32[]{:S(2)}) collective-permute-start(bf16[32,168,128]{2,1,0:T(8,128)(2,1)} %get-tuple-element.322), channel_id=1, source_target_pairs={{0,16},{8,24},{16,0},{24,8},{1,17},{9,25},{17,1},{25,9},{2,18},{10... | collective-permute-start | bytes 4128776 | tf_op jit(solution)/shard_map/ppermute | solution.py:409
  422.9 39.7 %collective-permute-start.62 = (bf16[1344,128]{1,0:T(8,128)(2,1)}, bf16[1344,128]{1,0:T(8,128)(2,1)}, u32[]{:S(2)}, u32[]{:S(2)}) collective-permute-start(bf16[1344,128]{1,0:T(8,128)(2,1)} %get-tuple-element.455), channel_id=1, source_target_pairs={{0,7},{1,6},{2,1},{3,0},{4,3},{5,2},{6,5},{7,4},{8,15},{9,14},{10,... | collective-permute-start | bytes 1032200 | tf_op jit(solution)/shard_map/ppermute | solution.py:409
  429.9 32.9 %collective-permute-start.58 = (bf16[1344,128]{1,0:T(8,128)(2,1)}, bf16[1344,128]{1,0:T(8,128)(2,1)}, u32[]{:S(2)}, u32[]{:S(2)}) collective-permute-start(bf16[1344,128]{1,0:T(8,128)(2,1)} %get-tuple-element.444), channel_id=1, source_target_pairs={{0,6},{1,7},{2,0},{3,1},{4,2},{5,3},{6,4},{7,5},{8,14},{9,15},{10,... | collective-permute-start | bytes 1032200 | tf_op jit(solution)/shard_map/ppermute | solution.py:409
  489.0 78.4 %collective-permute-start.44 = (bf16[32,168,128]{2,1,0:T(8,128)(2,1)}, bf16[32,168,128]{2,1,0:T(8,128)(2,1)S(1)}, u32[]{:S(2)}, u32[]{:S(2)}) collective-permute-start(bf16[32,168,128]{2,1,0:T(8,128)(2,1)} %get-tuple-element.411), channel_id=1, source_target_pairs={{0,8},{8,0},{16,24},{24,16},{1,9},{9,1},{17,25},{25,17},{2,10},{10... | collective-permute-start | bytes 4128776 | tf_op jit(solution)/shard_map/ppermute | solution.py:409
  489.1 78.3 %collective-permute-start.43 = (bf16[32,168,128]{2,1,0:T(8,128)(2,1)}, bf16[32,168,128]{2,1,0:T(8,128)(2,1)S(1)}, u32[]{:S(2)}, u32[]{:S(2)}) collective-permute-start(bf16[32,168,128]{2,1,0:T(8,128)(2,1)} %get-tuple-element.408), channel_id=1, source_target_pairs={{0,24},{8,16},{16,8},{24,0},{1,25},{9,17},{17,9},{25,1},{2,26},{10... | collective-permute-start | bytes 4128776 | tf_op jit(solution)/shard_map/ppermute | solution.py:409
  489.8 77.6 %collective-permute-start.42 = (bf16[32,168,128]{2,1,0:T(8,128)(2,1)}, bf16[32,168,128]{2,1,0:T(8,128)(2,1)S(1)}, u32[]{:S(2)}, u32[]{:S(2)}) collective-permute-start(bf16[32,168,128]{2,1,0:T(8,128)(2,1)} %get-tuple-element.405), channel_id=1, source_target_pairs={{0,16},{8,24},{16,0},{24,8},{1,17},{9,25},{17,1},{25,9},{2,18},{10... | collective-permute-start | bytes 4128776 | tf_op jit(solution)/shard_map/ppermute | solution.py:409
  581.9 61.7 %collective-permute-start.47 = (bf16[20,168,128]{2,1,0:T(8,128)(2,1)}, bf16[20,168,128]{2,1,0:T(8,128)(2,1)S(1)}, u32[]{:S(2)}, u32[]{:S(2)}) collective-permute-start(bf16[20,168,128]{2,1,0:T(8,128)(2,1)} %get-tuple-element.416), channel_id=1, source_target_pairs={{0,8},{8,0},{16,24},{24,16},{1,9},{9,1},{17,25},{25,17},{2,10},{10... | collective-permute-start | bytes 2580488 | tf_op jit(solution)/shard_map/ppermute | solution.py:409
  581.9 61.7 %collective-permute-start.46 = (bf16[20,168,128]{2,1,0:T(8,128)(2,1)}, bf16[20,168,128]{2,1,0:T(8,128)(2,1)S(1)}, u32[]{:S(2)}, u32[]{:S(2)}) collective-permute-start(bf16[20,168,128]{2,1,0:T(8,128)(2,1)} %get-tuple-element.415), channel_id=1, source_target_pairs={{0,24},{8,16},{16,8},{24,0},{1,25},{9,17},{17,9},{25,1},{2,26},{10... | collective-permute-start | bytes 2580488 | tf_op jit(solution)/shard_map/ppermute | solution.py:409
  582.6 61.0 %collective-permute-start.45 = (bf16[20,168,128]{2,1,0:T(8,128)(2,1)}, bf16[20,168,128]{2,1,0:T(8,128)(2,1)S(1)}, u32[]{:S(2)}, u32[]{:S(2)}) collective-permute-start(bf16[20,168,128]{2,1,0:T(8,128)(2,1)} %get-tuple-element.414), channel_id=1, source_target_pairs={{0,16},{8,24},{16,0},{24,8},{1,17},{9,25},{17,1},{25,9},{2,18},{10... | collective-permute-start | bytes 2580488 | tf_op jit(solution)/shard_map/ppermute | solution.py:409
  622.2 31.8 %collective-permute-start.79 = (bf16[1344,128]{1,0:T(8,128)(2,1)}, bf16[1344,128]{1,0:T(8,128)(2,1)}, u32[]{:S(2)}, u32[]{:S(2)}) collective-permute-start(bf16[1344,128]{1,0:T(8,128)(2,1)} %get-tuple-element.508), channel_id=1, source_target_pairs={{0,6},{1,7},{2,0},{3,1},{4,2},{5,3},{6,4},{7,5},{8,14},{9,15},{10,... | collective-permute-start | bytes 1032200 | tf_op jit(solution)/shard_map/ppermute | solution.py:409
  629.9 34.1 %collective-permute-start.83 = (bf16[1344,128]{1,0:T(8,128)(2,1)}, bf16[1344,128]{1,0:T(8,128)(2,1)}, u32[]{:S(2)}, u32[]{:S(2)}) collective-permute-start(bf16[1344,128]{1,0:T(8,128)(2,1)} %get-tuple-element.519), channel_id=1, source_target_pairs={{0,7},{1,6},{2,1},{3,0},{4,3},{5,2},{6,5},{7,4},{8,15},{9,14},{10,... | collective-permute-start | bytes 1032200 | tf_op jit(solution)/shard_map/ppermute | solution.py:409
  (130 other events, 3144.9 us)

commit v4 on v3

v4 whole, which is shorter than its diff:
```python
import functools

import jax
import jax.numpy as jnp
from jax import lax
from jax.experimental import pallas as pl
from jax.experimental.pallas import tpu as pltpu
from jax.sharding import PartitionSpec as P

LANES = 128
SUB = 32
STEP = 256
WINDOW = 5
AHEAD = 2
VMEM_BYTES = 56 * 1024 * 1024


def y_pieces(rows):
    count = -(-rows // SUB)
    size = rows // count
    return [(i * size, size) for i in range(count)]


def pitch_of(rows):
    return len(y_pieces(rows)) * SUB


def send_list(chunk, n_x):
    rows = chunk[1][1]
    half = rows // 2
    return [(partner, at, half) for at in (0, half) for partner in range(2, n_x)]


def copy_cells(fields, out, scalars, partner, cell, start, size, sem):
    column = pl.multiple_of(scalars[partner] + cell, LANES)
    return pltpu.make_async_copy(
        fields.at[pl.ds(start, size), :, pl.ds(column, LANES)], out, sem
    )


def chunk_copies(fields, outs, scalars, chunk, n_x, sems):
    cell, (start, _) = chunk
    return [
        copy_cells(fields, outs[i], scalars, partner, cell, start + at, size, sems.at[i])
        for i, (partner, at, size) in enumerate(send_list(chunk, n_x))
    ]


def run_pack(fields, scalars, shapes, make_copies):
    def body(scalars, fields, *rest):
        copies = make_copies(fields, rest[:-1], scalars, rest[-1])
        for copy in copies:
            copy.start()
        for copy in copies:
            copy.wait()

    return pl.pallas_call(
        body,
        out_shape=shapes,
        in_specs=[pl.BlockSpec(memory_space=pltpu.SMEM), pl.BlockSpec(memory_space=pl.ANY)],
        out_specs=[pl.BlockSpec(memory_space=pltpu.VMEM)] * len(shapes),
        scratch_shapes=[pltpu.SemaphoreType.DMA((len(shapes),))],
        compiler_params=pltpu.CompilerParams(vmem_limit_bytes=VMEM_BYTES),
        cost_estimate=pl.CostEstimate(flops=0, bytes_accessed=0, transcendentals=0),
        name="pack",
    )(scalars, fields)


def send_shapes(chunk, n_x, depth):
    return [
        jax.ShapeDtypeStruct((size, depth, LANES), jnp.bfloat16)
        for _, _, size in send_list(chunk, n_x)
    ]


def pack(fields, scalars, chunk, n_x):
    return run_pack(
        fields,
        scalars,
        send_shapes(chunk, n_x, fields.shape[1]),
        lambda fields, outs, scalars, sems: chunk_copies(fields, outs, scalars, chunk, n_x, sems),
    )


def pack_near(fields, scalars, cell):
    rows, depth = fields.shape[:2]
    return run_pack(
        fields,
        scalars,
        [jax.ShapeDtypeStruct((rows, depth, LANES), jnp.bfloat16)],
        lambda fields, outs, scalars, sems: [
            copy_cells(fields, outs[0], scalars, 1, cell, 0, rows, sems.at[0])
        ],
    )[0]


def project_kernel(chunk, following, n_x, rank, share, scalars, fields, near, got, factor, outs, sends, own, other, wide, sems):
    cell, (start, rows) = chunk
    copies = [
        copy_cells(fields, own, scalars, 0, cell, start, rows, sems.at[0]),
        pltpu.make_async_copy(near.at[pl.ds(start, rows)], other, sems.at[1]),
    ]
    for copy in copies:
        copy.start()
    packing = []
    if following is not None:
        packing = chunk_copies(
            fields, sends, scalars, following, n_x, sems.at[pl.ds(2, len(sends))]
        )
    for copy in packing:
        copy.start()
    for copy in copies:
        copy.wait()

    half = rows // 2
    many = max(n for n in range(1, 9) if half % n == 0)
    for start_row in (0, half):
        blocks = [(0, own, 0), (1, other, 0)]
        for (partner, at, _), block in zip(send_list(chunk, n_x), got):
            if at == start_row:
                blocks.append((partner, block, at))

        def one_group(group, _):
            y = start_row + group * many
            total = None
            for partner, block, at in blocks:
                right = jnp.concatenate([block[y - at + k] for k in range(many)], axis=1)
                term = jnp.dot(factor[partner], right, preferred_element_type=jnp.float32)
                total = term if total is None else total + term
            for k in range(many):
                at = pl.multiple_of((y + k) * rank, 8)
                wide[pl.ds(at, rank), :] = total[:, k * LANES : (k + 1) * LANES]
            return 0

        lax.fori_loop(0, half // many, one_group, 0)

    main = rows // 16 * 16
    left = rows - main
    for part in range(2 * len(outs)):
        out = outs[part // 2].at[part % 2]
        first = scalars[n_x + part]

        def one_row(i, _):
            picked = wide[pl.ds(first + i, main, stride=rank), :]
            out[pl.ds(pl.multiple_of(i * main, 16), main), :] = picked.astype(jnp.bfloat16)
            return 0

        lax.fori_loop(0, share, one_row, 0, unroll=6)
        for group in range(0, share if left else 0, 4):
            count = min(4, share - group)
            tile = [
                wide[pl.ds(main * rank + first + group + k, left, stride=rank), :]
                for k in range(count)
            ]
            tile = jnp.concatenate(tile, axis=0).astype(jnp.bfloat16)
            at = share * main + group * left
            out[at : at + count * left, :] = tile
    for copy in packing:
        copy.wait()


def project(fields, near, got, factor, scalars, chunk, following, n_x, share, slow, after):
    rows = chunk[1][1]
    rank = factor.shape[1]
    depth = fields.shape[1]
    n_got = len(got)
    n_sends = 0 if following is None else n_got
    n_after = len(after)
    vmem = pl.BlockSpec(memory_space=pltpu.VMEM)
    any_space = pl.BlockSpec(memory_space=pl.ANY)

    def body(scalars, fields, near, *rest):
        got = rest[:n_got]
        factor = rest[n_got]
        rest = rest[n_got + 1 + n_after :]
        outs = rest[:slow]
        sends = rest[slow : slow + n_sends]
        own, other, wide, sems = rest[slow + n_sends :]
        project_kernel(
            chunk, following, n_x, rank, share, scalars, fields, near, got, factor, outs, sends, own, other, wide, sems
        )

    shapes = [jax.ShapeDtypeStruct((2, share * rows, LANES), jnp.bfloat16)] * slow
    if following is not None:
        shapes += send_shapes(following, n_x, depth)
    outs = pl.pallas_call(
        body,
        out_shape=shapes,
        in_specs=[pl.BlockSpec(memory_space=pltpu.SMEM), any_space, any_space]
        + [vmem] * (n_got + 1)
        + [any_space] * n_after,
        out_specs=[vmem] * (slow + n_sends),
        scratch_shapes=[
            pltpu.VMEM((rows, depth, LANES), jnp.bfloat16),
            pltpu.VMEM((rows, depth, LANES), jnp.bfloat16),
            pltpu.VMEM((rows * rank, LANES), jnp.float32),
            pltpu.SemaphoreType.DMA((2 + n_got,)),
        ],
        compiler_params=pltpu.CompilerParams(vmem_limit_bytes=VMEM_BYTES),
        cost_estimate=pl.CostEstimate(flops=0, bytes_accessed=0, transcendentals=0),
        name="project",
    )(scalars, fields, near, *got, factor, *after)
    return outs[:slow], outs[slow:]


def block_pairs(whole):
    return [(i, j) for i in range(0, whole, STEP) for j in range(i, whole, STEP)]


def gram_kernel(pieces, share, places, blocks, carried, out, fibres):
    whole = fibres.shape[0]
    rows = pieces[0][1]
    main = rows // 16 * 16
    left = rows - main

    for place, block in zip(places, blocks):
        base = pl.multiple_of(place, 16)

        def one_row(i, _):
            at = pl.multiple_of(i * LANES, LANES)
            fibres[pl.ds(base, main), pl.ds(at, LANES)] = block[
                pl.ds(pl.multiple_of(i * main, 16), main), :
            ]
            return 0

        lax.fori_loop(0, share, one_row, 0, unroll=6)
        for group in range(0, share if left else 0, 4):
            count = min(4, share - group)
            at = share * main + group * left
            tile = block[at : at + count * left, :].astype(jnp.float32)
            for k in range(count):
                part = tile[k * left : (k + 1) * left, :]
                part = jnp.concatenate([part, jnp.zeros((16 - left, LANES), jnp.float32)], axis=0)
                fibres[
                    pl.ds(base + main, 16), (group + k) * LANES : (group + k + 1) * LANES
                ] = part.astype(jnp.bfloat16)

    at = 0
    for i, j in block_pairs(whole):
        product = lax.dot_general(
            fibres[i : i + STEP, :],
            fibres[j : j + STEP, :],
            (((1,), (1,)), ((), ())),
            preferred_element_type=jnp.float32,
        )
        if carried is not None:
            product = product + carried[at : at + STEP, :]
        out[at : at + STEP, :] = product
        at += STEP


def gram(straight, crossed, carried, sources, pieces, share):
    count = len(pieces)
    slow = len(straight[0])
    pitch = count * SUB
    whole = 2 * slow * pitch
    inputs = [block for piece in straight for block in piece]
    inputs += [block for piece in crossed for block in piece]
    size = inputs[0].shape[1]

    def body(sources, *rest):
        blocks, places = [], []
        refs = list(rest[: len(inputs)])
        for i in range(count):
            for dz in range(slow):
                blocks.append(refs.pop(0).at[0])
                places.append(sources[2 * dz] * pitch + i * SUB)
        for i in range(count):
            for j in range(slow // 2):
                ref = refs.pop(0)
                for k in range(2):
                    blocks.append(ref.at[k])
                    places.append(sources[2 * (2 * j + k) + 1] * pitch + i * SUB)
        if carried is None:
            out, fibres = rest[len(inputs) :]
            before = None
        else:
            before, out, fibres = rest[len(inputs) :]
        gram_kernel(pieces, share, places, blocks, before, out, fibres)

    half = pl.BlockSpec((1, size, LANES), lambda i: (0, 0, 0))
    both = pl.BlockSpec((2, size, LANES), lambda i: (0, 0, 0))
    shape = (len(block_pairs(whole)) * STEP, STEP)
    square = pl.BlockSpec(shape, lambda i: (0, 0))
    extra = [] if carried is None else [carried]
    return pl.pallas_call(
        body,
        grid=(1,),
        out_shape=jax.ShapeDtypeStruct(shape, jnp.float32),
        in_specs=[pl.BlockSpec(memory_space=pltpu.SMEM)]
        + [half] * (count * slow)
        + [both] * (count * slow // 2)
        + [square] * len(extra),
        out_specs=square,
        scratch_shapes=[pltpu.VMEM((whole, share * LANES), jnp.bfloat16)],
        compiler_params=pltpu.CompilerParams(vmem_limit_bytes=VMEM_BYTES),
        cost_estimate=pl.CostEstimate(flops=0, bytes_accessed=0, transcendentals=0),
        name="gram",
    )(sources, *inputs, *extra)


def slice_out(upper_r):
    row_block = upper_r.shape[0] // lax.axis_size("gy")
    col_block = upper_r.shape[1] // lax.axis_size("gx")
    return lax.dynamic_slice(
        upper_r,
        (lax.axis_index("gy") * row_block, lax.axis_index("gx") * col_block),
        (row_block, col_block),
    )


def finish(gram_sum, running_r):
    total = (
        jnp.dot(
            running_r.T,
            running_r,
            precision=lax.Precision.HIGHEST,
            preferred_element_type=jnp.float32,
        )
        + gram_sum
    )
    return slice_out(lax.linalg.cholesky(total.T, symmetrize_input=False).T)


def plain(fields, x_factor, running_r):
    exchanged = lax.all_to_all(fields, "gx", split_axis=2, concat_axis=0, tiled=True)
    full_x, middle, part_cells = exchanged.shape
    product = lax.dot_general(
        x_factor,
        exchanged.reshape(full_x, middle * part_cells),
        (((0,), (0,)), ((), ())),
        preferred_element_type=jnp.float32,
    )
    projected = product.astype(jnp.bfloat16).reshape(x_factor.shape[1], middle, part_cells)
    fibres = lax.all_to_all(projected, "gy", split_axis=2, concat_axis=1, tiled=True)
    local_gram = lax.dot_general(
        fibres, fibres, (((0, 2), (0, 2)), ((), ())), preferred_element_type=jnp.float32
    )
    return finish(lax.psum(local_gram, ("gx", "gy")), running_r)


def bit_of(axis, bit):
    return (lax.axis_index(axis) >> bit) & 1


def swap(value, axis, bit):
    flips = [(i, i ^ (1 << bit)) for i in range(lax.axis_size(axis))]
    return lax.ppermute(value, axis, flips)


def halve(value, axis, bit):
    halves = value.reshape(2, value.shape[0] // 2, value.shape[1])
    mine = bit_of(axis, bit)
    keep = lax.dynamic_index_in_dim(halves, mine, 0, keepdims=False)
    give = lax.dynamic_index_in_dim(halves, 1 - mine, 0, keepdims=False)
    return keep + swap(give, axis, bit)


def double(value, axis, bit):
    other = swap(value, axis, bit)
    return jnp.where(
        bit_of(axis, bit) == 0,
        jnp.concatenate([value, other]),
        jnp.concatenate([other, value]),
    )


def shift_slow(value, step, slow):
    n = slow * 2
    return lax.ppermute(value, "gy", [(i, (i + 2 * step) % n) for i in range(n)])


def sum_over_all(value):
    n_x, n_y = lax.axis_size("gx"), lax.axis_size("gy")
    bits = n_x.bit_length() - 1
    slow = n_y // 2
    mine = lax.axis_index("gy") // 2
    for bit in range(bits):
        value = halve(value, "gx", bit)
    value = halve(value, "gy", 0)
    rows, width = value.shape[0] // slow, value.shape[1]
    quarters = value.reshape(slow, rows, width)
    total = lax.dynamic_index_in_dim(quarters, mine, 0, keepdims=False)
    for step in range(1, slow):
        give = lax.dynamic_index_in_dim(quarters, (mine + step) % slow, 0, keepdims=False)
        total = total + shift_slow(give, step, slow)
    whole = jnp.zeros((slow, rows, width), value.dtype)
    whole = lax.dynamic_update_index_in_dim(whole, total, mine, 0)
    for step in range(1, slow):
        got = shift_slow(total, step, slow)
        whole = lax.dynamic_update_index_in_dim(whole, got, (mine + slow - step) % slow, 0)
    value = whole.reshape(slow * rows, width)
    value = double(value, "gy", 0)
    for bit in reversed(range(bits)):
        value = double(value, "gx", bit)
    return value


def pipelined(fields, x_factor, running_r):
    n_x, n_y = lax.axis_size("gx"), lax.axis_size("gy")
    me_x, me_y = lax.axis_index("gx"), lax.axis_index("gy")
    depth, rows, cells = fields.shape
    rank = x_factor.shape[1]
    share = rank // n_y
    cells_part = cells // n_x
    pieces = y_pieces(rows)
    by_y = jnp.transpose(fields, (1, 0, 2))

    factor = jnp.stack(
        [
            lax.dynamic_slice(x_factor, ((me_x ^ d) * depth, 0), (depth, rank)).T
            for d in range(n_x)
        ]
    )
    slow = n_y // 2
    shifts = [(dz, dy) for dz in range(slow) for dy in range(2)]

    def to(index, shift):
        return (index // 2 + shift[0]) % slow * 2 + (index % 2 + shift[1]) % 2

    def back(index, shift):
        return (index // 2 + slow - shift[0]) % slow * 2 + (index % 2 + shift[1]) % 2

    scalars = jnp.stack(
        [(me_x ^ d) * cells_part for d in range(n_x)] + [to(me_y, s) * share for s in shifts]
    ).astype(jnp.int32)
    sources = jnp.stack([back(me_y, s) for s in shifts]).astype(jnp.int32)

    chunks = [(cell, piece) for cell in range(0, cells_part, LANES) for piece in pieces]
    per_gram = len(pieces)

    flown = []

    def start(operand, axis, pairs):
        slots = range(max(0, len(flown) - 2 * WINDOW + 1), max(0, len(flown) - WINDOW + 1))
        if slots:
            operand, *passed = lax.optimization_barrier((operand, *[flown[i] for i in slots]))
            flown[slots.start : slots.stop] = passed
        flown.append(lax.ppermute(operand, axis, pairs))
        return len(flown) - 1

    def start_x(partner, send):
        return start(send, "gx", [(i, i ^ partner) for i in range(n_x)])

    def start_y(shift, send):
        return start(send, "gy", [(i, to(i, shift)) for i in range(n_y)])

    moving = []
    for index, chunk in enumerate(chunks[:AHEAD]):
        sends = pack(by_y, scalars, chunk, n_x)
        slots = []
        for (partner, _, _), send in zip(send_list(chunk, n_x), sends):
            slots.append(start_x(partner, send))
        moving.append(slots)
        if index == 0:
            near = [
                start_x(1, pack_near(by_y, scalars, cell)) for cell in range(0, cells_part, LANES)
            ]
    straight = []
    crossed = []
    carried = None

    def cross(k, j):
        pair = []
        for dz in (2 * j, 2 * j + 1):
            block = straight[k][dz]
            pair.append((flown[block] if isinstance(block, int) else block)[1])
        crossed[k][j] = start_y((0, 1), jnp.stack(pair))

    def add_gram(carried, first):
        group = range(first, first + per_gram)
        return gram(
            [[flown[b] if isinstance(b, int) else b for b in straight[k]] for k in group],
            [[flown[b] for b in crossed[k]] for k in group],
            carried,
            sources,
            pieces,
            share,
        )

    for k, chunk in enumerate(chunks):
        following = chunks[k + AHEAD] if k + AHEAD < len(chunks) else None
        after = []
        if k >= per_gram + 2 and (k - 2) % per_gram == 0:
            carried = add_gram(carried, k - 2 - per_gram)
            after.append(carried)
        outs, sends = project(
            by_y,
            flown[near[chunk[0] // LANES]],
            [flown[slot] for slot in moving[k]],
            factor,
            scalars,
            chunk,
            following,
            n_x,
            share,
            slow,
            after,
        )
        straight.append([outs[0]] + [None] * (slow - 1))
        crossed.append([None] * (slow // 2))
        steps = []
        for dz in range(1, slow):
            steps.append(((dz - 0.9) / (slow - 1), 0, dz))
        for j in range(slow // 2 if k else 0):
            steps.append(((j + 0.5) / (slow // 2), 1, j))
        slots = [None] * len(sends)
        for i in range(len(sends)):
            steps.append(((i + 0.3) / len(sends), 2, i))
        for _, kind, i in sorted(steps):
            if kind == 0:
                straight[k][i] = start_y((i, 0), outs[i])
            elif kind == 1:
                cross(k - 1, i)
            else:
                slots[i] = start_x(send_list(following, n_x)[i][0], sends[i])
        if sends:
            moving.append(slots)
    for j in range(slow // 2):
        cross(len(chunks) - 1, j)
    for first in range(0, len(chunks), per_gram):
        if first + per_gram + 2 >= len(chunks):
            carried = add_gram(carried, first)

    summed = sum_over_all(carried)
    count, size = len(pieces), pieces[0][1]
    whole = n_y * count * SUB
    blocks = {
        pair: summed[index * STEP : (index + 1) * STEP]
        for index, pair in enumerate(block_pairs(whole))
    }
    none = jnp.zeros((STEP, STEP), jnp.float32)
    starts = range(0, whole, STEP)
    upper = jnp.concatenate(
        [jnp.concatenate([blocks.get((i, j), none) for j in starts], axis=1) for i in starts]
    )
    gram_sum = upper.reshape(n_y * count, SUB, n_y * count, SUB)[:, :size, :, :size]
    return finish(gram_sum.reshape(n_y * rows, n_y * rows), running_r)


def on_device(fields, x_factor, running_r):
    n_x, n_y = lax.axis_size("gx"), lax.axis_size("gy")
    depth, rows, cells = fields.shape
    rank = x_factor.shape[1]
    fits = (
        cells % (n_x * LANES) == 0
        and rank % (2 * n_y) == 0
        and depth % 8 == 0
        and n_x & (n_x - 1) == 0
        and n_x >= 4
        and n_y % 4 == 0
        and rows >= 16
        and rows % (4 * len(y_pieces(rows))) == 0
        and n_y * pitch_of(rows) % STEP == 0
        and len(block_pairs(n_y * pitch_of(rows))) * STEP % (8 * n_x * n_y) == 0
    )
    if fits:
        return pipelined(fields, x_factor, running_r)
    return plain(fields, x_factor, running_r)


def solution(mesh):
    in_specs = (P("gx", "gy", None), P(), P())
    out_specs = P("gy", "gx")
    return jax.shard_map(
        on_device, mesh=mesh, in_specs=in_specs, out_specs=out_specs, check_vma=False
    )
```

time: 945 us -> 879 us (0.930)
  waiting for transfers between devices: 460 us -> 270 us
  starting transfers between devices: 132 us -> 233 us
    ppermute x90 -> x84, waiting for transfers between devices: 422 us -> 233 us  [start(): flown.append(lax.ppermute(operand, axis, pairs))]
    ppermute x90 -> x84, starting transfers between devices: 119 us -> 209 us  [start(): flown.append(lax.ppermute(operand, axis, pairs))]
    ppermute x6, starting transfers between devices: 8.39 us -> 20.2 us  [shift_slow(): lax.ppermute(value, 'gy', [(i, (i + 2 * step) % n) for i in range(n)])]
    pallas_call x6 -> x8, Pallas kernels: 54 us -> 61 us  [the longest x3 39.5 us: gram(): pl.pallas_call(body, grid=(1,), out_shape=jax.ShapeDtypeStruct(shape, jnp...]
  transfers between devices with their start and end apart: 102 -> 96, of which waited for: 56 -> 47; matrix products, arithmetic and copies ran while one was open for 1% -> 2% of each run, Pallas kernels for 14% -> 16%
where the time goes in v4:
time: 879 us; the launch traced here: 869 us
  waiting for transfers between devices  270 us (31%)
  starting transfers between devices  233 us (27%)
  Pallas kernels  160 us (18%)
  other arithmetic  135 us (15%)
  local copies, waits for them, and re-layouts  44.1 us (5%)
  matrix products  20.5 us (2%)
    ppermute x84, waiting for transfers between devices, start(): flown.append(lax.ppermute(operand, axis, pairs))  233 us
    ppermute x84, starting transfers between devices, start(): flown.append(lax.ppermute(operand, axis, pairs))  209 us
    another operation x22, other arithmetic, finish(): return slice_out(lax.linalg.cholesky(total.T, symmetrize_input=False).T)  117 us
    pallas_call x9, Pallas kernels, project(): pl.pallas_call(body, out_shape=shapes, in_specs=[pl.BlockSpec(memory_spac...  98.8 us
    pallas_call x3, Pallas kernels, gram(): pl.pallas_call(body, grid=(1,), out_shape=jax.ShapeDtypeStruct(shape, jnp...  39.5 us
    ppermute x6, waiting for transfers between devices, swap(): return lax.ppermute(value, axis, flips)  31.9 us
    pallas_call x5, Pallas kernels, run_pack(): pl.pallas_call(body, out_shape=shapes, in_specs=[pl.BlockSpec(memory_spac...  21.5 us
    ppermute x6, starting transfers between devices, shift_slow(): lax.ppermute(value, 'gy', [(i, (i + 2 * step) % n) for i in range(n)])  20.2 us
  transfers between devices with their start and end apart: 96, of which 47 were waited for; matrix products, arithmetic and copies ran while one was open for 2% of the time, Pallas kernels for 16%

profile of v4, /device:TPU:0, one launch (start us, length us, event | category | flops | bytes accessed | tf_op | source)
XLA Modules:
  0.0 868.9 jit_solution(6664006763932206222)
XLA Ops:
  39.9 10.6 %collective-permute-done.2.rest_2_ = bf16[14,168,128]{2,1,0:T(8,128)(2,1)S(1)} collective-permute-done((bf16[14,168,128]{2,1,0:T(8,128)(2,1)S(1)}, bf16[14,168,128]{2,1,0:T(8,128)(2,1)S(1)}, u32[]{:S(2)}, u32[]{:S(2)}) %collective-permute-start.2) | collective-permute-done | bytes 602144 | tf_op jit(solution)/shard_map/ppermute | solution.py:439
  69.2 11.1 %project.9 = (bf16[2,1176,128]{2,1,0:T(8,128)(2,1)}, bf16[2,1176,128]{2,1,0:T(8,128)(2,1)}, bf16[2,1176,128]{2,1,0:T(8,128)(2,1)}, bf16[2,1176,128]{2,1,0:T(8,12...) custom-call(s32[12]{0:T(128)} %stack.156.scalars, ...), custom_call_target="tpu_custom_call" | custom-call | tf_op jit(solution)/shard_map/project/pallas_call | solution.py:186
  90.7 11.5 %collective-permute-done.9.rest_2_ = bf16[14,168,128]{2,1,0:T(8,128)(2,1)} collective-permute-done((bf16[14,168,128]{2,1,0:T(8,128)(2,1)}, bf16[14,168,128]{2,1,0:T(8,128)(2,1)}, u32[]{:S(2)}, u32[]{:S(2)}) %collective-permute-start.9) | collective-permute-done | bytes 602144 | tf_op jit(solution)/shard_map/ppermute | solution.py:439
  128.0 11.4 %project.10 = (bf16[2,1176,128]{2,1,0:T(8,128)(2,1)}, bf16[2,1176,128]{2,1,0:T(8,128)(2,1)}, bf16[2,1176,128]{2,1,0:T(8,128)(2,1)}, bf16[2,1176,128]{2,1,0:T(8,1...) custom-call(s32[12]{0:T(128)} %stack.156.scalars, ...), custom_call_target="tpu_custom_call" | custom-call | tf_op jit(solution)/shard_map/project/pallas_call | solution.py:186
  143.0 10.8 %collective-permute-done.15.rest_2_ = bf16[14,168,128]{2,1,0:T(8,128)(2,1)} collective-permute-done((bf16[14,168,128]{2,1,0:T(8,128)(2,1)}, bf16[14,168,128]{2,1,0:T(8,128)(2,1)}, u32[]{:S(2)}, u32[]{:S(2)}) %collective-permute-start.15) | collective-permute-done | bytes 602144 | tf_op jit(solution)/shard_map/ppermute | solution.py:439
  169.2 10.3 %collective-permute-done.19.rest_0_ = bf16[14,168,128]{2,1,0:T(8,128)(2,1)S(1)} collective-permute-done((bf16[14,168,128]{2,1,0:T(8,128)(2,1)}, bf16[14,168,128]{2,1,0:T(8,128)(2,1)S(1)}, u32[]{:S(2)}, u32[]{:S(2)}) %collective-permute-start.19) | collective-permute-done | bytes 602144 | tf_op jit(solution)/shard_map/ppermute | solution.py:439
  194.8 11.1 %project.11 = (bf16[2,1176,128]{2,1,0:T(8,128)(2,1)}, bf16[2,1176,128]{2,1,0:T(8,128)(2,1)}, bf16[2,1176,128]{2,1,0:T(8,128)(2,1)}, bf16[2,1176,128]{2,1,0:T(8,1...) custom-call(s32[12]{0:T(128)} %stack.156.scalars, ...), custom_call_target="tpu_custom_call" | custom-call | tf_op jit(solution)/shard_map/project/pallas_call | solution.py:186
  245.7 11.1 %project.12 = (bf16[2,1176,128]{2,1,0:T(8,128)(2,1)}, bf16[2,1176,128]{2,1,0:T(8,128)(2,1)}, bf16[2,1176,128]{2,1,0:T(8,128)(2,1)}, bf16[2,1176,128]{2,1,0:T(8,1...) custom-call(s32[12]{0:T(128)} %stack.156.scalars, ...), custom_call_target="tpu_custom_call" | custom-call | tf_op jit(solution)/shard_map/project/pallas_call | solution.py:186
  297.3 11.1 %project.13 = (bf16[2,1176,128]{2,1,0:T(8,128)(2,1)}, bf16[2,1176,128]{2,1,0:T(8,128)(2,1)}, bf16[2,1176,128]{2,1,0:T(8,128)(2,1)}, bf16[2,1176,128]{2,1,0:T(8,1...) custom-call(s32[12]{0:T(128)} %stack.156.scalars, ...), custom_call_target="tpu_custom_call" | custom-call | tf_op jit(solution)/shard_map/project/pallas_call | solution.py:186
  321.7 11.4 %collective-permute-start.49 = (bf16[2,1176,128]{2,1,0:T(8,128)(2,1)}, bf16[2,1176,128]{2,1,0:T(8,128)(2,1)S(1)}, u32[]{:S(2)}, u32[]{:S(2)}) collective-permute-start(bf16[2,1176,128]{2,1,0:T(8,128)(2,1)} %get-tuple-element.849), channel_id=1, source_target_pairs={{0,4},{1,5},{2,6},{3,7},{4,0},{5,1},{6,2},{7,3},{8,12},{9,13},{10,... | collective-permute-start | bytes 1806344 | tf_op jit(solution)/shard_map/ppermute | solution.py:439
  350.0 12.8 %gram.3.rest_5_.rest_18_ = f32[1536,256]{1,0:T(8,128)} custom-call(s32[8]{0:T(128)} %stack.143.sources, bf16[2,1176,128]{2,1,0:T(8,128)(2,1)} %get-tuple-element.601.rest_0_, bf16[2,1176,128]{2,1,0:T(8,128)(2,1)} %copy-done.23, bf16[2,1176,128]{2,1,0:T(8,128)(2,1)} %copy-done.24, bf16[2,1176,128]{2,1,0:T(8,128)(2,1)} %copy-done.25, ...), custom_call_target="tpu_custom_call" | custom-call | tf_op jit(solution)/shard_map/gram/pallas_call | solution.py:286
  362.8 11.2 %project.14 = (bf16[2,1176,128]{2,1,0:T(8,128)(2,1)}, bf16[2,1176,128]{2,1,0:T(8,128)(2,1)}, bf16[2,1176,128]{2,1,0:T(8,128)(2,1)}, bf16[2,1176,128]{2,1,0:T(8,1...) custom-call(s32[12]{0:T(128)} %stack.156.scalars, ...), custom_call_target="tpu_custom_call" | custom-call | tf_op jit(solution)/shard_map/project/pallas_call | solution.py:186
  380.6 12.1 %collective-permute-done.54.rest_9_ = bf16[2,1176,128]{2,1,0:T(8,128)(2,1)S(1)} collective-permute-done((bf16[2,1176,128]{2,1,0:T(8,128)(2,1)}, bf16[2,1176,128]{2,1,0:T(8,128)(2,1)S(1)}, u32[]{:S(2)}, u32[]{:S(2)}) %collective-permute-start.54) | collective-permute-done | bytes 602144 | tf_op jit(solution)/shard_map/ppermute | solution.py:439
  405.9 11.0 %project.15 = (bf16[2,1176,128]{2,1,0:T(8,128)(2,1)}, bf16[2,1176,128]{2,1,0:T(8,128)(2,1)}, bf16[2,1176,128]{2,1,0:T(8,128)(2,1)}, bf16[2,1176,128]{2,1,0:T(8,1...) custom-call(s32[12]{0:T(128)} %stack.156.scalars, ...), custom_call_target="tpu_custom_call" | custom-call | tf_op jit(solution)/shard_map/project/pallas_call | solution.py:186
  417.0 14.4 %collective-permute-start.63 = (bf16[2,1176,128]{2,1,0:T(8,128)(2,1)}, bf16[2,1176,128]{2,1,0:T(8,128)(2,1)S(1)}, u32[]{:S(2)}, u32[]{:S(2)}) collective-permute-start(bf16[2,1176,128]{2,1,0:T(8,128)(2,1)} %get-tuple-element.942), channel_id=1, source_target_pairs={{0,2},{1,3},{2,4},{3,5},{4,6},{5,7},{6,0},{7,1},{8,10},{9,11},{10,... | collective-permute-start | bytes 1806344 | tf_op jit(solution)/shard_map/ppermute | solution.py:439
  462.8 10.3 %project.16 = (bf16[2,1176,128]{2,1,0:T(8,128)(2,1)}, bf16[2,1176,128]{2,1,0:T(8,128)(2,1)}, bf16[2,1176,128]{2,1,0:T(8,128)(2,1)}, bf16[2,1176,128]{2,1,0:T(8,128)(2,1)}) custom-call(s32[12]{0:T(128)} %stack.156.scalars, bf16[84,168,1536]{2,1,0:T(8,128)(2,1)} %bitcast.119, bf16[84,168,128]{2,1,0:T(8,128)(2,1)} %collective-permute-done.6.near, ...), custom_call_target="tpu_custom_call" | custom-call | tf_op jit(solution)/shard_map/project/pallas_call | solution.py:186
  475.1 13.9 %collective-permute-start.72 = (bf16[2,1176,128]{2,1,0:T(8,128)(2,1)}, bf16[2,1176,128]{2,1,0:T(8,128)(2,1)S(1)}, u32[]{:S(2)}, u32[]{:S(2)}) collective-permute-start(bf16[2,1176,128]{2,1,0:T(8,128)(2,1)} %get-tuple-element.1007), channel_id=1, source_target_pairs={{0,2},{1,3},{2,4},{3,5},{4,6},{5,7},{6,0},{7,1},{8,10},{9,11},{10,... | collective-permute-start | bytes 1806344 | tf_op jit(solution)/shard_map/ppermute | solution.py:439
  496.9 13.3 %gram.4.rest_5_.rest_18_ = f32[1536,256]{1,0:T(8,128)} custom-call(s32[8]{0:T(128)} %stack.143.sources, bf16[2,1176,128]{2,1,0:T(8,128)(2,1)} %get-tuple-element.789.rest_0_, bf16[2,1176,128]{2,1,0:T(8,128)(2,1)} %copy-done.3, bf16[2,1176,128]{2,1,0:T(8,128)(2,1)} %copy-done.4, bf16[2,1176,128]{2,1,0:T(8,128)(2,1)} %collective-permute-done.42.rest_3_, ...), custom_call_target="tpu_custom_call" | custom-call | tf_op jit(solution)/shard_map/gram/pallas_call | solution.py:286
  510.3 10.5 %project.17 = (bf16[2,1176,128]{2,1,0:T(8,128)(2,1)}, bf16[2,1176,128]{2,1,0:T(8,128)(2,1)}, bf16[2,1176,128]{2,1,0:T(8,128)(2,1)}, bf16[2,1176,128]{2,1,0:T(8,128)(2,1)}) custom-call(s32[12]{0:T(128)} %stack.156.scalars, bf16[84,168,1536]{2,1,0:T(8,128)(2,1)} %bitcast.120, bf16[84,168,128]{2,1,0:T(8,128)(2,1)} %collective-permute-done.6.near, ...), custom_call_target="tpu_custom_call" | custom-call | tf_op jit(solution)/shard_map/project/pallas_call | solution.py:186
  520.7 10.6 %collective-permute-start.79 = (bf16[2,1176,128]{2,1,0:T(8,128)(2,1)}, bf16[2,1176,128]{2,1,0:T(8,128)(2,1)S(1)}, u32[]{:S(2)}, u32[]{:S(2)}) collective-permute-start(bf16[2,1176,128]{2,1,0:T(8,128)(2,1)} %get-tuple-element.1030), channel_id=1, source_target_pairs={{0,2},{1,3},{2,4},{3,5},{4,6},{5,7},{6,0},{7,1},{8,10},{9,11},{10,... | collective-permute-start | bytes 1806344 | tf_op jit(solution)/shard_map/ppermute | solution.py:439
  534.2 25.9 %collective-permute-start.78 = (bf16[2,1176,128]{2,1,0:T(8,128)(2,1)}, bf16[2,1176,128]{2,1,0:T(8,128)(2,1)S(1)}, u32[]{:S(2)}, u32[]{:S(2)}) collective-permute-start(bf16[2,1176,128]{2,1,0:T(8,128)(2,1)} %get-tuple-element.1028), channel_id=1, source_target_pairs={{0,6},{1,7},{2,0},{3,1},{4,2},{5,3},{6,4},{7,5},{8,14},{9,15},{10,... | collective-permute-start | bytes 1806344 | tf_op jit(solution)/shard_map/ppermute | solution.py:439
  566.1 17.6 %collective-permute-done.77.rest_10_ = bf16[2,1176,128]{2,1,0:T(8,128)(2,1)S(1)} collective-permute-done((bf16[2,1176,128]{2,1,0:T(8,128)(2,1)}, bf16[2,1176,128]{2,1,0:T(8,128)(2,1)S(1)}, u32[]{:S(2)}, u32[]{:S(2)}) %collective-permute-start.77) | collective-permute-done | bytes 602144 | tf_op jit(solution)/shard_map/ppermute | solution.py:439
  590.7 12.9 %collective-permute-done.81.rest_15_ = bf16[2,1176,128]{2,1,0:T(8,128)(2,1)S(1)} collective-permute-done((bf16[2,1176,128]{2,1,0:T(8,128)(2,1)}, bf16[2,1176,128]{2,1,0:T(8,128)(2,1)S(1)}, u32[]{:S(2)}, u32[]{:S(2)}) %collective-permute-start.81) | collective-permute-done | bytes 602144 | tf_op jit(solution)/shard_map/ppermute | solution.py:439
  603.6 10.3 %collective-permute-done.83.rest_17_ = bf16[2,1176,128]{2,1,0:T(8,128)(2,1)} collective-permute-done((bf16[2,1176,128]{2,1,0:T(8,128)(2,1)}, bf16[2,1176,128]{2,1,0:T(8,128)(2,1)}, u32[]{:S(2)}, u32[]{:S(2)}) %collective-permute-start.83) | collective-permute-done | bytes 602144 | tf_op jit(solution)/shard_map/ppermute | solution.py:439
  613.9 13.3 %gram.5 = f32[1536,256]{1,0:T(8,128)} custom-call(s32[8]{0:T(128)} %stack.143.sources, bf16[2,1176,128]{2,1,0:T(8,128)(2,1)} %get-tuple-element.903.rest_0_, bf16[2,1176,128]{2,1,0:T(8,128)(2,1)} %copy-done.9, bf16[2,1176,128]{2,1,0:T(8,128)(2,1)} %copy-done.12, bf16[2,1176,128]{2,1,0:T(8,128)(2,1)} %copy-done.13, ...), custom_call_target="tpu_custom_call" | custom-call | tf_op jit(solution)/shard_map/gram/pallas_call | solution.py:286
  632.5 11.2 %collective-permute-done.85 = f32[384,256]{1,0:T(8,128)} collective-permute-done((f32[384,256]{1,0:T(8,128)S(1)}, f32[384,256]{1,0:T(8,128)}, u32[]{:S(2)}, u32[]{:S(2)}) %collective-permute-start.85) | collective-permute-done | bytes 393248 | tf_op jit(solution)/shard_map/ppermute | solution.py:348
  651.1 10.6 %collective-permute-start.87 = (f32[48,256]{1,0:T(8,128)S(1)}, f32[48,256]{1,0:T(8,128)S(1)}, u32[]{:S(2)}, u32[]{:S(2)}) collective-permute-start(f32[48,256]{1,0:T(8,128)S(1)} %get-tuple-element.1061), channel_id=1, source_target_pairs={{0,2},{1,3},{2,4},{3,5},{4,6},{5,7},{6,0},{7,1},{8,10},{9,11},{10,... | collective-permute-start | bytes 147464 | tf_op jit(solution)/shard_map/ppermute | solution.py:370
  730.7 11.7 %cholesky.166 = f32[128,128]{1,0:T(8,128)S(1)} custom-call(f32[128,128]{1,0:T(8,128)S(1)} %cholesky.430), custom_call_target="Cholesky" | custom-call | tf_op jit(solution)/shard_map/cholesky | solution.py:322
  757.4 11.7 %cholesky.189 = f32[128,128]{1,0:T(8,128)S(1)} custom-call(f32[128,128]{1,0:T(8,128)S(1)} %cholesky.434), custom_call_target="Cholesky" | custom-call | tf_op jit(solution)/shard_map/cholesky | solution.py:322
  782.2 11.7 %cholesky.356 = f32[128,128]{1,0:T(8,128)S(1)} custom-call(f32[128,128]{1,0:T(8,128)S(1)} %cholesky.439), custom_call_target="Cholesky" | custom-call | tf_op jit(solution)/shard_map/cholesky | solution.py:322
  807.9 11.7 %cholesky.375 = f32[128,128]{1,0:T(8,128)S(1)} custom-call(f32[128,128]{1,0:T(8,128)S(1)} %cholesky.444), custom_call_target="Cholesky" | custom-call | tf_op jit(solution)/shard_map/cholesky | solution.py:322
  833.1 11.9 %cholesky.394 = f32[128,128]{1,0:T(8,128)S(1)} custom-call(f32[128,128]{1,0:T(8,128)S(1)} %cholesky.449), custom_call_target="Cholesky" | custom-call | tf_op jit(solution)/shard_map/cholesky | solution.py:322
  (454 shorter events, 471.7 us)
Async XLA Ops:
  12.0 52.7 %collective-permute-start.4 = (bf16[84,168,128]{2,1,0:T(8,128)(2,1)}, bf16[84,168,128]{2,1,0:T(8,128)(2,1)}, u32[]{:S(2)}, u32[]{:S(2)}) collective-permute-start(bf16[84,168,128]{2,1,0:T(8,128)(2,1)} %pack.9), channel_id=1, source_target_pairs={{0,8},{8,0},{16,24},{24,16},{1,9},{9,1},{17,25},{25,17},{2,10},{10... | collective-permute-start | bytes 10838024 | tf_op jit(solution)/shard_map/ppermute | solution.py:439
  22.2 45.9 %collective-permute-start.5 = (bf16[84,168,128]{2,1,0:T(8,128)(2,1)}, bf16[84,168,128]{2,1,0:T(8,128)(2,1)}, u32[]{:S(2)}, u32[]{:S(2)}) collective-permute-start(bf16[84,168,128]{2,1,0:T(8,128)(2,1)} %pack.7), channel_id=1, source_target_pairs={{0,8},{8,0},{16,24},{24,16},{1,9},{9,1},{17,25},{25,17},{2,10},{10... | collective-permute-start | bytes 10838024 | tf_op jit(solution)/shard_map/ppermute | solution.py:439
  33.6 46.7 %collective-permute-start.6 = (bf16[84,168,128]{2,1,0:T(8,128)(2,1)}, bf16[84,168,128]{2,1,0:T(8,128)(2,1)}, u32[]{:S(2)}, u32[]{:S(2)}) collective-permute-start(bf16[84,168,128]{2,1,0:T(8,128)(2,1)} %pack.6), channel_id=1, source_target_pairs={{0,8},{8,0},{16,24},{24,16},{1,9},{9,1},{17,25},{25,17},{2,10},{10... | collective-permute-start | bytes 10838024 | tf_op jit(solution)/shard_map/ppermute | solution.py:439
  68.1 46.3 %collective-permute-start.10 = (bf16[14,168,128]{2,1,0:T(8,128)(2,1)}, bf16[14,168,128]{2,1,0:T(8,128)(2,1)S(1)}, u32[]{:S(2)}, u32[]{:S(2)}) collective-permute-start(bf16[14,168,128]{2,1,0:T(8,128)(2,1)} %get-tuple-element.580), channel_id=1, source_target_pairs={{0,24},{8,16},{16,8},{24,0},{1,25},{9,17},{17,9},{25,1},{2,26},{10... | collective-permute-start | bytes 1806344 | tf_op jit(solution)/shard_map/ppermute | solution.py:439
  82.2 45.7 %collective-permute-start.12 = (bf16[14,168,128]{2,1,0:T(8,128)(2,1)}, bf16[14,168,128]{2,1,0:T(8,128)(2,1)S(1)}, u32[]{:S(2)}, u32[]{:S(2)}) collective-permute-start(bf16[14,168,128]{2,1,0:T(8,128)(2,1)} %get-tuple-element.596), channel_id=1, source_target_pairs={{0,16},{8,24},{16,0},{24,8},{1,17},{9,25},{17,1},{25,9},{2,18},{10... | collective-permute-start | bytes 1806344 | tf_op jit(solution)/shard_map/ppermute | solution.py:439
  88.6 51.6 %collective-permute-start.13 = (bf16[14,168,128]{2,1,0:T(8,128)(2,1)}, bf16[14,168,128]{2,1,0:T(8,128)(2,1)S(1)}, u32[]{:S(2)}, u32[]{:S(2)}) collective-permute-start(bf16[14,168,128]{2,1,0:T(8,128)(2,1)} %get-tuple-element.606), channel_id=1, source_target_pairs={{0,24},{8,16},{16,8},{24,0},{1,25},{9,17},{17,9},{25,1},{2,26},{10... | collective-permute-start | bytes 1806344 | tf_op jit(solution)/shard_map/ppermute | solution.py:439
  102.3 39.5 %collective-permute-start.14 = (bf16[2,1176,128]{2,1,0:T(8,128)(2,1)}, bf16[2,1176,128]{2,1,0:T(8,128)(2,1)S(1)}, u32[]{:S(2)}, u32[]{:S(2)}) collective-permute-start(bf16[2,1176,128]{2,1,0:T(8,128)(2,1)} %get-tuple-element.610), channel_id=1, source_target_pairs={{0,4},{1,5},{2,6},{3,7},{4,0},{5,1},{6,2},{7,3},{8,12},{9,13},{10,... | collective-permute-start | bytes 1806344 | tf_op jit(solution)/shard_map/ppermute | solution.py:439
  114.4 39.4 %collective-permute-start.15 = (bf16[14,168,128]{2,1,0:T(8,128)(2,1)}, bf16[14,168,128]{2,1,0:T(8,128)(2,1)}, u32[]{:S(2)}, u32[]{:S(2)}) collective-permute-start(bf16[14,168,128]{2,1,0:T(8,128)(2,1)} %get-tuple-element.615), channel_id=1, source_target_pairs={{0,16},{8,24},{16,0},{24,8},{1,17},{9,25},{17,1},{25,9},{2,18},{10... | collective-permute-start | bytes 1806344 | tf_op jit(solution)/shard_map/ppermute | solution.py:439
  115.0 40.6 %collective-permute-start.16 = (bf16[2,1176,128]{2,1,0:T(8,128)(2,1)}, bf16[2,1176,128]{2,1,0:T(8,128)(2,1)S(1)}, u32[]{:S(2)}, u32[]{:S(2)}) collective-permute-start(bf16[2,1176,128]{2,1,0:T(8,128)(2,1)} %get-tuple-element.620), channel_id=1, source_target_pairs={{0,6},{1,7},{2,0},{3,1},{4,2},{5,3},{6,4},{7,5},{8,14},{9,15},{10,... | collective-permute-start | bytes 1806344 | tf_op jit(solution)/shard_map/ppermute | solution.py:439
  128.0 38.1 %collective-permute-start.17 = (bf16[14,168,128]{2,1,0:T(8,128)(2,1)}, bf16[14,168,128]{2,1,0:T(8,128)(2,1)S(1)}, u32[]{:S(2)}, u32[]{:S(2)}) collective-permute-start(bf16[14,168,128]{2,1,0:T(8,128)(2,1)} %get-tuple-element.627), channel_id=1, source_target_pairs={{0,24},{8,16},{16,8},{24,0},{1,25},{9,17},{17,9},{25,1},{2,26},{10... | collective-permute-start | bytes 1806344 | tf_op jit(solution)/shard_map/ppermute | solution.py:439
  166.0 39.8 %collective-permute-start.22 = (bf16[2,1176,128]{2,1,0:T(8,128)(2,1)}, bf16[2,1176,128]{2,1,0:T(8,128)(2,1)S(1)}, u32[]{:S(2)}, u32[]{:S(2)}) collective-permute-start(bf16[2,1176,128]{2,1,0:T(8,128)(2,1)} %get-tuple-element.661), channel_id=1, source_target_pairs={{0,4},{1,5},{2,6},{3,7},{4,0},{5,1},{6,2},{7,3},{8,12},{9,13},{10,... | collective-permute-start | bytes 1806344 | tf_op jit(solution)/shard_map/ppermute | solution.py:439
  168.6 41.6 %collective-permute-start.23 = (bf16[14,168,128]{2,1,0:T(8,128)(2,1)}, bf16[14,168,128]{2,1,0:T(8,128)(2,1)}, u32[]{:S(2)}, u32[]{:S(2)}) collective-permute-start(bf16[14,168,128]{2,1,0:T(8,128)(2,1)} %get-tuple-element.666), channel_id=1, source_target_pairs={{0,16},{8,24},{16,0},{24,8},{1,17},{9,25},{17,1},{25,9},{2,18},{10... | collective-permute-start | bytes 1806344 | tf_op jit(solution)/shard_map/ppermute | solution.py:439
  217.6 39.2 %collective-permute-start.31 = (bf16[2,1176,128]{2,1,0:T(8,128)(2,1)}, bf16[2,1176,128]{2,1,0:T(8,128)(2,1)S(1)}, u32[]{:S(2)}, u32[]{:S(2)}) collective-permute-start(bf16[2,1176,128]{2,1,0:T(8,128)(2,1)} %get-tuple-element.721), channel_id=1, source_target_pairs={{0,4},{1,5},{2,6},{3,7},{4,0},{5,1},{6,2},{7,3},{8,12},{9,13},{10,... | collective-permute-start | bytes 1806344 | tf_op jit(solution)/shard_map/ppermute | solution.py:439
  269.3 39.1 %collective-permute-start.40 = (bf16[2,1176,128]{2,1,0:T(8,128)(2,1)}, bf16[2,1176,128]{2,1,0:T(8,128)(2,1)S(1)}, u32[]{:S(2)}, u32[]{:S(2)}) collective-permute-start(bf16[2,1176,128]{2,1,0:T(8,128)(2,1)} %get-tuple-element.781), channel_id=1, source_target_pairs={{0,4},{1,5},{2,6},{3,7},{4,0},{5,1},{6,2},{7,3},{8,12},{9,13},{10,... | collective-permute-start | bytes 1806344 | tf_op jit(solution)/shard_map/ppermute | solution.py:439
  321.7 52.3 %collective-permute-start.49 = (bf16[2,1176,128]{2,1,0:T(8,128)(2,1)}, bf16[2,1176,128]{2,1,0:T(8,128)(2,1)S(1)}, u32[]{:S(2)}, u32[]{:S(2)}) collective-permute-start(bf16[2,1176,128]{2,1,0:T(8,128)(2,1)} %get-tuple-element.849), channel_id=1, source_target_pairs={{0,4},{1,5},{2,6},{3,7},{4,0},{5,1},{6,2},{7,3},{8,12},{9,13},{10,... | collective-permute-start | bytes 1806344 | tf_op jit(solution)/shard_map/ppermute | solution.py:439
  333.1 42.5 %collective-permute-start.50 = (bf16[14,168,128]{2,1,0:T(8,128)(2,1)}, bf16[14,168,128]{2,1,0:T(8,128)(2,1)}, u32[]{:S(2)}, u32[]{:S(2)}) collective-permute-start(bf16[14,168,128]{2,1,0:T(8,128)(2,1)} %get-tuple-element.854), channel_id=1, source_target_pairs={{0,16},{8,24},{16,0},{24,8},{1,17},{9,25},{17,1},{25,9},{2,18},{10... | collective-permute-start | bytes 1806344 | tf_op jit(solution)/shard_map/ppermute | solution.py:439
  335.6 41.2 %collective-permute-start.51 = (bf16[2,1176,128]{2,1,0:T(8,128)(2,1)S(1)}, bf16[2,1176,128]{2,1,0:T(8,128)(2,1)S(1)}, u32[]{:S(2)}, u32[]{:S(2)}) collective-permute-start(bf16[2,1176,128]{2,1,0:T(8,128)(2,1)S(1)} %copy-done.68), channel_id=1, source_target_pairs={{0,6},{1,7},{2,0},{3,1},{4,2},{5,3},{6,4},{7,5},{8,14},{9,15},{10,... | collective-permute-start | bytes 1806344 | tf_op jit(solution)/shard_map/ppermute | solution.py:439
  378.3 38.6 %collective-permute-start.58 = (bf16[2,1176,128]{2,1,0:T(8,128)(2,1)}, bf16[2,1176,128]{2,1,0:T(8,128)(2,1)S(1)}, u32[]{:S(2)}, u32[]{:S(2)}) collective-permute-start(bf16[2,1176,128]{2,1,0:T(8,128)(2,1)} %get-tuple-element.910), channel_id=1, source_target_pairs={{0,4},{1,5},{2,6},{3,7},{4,0},{5,1},{6,2},{7,3},{8,12},{9,13},{10,... | collective-permute-start | bytes 1806344 | tf_op jit(solution)/shard_map/ppermute | solution.py:439
  392.7 38.7 %collective-permute-start.59 = (bf16[14,168,128]{2,1,0:T(8,128)(2,1)}, bf16[14,168,128]{2,1,0:T(8,128)(2,1)}, u32[]{:S(2)}, u32[]{:S(2)}) collective-permute-start(bf16[14,168,128]{2,1,0:T(8,128)(2,1)} %get-tuple-element.915), channel_id=1, source_target_pairs={{0,16},{8,24},{16,0},{24,8},{1,17},{9,25},{17,1},{25,9},{2,18},{10... | collective-permute-start | bytes 1806344 | tf_op jit(solution)/shard_map/ppermute | solution.py:439
  393.2 40.3 %collective-permute-start.60 = (bf16[2,1176,128]{2,1,0:T(8,128)(2,1)}, bf16[2,1176,128]{2,1,0:T(8,128)(2,1)S(1)}, u32[]{:S(2)}, u32[]{:S(2)}) collective-permute-start(bf16[2,1176,128]{2,1,0:T(8,128)(2,1)} %get-tuple-element.924), channel_id=1, source_target_pairs={{0,6},{1,7},{2,0},{3,1},{4,2},{5,3},{6,4},{7,5},{8,14},{9,15},{10,... | collective-permute-start | bytes 1806344 | tf_op jit(solution)/shard_map/ppermute | solution.py:439
  395.8 39.0 %collective-permute-start.61 = (bf16[2,1176,128]{2,1,0:T(8,128)(2,1)}, bf16[2,1176,128]{2,1,0:T(8,128)(2,1)}, u32[]{:S(2)}, u32[]{:S(2)}) collective-permute-start(bf16[2,1176,128]{2,1,0:T(8,128)(2,1)} %pad_maximum_fusion.10), channel_id=1, source_target_pairs={{0,1},{1,0},{2,3},{3,2},{4,5},{5,4},{6,7},{7,6},{8,9},{9,8},{10,11... | collective-permute-start | bytes 1806344 | tf_op jit(solution)/shard_map/ppermute | solution.py:439
  435.7 39.3 %collective-permute-start.67 = (bf16[2,1176,128]{2,1,0:T(8,128)(2,1)}, bf16[2,1176,128]{2,1,0:T(8,128)(2,1)S(1)}, u32[]{:S(2)}, u32[]{:S(2)}) collective-permute-start(bf16[2,1176,128]{2,1,0:T(8,128)(2,1)} %get-tuple-element.969), channel_id=1, source_target_pairs={{0,4},{1,5},{2,6},{3,7},{4,0},{5,1},{6,2},{7,3},{8,12},{9,13},{10,... | collective-permute-start | bytes 1806344 | tf_op jit(solution)/shard_map/ppermute | solution.py:439
  448.1 41.0 %collective-permute-start.68 = (bf16[14,168,128]{2,1,0:T(8,128)(2,1)}, bf16[14,168,128]{2,1,0:T(8,128)(2,1)}, u32[]{:S(2)}, u32[]{:S(2)}) collective-permute-start(bf16[14,168,128]{2,1,0:T(8,128)(2,1)} %get-tuple-element.977), channel_id=1, source_target_pairs={{0,16},{8,24},{16,0},{24,8},{1,17},{9,25},{17,1},{25,9},{2,18},{10... | collective-permute-start | bytes 1806344 | tf_op jit(solution)/shard_map/ppermute | solution.py:439
  454.5 39.3 %collective-permute-start.70 = (bf16[2,1176,128]{2,1,0:T(8,128)(2,1)}, bf16[2,1176,128]{2,1,0:T(8,128)(2,1)}, u32[]{:S(2)}, u32[]{:S(2)}) collective-permute-start(bf16[2,1176,128]{2,1,0:T(8,128)(2,1)} %pad_maximum_fusion.12), channel_id=1, source_target_pairs={{0,1},{1,0},{2,3},{3,2},{4,5},{5,4},{6,7},{7,6},{8,9},{9,8},{10,11... | collective-permute-start | bytes 1806344 | tf_op jit(solution)/shard_map/ppermute | solution.py:439
  475.1 45.7 %collective-permute-start.72 = (bf16[2,1176,128]{2,1,0:T(8,128)(2,1)}, bf16[2,1176,128]{2,1,0:T(8,128)(2,1)S(1)}, u32[]{:S(2)}, u32[]{:S(2)}) collective-permute-start(bf16[2,1176,128]{2,1,0:T(8,128)(2,1)} %get-tuple-element.1007), channel_id=1, source_target_pairs={{0,2},{1,3},{2,4},{3,5},{4,6},{5,7},{6,0},{7,1},{8,10},{9,11},{10,... | collective-permute-start | bytes 1806344 | tf_op jit(solution)/shard_map/ppermute | solution.py:439
  489.3 43.1 %collective-permute-start.73 = (bf16[2,1176,128]{2,1,0:T(8,128)(2,1)S(1)}, bf16[2,1176,128]{2,1,0:T(8,128)(2,1)S(1)}, u32[]{:S(2)}, u32[]{:S(2)}) collective-permute-start(bf16[2,1176,128]{2,1,0:T(8,128)(2,1)S(1)} %pad_maximum_fusion.13), channel_id=1, source_target_pairs={{0,1},{1,0},{2,3},{3,2},{4,5},{5,4},{6,7},{7,6},{8,9},{9,8},{10,11... | collective-permute-start | bytes 1806344 | tf_op jit(solution)/shard_map/ppermute | solution.py:439
  490.4 42.3 %collective-permute-start.74 = (bf16[2,1176,128]{2,1,0:T(8,128)(2,1)}, bf16[2,1176,128]{2,1,0:T(8,128)(2,1)S(1)}, u32[]{:S(2)}, u32[]{:S(2)}) collective-permute-start(bf16[2,1176,128]{2,1,0:T(8,128)(2,1)} %get-tuple-element.1016), channel_id=1, source_target_pairs={{0,4},{1,5},{2,6},{3,7},{4,0},{5,1},{6,2},{7,3},{8,12},{9,13},{10,... | collective-permute-start | bytes 1806344 | tf_op jit(solution)/shard_map/ppermute | solution.py:439
  493.8 40.5 %collective-permute-start.75 = (bf16[2,1176,128]{2,1,0:T(8,128)(2,1)}, bf16[2,1176,128]{2,1,0:T(8,128)(2,1)S(1)}, u32[]{:S(2)}, u32[]{:S(2)}) collective-permute-start(bf16[2,1176,128]{2,1,0:T(8,128)(2,1)} %get-tuple-element.1020), channel_id=1, source_target_pairs={{0,6},{1,7},{2,0},{3,1},{4,2},{5,3},{6,4},{7,5},{8,14},{9,15},{10,... | collective-permute-start | bytes 1806344 | tf_op jit(solution)/shard_map/ppermute | solution.py:439
  520.7 42.3 %collective-permute-start.79 = (bf16[2,1176,128]{2,1,0:T(8,128)(2,1)}, bf16[2,1176,128]{2,1,0:T(8,128)(2,1)S(1)}, u32[]{:S(2)}, u32[]{:S(2)}) collective-permute-start(bf16[2,1176,128]{2,1,0:T(8,128)(2,1)} %get-tuple-element.1030), channel_id=1, source_target_pairs={{0,2},{1,3},{2,4},{3,5},{4,6},{5,7},{6,0},{7,1},{8,10},{9,11},{10,... | collective-permute-start | bytes 1806344 | tf_op jit(solution)/shard_map/ppermute | solution.py:439
  532.7 51.0 %collective-permute-start.77 = (bf16[2,1176,128]{2,1,0:T(8,128)(2,1)}, bf16[2,1176,128]{2,1,0:T(8,128)(2,1)S(1)}, u32[]{:S(2)}, u32[]{:S(2)}) collective-permute-start(bf16[2,1176,128]{2,1,0:T(8,128)(2,1)} %get-tuple-element.1027), channel_id=1, source_target_pairs={{0,4},{1,5},{2,6},{3,7},{4,0},{5,1},{6,2},{7,3},{8,12},{9,13},{10,... | collective-permute-start | bytes 1806344 | tf_op jit(solution)/shard_map/ppermute | solution.py:439
  534.2 49.8 %collective-permute-start.78 = (bf16[2,1176,128]{2,1,0:T(8,128)(2,1)}, bf16[2,1176,128]{2,1,0:T(8,128)(2,1)S(1)}, u32[]{:S(2)}, u32[]{:S(2)}) collective-permute-start(bf16[2,1176,128]{2,1,0:T(8,128)(2,1)} %get-tuple-element.1028), channel_id=1, source_target_pairs={{0,6},{1,7},{2,0},{3,1},{4,2},{5,3},{6,4},{7,5},{8,14},{9,15},{10,... | collective-permute-start | bytes 1806344 | tf_op jit(solution)/shard_map/ppermute | solution.py:439
  565.3 38.3 %collective-permute-start.81 = (bf16[2,1176,128]{2,1,0:T(8,128)(2,1)}, bf16[2,1176,128]{2,1,0:T(8,128)(2,1)S(1)}, u32[]{:S(2)}, u32[]{:S(2)}) collective-permute-start(bf16[2,1176,128]{2,1,0:T(8,128)(2,1)} %pad_maximum_fusion.16), channel_id=1, source_target_pairs={{0,1},{1,0},{2,3},{3,2},{4,5},{5,4},{6,7},{7,6},{8,9},{9,8},{10,11... | collective-permute-start | bytes 1806344 | tf_op jit(solution)/shard_map/ppermute | solution.py:439
  (141 other events, 3638.0 us)

commit v5 on v4

--- a/solution.py
+++ b/solution.py
@@ -136,8 +136,8 @@
 
     main = rows // 16 * 16
     left = rows - main
-    for part in range(2 * len(outs)):
-        out = outs[part // 2].at[part % 2]
+    halves = [out.at[i] for out in outs for i in range(out.shape[0])]
+    for part, out in enumerate(halves):
         first = scalars[n_x + part]
 
         def one_row(i, _):
@@ -159,13 +159,14 @@
         copy.wait()
 
 
-def project(fields, near, got, factor, scalars, chunk, following, n_x, share, slow, after):
+def project(fields, near, got, factor, scalars, chunk, following, n_x, share, slow, apart, after):
     rows = chunk[1][1]
     rank = factor.shape[1]
     depth = fields.shape[1]
     n_got = len(got)
     n_sends = 0 if following is None else n_got
     n_after = len(after)
+    n_outs = 2 * slow if apart else slow
     vmem = pl.BlockSpec(memory_space=pltpu.VMEM)
     any_space = pl.BlockSpec(memory_space=pl.ANY)
 
@@ -173,14 +174,15 @@
         got = rest[:n_got]
         factor = rest[n_got]
         rest = rest[n_got + 1 + n_after :]
-        outs = rest[:slow]
-        sends = rest[slow : slow + n_sends]
-        own, other, wide, sems = rest[slow + n_sends :]
+        outs = rest[:n_outs]
+        sends = rest[n_outs : n_outs + n_sends]
+        own, other, wide, sems = rest[n_outs + n_sends :]
         project_kernel(
             chunk, following, n_x, rank, share, scalars, fields, near, got, factor, outs, sends, own, other, wide, sems
         )
 
-    shapes = [jax.ShapeDtypeStruct((2, share * rows, LANES), jnp.bfloat16)] * slow
+    shape = (1 if apart else 2, share * rows, LANES)
+    shapes = [jax.ShapeDtypeStruct(shape, jnp.bfloat16)] * n_outs
     if following is not None:
         shapes += send_shapes(following, n_x, depth)
     outs = pl.pallas_call(
@@ -189,7 +191,7 @@
         in_specs=[pl.BlockSpec(memory_space=pltpu.SMEM), any_space, any_space]
         + [vmem] * (n_got + 1)
         + [any_space] * n_after,
-        out_specs=[vmem] * (slow + n_sends),
+        out_specs=[vmem] * (n_outs + n_sends),
         scratch_shapes=[
             pltpu.VMEM((rows, depth, LANES), jnp.bfloat16),
             pltpu.VMEM((rows, depth, LANES), jnp.bfloat16),
@@ -200,7 +202,7 @@
         cost_estimate=pl.CostEstimate(flops=0, bytes_accessed=0, transcendentals=0),
         name="project",
     )(scalars, fields, near, *got, factor, *after)
-    return outs[:slow], outs[slow:]
+    return outs[:n_outs], outs[n_outs:]
 
 
 def block_pairs(whole):
@@ -249,37 +251,29 @@
         at += STEP
 
 
-def gram(straight, crossed, carried, sources, pieces, share):
-    count = len(pieces)
-    slow = len(straight[0])
-    pitch = count * SUB
-    whole = 2 * slow * pitch
-    inputs = [block for piece in straight for block in piece]
-    inputs += [block for piece in crossed for block in piece]
+def gram(arrivals, carried, sources, pieces, share):
+    pitch = len(pieces) * SUB
+    whole = sources.shape[0] * pitch
+    entries = [(i, places) for i, piece in enumerate(arrivals) for _, places in piece]
+    inputs = [block for piece in arrivals for block, _ in piece]
     size = inputs[0].shape[1]
 
     def body(sources, *rest):
-        blocks, places = [], []
-        refs = list(rest[: len(inputs)])
-        for i in range(count):
-            for dz in range(slow):
-                blocks.append(refs.pop(0).at[0])
-                places.append(sources[2 * dz] * pitch + i * SUB)
-        for i in range(count):
-            for j in range(slow // 2):
-                ref = refs.pop(0)
-                for k in range(2):
-                    blocks.append(ref.at[k])
-                    places.append(sources[2 * (2 * j + k) + 1] * pitch + i * SUB)
+        blocks, starts = [], []
+        for ref, (i, places) in zip(rest, entries):
+            for k, (dz, dy) in enumerate(places):
+                blocks.append(ref.at[k])
+                starts.append(sources[2 * dz + dy] * pitch + i * SUB)
         if carried is None:
             out, fibres = rest[len(inputs) :]
             before = None
         else:
             before, out, fibres = rest[len(inputs) :]
-        gram_kernel(pieces, share, places, blocks, before, out, fibres)
-
-    half = pl.BlockSpec((1, size, LANES), lambda i: (0, 0, 0))
-    both = pl.BlockSpec((2, size, LANES), lambda i: (0, 0, 0))
+        gram_kernel(pieces, share, starts, blocks, before, out, fibres)
+
+    specs = [
+        pl.BlockSpec((len(places), size, LANES), lambda i: (0, 0, 0)) for _, places in entries
+    ]
     shape = (len(block_pairs(whole)) * STEP, STEP)
     square = pl.BlockSpec(shape, lambda i: (0, 0))
     extra = [] if carried is None else [carried]
@@ -288,8 +282,7 @@
         grid=(1,),
         out_shape=jax.ShapeDtypeStruct(shape, jnp.float32),
         in_specs=[pl.BlockSpec(memory_space=pltpu.SMEM)]
-        + [half] * (count * slow)
-        + [both] * (count * slow // 2)
+        + specs
         + [square] * len(extra),
         out_specs=square,
         scratch_shapes=[pltpu.VMEM((whole, share * LANES), jnp.bfloat16)],
@@ -297,6 +290,152 @@
         cost_estimate=pl.CostEstimate(flops=0, bytes_accessed=0, transcendentals=0),
         name="gram",
     )(sources, *inputs, *extra)
+
+
+def spread_row(block, row):
+    return jnp.broadcast_to(block[row : row + 1, :], block.shape)
+
+
+def spread_column(block, column):
+    return jnp.broadcast_to(block[:, column : column + 1], block.shape)
+
+
+def factor_block(square, inverse):
+    strips = len(square)
+    height = square[0].shape[0]
+    rows = lax.broadcasted_iota(jnp.int32, square[0].shape, 0)
+    for t in range(strips):
+        first = t * height
+        a = square[t]
+        columns = [spread_column(a, first + u) for u in range(height)]
+        b = {(v, u): spread_row(columns[u], v) for u in range(height) for v in range(u + 1)}
+        scale, r = [], {}
+        for u in range(height):
+            scale.append(lax.rsqrt(b[u, u]))
+            for w in range(u + 1, height):
+                r[u, w] = b[u, w] * scale[u]
+            for v in range(u + 1, height):
+                for w in range(v, height):
+                    b[v, w] = b[v, w] - r[u, v] * r[u, w]
+        inv = {}
+        for v in range(height):
+            for u in range(v):
+                acc = r[u, v] * inv[u, u]
+                for w in range(u + 1, v):
+                    acc = acc + r[w, v] * inv[w, u]
+                inv[v, u] = -(acc * scale[v])
+            inv[v, v] = scale[v]
+        new_square = new_inverse = None
+        for u in range(height):
+            weight = jnp.zeros_like(a)
+            for v in range(u, height):
+                weight = jnp.where(rows == v, inv[v, u], weight)
+            one = weight * spread_row(a, u)
+            two = weight * spread_row(inverse[t], u)
+            new_square = one if new_square is None else new_square + one
+            new_inverse = two if new_inverse is None else new_inverse + two
+        square[t], inverse[t] = new_square, new_inverse
+        rows_square = [spread_row(new_square, u) for u in range(height)]
+        rows_inverse = [spread_row(new_inverse, u) for u in range(height)]
+        for later in range(t + 1, strips):
+            target = square[later]
+            factors = []
+            for u in range(height):
+                x = spread_column(target, first + u)
+                for w in range(u):
+                    x = x - factors[w] * r[w, u]
+                factors.append(x * scale[u])
+            other = inverse[later]
+            for u in range(height):
+                target = target - factors[u] * rows_square[u]
+                other = other - factors[u] * rows_inverse[u]
+            square[later], inverse[later] = target, other
+
+
+def exact_dot(left, right, contract):
+    return lax.dot_general(
+        left,
+        right,
+        (contract, ((), ())),
+        precision=lax.Precision.HIGHEST,
+        preferred_element_type=jnp.float32,
+    )
+
+
+def cholesky_kernel(slab, place, gram_sum, before, out, work):
+    whole = work.shape[0]
+    panels = whole // LANES
+    at = 0
+    for i, j in block_pairs(whole):
+        work[i : i + STEP, j : j + STEP] = (
+            before[i : i + STEP, j : j + STEP] + gram_sum[at : at + STEP, :]
+        )
+        at += STEP
+
+    height = 8
+    lane = lax.broadcasted_iota(jnp.int32, (height, LANES), 1)
+    row = lax.broadcasted_iota(jnp.int32, (height, LANES), 0)
+
+    def one_panel(p, _):
+        start = pl.multiple_of(p * LANES, LANES)
+        strips = LANES // height
+        square, inverse = [], []
+        for t in range(strips):
+            square.append(work[pl.ds(start + t * height, height), pl.ds(start, LANES)])
+            inverse.append(jnp.where(lane == row + t * height, 1.0, 0.0))
+        factor_block(square, inverse)
+        for t in range(strips):
+            kept = jnp.where(lane >= row + t * height, square[t], 0.0)
+            work[pl.ds(start + t * height, height), pl.ds(start, LANES)] = kept
+        inverse = jnp.concatenate(inverse, axis=0)
+
+        def one_column(j, _):
+            at = pl.multiple_of(j * LANES, LANES)
+            work[pl.ds(start, LANES), pl.ds(at, LANES)] = exact_dot(
+                inverse, work[pl.ds(start, LANES), pl.ds(at, LANES)], ((1,), (0,))
+            )
+            return 0
+
+        lax.fori_loop(p + 1, panels, one_column, 0)
+
+        def one_row(i, _):
+            row_at = pl.multiple_of(i * LANES, LANES)
+            left = work[pl.ds(start, LANES), pl.ds(row_at, LANES)]
+
+            def one_block(j, _):
+                at = pl.multiple_of(j * LANES, LANES)
+                term = exact_dot(left, work[pl.ds(start, LANES), pl.ds(at, LANES)], ((0,), (0,)))
+                work[pl.ds(row_at, LANES), pl.ds(at, LANES)] = (
+                    work[pl.ds(row_at, LANES), pl.ds(at, LANES)] - term
+                )
+                return 0
+
+            lax.fori_loop(i, panels, one_block, 0)
+            return 0
+
+        lax.fori_loop(p + 1, panels, one_row, 0)
+        return 0
+
+    lax.fori_loop(0, panels, one_panel, 0)
+    first = pl.multiple_of(place[0] * slab, 8)
+    rows = first + lax.broadcasted_iota(jnp.int32, (slab, whole), 0)
+    columns = lax.broadcasted_iota(jnp.int32, (slab, whole), 1)
+    out[...] = jnp.where(columns >= rows, work[pl.ds(first, slab), :], 0.0)
+
+
+def cholesky_rows(gram_sum, before, place, slab):
+    whole = before.shape[0]
+    vmem = pl.BlockSpec(memory_space=pltpu.VMEM)
+    return pl.pallas_call(
+        functools.partial(cholesky_kernel, slab),
+        out_shape=jax.ShapeDtypeStruct((slab, whole), jnp.float32),
+        in_specs=[pl.BlockSpec(memory_space=pltpu.SMEM), vmem, vmem],
+        out_specs=vmem,
+        scratch_shapes=[pltpu.VMEM((whole, whole), jnp.float32)],
+        compiler_params=pltpu.CompilerParams(vmem_limit_bytes=VMEM_BYTES),
+        cost_estimate=pl.CostEstimate(flops=0, bytes_accessed=0, transcendentals=0),
+        name="cholesky",
+    )(place, gram_sum, before)
 
 
 def slice_out(upper_r):
@@ -429,6 +568,14 @@
     chunks = [(cell, piece) for cell in range(0, cells_part, LANES) for piece in pieces]
     per_gram = len(pieces)
 
+    size = pieces[0][1]
+    full = running_r.shape[0]
+    padding = ((0, 0), (0, 0), (0, SUB - size))
+    wide_r = jnp.pad(running_r.reshape(full, -1, size), padding).reshape(full, -1)
+    before = exact_dot(wide_r, wide_r, ((0,), (0,)))
+    padded = jnp.arange(wide_r.shape[1]) % SUB >= size
+    before = before + jnp.diag(padded.astype(jnp.float32))
+
     flown = []
 
     def start(operand, axis, pairs):
@@ -456,31 +603,26 @@
             near = [
                 start_x(1, pack_near(by_y, scalars, cell)) for cell in range(0, cells_part, LANES)
             ]
-    straight = []
-    crossed = []
+    arrived = []
     carried = None
 
+    def value_of(block):
+        return flown[block] if isinstance(block, int) else block
+
     def cross(k, j):
-        pair = []
-        for dz in (2 * j, 2 * j + 1):
-            block = straight[k][dz]
-            pair.append((flown[block] if isinstance(block, int) else block)[1])
-        crossed[k][j] = start_y((0, 1), jnp.stack(pair))
+        pair = [value_of(arrived[k][dz][0])[1] for dz in (2 * j, 2 * j + 1)]
+        slot = start_y((0, 1), jnp.stack(pair))
+        arrived[k].append((slot, ((2 * j, 1), (2 * j + 1, 1))))
 
     def add_gram(carried, first):
-        group = range(first, first + per_gram)
-        return gram(
-            [[flown[b] if isinstance(b, int) else b for b in straight[k]] for k in group],
-            [[flown[b] for b in crossed[k]] for k in group],
-            carried,
-            sources,
-            pieces,
-            share,
-        )
+        group = arrived[first : first + per_gram]
+        blocks = [[(value_of(block), places) for block, places in piece] for piece in group]
+        return gram(blocks, carried, sources, pieces, share)
 
     for k, chunk in enumerate(chunks):
         following = chunks[k + AHEAD] if k + AHEAD < len(chunks) else None
-        after = []
+        last = k == len(chunks) - 1
+        after = [before] if k == 1 else []
         if k >= per_gram + 2 and (k - 2) % per_gram == 0:
             carried = add_gram(carried, k - 2 - per_gram)
             after.append(carried)
@@ -495,47 +637,42 @@
             n_x,
             share,
             slow,
+            last,
             after,
         )
-        straight.append([outs[0]] + [None] * (slow - 1))
-        crossed.append([None] * (slow // 2))
         steps = []
-        for dz in range(1, slow):
-            steps.append(((dz - 0.9) / (slow - 1), 0, dz))
+        for i, place in enumerate(shifts if last else shifts[::2]):
+            if i:
+                steps.append(((i - 0.9) / (len(outs) - 1), 0, i))
         for j in range(slow // 2 if k else 0):
             steps.append(((j + 0.5) / (slow // 2), 1, j))
         slots = [None] * len(sends)
         for i in range(len(sends)):
             steps.append(((i + 0.3) / len(sends), 2, i))
+        landed = [(outs[0], ((0, 0),))]
+        arrived.append(landed)
         for _, kind, i in sorted(steps):
             if kind == 0:
-                straight[k][i] = start_y((i, 0), outs[i])
+                shift = shifts[i] if last else shifts[2 * i]
+                landed.append((start_y(shift, outs[i]), (shift,)))
             elif kind == 1:
                 cross(k - 1, i)
             else:
                 slots[i] = start_x(send_list(following, n_x)[i][0], sends[i])
         if sends:
             moving.append(slots)
-    for j in range(slow // 2):
-        cross(len(chunks) - 1, j)
     for first in range(0, len(chunks), per_gram):
         if first + per_gram + 2 >= len(chunks):
             carried = add_gram(carried, first)
 
     summed = sum_over_all(carried)
-    count, size = len(pieces), pieces[0][1]
-    whole = n_y * count * SUB
-    blocks = {
-        pair: summed[index * STEP : (index + 1) * STEP]
-        for index, pair in enumerate(block_pairs(whole))
-    }
-    none = jnp.zeros((STEP, STEP), jnp.float32)
-    starts = range(0, whole, STEP)
-    upper = jnp.concatenate(
-        [jnp.concatenate([blocks.get((i, j), none) for j in starts], axis=1) for i in starts]
-    )
-    gram_sum = upper.reshape(n_y * count, SUB, n_y * count, SUB)[:, :size, :, :size]
-    return finish(gram_sum.reshape(n_y * rows, n_y * rows), running_r)
+    slab = cholesky_rows(summed, before, me_y.astype(jnp.int32)[None], pitch_of(rows))
+    groups = rows * n_y // n_x // size
+    mine = lax.dynamic_slice(
+        slab, (0, me_x * (groups * SUB)), (slab.shape[0], groups * SUB)
+    )
+    mine = mine.reshape(-1, SUB, groups, SUB)[:, :size, :, :size]
+    return mine.reshape(rows, groups * size)
 
 
 def on_device(fields, x_factor, running_r):
@@ -552,6 +689,7 @@
         and rows >= 16
         and rows % (4 * len(y_pieces(rows))) == 0
         and n_y * pitch_of(rows) % STEP == 0
+        and rows * n_y // n_x % y_pieces(rows)[0][1] == 0
         and len(block_pairs(n_y * pitch_of(rows))) * STEP % (8 * n_x * n_y) == 0
     )
     if fits:

time: 879 us -> 732 us (0.83)
  other arithmetic: 135 us -> 7.96 us
  Pallas kernels: 160 us -> 203 us
  local copies, waits for them, and re-layouts: 44.1 us -> 19.2 us
  starting transfers between devices: 233 us -> 215 us
  matrix products: 20.5 us -> 7.34 us
    another operation x40 -> x16, other arithmetic: 125 us -> 4.22 us  [cross(): slot = start_y((0, 1), jnp.stack(pair))]
    pallas_call x0 -> x1, Pallas kernels: none -> 42.8 us  [cholesky_rows(): pl.pallas_call(functools.partial(cholesky_kernel, slab), out_shape=jax.Sh...]
    ppermute x84 -> x86, starting transfers between devices: 209 us -> 194 us  [start(): flown.append(lax.ppermute(operand, axis, pairs))]
    reshape x3 -> x4, local copies, waits for them, and re-layouts: 17 us -> 2.64 us  [the longest x1 1.65 us: pipelined(): running_r.reshape(full, -1, size)]
    another operation x10 -> x0, matrix products: 13.2 us -> none  [finish(): return slice_out(lax.linalg.cholesky(total.T, symmetrize_input=False).T)]
    slice x39 -> x33, local copies, waits for them, and re-layouts: 11.8 us -> 2.82 us  [the longest x32 2.8 us: cross(): pair = [value_of(arrived[k][dz][0])[1] for dz in (2 * j, 2 * j + 1)]]
    ppermute x84 -> x86, waiting for transfers between devices: 233 us -> 238 us  [start(): flown.append(lax.ppermute(operand, axis, pairs))]
  transfers between devices with their start and end apart: 96 -> 98, of which waited for: 47 -> 48; matrix products, arithmetic and copies ran while one was open for 2% -> 3% of each run, Pallas kernels for 16% -> 20%
where the time goes in v5:
time: 732 us; the launch traced here: 727 us
  waiting for transfers between devices  274 us (37%)
  starting transfers between devices  215 us (29%)
  Pallas kernels  203 us (28%)
  local copies, waits for them, and re-layouts  19.2 us (3%)
  other arithmetic  7.96 us (1%)
  matrix products  7.34 us (1%)
    ppermute x86, waiting for transfers between devices, start(): flown.append(lax.ppermute(operand, axis, pairs))  238 us
    ppermute x86, starting transfers between devices, start(): flown.append(lax.ppermute(operand, axis, pairs))  194 us
    pallas_call x9, Pallas kernels, project(): pl.pallas_call(body, out_shape=shapes, in_specs=[pl.BlockSpec(memory_spac...  98.9 us
    pallas_call x1, Pallas kernels, cholesky_rows(): pl.pallas_call(functools.partial(cholesky_kernel, slab), out_shape=jax.Sh...  42.8 us
    pallas_call x3, Pallas kernels, gram(): pl.pallas_call(body, grid=(1,), out_shape=jax.ShapeDtypeStruct(shape, jnp...  39.5 us
    ppermute x6, waiting for transfers between devices, swap(): return lax.ppermute(value, axis, flips)  30.3 us
    pallas_call x5, Pallas kernels, run_pack(): pl.pallas_call(body, out_shape=shapes, in_specs=[pl.BlockSpec(memory_spac...  21.4 us
  transfers between devices with their start and end apart: 98, of which 48 were waited for; matrix products, arithmetic and copies ran while one was open for 3% of the time, Pallas kernels for 20%

profile of v5, /device:TPU:0, one launch (start us, length us, event | category | flops | bytes accessed | tf_op | source)
XLA Modules:
  0.0 727.1 jit_solution(3084758134173431635)
XLA Ops:
  39.7 10.7 %collective-permute-done.2.rest_2_ = bf16[14,168,128]{2,1,0:T(8,128)(2,1)S(1)} collective-permute-done((bf16[14,168,128]{2,1,0:T(8,128)(2,1)S(1)}, bf16[14,168,128]{2,1,0:T(8,128)(2,1)S(1)}, u32[]{:S(2)}, u32[]{:S(2)}) %collective-permute-start.2) | collective-permute-done | bytes 602144 | tf_op jit(solution)/shard_map/ppermute | solution.py:586
  52.2 10.4 %collective-permute-done.3.rest_3_ = bf16[14,168,128]{2,1,0:T(8,128)(2,1)S(1)} collective-permute-done((bf16[14,168,128]{2,1,0:T(8,128)(2,1)S(1)}, bf16[14,168,128]{2,1,0:T(8,128)(2,1)S(1)}, u32[]{:S(2)}, u32[]{:S(2)}) %collective-permute-start.3) | collective-permute-done | bytes 602144 | tf_op jit(solution)/shard_map/ppermute | solution.py:586
  66.9 11.3 %project.9 = (bf16[2,1176,128]{2,1,0:T(8,128)(2,1)}, bf16[2,1176,128]{2,1,0:T(8,128)(2,1)}, bf16[2,1176,128]{2,1,0:T(8,128)(2,1)}, bf16[2,1176,128]{2,1,0:T(8,12...) custom-call(s32[12]{0:T(128)} %stack.150.scalars, ...), custom_call_target="tpu_custom_call" | custom-call | tf_op jit(solution)/shard_map/project/pallas_call | solution.py:188
  90.6 11.5 %collective-permute-done.9.rest_2_ = bf16[14,168,128]{2,1,0:T(8,128)(2,1)} collective-permute-done((bf16[14,168,128]{2,1,0:T(8,128)(2,1)}, bf16[14,168,128]{2,1,0:T(8,128)(2,1)}, u32[]{:S(2)}, u32[]{:S(2)}) %collective-permute-start.9) | collective-permute-done | bytes 602144 | tf_op jit(solution)/shard_map/ppermute | solution.py:586
  114.3 13.6 %collective-permute-done.12.rest_0_ = bf16[14,168,128]{2,1,0:T(8,128)(2,1)} collective-permute-done((bf16[14,168,128]{2,1,0:T(8,128)(2,1)}, bf16[14,168,128]{2,1,0:T(8,128)(2,1)}, u32[]{:S(2)}, u32[]{:S(2)}) %collective-permute-start.12) | collective-permute-done | bytes 602144 | tf_op jit(solution)/shard_map/ppermute | solution.py:586
  140.8 11.2 %project.10 = (bf16[2,1176,128]{2,1,0:T(8,128)(2,1)}, bf16[2,1176,128]{2,1,0:T(8,128)(2,1)}, bf16[2,1176,128]{2,1,0:T(8,128)(2,1)}, bf16[2,1176,128]{2,1,0:T(8,1...) custom-call(s32[12]{0:T(128)} %stack.150.scalars, ...), custom_call_target="tpu_custom_call" | custom-call | tf_op jit(solution)/shard_map/project/pallas_call | solution.py:188
  155.7 10.2 %collective-permute-done.17.rest_3_ = bf16[14,168,128]{2,1,0:T(8,128)(2,1)S(1)} collective-permute-done((bf16[14,168,128]{2,1,0:T(8,128)(2,1)}, bf16[14,168,128]{2,1,0:T(8,128)(2,1)S(1)}, u32[]{:S(2)}, u32[]{:S(2)}) %collective-permute-start.17) | collective-permute-done | bytes 602144 | tf_op jit(solution)/shard_map/ppermute | solution.py:586
  170.5 8.9 %collective-permute-done.19.rest_0_ = bf16[14,168,128]{2,1,0:T(8,128)(2,1)S(1)} collective-permute-done((bf16[14,168,128]{2,1,0:T(8,128)(2,1)}, bf16[14,168,128]{2,1,0:T(8,128)(2,1)S(1)}, u32[]{:S(2)}, u32[]{:S(2)}) %collective-permute-start.19) | collective-permute-done | bytes 602144 | tf_op jit(solution)/shard_map/ppermute | solution.py:586
  193.9 11.1 %project.11 = (bf16[2,1176,128]{2,1,0:T(8,128)(2,1)}, bf16[2,1176,128]{2,1,0:T(8,128)(2,1)}, bf16[2,1176,128]{2,1,0:T(8,128)(2,1)}, bf16[2,1176,128]{2,1,0:T(8,1...) custom-call(s32[12]{0:T(128)} %stack.150.scalars, ...), custom_call_target="tpu_custom_call" | custom-call | tf_op jit(solution)/shard_map/project/pallas_call | solution.py:188
  220.0 7.5 %collective-permute-done.27.rest_13_ = bf16[2,1176,128]{2,1,0:T(8,128)(2,1)S(1)} collective-permute-done((bf16[2,1176,128]{2,1,0:T(8,128)(2,1)}, bf16[2,1176,128]{2,1,0:T(8,128)(2,1)S(1)}, u32[]{:S(2)}, u32[]{:S(2)}) %collective-permute-start.27) | collective-permute-done | bytes 602144 | tf_op jit(solution)/shard_map/ppermute | solution.py:586
  246.2 11.1 %project.12 = (bf16[2,1176,128]{2,1,0:T(8,128)(2,1)}, bf16[2,1176,128]{2,1,0:T(8,128)(2,1)}, bf16[2,1176,128]{2,1,0:T(8,128)(2,1)}, bf16[2,1176,128]{2,1,0:T(8,1...) custom-call(s32[12]{0:T(128)} %stack.150.scalars, ...), custom_call_target="tpu_custom_call" | custom-call | tf_op jit(solution)/shard_map/project/pallas_call | solution.py:188
  271.7 8.3 %collective-permute-done.36.rest_1_ = bf16[2,1176,128]{2,1,0:T(8,128)(2,1)S(1)} collective-permute-done((bf16[2,1176,128]{2,1,0:T(8,128)(2,1)}, bf16[2,1176,128]{2,1,0:T(8,128)(2,1)S(1)}, u32[]{:S(2)}, u32[]{:S(2)}) %collective-permute-start.36) | collective-permute-done | bytes 602144 | tf_op jit(solution)/shard_map/ppermute | solution.py:586
  297.9 11.1 %project.13 = (bf16[2,1176,128]{2,1,0:T(8,128)(2,1)}, bf16[2,1176,128]{2,1,0:T(8,128)(2,1)}, bf16[2,1176,128]{2,1,0:T(8,128)(2,1)}, bf16[2,1176,128]{2,1,0:T(8,1...) custom-call(s32[12]{0:T(128)} %stack.150.scalars, ...), custom_call_target="tpu_custom_call" | custom-call | tf_op jit(solution)/shard_map/project/pallas_call | solution.py:188
  350.2 12.9 %gram.3.rest_5_.rest_18_ = f32[1536,256]{1,0:T(8,128)} custom-call(s32[8]{0:T(128)} %stack.137.sources, bf16[2,1176,128]{2,1,0:T(8,128)(2,1)} %get-tuple-element.617.rest_0_, bf16[2,1176,128]{2,1,0:T(8,128)(2,1)} %copy-done.21, bf16[2,1176,128]{2,1,0:T(8,128)(2,1)} %collective-permute-done.14.rest_2_, bf16[2,1176,128]{2,1,0:T(8,128)(2,1)} %copy-done.22, ...), custom_call_target="tpu_custom_call" | custom-call | tf_op jit(solution)/shard_map/gram/pallas_call | solution.py:280
  363.1 11.2 %project.14 = (bf16[2,1176,128]{2,1,0:T(8,128)(2,1)}, bf16[2,1176,128]{2,1,0:T(8,128)(2,1)}, bf16[2,1176,128]{2,1,0:T(8,128)(2,1)}, bf16[2,1176,128]{2,1,0:T(8,1...) custom-call(s32[12]{0:T(128)} %stack.150.scalars, ...), custom_call_target="tpu_custom_call" | custom-call | tf_op jit(solution)/shard_map/project/pallas_call | solution.py:188
  380.9 12.1 %collective-permute-done.54.rest_13_ = bf16[2,1176,128]{2,1,0:T(8,128)(2,1)S(1)} collective-permute-done((bf16[2,1176,128]{2,1,0:T(8,128)(2,1)}, bf16[2,1176,128]{2,1,0:T(8,128)(2,1)S(1)}, u32[]{:S(2)}, u32[]{:S(2)}) %collective-permute-start.54) | collective-permute-done | bytes 602144 | tf_op jit(solution)/shard_map/ppermute | solution.py:586
  406.0 11.1 %project.15 = (bf16[2,1176,128]{2,1,0:T(8,128)(2,1)}, bf16[2,1176,128]{2,1,0:T(8,128)(2,1)}, bf16[2,1176,128]{2,1,0:T(8,128)(2,1)}, bf16[2,1176,128]{2,1,0:T(8,1...) custom-call(s32[12]{0:T(128)} %stack.150.scalars, ...), custom_call_target="tpu_custom_call" | custom-call | tf_op jit(solution)/shard_map/project/pallas_call | solution.py:188
  417.2 15.7 %collective-permute-start.63 = (bf16[2,1176,128]{2,1,0:T(8,128)(2,1)}, bf16[2,1176,128]{2,1,0:T(8,128)(2,1)S(1)}, u32[]{:S(2)}, u32[]{:S(2)}) collective-permute-start(bf16[2,1176,128]{2,1,0:T(8,128)(2,1)} %get-tuple-element.958), channel_id=1, source_target_pairs={{0,2},{1,3},{2,4},{3,5},{4,6},{5,7},{6,0},{7,1},{8,10},{9,11},{10,... | collective-permute-start | bytes 1806344 | tf_op jit(solution)/shard_map/ppermute | solution.py:586
  442.4 7.6 %collective-permute-done.63.rest_1_ = bf16[2,1176,128]{2,1,0:T(8,128)(2,1)S(1)} collective-permute-done((bf16[2,1176,128]{2,1,0:T(8,128)(2,1)}, bf16[2,1176,128]{2,1,0:T(8,128)(2,1)S(1)}, u32[]{:S(2)}, u32[]{:S(2)}) %collective-permute-start.63) | collective-permute-done | bytes 602144 | tf_op jit(solution)/shard_map/ppermute | solution.py:586
  462.8 10.6 %project.16 = (bf16[2,1176,128]{2,1,0:T(8,128)(2,1)}, bf16[2,1176,128]{2,1,0:T(8,128)(2,1)}, bf16[2,1176,128]{2,1,0:T(8,128)(2,1)}, bf16[2,1176,128]{2,1,0:T(8,128)(2,1)}) custom-call(s32[12]{0:T(128)} %stack.150.scalars, bf16[84,168,1536]{2,1,0:T(8,128)(2,1)} %bitcast.89, bf16[84,168,128]{2,1,0:T(8,128)(2,1)} %collective-permute-done.6.near, ...), custom_call_target="tpu_custom_call" | custom-call | tf_op jit(solution)/shard_map/project/pallas_call | solution.py:188
  477.8 12.3 %collective-permute-start.72 = (bf16[2,1176,128]{2,1,0:T(8,128)(2,1)}, bf16[2,1176,128]{2,1,0:T(8,128)(2,1)S(1)}, u32[]{:S(2)}, u32[]{:S(2)}) collective-permute-start(bf16[2,1176,128]{2,1,0:T(8,128)(2,1)} %get-tuple-element.1023), channel_id=1, source_target_pairs={{0,2},{1,3},{2,4},{3,5},{4,6},{5,7},{6,0},{7,1},{8,10},{9,11},{10,... | collective-permute-start | bytes 1806344 | tf_op jit(solution)/shard_map/ppermute | solution.py:586
  499.0 13.3 %gram.4.rest_5_.rest_20_ = f32[1536,256]{1,0:T(8,128)} custom-call(s32[8]{0:T(128)} %stack.137.sources, bf16[2,1176,128]{2,1,0:T(8,128)(2,1)} %get-tuple-element.805.rest_0_, bf16[2,1176,128]{2,1,0:T(8,128)(2,1)} %copy-done.2, bf16[2,1176,128]{2,1,0:T(8,128)(2,1)} %copy-done.3, bf16[2,1176,128]{2,1,0:T(8,128)(2,1)} %copy-done.4, ...), custom_call_target="tpu_custom_call" | custom-call | tf_op jit(solution)/shard_map/gram/pallas_call | solution.py:280
  512.4 10.3 %project.17 = (bf16[1,1176,128]{2,1,0:T(8,128)(2,1)}, bf16[1,1176,128]{2,1,0:T(8,128)(2,1)}, bf16[1,1176,128]{2,1,0:T(8,128)(2,1)}, bf16[1,1176,128]{2,1,0:T(8,1...) custom-call(s32[12]{0:T(128)} %stack.150.scalars, ...), custom_call_target="tpu_custom_call" | custom-call | tf_op jit(solution)/shard_map/project/pallas_call | solution.py:188
  522.8 10.0 %collective-permute-done.74.rest_8_ = bf16[2,1176,128]{2,1,0:T(8,128)(2,1)S(1)} collective-permute-done((bf16[2,1176,128]{2,1,0:T(8,128)(2,1)}, bf16[2,1176,128]{2,1,0:T(8,128)(2,1)S(1)}, u32[]{:S(2)}, u32[]{:S(2)}) %collective-permute-start.74) | collective-permute-done | bytes 602144 | tf_op jit(solution)/shard_map/ppermute | solution.py:586
  534.8 11.4 %collective-permute-start.78 = (bf16[1,1176,128]{2,1,0:T(8,128)(2,1)}, bf16[1,1176,128]{2,1,0:T(8,128)(2,1)S(1)}, u32[]{:S(2)}, u32[]{:S(2)}) collective-permute-start(bf16[1,1176,128]{2,1,0:T(8,128)(2,1)} %get-tuple-element.1056), channel_id=1, source_target_pairs={{0,2},{1,3},{2,4},{3,5},{4,6},{5,7},{6,0},{7,1},{8,10},{9,11},{10,... | collective-permute-start | bytes 903176 | tf_op jit(solution)/shard_map/ppermute | solution.py:586
  546.2 8.4 %collective-permute-done.77.rest_13_ = bf16[1,1176,128]{2,1,0:T(8,128)(2,1)S(1)} collective-permute-done((bf16[1,1176,128]{2,1,0:T(8,128)(2,1)}, bf16[1,1176,128]{2,1,0:T(8,128)(2,1)S(1)}, u32[]{:S(2)}, u32[]{:S(2)}) %collective-permute-start.77) | collective-permute-done | bytes 301088 | tf_op jit(solution)/shard_map/ppermute | solution.py:586
  555.1 11.3 %collective-permute-start.80 = (bf16[1,1176,128]{2,1,0:T(8,128)(2,1)S(1)}, bf16[1,1176,128]{2,1,0:T(8,128)(2,1)S(1)}, u32[]{:S(2)}, u32[]{:S(2)}) collective-permute-start(bf16[1,1176,128]{2,1,0:T(8,128)(2,1)S(1)} %copy-done.87), channel_id=1, source_target_pairs={{0,3},{1,2},{2,5},{3,4},{4,7},{5,6},{6,1},{7,0},{8,11},{9,10},{10,... | collective-permute-start | bytes 903176 | tf_op jit(solution)/shard_map/ppermute | solution.py:586
  577.3 8.4 %collective-permute-start.85 = (bf16[1,1176,128]{2,1,0:T(8,128)(2,1)}, bf16[1,1176,128]{2,1,0:T(8,128)(2,1)}, u32[]{:S(2)}, u32[]{:S(2)}) collective-permute-start(bf16[1,1176,128]{2,1,0:T(8,128)(2,1)} %get-tuple-element.1080), channel_id=1, source_target_pairs={{0,7},{1,6},{2,1},{3,0},{4,3},{5,2},{6,5},{7,4},{8,15},{9,14},{10,... | collective-permute-start | bytes 903176 | tf_op jit(solution)/shard_map/ppermute | solution.py:586
  585.7 15.9 %collective-permute-done.83.rest_17_ = bf16[1,1176,128]{2,1,0:T(8,128)(2,1)} collective-permute-done((bf16[1,1176,128]{2,1,0:T(8,128)(2,1)}, bf16[1,1176,128]{2,1,0:T(8,128)(2,1)}, u32[]{:S(2)}, u32[]{:S(2)}) %collective-permute-start.83) | collective-permute-done | bytes 301088 | tf_op jit(solution)/shard_map/ppermute | solution.py:586
  607.6 13.3 %gram.5 = f32[1536,256]{1,0:T(8,128)} custom-call(s32[8]{0:T(128)} %stack.137.sources, bf16[2,1176,128]{2,1,0:T(8,128)(2,1)} %get-tuple-element.919.rest_0_, bf16[2,1176,128]{2,1,0:T(8,128)(2,1)} %copy-done.10, bf16[2,1176,128]{2,1,0:T(8,128)(2,1)} %copy-done.12, bf16[2,1176,128]{2,1,0:T(8,128)(2,1)} %copy-done.14, bf16[2,1176,128]{2,1,0:T(8,128)(2,1)} %copy-done.41, ...), custom_call_target="tpu_custom_call" | custom-call | tf_op jit(solution)/shard_map/gram/pallas_call | solution.py:280
  628.4 9.4 %collective-permute-done.87 = f32[384,256]{1,0:T(8,128)S(1)} collective-permute-done((f32[384,256]{1,0:T(8,128)S(1)}, f32[384,256]{1,0:T(8,128)S(1)}, u32[]{:S(2)}, u32[]{:S(2)}) %collective-permute-start.87) | collective-permute-done | bytes 393248 | tf_op jit(solution)/shard_map/ppermute | solution.py:487
  682.1 42.8 %cholesky.1 = f32[96,768]{1,0:T(8,128)} custom-call(s32[1]{0:T(128)} %bitcast.place, f32[1536,256]{1,0:T(8,128)} %maximum_select_fusion.gram_sum, f32[768,768]{1,0:T(8,128)} %select_add_fusion.rest_5_.before), custom_call_target="tpu_custom_call" | custom-call | tf_op jit(solution)/shard_map/cholesky/pallas_call | solution.py:429
  (439 shorter events, 340.6 us)
Async XLA Ops:
  12.0 52.5 %collective-permute-start.4 = (bf16[84,168,128]{2,1,0:T(8,128)(2,1)}, bf16[84,168,128]{2,1,0:T(8,128)(2,1)}, u32[]{:S(2)}, u32[]{:S(2)}) collective-permute-start(bf16[84,168,128]{2,1,0:T(8,128)(2,1)} %pack.9), channel_id=1, source_target_pairs={{0,8},{8,0},{16,24},{24,16},{1,9},{9,1},{17,25},{25,17},{2,10},{10... | collective-permute-start | bytes 10838024 | tf_op jit(solution)/shard_map/ppermute | solution.py:586
  22.1 44.3 %collective-permute-start.5 = (bf16[84,168,128]{2,1,0:T(8,128)(2,1)}, bf16[84,168,128]{2,1,0:T(8,128)(2,1)}, u32[]{:S(2)}, u32[]{:S(2)}) collective-permute-start(bf16[84,168,128]{2,1,0:T(8,128)(2,1)} %pack.7), channel_id=1, source_target_pairs={{0,8},{8,0},{16,24},{24,16},{1,9},{9,1},{17,25},{25,17},{2,10},{10... | collective-permute-start | bytes 10838024 | tf_op jit(solution)/shard_map/ppermute | solution.py:586
  33.5 44.6 %collective-permute-start.6 = (bf16[84,168,128]{2,1,0:T(8,128)(2,1)}, bf16[84,168,128]{2,1,0:T(8,128)(2,1)}, u32[]{:S(2)}, u32[]{:S(2)}) collective-permute-start(bf16[84,168,128]{2,1,0:T(8,128)(2,1)} %pack.6), channel_id=1, source_target_pairs={{0,8},{8,0},{16,24},{24,16},{1,9},{9,1},{17,25},{25,17},{2,10},{10... | collective-permute-start | bytes 10838024 | tf_op jit(solution)/shard_map/ppermute | solution.py:586
  64.5 37.6 %collective-permute-start.9 = (bf16[14,168,128]{2,1,0:T(8,128)(2,1)}, bf16[14,168,128]{2,1,0:T(8,128)(2,1)}, u32[]{:S(2)}, u32[]{:S(2)}) collective-permute-start(bf16[14,168,128]{2,1,0:T(8,128)(2,1)} %get-tuple-element.591), channel_id=1, source_target_pairs={{0,16},{8,24},{16,0},{24,8},{1,17},{9,25},{17,1},{25,9},{2,18},{10... | collective-permute-start | bytes 1806344 | tf_op jit(solution)/shard_map/ppermute | solution.py:586
  66.4 47.9 %collective-permute-start.10 = (bf16[14,168,128]{2,1,0:T(8,128)(2,1)}, bf16[14,168,128]{2,1,0:T(8,128)(2,1)}, u32[]{:S(2)}, u32[]{:S(2)}) collective-permute-start(bf16[14,168,128]{2,1,0:T(8,128)(2,1)} %get-tuple-element.596), channel_id=1, source_target_pairs={{0,24},{8,16},{16,8},{24,0},{1,25},{9,17},{17,9},{25,1},{2,26},{10... | collective-permute-start | bytes 1806344 | tf_op jit(solution)/shard_map/ppermute | solution.py:586
  78.1 36.2 %collective-permute-start.11 = (bf16[2,1176,128]{2,1,0:T(8,128)(2,1)}, bf16[2,1176,128]{2,1,0:T(8,128)(2,1)S(1)}, u32[]{:S(2)}, u32[]{:S(2)}) collective-permute-start(bf16[2,1176,128]{2,1,0:T(8,128)(2,1)} %get-tuple-element.605), channel_id=1, source_target_pairs={{0,2},{1,3},{2,4},{3,5},{4,6},{5,7},{6,0},{7,1},{8,10},{9,11},{10,... | collective-permute-start | bytes 1806344 | tf_op jit(solution)/shard_map/ppermute | solution.py:586
  79.7 48.2 %collective-permute-start.12 = (bf16[14,168,128]{2,1,0:T(8,128)(2,1)}, bf16[14,168,128]{2,1,0:T(8,128)(2,1)}, u32[]{:S(2)}, u32[]{:S(2)}) collective-permute-start(bf16[14,168,128]{2,1,0:T(8,128)(2,1)} %get-tuple-element.612), channel_id=1, source_target_pairs={{0,16},{8,24},{16,0},{24,8},{1,17},{9,25},{17,1},{25,9},{2,18},{10... | collective-permute-start | bytes 1806344 | tf_op jit(solution)/shard_map/ppermute | solution.py:586
  88.5 63.5 %collective-permute-start.13 = (bf16[14,168,128]{2,1,0:T(8,128)(2,1)}, bf16[14,168,128]{2,1,0:T(8,128)(2,1)}, u32[]{:S(2)}, u32[]{:S(2)}) collective-permute-start(bf16[14,168,128]{2,1,0:T(8,128)(2,1)} %get-tuple-element.622), channel_id=1, source_target_pairs={{0,24},{8,16},{16,8},{24,0},{1,25},{9,17},{17,9},{25,1},{2,26},{10... | collective-permute-start | bytes 1806344 | tf_op jit(solution)/shard_map/ppermute | solution.py:586
  102.1 50.0 %collective-permute-start.14 = (bf16[2,1176,128]{2,1,0:T(8,128)(2,1)}, bf16[2,1176,128]{2,1,0:T(8,128)(2,1)}, u32[]{:S(2)}, u32[]{:S(2)}) collective-permute-start(bf16[2,1176,128]{2,1,0:T(8,128)(2,1)} %get-tuple-element.626), channel_id=1, source_target_pairs={{0,4},{1,5},{2,6},{3,7},{4,0},{5,1},{6,2},{7,3},{8,12},{9,13},{10,... | collective-permute-start | bytes 1806344 | tf_op jit(solution)/shard_map/ppermute | solution.py:586
  155.4 36.2 %collective-permute-start.21 = (bf16[14,168,128]{2,1,0:T(8,128)(2,1)S(1)}, bf16[14,168,128]{2,1,0:T(8,128)(2,1)S(1)}, u32[]{:S(2)}, u32[]{:S(2)}) collective-permute-start(bf16[14,168,128]{2,1,0:T(8,128)(2,1)S(1)} %copy-done.83), channel_id=1, source_target_pairs={{0,24},{8,16},{16,8},{24,0},{1,25},{9,17},{17,9},{25,1},{2,26},{10... | collective-permute-start | bytes 1806344 | tf_op jit(solution)/shard_map/ppermute | solution.py:586
  165.9 39.1 %collective-permute-start.22 = (bf16[2,1176,128]{2,1,0:T(8,128)(2,1)}, bf16[2,1176,128]{2,1,0:T(8,128)(2,1)S(1)}, u32[]{:S(2)}, u32[]{:S(2)}) collective-permute-start(bf16[2,1176,128]{2,1,0:T(8,128)(2,1)} %get-tuple-element.677), channel_id=1, source_target_pairs={{0,4},{1,5},{2,6},{3,7},{4,0},{5,1},{6,2},{7,3},{8,12},{9,13},{10,... | collective-permute-start | bytes 1806344 | tf_op jit(solution)/shard_map/ppermute | solution.py:586
  170.2 39.8 %collective-permute-start.23 = (bf16[14,168,128]{2,1,0:T(8,128)(2,1)}, bf16[14,168,128]{2,1,0:T(8,128)(2,1)S(1)}, u32[]{:S(2)}, u32[]{:S(2)}) collective-permute-start(bf16[14,168,128]{2,1,0:T(8,128)(2,1)} %get-tuple-element.682), channel_id=1, source_target_pairs={{0,16},{8,24},{16,0},{24,8},{1,17},{9,25},{17,1},{25,9},{2,18},{10... | collective-permute-start | bytes 1806344 | tf_op jit(solution)/shard_map/ppermute | solution.py:586
  217.4 40.0 %collective-permute-start.31 = (bf16[2,1176,128]{2,1,0:T(8,128)(2,1)}, bf16[2,1176,128]{2,1,0:T(8,128)(2,1)S(1)}, u32[]{:S(2)}, u32[]{:S(2)}) collective-permute-start(bf16[2,1176,128]{2,1,0:T(8,128)(2,1)} %get-tuple-element.737), channel_id=1, source_target_pairs={{0,4},{1,5},{2,6},{3,7},{4,0},{5,1},{6,2},{7,3},{8,12},{9,13},{10,... | collective-permute-start | bytes 1806344 | tf_op jit(solution)/shard_map/ppermute | solution.py:586
  227.5 35.0 %collective-permute-start.32 = (bf16[14,168,128]{2,1,0:T(8,128)(2,1)}, bf16[14,168,128]{2,1,0:T(8,128)(2,1)S(1)}, u32[]{:S(2)}, u32[]{:S(2)}) collective-permute-start(bf16[14,168,128]{2,1,0:T(8,128)(2,1)} %get-tuple-element.742), channel_id=1, source_target_pairs={{0,16},{8,24},{16,0},{24,8},{1,17},{9,25},{17,1},{25,9},{2,18},{10... | collective-permute-start | bytes 1806344 | tf_op jit(solution)/shard_map/ppermute | solution.py:586
  269.1 39.9 %collective-permute-start.40 = (bf16[2,1176,128]{2,1,0:T(8,128)(2,1)}, bf16[2,1176,128]{2,1,0:T(8,128)(2,1)S(1)}, u32[]{:S(2)}, u32[]{:S(2)}) collective-permute-start(bf16[2,1176,128]{2,1,0:T(8,128)(2,1)} %get-tuple-element.797), channel_id=1, source_target_pairs={{0,4},{1,5},{2,6},{3,7},{4,0},{5,1},{6,2},{7,3},{8,12},{9,13},{10,... | collective-permute-start | bytes 1806344 | tf_op jit(solution)/shard_map/ppermute | solution.py:586
  320.7 53.5 %collective-permute-start.49 = (bf16[2,1176,128]{2,1,0:T(8,128)(2,1)}, bf16[2,1176,128]{2,1,0:T(8,128)(2,1)S(1)}, u32[]{:S(2)}, u32[]{:S(2)}) collective-permute-start(bf16[2,1176,128]{2,1,0:T(8,128)(2,1)} %get-tuple-element.865), channel_id=1, source_target_pairs={{0,4},{1,5},{2,6},{3,7},{4,0},{5,1},{6,2},{7,3},{8,12},{9,13},{10,... | collective-permute-start | bytes 1806344 | tf_op jit(solution)/shard_map/ppermute | solution.py:586
  330.4 45.5 %collective-permute-start.50 = (bf16[14,168,128]{2,1,0:T(8,128)(2,1)}, bf16[14,168,128]{2,1,0:T(8,128)(2,1)}, u32[]{:S(2)}, u32[]{:S(2)}) collective-permute-start(bf16[14,168,128]{2,1,0:T(8,128)(2,1)} %get-tuple-element.870), channel_id=1, source_target_pairs={{0,16},{8,24},{16,0},{24,8},{1,17},{9,25},{17,1},{25,9},{2,18},{10... | collective-permute-start | bytes 1806344 | tf_op jit(solution)/shard_map/ppermute | solution.py:586
  334.3 41.8 %collective-permute-start.51 = (bf16[2,1176,128]{2,1,0:T(8,128)(2,1)}, bf16[2,1176,128]{2,1,0:T(8,128)(2,1)S(1)}, u32[]{:S(2)}, u32[]{:S(2)}) collective-permute-start(bf16[2,1176,128]{2,1,0:T(8,128)(2,1)} %get-tuple-element.879), channel_id=1, source_target_pairs={{0,6},{1,7},{2,0},{3,1},{4,2},{5,3},{6,4},{7,5},{8,14},{9,15},{10,... | collective-permute-start | bytes 1806344 | tf_op jit(solution)/shard_map/ppermute | solution.py:586
  339.1 38.7 %collective-permute-start.52 = (bf16[2,1176,128]{2,1,0:T(8,128)(2,1)}, bf16[2,1176,128]{2,1,0:T(8,128)(2,1)}, u32[]{:S(2)}, u32[]{:S(2)}) collective-permute-start(bf16[2,1176,128]{2,1,0:T(8,128)(2,1)} %pad_maximum_fusion.8), channel_id=1, source_target_pairs={{0,1},{1,0},{2,3},{3,2},{4,5},{5,4},{6,7},{7,6},{8,9},{9,8},{10,11... | collective-permute-start | bytes 1806344 | tf_op jit(solution)/shard_map/ppermute | solution.py:586
  377.8 39.4 %collective-permute-start.58 = (bf16[2,1176,128]{2,1,0:T(8,128)(2,1)}, bf16[2,1176,128]{2,1,0:T(8,128)(2,1)S(1)}, u32[]{:S(2)}, u32[]{:S(2)}) collective-permute-start(bf16[2,1176,128]{2,1,0:T(8,128)(2,1)} %get-tuple-element.926), channel_id=1, source_target_pairs={{0,4},{1,5},{2,6},{3,7},{4,0},{5,1},{6,2},{7,3},{8,12},{9,13},{10,... | collective-permute-start | bytes 1806344 | tf_op jit(solution)/shard_map/ppermute | solution.py:586
  393.0 39.9 %collective-permute-start.59 = (bf16[14,168,128]{2,1,0:T(8,128)(2,1)}, bf16[14,168,128]{2,1,0:T(8,128)(2,1)S(1)}, u32[]{:S(2)}, u32[]{:S(2)}) collective-permute-start(bf16[14,168,128]{2,1,0:T(8,128)(2,1)} %get-tuple-element.931), channel_id=1, source_target_pairs={{0,16},{8,24},{16,0},{24,8},{1,17},{9,25},{17,1},{25,9},{2,18},{10... | collective-permute-start | bytes 1806344 | tf_op jit(solution)/shard_map/ppermute | solution.py:586
  394.1 40.5 %collective-permute-start.60 = (bf16[2,1176,128]{2,1,0:T(8,128)(2,1)}, bf16[2,1176,128]{2,1,0:T(8,128)(2,1)S(1)}, u32[]{:S(2)}, u32[]{:S(2)}) collective-permute-start(bf16[2,1176,128]{2,1,0:T(8,128)(2,1)} %get-tuple-element.940), channel_id=1, source_target_pairs={{0,6},{1,7},{2,0},{3,1},{4,2},{5,3},{6,4},{7,5},{8,14},{9,15},{10,... | collective-permute-start | bytes 1806344 | tf_op jit(solution)/shard_map/ppermute | solution.py:586
  395.9 39.3 %collective-permute-start.61 = (bf16[2,1176,128]{2,1,0:T(8,128)(2,1)S(1)}, bf16[2,1176,128]{2,1,0:T(8,128)(2,1)S(1)}, u32[]{:S(2)}, u32[]{:S(2)}) collective-permute-start(bf16[2,1176,128]{2,1,0:T(8,128)(2,1)S(1)} %pad_maximum_fusion.10), channel_id=1, source_target_pairs={{0,1},{1,0},{2,3},{3,2},{4,5},{5,4},{6,7},{7,6},{8,9},{9,8},{10,11... | collective-permute-start | bytes 1806344 | tf_op jit(solution)/shard_map/ppermute | solution.py:586
  436.8 39.7 %collective-permute-start.67 = (bf16[2,1176,128]{2,1,0:T(8,128)(2,1)}, bf16[2,1176,128]{2,1,0:T(8,128)(2,1)S(1)}, u32[]{:S(2)}, u32[]{:S(2)}) collective-permute-start(bf16[2,1176,128]{2,1,0:T(8,128)(2,1)} %get-tuple-element.985), channel_id=1, source_target_pairs={{0,4},{1,5},{2,6},{3,7},{4,0},{5,1},{6,2},{7,3},{8,12},{9,13},{10,... | collective-permute-start | bytes 1806344 | tf_op jit(solution)/shard_map/ppermute | solution.py:586
  450.0 40.1 %collective-permute-start.68 = (bf16[14,168,128]{2,1,0:T(8,128)(2,1)}, bf16[14,168,128]{2,1,0:T(8,128)(2,1)S(1)}, u32[]{:S(2)}, u32[]{:S(2)}) collective-permute-start(bf16[14,168,128]{2,1,0:T(8,128)(2,1)} %get-tuple-element.993), channel_id=1, source_target_pairs={{0,16},{8,24},{16,0},{24,8},{1,17},{9,25},{17,1},{25,9},{2,18},{10... | collective-permute-start | bytes 1806344 | tf_op jit(solution)/shard_map/ppermute | solution.py:586
  452.5 38.8 %collective-permute-start.69 = (bf16[2,1176,128]{2,1,0:T(8,128)(2,1)}, bf16[2,1176,128]{2,1,0:T(8,128)(2,1)S(1)}, u32[]{:S(2)}, u32[]{:S(2)}) collective-permute-start(bf16[2,1176,128]{2,1,0:T(8,128)(2,1)} %get-tuple-element.998), channel_id=1, source_target_pairs={{0,6},{1,7},{2,0},{3,1},{4,2},{5,3},{6,4},{7,5},{8,14},{9,15},{10,... | collective-permute-start | bytes 1806344 | tf_op jit(solution)/shard_map/ppermute | solution.py:586
  455.0 40.8 %collective-permute-start.70 = (bf16[2,1176,128]{2,1,0:T(8,128)(2,1)}, bf16[2,1176,128]{2,1,0:T(8,128)(2,1)S(1)}, u32[]{:S(2)}, u32[]{:S(2)}) collective-permute-start(bf16[2,1176,128]{2,1,0:T(8,128)(2,1)} %pad_maximum_fusion.12), channel_id=1, source_target_pairs={{0,1},{1,0},{2,3},{3,2},{4,5},{5,4},{6,7},{7,6},{8,9},{9,8},{10,11... | collective-permute-start | bytes 1806344 | tf_op jit(solution)/shard_map/ppermute | solution.py:586
  477.8 44.8 %collective-permute-start.72 = (bf16[2,1176,128]{2,1,0:T(8,128)(2,1)}, bf16[2,1176,128]{2,1,0:T(8,128)(2,1)S(1)}, u32[]{:S(2)}, u32[]{:S(2)}) collective-permute-start(bf16[2,1176,128]{2,1,0:T(8,128)(2,1)} %get-tuple-element.1023), channel_id=1, source_target_pairs={{0,2},{1,3},{2,4},{3,5},{4,6},{5,7},{6,0},{7,1},{8,10},{9,11},{10,... | collective-permute-start | bytes 1806344 | tf_op jit(solution)/shard_map/ppermute | solution.py:586
  491.3 41.5 %collective-permute-start.74 = (bf16[2,1176,128]{2,1,0:T(8,128)(2,1)}, bf16[2,1176,128]{2,1,0:T(8,128)(2,1)S(1)}, u32[]{:S(2)}, u32[]{:S(2)}) collective-permute-start(bf16[2,1176,128]{2,1,0:T(8,128)(2,1)} %get-tuple-element.1034), channel_id=1, source_target_pairs={{0,4},{1,5},{2,6},{3,7},{4,0},{5,1},{6,2},{7,3},{8,12},{9,13},{10,... | collective-permute-start | bytes 1806344 | tf_op jit(solution)/shard_map/ppermute | solution.py:586
  496.7 49.5 %collective-permute-start.75 = (bf16[2,1176,128]{2,1,0:T(8,128)(2,1)}, bf16[2,1176,128]{2,1,0:T(8,128)(2,1)S(1)}, u32[]{:S(2)}, u32[]{:S(2)}) collective-permute-start(bf16[2,1176,128]{2,1,0:T(8,128)(2,1)} %get-tuple-element.1038), channel_id=1, source_target_pairs={{0,6},{1,7},{2,0},{3,1},{4,2},{5,3},{6,4},{7,5},{8,14},{9,15},{10,... | collective-permute-start | bytes 1806344 | tf_op jit(solution)/shard_map/ppermute | solution.py:586
  498.0 48.2 %collective-permute-start.76 = (bf16[2,1176,128]{2,1,0:T(8,128)(2,1)S(1)}, bf16[2,1176,128]{2,1,0:T(8,128)(2,1)S(1)}, u32[]{:S(2)}, u32[]{:S(2)}) collective-permute-start(bf16[2,1176,128]{2,1,0:T(8,128)(2,1)S(1)} %pad_maximum_fusion.14), channel_id=1, source_target_pairs={{0,1},{1,0},{2,3},{3,2},{4,5},{5,4},{6,7},{7,6},{8,9},{9,8},{10,11... | collective-permute-start | bytes 1806344 | tf_op jit(solution)/shard_map/ppermute | solution.py:586
  567.3 39.4 %collective-permute-start.81 = (bf16[2,1176,128]{2,1,0:T(8,128)(2,1)}, bf16[2,1176,128]{2,1,0:T(8,128)(2,1)S(1)}, u32[]{:S(2)}, u32[]{:S(2)}) collective-permute-start(bf16[2,1176,128]{2,1,0:T(8,128)(2,1)} %pad_maximum_fusion.16), channel_id=1, source_target_pairs={{0,1},{1,0},{2,3},{3,2},{4,5},{5,4},{6,7},{7,6},{8,9},{9,8},{10,11... | collective-permute-start | bytes 1806344 | tf_op jit(solution)/shard_map/ppermute | solution.py:586
  (154 other events, 3489.0 us)

commit v6 on v5

--- a/solution.py
+++ b/solution.py
@@ -137,23 +137,26 @@
     main = rows // 16 * 16
     left = rows - main
     halves = [out.at[i] for out in outs for i in range(out.shape[0])]
-    for part, out in enumerate(halves):
-        first = scalars[n_x + part]
+    groups = halves[0].shape[0]
+    per = share // groups
+    for part, at_group in [(p, g) for p in range(len(halves)) for g in range(groups)]:
+        out = halves[part].at[at_group]
+        first = scalars[n_x + part] + at_group * per
 
         def one_row(i, _):
             picked = wide[pl.ds(first + i, main, stride=rank), :]
             out[pl.ds(pl.multiple_of(i * main, 16), main), :] = picked.astype(jnp.bfloat16)
             return 0
 
-        lax.fori_loop(0, share, one_row, 0, unroll=6)
-        for group in range(0, share if left else 0, 4):
-            count = min(4, share - group)
+        lax.fori_loop(0, per, one_row, 0, unroll=7)
+        for four in range(0, per if left else 0, 4):
+            count = min(4, per - four)
             tile = [
-                wide[pl.ds(main * rank + first + group + k, left, stride=rank), :]
+                wide[pl.ds(main * rank + first + four + k, left, stride=rank), :]
                 for k in range(count)
             ]
             tile = jnp.concatenate(tile, axis=0).astype(jnp.bfloat16)
-            at = share * main + group * left
+            at = per * main + four * left
             out[at : at + count * left, :] = tile
     for copy in packing:
         copy.wait()
@@ -181,7 +184,8 @@
             chunk, following, n_x, rank, share, scalars, fields, near, got, factor, outs, sends, own, other, wide, sems
         )
 
-    shape = (1 if apart else 2, share * rows, LANES)
+    groups = column_groups(share)
+    shape = (1 if apart else 2, groups, share // groups * rows, LANES)
     shapes = [jax.ShapeDtypeStruct(shape, jnp.bfloat16)] * n_outs
     if following is not None:
         shapes += send_shapes(following, n_x, depth)
@@ -205,15 +209,23 @@
     return outs[:n_outs], outs[n_outs:]
 
 
+def column_groups(share):
+    return 3 if share % 6 == 0 else 1
+
+
 def block_pairs(whole):
     return [(i, j) for i in range(0, whole, STEP) for j in range(i, whole, STEP)]
 
 
-def gram_kernel(pieces, share, places, blocks, carried, out, fibres):
+def gram_kernel(pieces, per, places, blocks, carried, out, fibres):
     whole = fibres.shape[0]
     rows = pieces[0][1]
     main = rows // 16 * 16
     left = rows - main
+
+    @pl.when(pl.program_id(0) == 0)
+    def _():
+        out[...] = jnp.zeros_like(out) if carried is None else carried[...]
 
     for place, block in zip(places, blocks):
         base = pl.multiple_of(place, 16)
@@ -225,10 +237,10 @@
             ]
             return 0
 
-        lax.fori_loop(0, share, one_row, 0, unroll=6)
-        for group in range(0, share if left else 0, 4):
-            count = min(4, share - group)
-            at = share * main + group * left
+        lax.fori_loop(0, per, one_row, 0, unroll=7)
+        for group in range(0, per if left else 0, 4):
+            count = min(4, per - group)
+            at = per * main + group * left
             tile = block[at : at + count * left, :].astype(jnp.float32)
             for k in range(count):
                 part = tile[k * left : (k + 1) * left, :]
@@ -238,17 +250,16 @@
                 ] = part.astype(jnp.bfloat16)
 
     at = 0
-    for i, j in block_pairs(whole):
+    for i in range(0, whole, STEP):
         product = lax.dot_general(
             fibres[i : i + STEP, :],
-            fibres[j : j + STEP, :],
+            fibres[i:, :],
             (((1,), (1,)), ((), ())),
             preferred_element_type=jnp.float32,
         )
-        if carried is not None:
-            product = product + carried[at : at + STEP, :]
-        out[at : at + STEP, :] = product
-        at += STEP
+        for j in range(0, whole - i, STEP):
+            out[at : at + STEP, :] = out[at : at + STEP, :] + product[:, j : j + STEP]
+            at += STEP
 
 
 def gram(arrivals, carried, sources, pieces, share):
@@ -256,36 +267,36 @@
     whole = sources.shape[0] * pitch
     entries = [(i, places) for i, piece in enumerate(arrivals) for _, places in piece]
     inputs = [block for piece in arrivals for block, _ in piece]
-    size = inputs[0].shape[1]
+    groups, size = inputs[0].shape[1:3]
 
     def body(sources, *rest):
         blocks, starts = [], []
         for ref, (i, places) in zip(rest, entries):
             for k, (dz, dy) in enumerate(places):
-                blocks.append(ref.at[k])
+                blocks.append(ref.at[k, 0])
                 starts.append(sources[2 * dz + dy] * pitch + i * SUB)
         if carried is None:
             out, fibres = rest[len(inputs) :]
             before = None
         else:
             before, out, fibres = rest[len(inputs) :]
-        gram_kernel(pieces, share, starts, blocks, before, out, fibres)
+        gram_kernel(pieces, share // groups, starts, blocks, before, out, fibres)
 
     specs = [
-        pl.BlockSpec((len(places), size, LANES), lambda i: (0, 0, 0)) for _, places in entries
+        pl.BlockSpec((len(places), 1, size, LANES), lambda g: (0, g, 0, 0)) for _, places in entries
     ]
     shape = (len(block_pairs(whole)) * STEP, STEP)
-    square = pl.BlockSpec(shape, lambda i: (0, 0))
+    square = pl.BlockSpec(shape, lambda g: (0, 0))
     extra = [] if carried is None else [carried]
     return pl.pallas_call(
         body,
-        grid=(1,),
+        grid=(groups,),
         out_shape=jax.ShapeDtypeStruct(shape, jnp.float32),
         in_specs=[pl.BlockSpec(memory_space=pltpu.SMEM)]
         + specs
         + [square] * len(extra),
         out_specs=square,
-        scratch_shapes=[pltpu.VMEM((whole, share * LANES), jnp.bfloat16)],
+        scratch_shapes=[pltpu.VMEM((whole, share // groups * LANES), jnp.bfloat16)],
         compiler_params=pltpu.CompilerParams(vmem_limit_bytes=VMEM_BYTES),
         cost_estimate=pl.CostEstimate(flops=0, bytes_accessed=0, transcendentals=0),
         name="gram",
@@ -643,18 +654,18 @@
         steps = []
         for i, place in enumerate(shifts if last else shifts[::2]):
             if i:
-                steps.append(((i - 0.9) / (len(outs) - 1), 0, i))
+                steps.append((((i if last else [1, 3, 2][i - 1]) - (3.5 if k == 0 else 0.9)) / (len(outs) - 1), 0, i))
         for j in range(slow // 2 if k else 0):
             steps.append(((j + 0.5) / (slow // 2), 1, j))
         slots = [None] * len(sends)
         for i in range(len(sends)):
-            steps.append(((i + 0.3) / len(sends), 2, i))
-        landed = [(outs[0], ((0, 0),))]
+            steps.append(((i + 1.2) / len(sends), 2, i))
+        landed = [(outs[0], ((0, 0),))] + [None] * (len(outs) - 1)
         arrived.append(landed)
         for _, kind, i in sorted(steps):
             if kind == 0:
                 shift = shifts[i] if last else shifts[2 * i]
-                landed.append((start_y(shift, outs[i]), (shift,)))
+                landed[i] = (start_y(shift, outs[i]), (shift,))
             elif kind == 1:
                 cross(k - 1, i)
             else:

time: 732 us -> 705 us (0.963)
  starting transfers between devices: 215 us -> 180 us
  waiting for transfers between devices: 274 us -> 287 us
    ppermute x86, starting transfers between devices: 194 us -> 166 us  [start(): flown.append(lax.ppermute(operand, axis, pairs))]
    ppermute x86, waiting for transfers between devices: 238 us -> 248 us  [start(): flown.append(lax.ppermute(operand, axis, pairs))]
  transfers between devices with their start and end apart: 98 -> 98, of which waited for: 48 -> 44; matrix products, arithmetic and copies ran while one was open for 3% -> 3% of each run, Pallas kernels for 20% -> 20%
where the time goes in v6:
time: 705 us; the launch traced here: 701 us
  waiting for transfers between devices  287 us (41%)
  Pallas kernels  201 us (29%)
  starting transfers between devices  180 us (26%)
  local copies, waits for them, and re-layouts  15.2 us (2%)
  other arithmetic  7.95 us (1%)
  matrix products  7.31 us (1%)
    ppermute x86, waiting for transfers between devices, start(): flown.append(lax.ppermute(operand, axis, pairs))  248 us
    ppermute x86, starting transfers between devices, start(): flown.append(lax.ppermute(operand, axis, pairs))  166 us
    pallas_call x9, Pallas kernels, project(): pl.pallas_call(body, out_shape=shapes, in_specs=[pl.BlockSpec(memory_spac...  99.3 us
    pallas_call x1, Pallas kernels, cholesky_rows(): pl.pallas_call(functools.partial(cholesky_kernel, slab), out_shape=jax.Sh...  42.8 us
    pallas_call x3, Pallas kernels, gram(): pl.pallas_call(body, grid=(groups,), out_shape=jax.ShapeDtypeStruct(shape...  37.8 us
    ppermute x6, waiting for transfers between devices, swap(): return lax.ppermute(value, axis, flips)  32.1 us
    pallas_call x5, Pallas kernels, run_pack(): pl.pallas_call(body, out_shape=shapes, in_specs=[pl.BlockSpec(memory_spac...  21.2 us
  transfers between devices with their start and end apart: 98, of which 44 were waited for; matrix products, arithmetic and copies ran while one was open for 3% of the time, Pallas kernels for 20%

profile of v6, /device:TPU:0, one launch (start us, length us, event | category | flops | bytes accessed | tf_op | source)
XLA Modules:
  0.0 700.6 jit_solution(2034928063596293067)
XLA Ops:
  39.7 10.8 %collective-permute-done.2.rest_2_ = bf16[14,168,128]{2,1,0:T(8,128)(2,1)S(1)} collective-permute-done((bf16[14,168,128]{2,1,0:T(8,128)(2,1)S(1)}, bf16[14,168,128]{2,1,0:T(8,128)(2,1)S(1)}, u32[]{:S(2)}, u32[]{:S(2)}) %collective-permute-start.2) | collective-permute-done | bytes 602144 | tf_op jit(solution)/shard_map/ppermute | solution.py:597
  52.2 10.4 %collective-permute-done.3.rest_3_ = bf16[14,168,128]{2,1,0:T(8,128)(2,1)S(1)} collective-permute-done((bf16[14,168,128]{2,1,0:T(8,128)(2,1)S(1)}, bf16[14,168,128]{2,1,0:T(8,128)(2,1)S(1)}, u32[]{:S(2)}, u32[]{:S(2)}) %collective-permute-start.3) | collective-permute-done | bytes 602144 | tf_op jit(solution)/shard_map/ppermute | solution.py:597
  67.0 11.2 %project.9 = (bf16[2,3,392,128]{3,2,1,0:T(8,128)(2,1)}, bf16[2,3,392,128]{3,2,1,0:T(8,128)(2,1)}, bf16[2,3,392,128]{3,2,1,0:T(8,128)(2,1)}, bf16[2,3,392,128]{3,...) custom-call(s32[12]{0:T(128)} %stack.150.scalars, ...), custom_call_target="tpu_custom_call" | custom-call | tf_op jit(solution)/shard_map/project/pallas_call | solution.py:192
  103.9 10.4 %collective-permute-done.10.rest_3_ = bf16[14,168,128]{2,1,0:T(8,128)(2,1)} collective-permute-done((bf16[14,168,128]{2,1,0:T(8,128)(2,1)}, bf16[14,168,128]{2,1,0:T(8,128)(2,1)}, u32[]{:S(2)}, u32[]{:S(2)}) %collective-permute-start.10) | collective-permute-done | bytes 602144 | tf_op jit(solution)/shard_map/ppermute | solution.py:597
  116.9 7.3 %select_add_fusion.rest_5_.before = f32[768,768]{1,0:T(8,128)} fusion(f32[672,768]{0,1:T(8,128)S(1)} %bitcast.91, f32[768]{0:T(1024)S(1)} %fusion.6), kind=kOutput, calls=%fused_computation | convolution fusion | flops 4758110208 | bytes 4426752 | tf_op jit(solution)/shard_map/dot_general | solution.py:367
  124.2 11.1 %project.10 = (bf16[2,3,392,128]{3,2,1,0:T(8,128)(2,1)}, bf16[2,3,392,128]{3,2,1,0:T(8,128)(2,1)}, bf16[2,3,392,128]{3,2,1,0:T(8,128)(2,1)}, bf16[2,3,392,128]{3...) custom-call(s32[12]{0:T(128)} %stack.150.scalars, ...), custom_call_target="tpu_custom_call" | custom-call | tf_op jit(solution)/shard_map/project/pallas_call | solution.py:192
  135.6 7.7 %collective-permute-start.18 = (bf16[2,3,392,128]{3,2,1,0:T(8,128)(2,1)}, bf16[2,3,392,128]{3,2,1,0:T(8,128)(2,1)S(1)}, u32[]{:S(2)}, u32[]{:S(2)}) collective-permute-start(bf16[2,3,392,128]{3,2,1,0:T(8,128)(2,1)} %get-tuple-element.647), channel_id=1, source_target_pairs={{0,2},{1,3},{2,4},{3,5},{4,6},{5,7},{6,0},{7,1},{8,10},{9,11},{10,... | collective-permute-start | bytes 1806344 | tf_op jit(solution)/shard_map/ppermute | solution.py:597
  145.4 8.3 %collective-permute-done.16.rest_2_ = bf16[14,168,128]{2,1,0:T(8,128)(2,1)S(1)} collective-permute-done((bf16[14,168,128]{2,1,0:T(8,128)(2,1)}, bf16[14,168,128]{2,1,0:T(8,128)(2,1)S(1)}, u32[]{:S(2)}, u32[]{:S(2)}) %collective-permute-start.16) | collective-permute-done | bytes 602144 | tf_op jit(solution)/shard_map/ppermute | solution.py:597
  157.7 8.2 %collective-permute-done.17.rest_3_ = bf16[14,168,128]{2,1,0:T(8,128)(2,1)S(1)} collective-permute-done((bf16[14,168,128]{2,1,0:T(8,128)(2,1)S(1)}, bf16[14,168,128]{2,1,0:T(8,128)(2,1)S(1)}, u32[]{:S(2)}, u32[]{:S(2)}) %collective-permute-start.17) | collective-permute-done | bytes 602144 | tf_op jit(solution)/shard_map/ppermute | solution.py:597
  181.3 11.4 %project.11 = (bf16[2,3,392,128]{3,2,1,0:T(8,128)(2,1)}, bf16[2,3,392,128]{3,2,1,0:T(8,128)(2,1)}, bf16[2,3,392,128]{3,2,1,0:T(8,128)(2,1)}, bf16[2,3,392,128]{3...) custom-call(s32[12]{0:T(128)} %stack.150.scalars, ...), custom_call_target="tpu_custom_call" | custom-call | tf_op jit(solution)/shard_map/project/pallas_call | solution.py:192
  198.1 15.5 %collective-permute-start.29 = (bf16[14,168,128]{2,1,0:T(8,128)(2,1)S(1)}, bf16[14,168,128]{2,1,0:T(8,128)(2,1)S(1)}, u32[]{:S(2)}, u32[]{:S(2)}) collective-permute-start(bf16[14,168,128]{2,1,0:T(8,128)(2,1)S(1)} %copy-done.79), channel_id=1, source_target_pairs={{0,16},{8,24},{16,0},{24,8},{1,17},{9,25},{17,1},{25,9},{2,18},{10... | collective-permute-start | bytes 1806344 | tf_op jit(solution)/shard_map/ppermute | solution.py:597
  232.9 11.3 %project.12 = (bf16[2,3,392,128]{3,2,1,0:T(8,128)(2,1)}, bf16[2,3,392,128]{3,2,1,0:T(8,128)(2,1)}, bf16[2,3,392,128]{3,2,1,0:T(8,128)(2,1)}, bf16[2,3,392,128]{3...) custom-call(s32[12]{0:T(128)} %stack.150.scalars, ...), custom_call_target="tpu_custom_call" | custom-call | tf_op jit(solution)/shard_map/project/pallas_call | solution.py:192
  261.6 7.6 %collective-permute-done.35.rest_3_ = bf16[14,168,128]{2,1,0:T(8,128)(2,1)S(1)} collective-permute-done((bf16[14,168,128]{2,1,0:T(8,128)(2,1)}, bf16[14,168,128]{2,1,0:T(8,128)(2,1)S(1)}, u32[]{:S(2)}, u32[]{:S(2)}) %collective-permute-start.35) | collective-permute-done | bytes 602144 | tf_op jit(solution)/shard_map/ppermute | solution.py:597
  284.5 11.4 %project.13 = (bf16[2,3,392,128]{3,2,1,0:T(8,128)(2,1)}, bf16[2,3,392,128]{3,2,1,0:T(8,128)(2,1)}, bf16[2,3,392,128]{3,2,1,0:T(8,128)(2,1)}, bf16[2,3,392,128]{3...) custom-call(s32[12]{0:T(128)} %stack.150.scalars, ...), custom_call_target="tpu_custom_call" | custom-call | tf_op jit(solution)/shard_map/project/pallas_call | solution.py:192
  297.7 16.9 %collective-permute-done.41.rest_2_ = bf16[2,3,392,128]{3,2,1,0:T(8,128)(2,1)S(1)} collective-permute-done((bf16[2,3,392,128]{3,2,1,0:T(8,128)(2,1)}, bf16[2,3,392,128]{3,2,1,0:T(8,128)(2,1)S(1)}, u32[]{:S(2)}, u32[]{:S(2)}) %collective-permute-start.41) | collective-permute-done | bytes 602144 | tf_op jit(solution)/shard_map/ppermute | solution.py:597
  336.8 12.3 %gram.3.rest_5_.rest_18_ = f32[1536,256]{1,0:T(8,128)} custom-call(s32[8]{0:T(128)} %stack.137.sources, bf16[2,3,392,128]{3,2,1,0:T(8,128)(2,1)} %get-tuple-element.619.rest_0_, bf16[2,3,392,128]{3,2,1,0:T(8,128)(2,1)} %copy-done.21, bf16[2,3,392,128]{3,2,1,0:T(8,128)(2,1)} %collective-permute-done.13.rest_2_, ...), custom_call_target="tpu_custom_call" | custom-call | tf_op jit(solution)/shard_map/gram/pallas_call | solution.py:291
  349.1 11.1 %project.14 = (bf16[2,3,392,128]{3,2,1,0:T(8,128)(2,1)}, bf16[2,3,392,128]{3,2,1,0:T(8,128)(2,1)}, bf16[2,3,392,128]{3,2,1,0:T(8,128)(2,1)}, bf16[2,3,392,128]{3...) custom-call(s32[12]{0:T(128)} %stack.150.scalars, ...), custom_call_target="tpu_custom_call" | custom-call | tf_op jit(solution)/shard_map/project/pallas_call | solution.py:192
  360.2 9.2 %collective-permute-start.54 = (bf16[2,3,392,128]{3,2,1,0:T(8,128)(2,1)}, bf16[2,3,392,128]{3,2,1,0:T(8,128)(2,1)S(1)}, u32[]{:S(2)}, u32[]{:S(2)}) collective-permute-start(bf16[2,3,392,128]{3,2,1,0:T(8,128)(2,1)} %get-tuple-element.897), channel_id=1, source_target_pairs={{0,2},{1,3},{2,4},{3,5},{4,6},{5,7},{6,0},{7,1},{8,10},{9,11},{10,... | collective-permute-start | bytes 1806344 | tf_op jit(solution)/shard_map/ppermute | solution.py:597
  373.6 10.1 %collective-permute-done.54.rest_13_ = bf16[2,3,392,128]{3,2,1,0:T(8,128)(2,1)S(1)} collective-permute-done((bf16[2,3,392,128]{3,2,1,0:T(8,128)(2,1)}, bf16[2,3,392,128]{3,2,1,0:T(8,128)(2,1)S(1)}, u32[]{:S(2)}, u32[]{:S(2)}) %collective-permute-start.54) | collective-permute-done | bytes 602144 | tf_op jit(solution)/shard_map/ppermute | solution.py:597
  387.5 9.0 %collective-permute-done.57.rest_15_ = bf16[2,3,392,128]{3,2,1,0:T(8,128)(2,1)S(1)} collective-permute-done((bf16[2,3,392,128]{3,2,1,0:T(8,128)(2,1)S(1)}, bf16[2,3,392,128]{3,2,1,0:T(8,128)(2,1)S(1)}, u32[]{:S(2)}, u32[]{:S(2)}) %collective-permute-start.57) | collective-permute-done | bytes 602144 | tf_op jit(solution)/shard_map/ppermute | solution.py:597
  397.4 11.1 %project.15 = (bf16[2,3,392,128]{3,2,1,0:T(8,128)(2,1)}, bf16[2,3,392,128]{3,2,1,0:T(8,128)(2,1)}, bf16[2,3,392,128]{3,2,1,0:T(8,128)(2,1)}, bf16[2,3,392,128]{3...) custom-call(s32[12]{0:T(128)} %stack.150.scalars, ...), custom_call_target="tpu_custom_call" | custom-call | tf_op jit(solution)/shard_map/project/pallas_call | solution.py:192
  408.8 21.5 %collective-permute-done.59.rest_14_ = bf16[2,3,392,128]{3,2,1,0:T(8,128)(2,1)S(1)} collective-permute-done((bf16[2,3,392,128]{3,2,1,0:T(8,128)(2,1)}, bf16[2,3,392,128]{3,2,1,0:T(8,128)(2,1)S(1)}, u32[]{:S(2)}, u32[]{:S(2)}) %collective-permute-start.59) | collective-permute-done | bytes 602144 | tf_op jit(solution)/shard_map/ppermute | solution.py:597
  433.9 17.8 %collective-permute-start.68 = (bf16[2,3,392,128]{3,2,1,0:T(8,128)(2,1)}, bf16[2,3,392,128]{3,2,1,0:T(8,128)(2,1)S(1)}, u32[]{:S(2)}, u32[]{:S(2)}) collective-permute-start(bf16[2,3,392,128]{3,2,1,0:T(8,128)(2,1)} %get-tuple-element.991), channel_id=1, source_target_pairs={{0,4},{1,5},{2,6},{3,7},{4,0},{5,1},{6,2},{7,3},{8,12},{9,13},{10,... | collective-permute-start | bytes 1806344 | tf_op jit(solution)/shard_map/ppermute | solution.py:597
  454.1 10.5 %project.16 = (bf16[2,3,392,128]{3,2,1,0:T(8,128)(2,1)}, bf16[2,3,392,128]{3,2,1,0:T(8,128)(2,1)}, bf16[2,3,392,128]{3,2,1,0:T(8,128)(2,1)}, bf16[2,3,392,128]{3,2,1,0:T(8,128)(2,1)}) custom-call(s32[12]{0:T(128)} %stack.150.scalars, bf16[84,168,1536]{2,1,0:T(8,128)(2,1)} %bitcast.89, bf16[84,168,128]{2,1,0:T(8,128)(2,1)} %collective-permute-done.6.near, ...), custom_call_target="tpu_custom_call" | custom-call | tf_op jit(solution)/shard_map/project/pallas_call | solution.py:192
  466.3 25.2 %collective-permute-done.68.rest_2_ = bf16[2,3,392,128]{3,2,1,0:T(8,128)(2,1)S(1)} collective-permute-done((bf16[2,3,392,128]{3,2,1,0:T(8,128)(2,1)}, bf16[2,3,392,128]{3,2,1,0:T(8,128)(2,1)S(1)}, u32[]{:S(2)}, u32[]{:S(2)}) %collective-permute-start.68) | collective-permute-done | bytes 602144 | tf_op jit(solution)/shard_map/ppermute | solution.py:597
  495.9 12.8 %gram.4.rest_5_.rest_20_ = f32[1536,256]{1,0:T(8,128)} custom-call(s32[8]{0:T(128)} %stack.137.sources, bf16[2,3,392,128]{3,2,1,0:T(8,128)(2,1)} %get-tuple-element.792.rest_0_, bf16[2,3,392,128]{3,2,1,0:T(8,128)(2,1)} %copy-done.2, bf16[2,3,392,128]{3,2,1,0:T(8,128)(2,1)} %copy-done.4, bf16[2,3,392,128]{3,2,1,0:T(8,128)(2,1)} %copy-done.3, ...), custom_call_target="tpu_custom_call" | custom-call | tf_op jit(solution)/shard_map/gram/pallas_call | solution.py:291
  508.7 10.3 %project.17 = (bf16[1,3,392,128]{3,2,1,0:T(8,128)(2,1)}, bf16[1,3,392,128]{3,2,1,0:T(8,128)(2,1)}, bf16[1,3,392,128]{3,2,1,0:T(8,128)(2,1)}, bf16[1,3,392,128]{3...) custom-call(s32[12]{0:T(128)} %stack.150.scalars, ...), custom_call_target="tpu_custom_call" | custom-call | tf_op jit(solution)/shard_map/project/pallas_call | solution.py:192
  523.3 14.0 %collective-permute-done.75.rest_8_ = bf16[2,3,392,128]{3,2,1,0:T(8,128)(2,1)S(1)} collective-permute-done((bf16[2,3,392,128]{3,2,1,0:T(8,128)(2,1)}, bf16[2,3,392,128]{3,2,1,0:T(8,128)(2,1)S(1)}, u32[]{:S(2)}, u32[]{:S(2)}) %collective-permute-start.75) | collective-permute-done | bytes 602144 | tf_op jit(solution)/shard_map/ppermute | solution.py:597
  559.0 17.9 %collective-permute-done.83.rest_17_ = bf16[1,3,392,128]{3,2,1,0:T(8,128)(2,1)} collective-permute-done((bf16[1,3,392,128]{3,2,1,0:T(8,128)(2,1)}, bf16[1,3,392,128]{3,2,1,0:T(8,128)(2,1)}, u32[]{:S(2)}, u32[]{:S(2)}) %collective-permute-start.83) | collective-permute-done | bytes 301088 | tf_op jit(solution)/shard_map/ppermute | solution.py:597
  585.8 12.8 %gram.5 = f32[1536,256]{1,0:T(8,128)} custom-call(s32[8]{0:T(128)} %stack.137.sources, bf16[2,3,392,128]{3,2,1,0:T(8,128)(2,1)} %get-tuple-element.918.rest_0_, bf16[2,3,392,128]{3,2,1,0:T(8,128)(2,1)} %copy-done.10, bf16[2,3,392,128]{3,2,1,0:T(8,128)(2,1)} %copy-done.14, bf16[2,3,392,128]{3,2,1,0:T(8,128)(2,1)} %copy-done.11, ...), custom_call_target="tpu_custom_call" | custom-call | tf_op jit(solution)/shard_map/gram/pallas_call | solution.py:291
  604.5 10.1 %collective-permute-done.87 = f32[384,256]{1,0:T(8,128)S(1)} collective-permute-done((f32[384,256]{1,0:T(8,128)S(1)}, f32[384,256]{1,0:T(8,128)S(1)}, u32[]{:S(2)}, u32[]{:S(2)}) %collective-permute-start.87) | collective-permute-done | bytes 393248 | tf_op jit(solution)/shard_map/ppermute | solution.py:498
  655.7 42.8 %cholesky.1 = f32[96,768]{1,0:T(8,128)} custom-call(s32[1]{0:T(128)} %bitcast.place, f32[1536,256]{1,0:T(8,128)} %maximum_select_fusion.gram_sum, f32[768,768]{1,0:T(8,128)} %select_add_fusion.rest_5_.before), custom_call_target="tpu_custom_call" | custom-call | tf_op jit(solution)/shard_map/cholesky/pallas_call | solution.py:440
  (437 shorter events, 281.1 us)
Async XLA Ops:
  11.9 53.2 %collective-permute-start.4 = (bf16[84,168,128]{2,1,0:T(8,128)(2,1)}, bf16[84,168,128]{2,1,0:T(8,128)(2,1)}, u32[]{:S(2)}, u32[]{:S(2)}) collective-permute-start(bf16[84,168,128]{2,1,0:T(8,128)(2,1)} %pack.9), channel_id=1, source_target_pairs={{0,8},{8,0},{16,24},{24,16},{1,9},{9,1},{17,25},{25,17},{2,10},{10... | collective-permute-start | bytes 10838024 | tf_op jit(solution)/shard_map/ppermute | solution.py:597
  22.1 44.4 %collective-permute-start.5 = (bf16[84,168,128]{2,1,0:T(8,128)(2,1)}, bf16[84,168,128]{2,1,0:T(8,128)(2,1)}, u32[]{:S(2)}, u32[]{:S(2)}) collective-permute-start(bf16[84,168,128]{2,1,0:T(8,128)(2,1)} %pack.7), channel_id=1, source_target_pairs={{0,8},{8,0},{16,24},{24,16},{1,9},{9,1},{17,25},{25,17},{2,10},{10... | collective-permute-start | bytes 10838024 | tf_op jit(solution)/shard_map/ppermute | solution.py:597
  33.5 44.6 %collective-permute-start.6 = (bf16[84,168,128]{2,1,0:T(8,128)(2,1)}, bf16[84,168,128]{2,1,0:T(8,128)(2,1)}, u32[]{:S(2)}, u32[]{:S(2)}) collective-permute-start(bf16[84,168,128]{2,1,0:T(8,128)(2,1)} %pack.6), channel_id=1, source_target_pairs={{0,8},{8,0},{16,24},{24,16},{1,9},{9,1},{17,25},{25,17},{2,10},{10... | collective-permute-start | bytes 10838024 | tf_op jit(solution)/shard_map/ppermute | solution.py:597
  65.1 37.0 %collective-permute-start.9 = (bf16[14,168,128]{2,1,0:T(8,128)(2,1)}, bf16[14,168,128]{2,1,0:T(8,128)(2,1)}, u32[]{:S(2)}, u32[]{:S(2)}) collective-permute-start(bf16[14,168,128]{2,1,0:T(8,128)(2,1)} %get-tuple-element.590), channel_id=1, source_target_pairs={{0,16},{8,24},{16,0},{24,8},{1,17},{9,25},{17,1},{25,9},{2,18},{10... | collective-permute-start | bytes 1806344 | tf_op jit(solution)/shard_map/ppermute | solution.py:597
  66.5 47.8 %collective-permute-start.10 = (bf16[14,168,128]{2,1,0:T(8,128)(2,1)}, bf16[14,168,128]{2,1,0:T(8,128)(2,1)}, u32[]{:S(2)}, u32[]{:S(2)}) collective-permute-start(bf16[14,168,128]{2,1,0:T(8,128)(2,1)} %get-tuple-element.595), channel_id=1, source_target_pairs={{0,24},{8,16},{16,8},{24,0},{1,25},{9,17},{17,9},{25,1},{2,26},{10... | collective-permute-start | bytes 1806344 | tf_op jit(solution)/shard_map/ppermute | solution.py:597
  78.2 36.1 %collective-permute-start.11 = (bf16[2,3,392,128]{3,2,1,0:T(8,128)(2,1)}, bf16[2,3,392,128]{3,2,1,0:T(8,128)(2,1)S(1)}, u32[]{:S(2)}, u32[]{:S(2)}) collective-permute-start(bf16[2,3,392,128]{3,2,1,0:T(8,128)(2,1)} %get-tuple-element.604), channel_id=1, source_target_pairs={{0,2},{1,3},{2,4},{3,5},{4,6},{5,7},{6,0},{7,1},{8,10},{9,11},{10,... | collective-permute-start | bytes 1806344 | tf_op jit(solution)/shard_map/ppermute | solution.py:597
  88.5 47.0 %collective-permute-start.13 = (bf16[2,3,392,128]{3,2,1,0:T(8,128)(2,1)}, bf16[2,3,392,128]{3,2,1,0:T(8,128)(2,1)}, u32[]{:S(2)}, u32[]{:S(2)}) collective-permute-start(bf16[2,3,392,128]{3,2,1,0:T(8,128)(2,1)} %get-tuple-element.623), channel_id=1, source_target_pairs={{0,4},{1,5},{2,6},{3,7},{4,0},{5,1},{6,2},{7,3},{8,12},{9,13},{10,... | collective-permute-start | bytes 1806344 | tf_op jit(solution)/shard_map/ppermute | solution.py:597
  102.2 41.2 %collective-permute-start.14 = (bf16[14,168,128]{2,1,0:T(8,128)(2,1)}, bf16[14,168,128]{2,1,0:T(8,128)(2,1)S(1)}, u32[]{:S(2)}, u32[]{:S(2)}) collective-permute-start(bf16[14,168,128]{2,1,0:T(8,128)(2,1)} %get-tuple-element.627), channel_id=1, source_target_pairs={{0,16},{8,24},{16,0},{24,8},{1,17},{9,25},{17,1},{25,9},{2,18},{10... | collective-permute-start | bytes 1806344 | tf_op jit(solution)/shard_map/ppermute | solution.py:597
  116.6 37.1 %collective-permute-start.16 = (bf16[14,168,128]{2,1,0:T(8,128)(2,1)}, bf16[14,168,128]{2,1,0:T(8,128)(2,1)S(1)}, u32[]{:S(2)}, u32[]{:S(2)}) collective-permute-start(bf16[14,168,128]{2,1,0:T(8,128)(2,1)} %get-tuple-element.637), channel_id=1, source_target_pairs={{0,16},{8,24},{16,0},{24,8},{1,17},{9,25},{17,1},{25,9},{2,18},{10... | collective-permute-start | bytes 1806344 | tf_op jit(solution)/shard_map/ppermute | solution.py:597
  116.9 48.9 %collective-permute-start.17 = (bf16[14,168,128]{2,1,0:T(8,128)(2,1)S(1)}, bf16[14,168,128]{2,1,0:T(8,128)(2,1)S(1)}, u32[]{:S(2)}, u32[]{:S(2)}) collective-permute-start(bf16[14,168,128]{2,1,0:T(8,128)(2,1)S(1)} %copy-done.71), channel_id=1, source_target_pairs={{0,24},{8,16},{16,8},{24,0},{1,25},{9,17},{17,9},{25,1},{2,26},{10... | collective-permute-start | bytes 1806344 | tf_op jit(solution)/shard_map/ppermute | solution.py:597
  181.2 36.3 %collective-permute-start.26 = (bf16[14,168,128]{2,1,0:T(8,128)(2,1)}, bf16[14,168,128]{2,1,0:T(8,128)(2,1)}, u32[]{:S(2)}, u32[]{:S(2)}) collective-permute-start(bf16[14,168,128]{2,1,0:T(8,128)(2,1)} %get-tuple-element.702), channel_id=1, source_target_pairs={{0,24},{8,16},{16,8},{24,0},{1,25},{9,17},{17,9},{25,1},{2,26},{10... | collective-permute-start | bytes 1806344 | tf_op jit(solution)/shard_map/ppermute | solution.py:597
  232.8 36.3 %collective-permute-start.35 = (bf16[14,168,128]{2,1,0:T(8,128)(2,1)}, bf16[14,168,128]{2,1,0:T(8,128)(2,1)S(1)}, u32[]{:S(2)}, u32[]{:S(2)}) collective-permute-start(bf16[14,168,128]{2,1,0:T(8,128)(2,1)} %get-tuple-element.762), channel_id=1, source_target_pairs={{0,24},{8,16},{16,8},{24,0},{1,25},{9,17},{17,9},{25,1},{2,26},{10... | collective-permute-start | bytes 1806344 | tf_op jit(solution)/shard_map/ppermute | solution.py:597
  271.3 43.3 %collective-permute-start.41 = (bf16[2,3,392,128]{3,2,1,0:T(8,128)(2,1)}, bf16[2,3,392,128]{3,2,1,0:T(8,128)(2,1)S(1)}, u32[]{:S(2)}, u32[]{:S(2)}) collective-permute-start(bf16[2,3,392,128]{3,2,1,0:T(8,128)(2,1)} %get-tuple-element.804), channel_id=1, source_target_pairs={{0,4},{1,5},{2,6},{3,7},{4,0},{5,1},{6,2},{7,3},{8,12},{9,13},{10,... | collective-permute-start | bytes 1806344 | tf_op jit(solution)/shard_map/ppermute | solution.py:597
  274.1 42.1 %collective-permute-start.42 = (bf16[2,3,392,128]{3,2,1,0:T(8,128)(2,1)S(1)}, bf16[2,3,392,128]{3,2,1,0:T(8,128)(2,1)S(1)}, u32[]{:S(2)}, u32[]{:S(2)}) collective-permute-start(bf16[2,3,392,128]{3,2,1,0:T(8,128)(2,1)S(1)} %pad_maximum_fusion.6), channel_id=1, source_target_pairs={{0,1},{1,0},{2,3},{3,2},{4,5},{5,4},{6,7},{7,6},{8,9},{9,8},{10,11... | collective-permute-start | bytes 1806344 | tf_op jit(solution)/shard_map/ppermute | solution.py:597
  284.5 36.3 %collective-permute-start.44 = (bf16[14,168,128]{2,1,0:T(8,128)(2,1)}, bf16[14,168,128]{2,1,0:T(8,128)(2,1)S(1)}, u32[]{:S(2)}, u32[]{:S(2)}) collective-permute-start(bf16[14,168,128]{2,1,0:T(8,128)(2,1)} %get-tuple-element.822), channel_id=1, source_target_pairs={{0,24},{8,16},{16,8},{24,0},{1,25},{9,17},{17,9},{25,1},{2,26},{10... | collective-permute-start | bytes 1806344 | tf_op jit(solution)/shard_map/ppermute | solution.py:597
  320.8 39.5 %collective-permute-start.49 = (bf16[14,168,128]{2,1,0:T(8,128)(2,1)}, bf16[14,168,128]{2,1,0:T(8,128)(2,1)}, u32[]{:S(2)}, u32[]{:S(2)}) collective-permute-start(bf16[14,168,128]{2,1,0:T(8,128)(2,1)} %get-tuple-element.865), channel_id=1, source_target_pairs={{0,24},{8,16},{16,8},{24,0},{1,25},{9,17},{17,9},{25,1},{2,26},{10... | collective-permute-start | bytes 1806344 | tf_op jit(solution)/shard_map/ppermute | solution.py:597
  322.9 46.6 %collective-permute-start.50 = (bf16[2,3,392,128]{3,2,1,0:T(8,128)(2,1)}, bf16[2,3,392,128]{3,2,1,0:T(8,128)(2,1)S(1)}, u32[]{:S(2)}, u32[]{:S(2)}) collective-permute-start(bf16[2,3,392,128]{3,2,1,0:T(8,128)(2,1)} %get-tuple-element.871), channel_id=1, source_target_pairs={{0,4},{1,5},{2,6},{3,7},{4,0},{5,1},{6,2},{7,3},{8,12},{9,13},{10,... | collective-permute-start | bytes 1806344 | tf_op jit(solution)/shard_map/ppermute | solution.py:597
  330.1 39.8 %collective-permute-start.51 = (bf16[2,3,392,128]{3,2,1,0:T(8,128)(2,1)}, bf16[2,3,392,128]{3,2,1,0:T(8,128)(2,1)}, u32[]{:S(2)}, u32[]{:S(2)}) collective-permute-start(bf16[2,3,392,128]{3,2,1,0:T(8,128)(2,1)} %pad_maximum_fusion.8), channel_id=1, source_target_pairs={{0,1},{1,0},{2,3},{3,2},{4,5},{5,4},{6,7},{7,6},{8,9},{9,8},{10,11... | collective-permute-start | bytes 1806344 | tf_op jit(solution)/shard_map/ppermute | solution.py:597
  334.3 36.8 %collective-permute-start.52 = (bf16[14,168,128]{2,1,0:T(8,128)(2,1)}, bf16[14,168,128]{2,1,0:T(8,128)(2,1)}, u32[]{:S(2)}, u32[]{:S(2)}) collective-permute-start(bf16[14,168,128]{2,1,0:T(8,128)(2,1)} %get-tuple-element.884), channel_id=1, source_target_pairs={{0,16},{8,24},{16,0},{24,8},{1,17},{9,25},{17,1},{25,9},{2,18},{10... | collective-permute-start | bytes 1806344 | tf_op jit(solution)/shard_map/ppermute | solution.py:597
  371.5 37.0 %collective-permute-start.58 = (bf16[14,168,128]{2,1,0:T(8,128)(2,1)}, bf16[14,168,128]{2,1,0:T(8,128)(2,1)}, u32[]{:S(2)}, u32[]{:S(2)}) collective-permute-start(bf16[14,168,128]{2,1,0:T(8,128)(2,1)} %get-tuple-element.926), channel_id=1, source_target_pairs={{0,24},{8,16},{16,8},{24,0},{1,25},{9,17},{17,9},{25,1},{2,26},{10... | collective-permute-start | bytes 1806344 | tf_op jit(solution)/shard_map/ppermute | solution.py:597
  383.7 46.5 %collective-permute-start.59 = (bf16[2,3,392,128]{3,2,1,0:T(8,128)(2,1)}, bf16[2,3,392,128]{3,2,1,0:T(8,128)(2,1)S(1)}, u32[]{:S(2)}, u32[]{:S(2)}) collective-permute-start(bf16[2,3,392,128]{3,2,1,0:T(8,128)(2,1)} %get-tuple-element.932), channel_id=1, source_target_pairs={{0,4},{1,5},{2,6},{3,7},{4,0},{5,1},{6,2},{7,3},{8,12},{9,13},{10,... | collective-permute-start | bytes 1806344 | tf_op jit(solution)/shard_map/ppermute | solution.py:597
  385.9 45.9 %collective-permute-start.60 = (bf16[2,3,392,128]{3,2,1,0:T(8,128)(2,1)S(1)}, bf16[2,3,392,128]{3,2,1,0:T(8,128)(2,1)S(1)}, u32[]{:S(2)}, u32[]{:S(2)}) collective-permute-start(bf16[2,3,392,128]{3,2,1,0:T(8,128)(2,1)S(1)} %pad_maximum_fusion.10), channel_id=1, source_target_pairs={{0,1},{1,0},{2,3},{3,2},{4,5},{5,4},{6,7},{7,6},{8,9},{9,8},{10,11... | collective-permute-start | bytes 1806344 | tf_op jit(solution)/shard_map/ppermute | solution.py:597
  386.4 46.2 %collective-permute-start.61 = (bf16[14,168,128]{2,1,0:T(8,128)(2,1)}, bf16[14,168,128]{2,1,0:T(8,128)(2,1)S(1)}, u32[]{:S(2)}, u32[]{:S(2)}) collective-permute-start(bf16[14,168,128]{2,1,0:T(8,128)(2,1)} %get-tuple-element.945), channel_id=1, source_target_pairs={{0,16},{8,24},{16,0},{24,8},{1,17},{9,25},{17,1},{25,9},{2,18},{10... | collective-permute-start | bytes 1806344 | tf_op jit(solution)/shard_map/ppermute | solution.py:597
  396.6 36.1 %collective-permute-start.62 = (bf16[14,168,128]{2,1,0:T(8,128)(2,1)}, bf16[14,168,128]{2,1,0:T(8,128)(2,1)}, u32[]{:S(2)}, u32[]{:S(2)}) collective-permute-start(bf16[14,168,128]{2,1,0:T(8,128)(2,1)} %get-tuple-element.950), channel_id=1, source_target_pairs={{0,24},{8,16},{16,8},{24,0},{1,25},{9,17},{17,9},{25,1},{2,26},{10... | collective-permute-start | bytes 1806344 | tf_op jit(solution)/shard_map/ppermute | solution.py:597
  433.9 57.6 %collective-permute-start.68 = (bf16[2,3,392,128]{3,2,1,0:T(8,128)(2,1)}, bf16[2,3,392,128]{3,2,1,0:T(8,128)(2,1)S(1)}, u32[]{:S(2)}, u32[]{:S(2)}) collective-permute-start(bf16[2,3,392,128]{3,2,1,0:T(8,128)(2,1)} %get-tuple-element.991), channel_id=1, source_target_pairs={{0,4},{1,5},{2,6},{3,7},{4,0},{5,1},{6,2},{7,3},{8,12},{9,13},{10,... | collective-permute-start | bytes 1806344 | tf_op jit(solution)/shard_map/ppermute | solution.py:597
  452.6 39.3 %collective-permute-start.69 = (bf16[2,3,392,128]{3,2,1,0:T(8,128)(2,1)}, bf16[2,3,392,128]{3,2,1,0:T(8,128)(2,1)}, u32[]{:S(2)}, u32[]{:S(2)}) collective-permute-start(bf16[2,3,392,128]{3,2,1,0:T(8,128)(2,1)} %pad_maximum_fusion.12), channel_id=1, source_target_pairs={{0,1},{1,0},{2,3},{3,2},{4,5},{5,4},{6,7},{7,6},{8,9},{9,8},{10,11... | collective-permute-start | bytes 1806344 | tf_op jit(solution)/shard_map/ppermute | solution.py:597
  452.9 40.2 %collective-permute-start.70 = (bf16[14,168,128]{2,1,0:T(8,128)(2,1)}, bf16[14,168,128]{2,1,0:T(8,128)(2,1)S(1)}, u32[]{:S(2)}, u32[]{:S(2)}) collective-permute-start(bf16[14,168,128]{2,1,0:T(8,128)(2,1)} %get-tuple-element.1003), channel_id=1, source_target_pairs={{0,16},{8,24},{16,0},{24,8},{1,17},{9,25},{17,1},{25,9},{2,18},{10... | collective-permute-start | bytes 1806344 | tf_op jit(solution)/shard_map/ppermute | solution.py:597
  464.8 54.2 %collective-permute-start.72 = (bf16[2,3,392,128]{3,2,1,0:T(8,128)(2,1)}, bf16[2,3,392,128]{3,2,1,0:T(8,128)(2,1)S(1)}, u32[]{:S(2)}, u32[]{:S(2)}) collective-permute-start(bf16[2,3,392,128]{3,2,1,0:T(8,128)(2,1)} %get-tuple-element.1021), channel_id=1, source_target_pairs={{0,2},{1,3},{2,4},{3,5},{4,6},{5,7},{6,0},{7,1},{8,10},{9,11},{10,... | collective-permute-start | bytes 1806344 | tf_op jit(solution)/shard_map/ppermute | solution.py:597
  493.2 44.1 %collective-permute-start.75 = (bf16[2,3,392,128]{3,2,1,0:T(8,128)(2,1)}, bf16[2,3,392,128]{3,2,1,0:T(8,128)(2,1)S(1)}, u32[]{:S(2)}, u32[]{:S(2)}) collective-permute-start(bf16[2,3,392,128]{3,2,1,0:T(8,128)(2,1)} %get-tuple-element.1036), channel_id=1, source_target_pairs={{0,4},{1,5},{2,6},{3,7},{4,0},{5,1},{6,2},{7,3},{8,12},{9,13},{10,... | collective-permute-start | bytes 1806344 | tf_op jit(solution)/shard_map/ppermute | solution.py:597
  494.2 43.2 %collective-permute-start.76 = (bf16[2,3,392,128]{3,2,1,0:T(8,128)(2,1)}, bf16[2,3,392,128]{3,2,1,0:T(8,128)(2,1)S(1)}, u32[]{:S(2)}, u32[]{:S(2)}) collective-permute-start(bf16[2,3,392,128]{3,2,1,0:T(8,128)(2,1)} %pad_maximum_fusion.14), channel_id=1, source_target_pairs={{0,1},{1,0},{2,3},{3,2},{4,5},{5,4},{6,7},{7,6},{8,9},{9,8},{10,11... | collective-permute-start | bytes 1806344 | tf_op jit(solution)/shard_map/ppermute | solution.py:597
  542.8 40.3 %collective-permute-start.81 = (bf16[2,3,392,128]{3,2,1,0:T(8,128)(2,1)}, bf16[2,3,392,128]{3,2,1,0:T(8,128)(2,1)}, u32[]{:S(2)}, u32[]{:S(2)}) collective-permute-start(bf16[2,3,392,128]{3,2,1,0:T(8,128)(2,1)} %pad_maximum_fusion.16), channel_id=1, source_target_pairs={{0,1},{1,0},{2,3},{3,2},{4,5},{5,4},{6,7},{7,6},{8,9},{9,8},{10,11... | collective-permute-start | bytes 1806344 | tf_op jit(solution)/shard_map/ppermute | solution.py:597
  547.3 35.8 %collective-permute-start.82 = (bf16[1,3,392,128]{3,2,1,0:T(8,128)(2,1)}, bf16[1,3,392,128]{3,2,1,0:T(8,128)(2,1)}, u32[]{:S(2)}, u32[]{:S(2)}) collective-permute-start(bf16[1,3,392,128]{3,2,1,0:T(8,128)(2,1)} %get-tuple-element.1075), channel_id=1, source_target_pairs={{0,4},{1,5},{2,6},{3,7},{4,0},{5,1},{6,2},{7,3},{8,12},{9,13},{10,... | collective-permute-start | bytes 903176 | tf_op jit(solution)/shard_map/ppermute | solution.py:597
  (153 other events, 3453.6 us)

commit v7 on v6

--- a/solution.py
+++ b/solution.py
@@ -46,8 +46,9 @@
     ]
 
 
-def run_pack(fields, scalars, shapes, make_copies):
+def run_pack(fields, scalars, shapes, make_copies, after=()):
     def body(scalars, fields, *rest):
+        rest = rest[len(after) :]
         copies = make_copies(fields, rest[:-1], scalars, rest[-1])
         for copy in copies:
             copy.start()
@@ -57,13 +58,14 @@
     return pl.pallas_call(
         body,
         out_shape=shapes,
-        in_specs=[pl.BlockSpec(memory_space=pltpu.SMEM), pl.BlockSpec(memory_space=pl.ANY)],
+        in_specs=[pl.BlockSpec(memory_space=pltpu.SMEM)]
+        + [pl.BlockSpec(memory_space=pl.ANY)] * (1 + len(after)),
         out_specs=[pl.BlockSpec(memory_space=pltpu.VMEM)] * len(shapes),
         scratch_shapes=[pltpu.SemaphoreType.DMA((len(shapes),))],
         compiler_params=pltpu.CompilerParams(vmem_limit_bytes=VMEM_BYTES),
         cost_estimate=pl.CostEstimate(flops=0, bytes_accessed=0, transcendentals=0),
         name="pack",
-    )(scalars, fields)
+    )(scalars, fields, *after)
 
 
 def send_shapes(chunk, n_x, depth):
@@ -73,12 +75,13 @@
     ]
 
 
-def pack(fields, scalars, chunk, n_x):
+def pack(fields, scalars, chunk, n_x, after):
     return run_pack(
         fields,
         scalars,
         send_shapes(chunk, n_x, fields.shape[1]),
         lambda fields, outs, scalars, sems: chunk_copies(fields, outs, scalars, chunk, n_x, sems),
+        after,
     )
 
 
@@ -94,7 +97,7 @@
     )[0]
 
 
-def project_kernel(chunk, following, n_x, rank, share, scalars, fields, near, got, factor, outs, sends, own, other, wide, sems):
+def project_kernel(chunk, following, n_x, rank, share, scalars, fields, near, got, factor, outs, sends, own, other, wide, held, sems, out_sems):
     cell, (start, rows) = chunk
     copies = [
         copy_cells(fields, own, scalars, 0, cell, start, rows, sems.at[0]),
@@ -105,13 +108,14 @@
     packing = []
     if following is not None:
         packing = chunk_copies(
-            fields, sends, scalars, following, n_x, sems.at[pl.ds(2, len(sends))]
+            fields, held, scalars, following, n_x, sems.at[pl.ds(2, len(sends))]
         )
     for copy in packing:
         copy.start()
     for copy in copies:
         copy.wait()
 
+    leaving = []
     half = rows // 2
     many = max(n for n in range(1, 9) if half % n == 0)
     for start_row in (0, half):
@@ -133,6 +137,11 @@
             return 0
 
         lax.fori_loop(0, half // many, one_group, 0)
+        if start_row == 0:
+            for i, copy in enumerate(packing):
+                copy.wait()
+                leaving.append(pltpu.make_async_copy(held[i], sends[i], out_sems.at[i]))
+                leaving[i].start()
 
     main = rows // 16 * 16
     left = rows - main
@@ -158,7 +167,7 @@
             tile = jnp.concatenate(tile, axis=0).astype(jnp.bfloat16)
             at = per * main + four * left
             out[at : at + count * left, :] = tile
-    for copy in packing:
+    for copy in leaving:
         copy.wait()
 
 
@@ -179,9 +188,10 @@
         rest = rest[n_got + 1 + n_after :]
         outs = rest[:n_outs]
         sends = rest[n_outs : n_outs + n_sends]
-        own, other, wide, sems = rest[n_outs + n_sends :]
+        own, other, wide, sems, out_sems = rest[n_outs + n_sends : n_outs + n_sends + 5]
+        held = rest[n_outs + n_sends + 5 :]
         project_kernel(
-            chunk, following, n_x, rank, share, scalars, fields, near, got, factor, outs, sends, own, other, wide, sems
+            chunk, following, n_x, rank, share, scalars, fields, near, got, factor, outs, sends, own, other, wide, held, sems, out_sems
         )
 
     groups = column_groups(share)
@@ -195,13 +205,15 @@
         in_specs=[pl.BlockSpec(memory_space=pltpu.SMEM), any_space, any_space]
         + [vmem] * (n_got + 1)
         + [any_space] * n_after,
-        out_specs=[vmem] * (n_outs + n_sends),
+        out_specs=[vmem] * n_outs + [any_space] * n_sends,
         scratch_shapes=[
             pltpu.VMEM((rows, depth, LANES), jnp.bfloat16),
             pltpu.VMEM((rows, depth, LANES), jnp.bfloat16),
             pltpu.VMEM((rows * rank, LANES), jnp.float32),
             pltpu.SemaphoreType.DMA((2 + n_got,)),
-        ],
+            pltpu.SemaphoreType.DMA((n_got,)),
+        ]
+        + [pltpu.VMEM(shape.shape, shape.dtype) for shape in shapes[n_outs:]],
         compiler_params=pltpu.CompilerParams(vmem_limit_bytes=VMEM_BYTES),
         cost_estimate=pl.CostEstimate(flops=0, bytes_accessed=0, transcendentals=0),
         name="project",
@@ -309,6 +321,13 @@
 
 def spread_column(block, column):
     return jnp.broadcast_to(block[:, column : column + 1], block.shape)
+
+
+def add_up(terms):
+    while len(terms) > 1:
+        pairs = [a + b for a, b in zip(terms[::2], terms[1::2])]
+        terms = pairs + terms[len(pairs) * 2 :]
+    return terms[0]
 
 
 def factor_block(square, inverse):
@@ -336,15 +355,14 @@
                     acc = acc + r[w, v] * inv[w, u]
                 inv[v, u] = -(acc * scale[v])
             inv[v, v] = scale[v]
-        new_square = new_inverse = None
+        ones, twos = [], []
         for u in range(height):
             weight = jnp.zeros_like(a)
             for v in range(u, height):
                 weight = jnp.where(rows == v, inv[v, u], weight)
-            one = weight * spread_row(a, u)
-            two = weight * spread_row(inverse[t], u)
-            new_square = one if new_square is None else new_square + one
-            new_inverse = two if new_inverse is None else new_inverse + two
+            ones.append(weight * spread_row(a, u))
+            twos.append(weight * spread_row(inverse[t], u))
+        new_square, new_inverse = add_up(ones), add_up(twos)
         square[t], inverse[t] = new_square, new_inverse
         rows_square = [spread_row(new_square, u) for u in range(height)]
         rows_inverse = [spread_row(new_inverse, u) for u in range(height)]
@@ -356,11 +374,10 @@
                 for w in range(u):
                     x = x - factors[w] * r[w, u]
                 factors.append(x * scale[u])
-            other = inverse[later]
-            for u in range(height):
-                target = target - factors[u] * rows_square[u]
-                other = other - factors[u] * rows_inverse[u]
-            square[later], inverse[later] = target, other
+            square[later] = target - add_up([f * row for f, row in zip(factors, rows_square)])
+            inverse[later] = inverse[later] - add_up(
+                [f * row for f, row in zip(factors, rows_inverse)]
+            )
 
 
 def exact_dot(left, right, contract):
@@ -386,6 +403,8 @@
     height = 8
     lane = lax.broadcasted_iota(jnp.int32, (height, LANES), 1)
     row = lax.broadcasted_iota(jnp.int32, (height, LANES), 0)
+    columns = lax.broadcasted_iota(jnp.int32, (LANES, whole), 1)
+    half = panels // 2 * LANES
 
     def one_panel(p, _):
         start = pl.multiple_of(p * LANES, LANES)
@@ -395,36 +414,22 @@
             square.append(work[pl.ds(start + t * height, height), pl.ds(start, LANES)])
             inverse.append(jnp.where(lane == row + t * height, 1.0, 0.0))
         factor_block(square, inverse)
-        for t in range(strips):
-            kept = jnp.where(lane >= row + t * height, square[t], 0.0)
-            work[pl.ds(start + t * height, height), pl.ds(start, LANES)] = kept
         inverse = jnp.concatenate(inverse, axis=0)
-
-        def one_column(j, _):
-            at = pl.multiple_of(j * LANES, LANES)
-            work[pl.ds(start, LANES), pl.ds(at, LANES)] = exact_dot(
-                inverse, work[pl.ds(start, LANES), pl.ds(at, LANES)], ((1,), (0,))
+        done = exact_dot(inverse, work[pl.ds(start, LANES), :], ((1,), (0,)))
+        done = jnp.where(columns >= start, done, 0.0)
+        work[pl.ds(start, LANES), :] = done
+        rest = jnp.where(columns >= start + LANES, done, 0.0)
+
+        @pl.when(p + 1 < panels // 2)
+        def _():
+            work[:half, :] = work[:half, :] - exact_dot(rest[:, :half], done, ((0,), (0,)))
+
+        @pl.when(p + 1 < panels)
+        def _():
+            work[half:, half:] = work[half:, half:] - exact_dot(
+                rest[:, half:], done[:, half:], ((0,), (0,))
             )
-            return 0
-
-        lax.fori_loop(p + 1, panels, one_column, 0)
-
-        def one_row(i, _):
-            row_at = pl.multiple_of(i * LANES, LANES)
-            left = work[pl.ds(start, LANES), pl.ds(row_at, LANES)]
-
-            def one_block(j, _):
-                at = pl.multiple_of(j * LANES, LANES)
-                term = exact_dot(left, work[pl.ds(start, LANES), pl.ds(at, LANES)], ((0,), (0,)))
-                work[pl.ds(row_at, LANES), pl.ds(at, LANES)] = (
-                    work[pl.ds(row_at, LANES), pl.ds(at, LANES)] - term
-                )
-                return 0
-
-            lax.fori_loop(i, panels, one_block, 0)
-            return 0
-
-        lax.fori_loop(p + 1, panels, one_row, 0)
+
         return 0
 
     lax.fori_loop(0, panels, one_panel, 0)
@@ -605,7 +610,7 @@
 
     moving = []
     for index, chunk in enumerate(chunks[:AHEAD]):
-        sends = pack(by_y, scalars, chunk, n_x)
+        sends = pack(by_y, scalars, chunk, n_x, [factor] if index else [])
         slots = []
         for (partner, _, _), send in zip(send_list(chunk, n_x), sends):
             slots.append(start_x(partner, send))

time: 705 us -> 706 us (level)
  waiting for transfers between devices: 287 us -> 302 us
  Pallas kernels: 201 us -> 193 us
    ppermute x86, waiting for transfers between devices: 248 us -> 265 us  [start(): flown.append(lax.ppermute(operand, axis, pairs))]
    ppermute x86, starting transfers between devices: 166 us -> 158 us  [start(): flown.append(lax.ppermute(operand, axis, pairs))]
  transfers between devices with their start and end apart: 98 -> 98, of which waited for: 44 -> 46; matrix products, arithmetic and copies ran while one was open for 3% -> 3% of each run, Pallas kernels for 20% -> 19%
where the time goes in v7:
time: 706 us; the launch traced here: 701 us
  waiting for transfers between devices  302 us (43%)
  Pallas kernels  193 us (27%)
  starting transfers between devices  174 us (25%)
  local copies, waits for them, and re-layouts  15.5 us (2%)
  other arithmetic  7.96 us (1%)
  matrix products  7.3 us (1%)
    ppermute x86, waiting for transfers between devices, start(): flown.append(lax.ppermute(operand, axis, pairs))  265 us
    ppermute x86, starting transfers between devices, start(): flown.append(lax.ppermute(operand, axis, pairs))  158 us
    pallas_call x9, Pallas kernels, project(): pl.pallas_call(body, out_shape=shapes, in_specs=[pl.BlockSpec(memory_spac...  94.4 us
    pallas_call x1, Pallas kernels, cholesky_rows(): pl.pallas_call(functools.partial(cholesky_kernel, slab), out_shape=jax.Sh...  39.9 us
    pallas_call x3, Pallas kernels, gram(): pl.pallas_call(body, grid=(groups,), out_shape=jax.ShapeDtypeStruct(shape...  37.8 us
    ppermute x6, waiting for transfers between devices, swap(): return lax.ppermute(value, axis, flips)  30.4 us
    pallas_call x5, Pallas kernels, run_pack(): pl.pallas_call(body, out_shape=shapes, in_specs=[pl.BlockSpec(memory_spac...  21 us
  transfers between devices with their start and end apart: 98, of which 46 were waited for; matrix products, arithmetic and copies ran while one was open for 3% of the time, Pallas kernels for 19%

profile of v7, /device:TPU:0, one launch (start us, length us, event | category | flops | bytes accessed | tf_op | source)
XLA Modules:
  0.0 701.1 jit_solution(8307638396847048822)
XLA Ops:
  41.2 9.5 %collective-permute-done.2.rest_2_ = bf16[14,168,128]{2,1,0:T(8,128)(2,1)S(1)} collective-permute-done((bf16[14,168,128]{2,1,0:T(8,128)(2,1)}, bf16[14,168,128]{2,1,0:T(8,128)(2,1)S(1)}, u32[]{:S(2)}, u32[]{:S(2)}) %collective-permute-start.2) | collective-permute-done | bytes 602144 | tf_op jit(solution)/shard_map/ppermute | solution.py:602
  52.4 10.5 %collective-permute-done.3.rest_3_ = bf16[14,168,128]{2,1,0:T(8,128)(2,1)S(1)} collective-permute-done((bf16[14,168,128]{2,1,0:T(8,128)(2,1)}, bf16[14,168,128]{2,1,0:T(8,128)(2,1)S(1)}, u32[]{:S(2)}, u32[]{:S(2)}) %collective-permute-start.3) | collective-permute-done | bytes 602144 | tf_op jit(solution)/shard_map/ppermute | solution.py:602
  65.6 10.4 %project.9 = (bf16[2,3,392,128]{3,2,1,0:T(8,128)(2,1)}, bf16[2,3,392,128]{3,2,1,0:T(8,128)(2,1)}, bf16[2,3,392,128]{3,2,1,0:T(8,128)(2,1)}, bf16[2,3,392,128]{3,...) custom-call(s32[12]{0:T(128)} %stack.150.scalars, ...), custom_call_target="tpu_custom_call" | custom-call | tf_op jit(solution)/shard_map/project/pallas_call | solution.py:202
  80.9 7.8 %collective-permute-done.8.rest_1_ = bf16[14,168,128]{2,1,0:T(8,128)(2,1)} collective-permute-done((bf16[14,168,128]{2,1,0:T(8,128)(2,1)}, bf16[14,168,128]{2,1,0:T(8,128)(2,1)}, u32[]{:S(2)}, u32[]{:S(2)}) %collective-permute-start.8) | collective-permute-done | bytes 602144 | tf_op jit(solution)/shard_map/ppermute | solution.py:602
  104.1 10.4 %collective-permute-done.10.rest_3_ = bf16[14,168,128]{2,1,0:T(8,128)(2,1)} collective-permute-done((bf16[14,168,128]{2,1,0:T(8,128)(2,1)}, bf16[14,168,128]{2,1,0:T(8,128)(2,1)}, u32[]{:S(2)}, u32[]{:S(2)}) %collective-permute-start.10) | collective-permute-done | bytes 602144 | tf_op jit(solution)/shard_map/ppermute | solution.py:602
  117.1 7.3 %select_add_fusion.rest_5_.before = f32[768,768]{1,0:T(8,128)} fusion(f32[672,768]{0,1:T(8,128)S(1)} %bitcast.91, f32[768]{0:T(1024)S(1)} %fusion.6), kind=kOutput, calls=%fused_computation | convolution fusion | flops 4758110208 | bytes 4426752 | tf_op jit(solution)/shard_map/dot_general | solution.py:384
  124.4 10.5 %project.10 = (bf16[2,3,392,128]{3,2,1,0:T(8,128)(2,1)}, bf16[2,3,392,128]{3,2,1,0:T(8,128)(2,1)}, bf16[2,3,392,128]{3,2,1,0:T(8,128)(2,1)}, bf16[2,3,392,128]{3...) custom-call(s32[12]{0:T(128)} %stack.150.scalars, ...), custom_call_target="tpu_custom_call" | custom-call | tf_op jit(solution)/shard_map/project/pallas_call | solution.py:202
  140.8 13.1 %collective-permute-done.16.rest_2_ = bf16[14,168,128]{2,1,0:T(8,128)(2,1)S(1)} collective-permute-done((bf16[14,168,128]{2,1,0:T(8,128)(2,1)}, bf16[14,168,128]{2,1,0:T(8,128)(2,1)S(1)}, u32[]{:S(2)}, u32[]{:S(2)}) %collective-permute-start.16) | collective-permute-done | bytes 602144 | tf_op jit(solution)/shard_map/ppermute | solution.py:602
  157.9 8.2 %collective-permute-done.17.rest_3_ = bf16[14,168,128]{2,1,0:T(8,128)(2,1)S(1)} collective-permute-done((bf16[14,168,128]{2,1,0:T(8,128)(2,1)S(1)}, bf16[14,168,128]{2,1,0:T(8,128)(2,1)S(1)}, u32[]{:S(2)}, u32[]{:S(2)}) %collective-permute-start.17) | collective-permute-done | bytes 602144 | tf_op jit(solution)/shard_map/ppermute | solution.py:602
  181.6 10.8 %project.11 = (bf16[2,3,392,128]{3,2,1,0:T(8,128)(2,1)}, bf16[2,3,392,128]{3,2,1,0:T(8,128)(2,1)}, bf16[2,3,392,128]{3,2,1,0:T(8,128)(2,1)}, bf16[2,3,392,128]{3...) custom-call(s32[12]{0:T(128)} %stack.150.scalars, ...), custom_call_target="tpu_custom_call" | custom-call | tf_op jit(solution)/shard_map/project/pallas_call | solution.py:202
  209.5 8.3 %collective-permute-done.26.rest_3_ = bf16[14,168,128]{2,1,0:T(8,128)(2,1)} collective-permute-done((bf16[14,168,128]{2,1,0:T(8,128)(2,1)}, bf16[14,168,128]{2,1,0:T(8,128)(2,1)}, u32[]{:S(2)}, u32[]{:S(2)}) %collective-permute-start.26) | collective-permute-done | bytes 602144 | tf_op jit(solution)/shard_map/ppermute | solution.py:602
  233.2 10.6 %project.12 = (bf16[2,3,392,128]{3,2,1,0:T(8,128)(2,1)}, bf16[2,3,392,128]{3,2,1,0:T(8,128)(2,1)}, bf16[2,3,392,128]{3,2,1,0:T(8,128)(2,1)}, bf16[2,3,392,128]{3...) custom-call(s32[12]{0:T(128)} %stack.150.scalars, ...), custom_call_target="tpu_custom_call" | custom-call | tf_op jit(solution)/shard_map/project/pallas_call | solution.py:202
  246.3 18.8 %collective-permute-done.32.rest_14_ = bf16[2,3,392,128]{3,2,1,0:T(8,128)(2,1)S(1)} collective-permute-done((bf16[2,3,392,128]{3,2,1,0:T(8,128)(2,1)}, bf16[2,3,392,128]{3,2,1,0:T(8,128)(2,1)S(1)}, u32[]{:S(2)}, u32[]{:S(2)}) %collective-permute-start.32) | collective-permute-done | bytes 602144 | tf_op jit(solution)/shard_map/ppermute | solution.py:602
  285.1 10.6 %project.13 = (bf16[2,3,392,128]{3,2,1,0:T(8,128)(2,1)}, bf16[2,3,392,128]{3,2,1,0:T(8,128)(2,1)}, bf16[2,3,392,128]{3,2,1,0:T(8,128)(2,1)}, bf16[2,3,392,128]{3...) custom-call(s32[12]{0:T(128)} %stack.150.scalars, ...), custom_call_target="tpu_custom_call" | custom-call | tf_op jit(solution)/shard_map/project/pallas_call | solution.py:202
  295.8 11.7 %collective-permute-start.45 = (bf16[2,3,392,128]{3,2,1,0:T(8,128)(2,1)}, bf16[2,3,392,128]{3,2,1,0:T(8,128)(2,1)S(1)}, u32[]{:S(2)}, u32[]{:S(2)}) collective-permute-start(bf16[2,3,392,128]{3,2,1,0:T(8,128)(2,1)} %get-tuple-element.830), channel_id=1, source_target_pairs={{0,2},{1,3},{2,4},{3,5},{4,6},{5,7},{6,0},{7,1},{8,10},{9,11},{10,... | collective-permute-start | bytes 1806344 | tf_op jit(solution)/shard_map/ppermute | solution.py:602
  307.6 12.8 %collective-permute-done.41.rest_2_ = bf16[2,3,392,128]{3,2,1,0:T(8,128)(2,1)S(1)} collective-permute-done((bf16[2,3,392,128]{3,2,1,0:T(8,128)(2,1)}, bf16[2,3,392,128]{3,2,1,0:T(8,128)(2,1)S(1)}, u32[]{:S(2)}, u32[]{:S(2)}) %collective-permute-start.41) | collective-permute-done | bytes 602144 | tf_op jit(solution)/shard_map/ppermute | solution.py:602
  338.6 12.3 %gram.3.rest_5_.rest_18_ = f32[1536,256]{1,0:T(8,128)} custom-call(s32[8]{0:T(128)} %stack.137.sources, bf16[2,3,392,128]{3,2,1,0:T(8,128)(2,1)} %get-tuple-element.619.rest_0_, bf16[2,3,392,128]{3,2,1,0:T(8,128)(2,1)} %copy-done.21, bf16[2,3,392,128]{3,2,1,0:T(8,128)(2,1)} %collective-permute-done.13.rest_2_, ...), custom_call_target="tpu_custom_call" | custom-call | tf_op jit(solution)/shard_map/gram/pallas_call | solution.py:303
  350.9 10.4 %project.14 = (bf16[2,3,392,128]{3,2,1,0:T(8,128)(2,1)}, bf16[2,3,392,128]{3,2,1,0:T(8,128)(2,1)}, bf16[2,3,392,128]{3,2,1,0:T(8,128)(2,1)}, bf16[2,3,392,128]{3...) custom-call(s32[12]{0:T(128)} %stack.150.scalars, ...), custom_call_target="tpu_custom_call" | custom-call | tf_op jit(solution)/shard_map/project/pallas_call | solution.py:202
  361.4 11.2 %collective-permute-start.54 = (bf16[2,3,392,128]{3,2,1,0:T(8,128)(2,1)}, bf16[2,3,392,128]{3,2,1,0:T(8,128)(2,1)S(1)}, u32[]{:S(2)}, u32[]{:S(2)}) collective-permute-start(bf16[2,3,392,128]{3,2,1,0:T(8,128)(2,1)} %get-tuple-element.897), channel_id=1, source_target_pairs={{0,2},{1,3},{2,4},{3,5},{4,6},{5,7},{6,0},{7,1},{8,10},{9,11},{10,... | collective-permute-start | bytes 1806344 | tf_op jit(solution)/shard_map/ppermute | solution.py:602
  377.1 9.3 %collective-permute-done.54.rest_13_ = bf16[2,3,392,128]{3,2,1,0:T(8,128)(2,1)S(1)} collective-permute-done((bf16[2,3,392,128]{3,2,1,0:T(8,128)(2,1)}, bf16[2,3,392,128]{3,2,1,0:T(8,128)(2,1)S(1)}, u32[]{:S(2)}, u32[]{:S(2)}) %collective-permute-start.54) | collective-permute-done | bytes 602144 | tf_op jit(solution)/shard_map/ppermute | solution.py:602
  400.3 10.3 %project.15 = (bf16[2,3,392,128]{3,2,1,0:T(8,128)(2,1)}, bf16[2,3,392,128]{3,2,1,0:T(8,128)(2,1)}, bf16[2,3,392,128]{3,2,1,0:T(8,128)(2,1)}, bf16[2,3,392,128]{3...) custom-call(s32[12]{0:T(128)} %stack.150.scalars, ...), custom_call_target="tpu_custom_call" | custom-call | tf_op jit(solution)/shard_map/project/pallas_call | solution.py:202
  411.0 20.5 %collective-permute-done.59.rest_14_ = bf16[2,3,392,128]{3,2,1,0:T(8,128)(2,1)S(1)} collective-permute-done((bf16[2,3,392,128]{3,2,1,0:T(8,128)(2,1)}, bf16[2,3,392,128]{3,2,1,0:T(8,128)(2,1)S(1)}, u32[]{:S(2)}, u32[]{:S(2)}) %collective-permute-start.59) | collective-permute-done | bytes 602144 | tf_op jit(solution)/shard_map/ppermute | solution.py:602
  435.4 19.4 %collective-permute-start.68 = (bf16[2,3,392,128]{3,2,1,0:T(8,128)(2,1)}, bf16[2,3,392,128]{3,2,1,0:T(8,128)(2,1)S(1)}, u32[]{:S(2)}, u32[]{:S(2)}) collective-permute-start(bf16[2,3,392,128]{3,2,1,0:T(8,128)(2,1)} %get-tuple-element.991), channel_id=1, source_target_pairs={{0,4},{1,5},{2,6},{3,7},{4,0},{5,1},{6,2},{7,3},{8,12},{9,13},{10,... | collective-permute-start | bytes 1806344 | tf_op jit(solution)/shard_map/ppermute | solution.py:602
  458.5 10.5 %project.16 = (bf16[2,3,392,128]{3,2,1,0:T(8,128)(2,1)}, bf16[2,3,392,128]{3,2,1,0:T(8,128)(2,1)}, bf16[2,3,392,128]{3,2,1,0:T(8,128)(2,1)}, bf16[2,3,392,128]{3,2,1,0:T(8,128)(2,1)}) custom-call(s32[12]{0:T(128)} %stack.150.scalars, bf16[84,168,1536]{2,1,0:T(8,128)(2,1)} %bitcast.89, bf16[84,168,128]{2,1,0:T(8,128)(2,1)} %collective-permute-done.6.near, ...), custom_call_target="tpu_custom_call" | custom-call | tf_op jit(solution)/shard_map/project/pallas_call | solution.py:202
  470.7 24.1 %collective-permute-done.68.rest_2_ = bf16[2,3,392,128]{3,2,1,0:T(8,128)(2,1)S(1)} collective-permute-done((bf16[2,3,392,128]{3,2,1,0:T(8,128)(2,1)}, bf16[2,3,392,128]{3,2,1,0:T(8,128)(2,1)S(1)}, u32[]{:S(2)}, u32[]{:S(2)}) %collective-permute-start.68) | collective-permute-done | bytes 602144 | tf_op jit(solution)/shard_map/ppermute | solution.py:602
  499.3 12.8 %gram.4.rest_5_.rest_20_ = f32[1536,256]{1,0:T(8,128)} custom-call(s32[8]{0:T(128)} %stack.137.sources, bf16[2,3,392,128]{3,2,1,0:T(8,128)(2,1)} %get-tuple-element.792.rest_0_, bf16[2,3,392,128]{3,2,1,0:T(8,128)(2,1)} %copy-done.2, bf16[2,3,392,128]{3,2,1,0:T(8,128)(2,1)} %copy-done.4, bf16[2,3,392,128]{3,2,1,0:T(8,128)(2,1)} %copy-done.3, ...), custom_call_target="tpu_custom_call" | custom-call | tf_op jit(solution)/shard_map/gram/pallas_call | solution.py:303
  512.1 10.3 %project.17 = (bf16[1,3,392,128]{3,2,1,0:T(8,128)(2,1)}, bf16[1,3,392,128]{3,2,1,0:T(8,128)(2,1)}, bf16[1,3,392,128]{3,2,1,0:T(8,128)(2,1)}, bf16[1,3,392,128]{3...) custom-call(s32[12]{0:T(128)} %stack.150.scalars, ...), custom_call_target="tpu_custom_call" | custom-call | tf_op jit(solution)/shard_map/project/pallas_call | solution.py:202
  526.7 15.3 %collective-permute-done.75.rest_8_ = bf16[2,3,392,128]{3,2,1,0:T(8,128)(2,1)S(1)} collective-permute-done((bf16[2,3,392,128]{3,2,1,0:T(8,128)(2,1)}, bf16[2,3,392,128]{3,2,1,0:T(8,128)(2,1)S(1)}, u32[]{:S(2)}, u32[]{:S(2)}) %collective-permute-start.75) | collective-permute-done | bytes 602144 | tf_op jit(solution)/shard_map/ppermute | solution.py:602
  562.2 18.9 %collective-permute-done.83.rest_17_ = bf16[1,3,392,128]{3,2,1,0:T(8,128)(2,1)} collective-permute-done((bf16[1,3,392,128]{3,2,1,0:T(8,128)(2,1)}, bf16[1,3,392,128]{3,2,1,0:T(8,128)(2,1)}, u32[]{:S(2)}, u32[]{:S(2)}) %collective-permute-start.83) | collective-permute-done | bytes 301088 | tf_op jit(solution)/shard_map/ppermute | solution.py:602
  589.4 12.8 %gram.5 = f32[1536,256]{1,0:T(8,128)} custom-call(s32[8]{0:T(128)} %stack.137.sources, bf16[2,3,392,128]{3,2,1,0:T(8,128)(2,1)} %get-tuple-element.918.rest_0_, bf16[2,3,392,128]{3,2,1,0:T(8,128)(2,1)} %copy-done.10, bf16[2,3,392,128]{3,2,1,0:T(8,128)(2,1)} %copy-done.14, bf16[2,3,392,128]{3,2,1,0:T(8,128)(2,1)} %copy-done.11, ...), custom_call_target="tpu_custom_call" | custom-call | tf_op jit(solution)/shard_map/gram/pallas_call | solution.py:303
  607.8 10.4 %collective-permute-done.87 = f32[384,256]{1,0:T(8,128)S(1)} collective-permute-done((f32[384,256]{1,0:T(8,128)S(1)}, f32[384,256]{1,0:T(8,128)S(1)}, u32[]{:S(2)}, u32[]{:S(2)}) %collective-permute-start.87) | collective-permute-done | bytes 393248 | tf_op jit(solution)/shard_map/ppermute | solution.py:503
  658.9 39.9 %cholesky.1 = f32[96,768]{1,0:T(8,128)} custom-call(s32[1]{0:T(128)} %bitcast.place, f32[1536,256]{1,0:T(8,128)} %maximum_select_fusion.gram_sum, f32[768,768]{1,0:T(8,128)} %select_add_fusion.rest_5_.before), custom_call_target="tpu_custom_call" | custom-call | tf_op jit(solution)/shard_map/cholesky/pallas_call | solution.py:445
  (433 shorter events, 279.8 us)
Async XLA Ops:
  11.9 52.8 %collective-permute-start.4 = (bf16[84,168,128]{2,1,0:T(8,128)(2,1)}, bf16[84,168,128]{2,1,0:T(8,128)(2,1)}, u32[]{:S(2)}, u32[]{:S(2)}) collective-permute-start(bf16[84,168,128]{2,1,0:T(8,128)(2,1)} %pack.9), channel_id=1, source_target_pairs={{0,8},{8,0},{16,24},{24,16},{1,9},{9,1},{17,25},{25,17},{2,10},{10... | collective-permute-start | bytes 10838024 | tf_op jit(solution)/shard_map/ppermute | solution.py:602
  22.1 42.9 %collective-permute-start.5 = (bf16[84,168,128]{2,1,0:T(8,128)(2,1)}, bf16[84,168,128]{2,1,0:T(8,128)(2,1)}, u32[]{:S(2)}, u32[]{:S(2)}) collective-permute-start(bf16[84,168,128]{2,1,0:T(8,128)(2,1)} %pack.7), channel_id=1, source_target_pairs={{0,8},{8,0},{16,24},{24,16},{1,9},{9,1},{17,25},{25,17},{2,10},{10... | collective-permute-start | bytes 10838024 | tf_op jit(solution)/shard_map/ppermute | solution.py:602
  33.6 42.4 %collective-permute-start.6 = (bf16[84,168,128]{2,1,0:T(8,128)(2,1)}, bf16[84,168,128]{2,1,0:T(8,128)(2,1)}, u32[]{:S(2)}, u32[]{:S(2)}) collective-permute-start(bf16[84,168,128]{2,1,0:T(8,128)(2,1)} %pack.6), channel_id=1, source_target_pairs={{0,8},{8,0},{16,24},{24,16},{1,9},{9,1},{17,25},{25,17},{2,10},{10... | collective-permute-start | bytes 10838024 | tf_op jit(solution)/shard_map/ppermute | solution.py:602
  64.8 37.6 %collective-permute-start.9 = (bf16[14,168,128]{2,1,0:T(8,128)(2,1)}, bf16[14,168,128]{2,1,0:T(8,128)(2,1)}, u32[]{:S(2)}, u32[]{:S(2)}) collective-permute-start(bf16[14,168,128]{2,1,0:T(8,128)(2,1)} %get-tuple-element.590), channel_id=1, source_target_pairs={{0,16},{8,24},{16,0},{24,8},{1,17},{9,25},{17,1},{25,9},{2,18},{10... | collective-permute-start | bytes 1806344 | tf_op jit(solution)/shard_map/ppermute | solution.py:602
  65.0 49.5 %collective-permute-start.10 = (bf16[14,168,128]{2,1,0:T(8,128)(2,1)}, bf16[14,168,128]{2,1,0:T(8,128)(2,1)}, u32[]{:S(2)}, u32[]{:S(2)}) collective-permute-start(bf16[14,168,128]{2,1,0:T(8,128)(2,1)} %get-tuple-element.595), channel_id=1, source_target_pairs={{0,24},{8,16},{16,8},{24,0},{1,25},{9,17},{17,9},{25,1},{2,26},{10... | collective-permute-start | bytes 1806344 | tf_op jit(solution)/shard_map/ppermute | solution.py:602
  76.0 38.6 %collective-permute-start.11 = (bf16[2,3,392,128]{3,2,1,0:T(8,128)(2,1)}, bf16[2,3,392,128]{3,2,1,0:T(8,128)(2,1)S(1)}, u32[]{:S(2)}, u32[]{:S(2)}) collective-permute-start(bf16[2,3,392,128]{3,2,1,0:T(8,128)(2,1)} %get-tuple-element.604), channel_id=1, source_target_pairs={{0,2},{1,3},{2,4},{3,5},{4,6},{5,7},{6,0},{7,1},{8,10},{9,11},{10,... | collective-permute-start | bytes 1806344 | tf_op jit(solution)/shard_map/ppermute | solution.py:602
  77.7 36.9 %collective-permute-start.12 = (bf16[2,3,392,128]{3,2,1,0:T(8,128)(2,1)}, bf16[2,3,392,128]{3,2,1,0:T(8,128)(2,1)}, u32[]{:S(2)}, u32[]{:S(2)}) collective-permute-start(bf16[2,3,392,128]{3,2,1,0:T(8,128)(2,1)} %get-tuple-element.611), channel_id=1, source_target_pairs={{0,6},{1,7},{2,0},{3,1},{4,2},{5,3},{6,4},{7,5},{8,14},{9,15},{10,... | collective-permute-start | bytes 1806344 | tf_op jit(solution)/shard_map/ppermute | solution.py:602
  88.8 46.1 %collective-permute-start.13 = (bf16[2,3,392,128]{3,2,1,0:T(8,128)(2,1)}, bf16[2,3,392,128]{3,2,1,0:T(8,128)(2,1)}, u32[]{:S(2)}, u32[]{:S(2)}) collective-permute-start(bf16[2,3,392,128]{3,2,1,0:T(8,128)(2,1)} %get-tuple-element.623), channel_id=1, source_target_pairs={{0,4},{1,5},{2,6},{3,7},{4,0},{5,1},{6,2},{7,3},{8,12},{9,13},{10,... | collective-permute-start | bytes 1806344 | tf_op jit(solution)/shard_map/ppermute | solution.py:602
  116.8 37.1 %collective-permute-start.16 = (bf16[14,168,128]{2,1,0:T(8,128)(2,1)}, bf16[14,168,128]{2,1,0:T(8,128)(2,1)S(1)}, u32[]{:S(2)}, u32[]{:S(2)}) collective-permute-start(bf16[14,168,128]{2,1,0:T(8,128)(2,1)} %get-tuple-element.637), channel_id=1, source_target_pairs={{0,16},{8,24},{16,0},{24,8},{1,17},{9,25},{17,1},{25,9},{2,18},{10... | collective-permute-start | bytes 1806344 | tf_op jit(solution)/shard_map/ppermute | solution.py:602
  117.1 49.0 %collective-permute-start.17 = (bf16[14,168,128]{2,1,0:T(8,128)(2,1)S(1)}, bf16[14,168,128]{2,1,0:T(8,128)(2,1)S(1)}, u32[]{:S(2)}, u32[]{:S(2)}) collective-permute-start(bf16[14,168,128]{2,1,0:T(8,128)(2,1)S(1)} %copy-done.71), channel_id=1, source_target_pairs={{0,24},{8,16},{16,8},{24,0},{1,25},{9,17},{17,9},{25,1},{2,26},{10... | collective-permute-start | bytes 1806344 | tf_op jit(solution)/shard_map/ppermute | solution.py:602
  140.4 39.3 %collective-permute-start.20 = (bf16[14,168,128]{2,1,0:T(8,128)(2,1)S(1)}, bf16[14,168,128]{2,1,0:T(8,128)(2,1)S(1)}, u32[]{:S(2)}, u32[]{:S(2)}) collective-permute-start(bf16[14,168,128]{2,1,0:T(8,128)(2,1)S(1)} %copy-done.80), channel_id=1, source_target_pairs={{0,16},{8,24},{16,0},{24,8},{1,17},{9,25},{17,1},{25,9},{2,18},{10... | collective-permute-start | bytes 1806344 | tf_op jit(solution)/shard_map/ppermute | solution.py:602
  220.0 45.1 %collective-permute-start.32 = (bf16[2,3,392,128]{3,2,1,0:T(8,128)(2,1)}, bf16[2,3,392,128]{3,2,1,0:T(8,128)(2,1)S(1)}, u32[]{:S(2)}, u32[]{:S(2)}) collective-permute-start(bf16[2,3,392,128]{3,2,1,0:T(8,128)(2,1)} %get-tuple-element.744), channel_id=1, source_target_pairs={{0,4},{1,5},{2,6},{3,7},{4,0},{5,1},{6,2},{7,3},{8,12},{9,13},{10,... | collective-permute-start | bytes 1806344 | tf_op jit(solution)/shard_map/ppermute | solution.py:602
  225.4 41.2 %collective-permute-start.33 = (bf16[2,3,392,128]{3,2,1,0:T(8,128)(2,1)S(1)}, bf16[2,3,392,128]{3,2,1,0:T(8,128)(2,1)S(1)}, u32[]{:S(2)}, u32[]{:S(2)}) collective-permute-start(bf16[2,3,392,128]{3,2,1,0:T(8,128)(2,1)S(1)} %pad_maximum_fusion.4), channel_id=1, source_target_pairs={{0,1},{1,0},{2,3},{3,2},{4,5},{5,4},{6,7},{7,6},{8,9},{9,8},{10,11... | collective-permute-start | bytes 1806344 | tf_op jit(solution)/shard_map/ppermute | solution.py:602
  231.3 36.9 %collective-permute-start.34 = (bf16[14,168,128]{2,1,0:T(8,128)(2,1)}, bf16[14,168,128]{2,1,0:T(8,128)(2,1)S(1)}, u32[]{:S(2)}, u32[]{:S(2)}) collective-permute-start(bf16[14,168,128]{2,1,0:T(8,128)(2,1)} %get-tuple-element.757), channel_id=1, source_target_pairs={{0,16},{8,24},{16,0},{24,8},{1,17},{9,25},{17,1},{25,9},{2,18},{10... | collective-permute-start | bytes 1806344 | tf_op jit(solution)/shard_map/ppermute | solution.py:602
  271.4 49.0 %collective-permute-start.41 = (bf16[2,3,392,128]{3,2,1,0:T(8,128)(2,1)}, bf16[2,3,392,128]{3,2,1,0:T(8,128)(2,1)S(1)}, u32[]{:S(2)}, u32[]{:S(2)}) collective-permute-start(bf16[2,3,392,128]{3,2,1,0:T(8,128)(2,1)} %get-tuple-element.804), channel_id=1, source_target_pairs={{0,4},{1,5},{2,6},{3,7},{4,0},{5,1},{6,2},{7,3},{8,12},{9,13},{10,... | collective-permute-start | bytes 1806344 | tf_op jit(solution)/shard_map/ppermute | solution.py:602
  280.1 40.5 %collective-permute-start.42 = (bf16[2,3,392,128]{3,2,1,0:T(8,128)(2,1)S(1)}, bf16[2,3,392,128]{3,2,1,0:T(8,128)(2,1)S(1)}, u32[]{:S(2)}, u32[]{:S(2)}) collective-permute-start(bf16[2,3,392,128]{3,2,1,0:T(8,128)(2,1)S(1)} %pad_maximum_fusion.6), channel_id=1, source_target_pairs={{0,1},{1,0},{2,3},{3,2},{4,5},{5,4},{6,7},{7,6},{8,9},{9,8},{10,11... | collective-permute-start | bytes 1806344 | tf_op jit(solution)/shard_map/ppermute | solution.py:602
  283.2 38.0 %collective-permute-start.43 = (bf16[14,168,128]{2,1,0:T(8,128)(2,1)}, bf16[14,168,128]{2,1,0:T(8,128)(2,1)S(1)}, u32[]{:S(2)}, u32[]{:S(2)}) collective-permute-start(bf16[14,168,128]{2,1,0:T(8,128)(2,1)} %get-tuple-element.817), channel_id=1, source_target_pairs={{0,16},{8,24},{16,0},{24,8},{1,17},{9,25},{17,1},{25,9},{2,18},{10... | collective-permute-start | bytes 1806344 | tf_op jit(solution)/shard_map/ppermute | solution.py:602
  321.5 39.9 %collective-permute-start.49 = (bf16[14,168,128]{2,1,0:T(8,128)(2,1)}, bf16[14,168,128]{2,1,0:T(8,128)(2,1)}, u32[]{:S(2)}, u32[]{:S(2)}) collective-permute-start(bf16[14,168,128]{2,1,0:T(8,128)(2,1)} %get-tuple-element.865), channel_id=1, source_target_pairs={{0,24},{8,16},{16,8},{24,0},{1,25},{9,17},{17,9},{25,1},{2,26},{10... | collective-permute-start | bytes 1806344 | tf_op jit(solution)/shard_map/ppermute | solution.py:602
  322.5 50.2 %collective-permute-start.50 = (bf16[2,3,392,128]{3,2,1,0:T(8,128)(2,1)}, bf16[2,3,392,128]{3,2,1,0:T(8,128)(2,1)S(1)}, u32[]{:S(2)}, u32[]{:S(2)}) collective-permute-start(bf16[2,3,392,128]{3,2,1,0:T(8,128)(2,1)} %get-tuple-element.871), channel_id=1, source_target_pairs={{0,4},{1,5},{2,6},{3,7},{4,0},{5,1},{6,2},{7,3},{8,12},{9,13},{10,... | collective-permute-start | bytes 1806344 | tf_op jit(solution)/shard_map/ppermute | solution.py:602
  333.9 40.4 %collective-permute-start.51 = (bf16[2,3,392,128]{3,2,1,0:T(8,128)(2,1)}, bf16[2,3,392,128]{3,2,1,0:T(8,128)(2,1)}, u32[]{:S(2)}, u32[]{:S(2)}) collective-permute-start(bf16[2,3,392,128]{3,2,1,0:T(8,128)(2,1)} %pad_maximum_fusion.8), channel_id=1, source_target_pairs={{0,1},{1,0},{2,3},{3,2},{4,5},{5,4},{6,7},{7,6},{8,9},{9,8},{10,11... | collective-permute-start | bytes 1806344 | tf_op jit(solution)/shard_map/ppermute | solution.py:602
  337.2 39.0 %collective-permute-start.52 = (bf16[14,168,128]{2,1,0:T(8,128)(2,1)}, bf16[14,168,128]{2,1,0:T(8,128)(2,1)}, u32[]{:S(2)}, u32[]{:S(2)}) collective-permute-start(bf16[14,168,128]{2,1,0:T(8,128)(2,1)} %get-tuple-element.884), channel_id=1, source_target_pairs={{0,16},{8,24},{16,0},{24,8},{1,17},{9,25},{17,1},{25,9},{2,18},{10... | collective-permute-start | bytes 1806344 | tf_op jit(solution)/shard_map/ppermute | solution.py:602
  338.0 38.2 %collective-permute-start.53 = (bf16[14,168,128]{2,1,0:T(8,128)(2,1)}, bf16[14,168,128]{2,1,0:T(8,128)(2,1)}, u32[]{:S(2)}, u32[]{:S(2)}) collective-permute-start(bf16[14,168,128]{2,1,0:T(8,128)(2,1)} %get-tuple-element.889), channel_id=1, source_target_pairs={{0,24},{8,16},{16,8},{24,0},{1,25},{9,17},{17,9},{25,1},{2,26},{10... | collective-permute-start | bytes 1806344 | tf_op jit(solution)/shard_map/ppermute | solution.py:602
  386.4 45.1 %collective-permute-start.59 = (bf16[2,3,392,128]{3,2,1,0:T(8,128)(2,1)}, bf16[2,3,392,128]{3,2,1,0:T(8,128)(2,1)S(1)}, u32[]{:S(2)}, u32[]{:S(2)}) collective-permute-start(bf16[2,3,392,128]{3,2,1,0:T(8,128)(2,1)} %get-tuple-element.932), channel_id=1, source_target_pairs={{0,4},{1,5},{2,6},{3,7},{4,0},{5,1},{6,2},{7,3},{8,12},{9,13},{10,... | collective-permute-start | bytes 1806344 | tf_op jit(solution)/shard_map/ppermute | solution.py:602
  389.0 44.4 %collective-permute-start.60 = (bf16[2,3,392,128]{3,2,1,0:T(8,128)(2,1)S(1)}, bf16[2,3,392,128]{3,2,1,0:T(8,128)(2,1)S(1)}, u32[]{:S(2)}, u32[]{:S(2)}) collective-permute-start(bf16[2,3,392,128]{3,2,1,0:T(8,128)(2,1)S(1)} %pad_maximum_fusion.10), channel_id=1, source_target_pairs={{0,1},{1,0},{2,3},{3,2},{4,5},{5,4},{6,7},{7,6},{8,9},{9,8},{10,11... | collective-permute-start | bytes 1806344 | tf_op jit(solution)/shard_map/ppermute | solution.py:602
  390.6 44.0 %collective-permute-start.61 = (bf16[14,168,128]{2,1,0:T(8,128)(2,1)}, bf16[14,168,128]{2,1,0:T(8,128)(2,1)S(1)}, u32[]{:S(2)}, u32[]{:S(2)}) collective-permute-start(bf16[14,168,128]{2,1,0:T(8,128)(2,1)} %get-tuple-element.945), channel_id=1, source_target_pairs={{0,16},{8,24},{16,0},{24,8},{1,17},{9,25},{17,1},{25,9},{2,18},{10... | collective-permute-start | bytes 1806344 | tf_op jit(solution)/shard_map/ppermute | solution.py:602
  435.4 59.3 %collective-permute-start.68 = (bf16[2,3,392,128]{3,2,1,0:T(8,128)(2,1)}, bf16[2,3,392,128]{3,2,1,0:T(8,128)(2,1)S(1)}, u32[]{:S(2)}, u32[]{:S(2)}) collective-permute-start(bf16[2,3,392,128]{3,2,1,0:T(8,128)(2,1)} %get-tuple-element.991), channel_id=1, source_target_pairs={{0,4},{1,5},{2,6},{3,7},{4,0},{5,1},{6,2},{7,3},{8,12},{9,13},{10,... | collective-permute-start | bytes 1806344 | tf_op jit(solution)/shard_map/ppermute | solution.py:602
  455.7 40.6 %collective-permute-start.69 = (bf16[2,3,392,128]{3,2,1,0:T(8,128)(2,1)}, bf16[2,3,392,128]{3,2,1,0:T(8,128)(2,1)}, u32[]{:S(2)}, u32[]{:S(2)}) collective-permute-start(bf16[2,3,392,128]{3,2,1,0:T(8,128)(2,1)} %pad_maximum_fusion.12), channel_id=1, source_target_pairs={{0,1},{1,0},{2,3},{3,2},{4,5},{5,4},{6,7},{7,6},{8,9},{9,8},{10,11... | collective-permute-start | bytes 1806344 | tf_op jit(solution)/shard_map/ppermute | solution.py:602
  457.2 40.5 %collective-permute-start.70 = (bf16[14,168,128]{2,1,0:T(8,128)(2,1)}, bf16[14,168,128]{2,1,0:T(8,128)(2,1)S(1)}, u32[]{:S(2)}, u32[]{:S(2)}) collective-permute-start(bf16[14,168,128]{2,1,0:T(8,128)(2,1)} %get-tuple-element.1003), channel_id=1, source_target_pairs={{0,16},{8,24},{16,0},{24,8},{1,17},{9,25},{17,1},{25,9},{2,18},{10... | collective-permute-start | bytes 1806344 | tf_op jit(solution)/shard_map/ppermute | solution.py:602
  469.2 53.3 %collective-permute-start.72 = (bf16[2,3,392,128]{3,2,1,0:T(8,128)(2,1)}, bf16[2,3,392,128]{3,2,1,0:T(8,128)(2,1)S(1)}, u32[]{:S(2)}, u32[]{:S(2)}) collective-permute-start(bf16[2,3,392,128]{3,2,1,0:T(8,128)(2,1)} %get-tuple-element.1021), channel_id=1, source_target_pairs={{0,2},{1,3},{2,4},{3,5},{4,6},{5,7},{6,0},{7,1},{8,10},{9,11},{10,... | collective-permute-start | bytes 1806344 | tf_op jit(solution)/shard_map/ppermute | solution.py:602
  497.8 44.2 %collective-permute-start.75 = (bf16[2,3,392,128]{3,2,1,0:T(8,128)(2,1)}, bf16[2,3,392,128]{3,2,1,0:T(8,128)(2,1)S(1)}, u32[]{:S(2)}, u32[]{:S(2)}) collective-permute-start(bf16[2,3,392,128]{3,2,1,0:T(8,128)(2,1)} %get-tuple-element.1036), channel_id=1, source_target_pairs={{0,4},{1,5},{2,6},{3,7},{4,0},{5,1},{6,2},{7,3},{8,12},{9,13},{10,... | collective-permute-start | bytes 1806344 | tf_op jit(solution)/shard_map/ppermute | solution.py:602
  498.7 43.3 %collective-permute-start.76 = (bf16[2,3,392,128]{3,2,1,0:T(8,128)(2,1)}, bf16[2,3,392,128]{3,2,1,0:T(8,128)(2,1)S(1)}, u32[]{:S(2)}, u32[]{:S(2)}) collective-permute-start(bf16[2,3,392,128]{3,2,1,0:T(8,128)(2,1)} %pad_maximum_fusion.14), channel_id=1, source_target_pairs={{0,1},{1,0},{2,3},{3,2},{4,5},{5,4},{6,7},{7,6},{8,9},{9,8},{10,11... | collective-permute-start | bytes 1806344 | tf_op jit(solution)/shard_map/ppermute | solution.py:602
  547.5 39.7 %collective-permute-start.81 = (bf16[2,3,392,128]{3,2,1,0:T(8,128)(2,1)}, bf16[2,3,392,128]{3,2,1,0:T(8,128)(2,1)}, u32[]{:S(2)}, u32[]{:S(2)}) collective-permute-start(bf16[2,3,392,128]{3,2,1,0:T(8,128)(2,1)} %pad_maximum_fusion.16), channel_id=1, source_target_pairs={{0,1},{1,0},{2,3},{3,2},{4,5},{5,4},{6,7},{7,6},{8,9},{9,8},{10,11... | collective-permute-start | bytes 1806344 | tf_op jit(solution)/shard_map/ppermute | solution.py:602
  (151 other events, 3405.3 us)

commit v8 on v7

--- a/solution.py
+++ b/solution.py
@@ -171,13 +171,12 @@
         copy.wait()
 
 
-def project(fields, near, got, factor, scalars, chunk, following, n_x, share, slow, apart, after):
+def project(fields, near, got, factor, scalars, chunk, following, n_x, share, slow, apart):
     rows = chunk[1][1]
     rank = factor.shape[1]
     depth = fields.shape[1]
     n_got = len(got)
     n_sends = 0 if following is None else n_got
-    n_after = len(after)
     n_outs = 2 * slow if apart else slow
     vmem = pl.BlockSpec(memory_space=pltpu.VMEM)
     any_space = pl.BlockSpec(memory_space=pl.ANY)
@@ -185,7 +184,7 @@
     def body(scalars, fields, near, *rest):
         got = rest[:n_got]
         factor = rest[n_got]
-        rest = rest[n_got + 1 + n_after :]
+        rest = rest[n_got + 1 :]
         outs = rest[:n_outs]
         sends = rest[n_outs : n_outs + n_sends]
         own, other, wide, sems, out_sems = rest[n_outs + n_sends : n_outs + n_sends + 5]
@@ -203,13 +202,12 @@
         body,
         out_shape=shapes,
         in_specs=[pl.BlockSpec(memory_space=pltpu.SMEM), any_space, any_space]
-        + [vmem] * (n_got + 1)
-        + [any_space] * n_after,
+        + [vmem] * (n_got + 1),
         out_specs=[vmem] * n_outs + [any_space] * n_sends,
         scratch_shapes=[
             pltpu.VMEM((rows, depth, LANES), jnp.bfloat16),
             pltpu.VMEM((rows, depth, LANES), jnp.bfloat16),
-            pltpu.VMEM((rows * rank, LANES), jnp.float32),
+            pltpu.VMEM((-(-rows // 8) * 8 * rank, LANES), jnp.float32),
             pltpu.SemaphoreType.DMA((2 + n_got,)),
             pltpu.SemaphoreType.DMA((n_got,)),
         ]
@@ -217,7 +215,7 @@
         compiler_params=pltpu.CompilerParams(vmem_limit_bytes=VMEM_BYTES),
         cost_estimate=pl.CostEstimate(flops=0, bytes_accessed=0, transcendentals=0),
         name="project",
-    )(scalars, fields, near, *got, factor, *after)
+    )(scalars, fields, near, *got, factor)
     return outs[:n_outs], outs[n_outs:]
 
 
@@ -610,7 +608,7 @@
 
     moving = []
     for index, chunk in enumerate(chunks[:AHEAD]):
-        sends = pack(by_y, scalars, chunk, n_x, [factor] if index else [])
+        sends = pack(by_y, scalars, chunk, n_x, [factor, before] if index else [])
         slots = []
         for (partner, _, _), send in zip(send_list(chunk, n_x), sends):
             slots.append(start_x(partner, send))
@@ -625,10 +623,14 @@
     def value_of(block):
         return flown[block] if isinstance(block, int) else block
 
-    def cross(k, j):
+    def cross(k, j, with_gram=None):
         pair = [value_of(arrived[k][dz][0])[1] for dz in (2 * j, 2 * j + 1)]
-        slot = start_y((0, 1), jnp.stack(pair))
+        send = jnp.stack(pair)
+        if with_gram is not None:
+            send, with_gram = lax.optimization_barrier((send, with_gram))
+        slot = start_y((0, 1), send)
         arrived[k].append((slot, ((2 * j, 1), (2 * j + 1, 1))))
+        return with_gram
 
     def add_gram(carried, first):
         group = arrived[first : first + per_gram]
@@ -638,10 +640,6 @@
     for k, chunk in enumerate(chunks):
         following = chunks[k + AHEAD] if k + AHEAD < len(chunks) else None
         last = k == len(chunks) - 1
-        after = [before] if k == 1 else []
-        if k >= per_gram + 2 and (k - 2) % per_gram == 0:
-            carried = add_gram(carried, k - 2 - per_gram)
-            after.append(carried)
         outs, sends = project(
             by_y,
             flown[near[chunk[0] // LANES]],
@@ -654,7 +652,6 @@
             share,
             slow,
             last,
-            after,
         )
         steps = []
         for i, place in enumerate(shifts if last else shifts[::2]):
@@ -672,13 +669,17 @@
                 shift = shifts[i] if last else shifts[2 * i]
                 landed[i] = (start_y(shift, outs[i]), (shift,))
             elif kind == 1:
-                cross(k - 1, i)
+                if i == slow // 2 - 1 and k > per_gram and k % per_gram == 1:
+                    carried = add_gram(carried, k - 1 - per_gram)
+                    carried = cross(k - 1, i, carried)
+                else:
+                    cross(k - 1, i)
             else:
                 slots[i] = start_x(send_list(following, n_x)[i][0], sends[i])
         if sends:
             moving.append(slots)
     for first in range(0, len(chunks), per_gram):
-        if first + per_gram + 2 >= len(chunks):
+        if first + per_gram + 1 >= len(chunks):
             carried = add_gram(carried, first)
 
     summed = sum_over_all(carried)

time: 706 us -> 701 us (level)
  waiting for transfers between devices: 302 us -> 281 us
  starting transfers between devices: 174 us -> 189 us
    ppermute x86, waiting for transfers between devices: 265 us -> 244 us  [start(): flown.append(lax.ppermute(operand, axis, pairs))]
    ppermute x86, starting transfers between devices: 158 us -> 173 us  [start(): flown.append(lax.ppermute(operand, axis, pairs))]
  transfers between devices with their start and end apart: 98 -> 98, of which waited for: 46 -> 43; matrix products, arithmetic and copies ran while one was open for 3% -> 2% of each run, Pallas kernels for 19% -> 20%
where the time goes in v8:
time: 701 us; the launch traced here: 695 us
  waiting for transfers between devices  281 us (40%)
  Pallas kernels  194 us (28%)
  starting transfers between devices  189 us (27%)
  local copies, waits for them, and re-layouts  14.9 us (2%)
  matrix products  7.31 us (1%)
    ppermute x86, waiting for transfers between devices, start(): flown.append(lax.ppermute(operand, axis, pairs))  244 us
    ppermute x86, starting transfers between devices, start(): flown.append(lax.ppermute(operand, axis, pairs))  173 us
    pallas_call x9, Pallas kernels, project(): pl.pallas_call(body, out_shape=shapes, in_specs=[pl.BlockSpec(memory_spac...  94.7 us
    pallas_call x1, Pallas kernels, cholesky_rows(): pl.pallas_call(functools.partial(cholesky_kernel, slab), out_shape=jax.Sh...  39.9 us
    pallas_call x3, Pallas kernels, gram(): pl.pallas_call(body, grid=(groups,), out_shape=jax.ShapeDtypeStruct(shape...  37.9 us
    ppermute x6, waiting for transfers between devices, swap(): return lax.ppermute(value, axis, flips)  31.3 us
    pallas_call x5, Pallas kernels, run_pack(): pl.pallas_call(body, out_shape=shapes, in_specs=[pl.BlockSpec(memory_spac...  21.1 us
  transfers between devices with their start and end apart: 98, of which 43 were waited for; matrix products, arithmetic and copies ran while one was open for 2% of the time, Pallas kernels for 20%

profile of v8, /device:TPU:0, one launch (start us, length us, event | category | flops | bytes accessed | tf_op | source)
XLA Modules:
  0.0 694.7 jit_solution(8704219707652034039)
XLA Ops:
  54.6 9.2 %collective-permute-done.3.rest_3_ = bf16[14,168,128]{2,1,0:T(8,128)(2,1)} collective-permute-done((bf16[14,168,128]{2,1,0:T(8,128)(2,1)}, bf16[14,168,128]{2,1,0:T(8,128)(2,1)}, u32[]{:S(2)}, u32[]{:S(2)}) %collective-permute-start.3) | collective-permute-done | bytes 602144 | tf_op jit(solution)/shard_map/ppermute | solution.py:600
  66.0 10.3 %project.9 = (bf16[2,3,392,128]{3,2,1,0:T(8,128)(2,1)}, bf16[2,3,392,128]{3,2,1,0:T(8,128)(2,1)}, bf16[2,3,392,128]{3,2,1,0:T(8,128)(2,1)}, bf16[2,3,392,128]{3,...) custom-call(s32[12]{0:T(128)} %stack.150.scalars, ...), custom_call_target="tpu_custom_call" | custom-call | tf_op jit(solution)/shard_map/project/pallas_call | solution.py:201
  81.6 8.0 %collective-permute-done.8.rest_1_ = bf16[14,168,128]{2,1,0:T(8,128)(2,1)S(1)} collective-permute-done((bf16[14,168,128]{2,1,0:T(8,128)(2,1)}, bf16[14,168,128]{2,1,0:T(8,128)(2,1)S(1)}, u32[]{:S(2)}, u32[]{:S(2)}) %collective-permute-start.8) | collective-permute-done | bytes 602144 | tf_op jit(solution)/shard_map/ppermute | solution.py:600
  92.2 10.9 %collective-permute-done.9.rest_2_ = bf16[14,168,128]{2,1,0:T(8,128)(2,1)S(1)} collective-permute-done((bf16[14,168,128]{2,1,0:T(8,128)(2,1)}, bf16[14,168,128]{2,1,0:T(8,128)(2,1)S(1)}, u32[]{:S(2)}, u32[]{:S(2)}) %collective-permute-start.9) | collective-permute-done | bytes 602144 | tf_op jit(solution)/shard_map/ppermute | solution.py:600
  104.9 10.5 %collective-permute-done.10.rest_3_ = bf16[14,168,128]{2,1,0:T(8,128)(2,1)S(1)} collective-permute-done((bf16[14,168,128]{2,1,0:T(8,128)(2,1)}, bf16[14,168,128]{2,1,0:T(8,128)(2,1)S(1)}, u32[]{:S(2)}, u32[]{:S(2)}) %collective-permute-start.10) | collective-permute-done | bytes 602144 | tf_op jit(solution)/shard_map/ppermute | solution.py:600
  117.8 10.7 %project.10 = (bf16[2,3,392,128]{3,2,1,0:T(8,128)(2,1)}, bf16[2,3,392,128]{3,2,1,0:T(8,128)(2,1)}, bf16[2,3,392,128]{3,2,1,0:T(8,128)(2,1)}, bf16[2,3,392,128]{3...) custom-call(s32[12]{0:T(128)} %stack.150.scalars, ...), custom_call_target="tpu_custom_call" | custom-call | tf_op jit(solution)/shard_map/project/pallas_call | solution.py:201
  141.6 13.1 %collective-permute-done.16.rest_2_ = bf16[14,168,128]{2,1,0:T(8,128)(2,1)S(1)} collective-permute-done((bf16[14,168,128]{2,1,0:T(8,128)(2,1)}, bf16[14,168,128]{2,1,0:T(8,128)(2,1)S(1)}, u32[]{:S(2)}, u32[]{:S(2)}) %collective-permute-start.16) | collective-permute-done | bytes 602144 | tf_op jit(solution)/shard_map/ppermute | solution.py:600
  158.6 8.4 %collective-permute-done.17.rest_3_ = bf16[14,168,128]{2,1,0:T(8,128)(2,1)S(1)} collective-permute-done((bf16[14,168,128]{2,1,0:T(8,128)(2,1)}, bf16[14,168,128]{2,1,0:T(8,128)(2,1)S(1)}, u32[]{:S(2)}, u32[]{:S(2)}) %collective-permute-start.17) | collective-permute-done | bytes 602144 | tf_op jit(solution)/shard_map/ppermute | solution.py:600
  182.3 10.6 %project.11 = (bf16[2,3,392,128]{3,2,1,0:T(8,128)(2,1)}, bf16[2,3,392,128]{3,2,1,0:T(8,128)(2,1)}, bf16[2,3,392,128]{3,2,1,0:T(8,128)(2,1)}, bf16[2,3,392,128]{3...) custom-call(s32[12]{0:T(128)} %stack.150.scalars, ...), custom_call_target="tpu_custom_call" | custom-call | tf_op jit(solution)/shard_map/project/pallas_call | solution.py:201
  199.9 15.1 %collective-permute-start.29 = (bf16[14,168,128]{2,1,0:T(8,128)(2,1)S(1)}, bf16[14,168,128]{2,1,0:T(8,128)(2,1)S(1)}, u32[]{:S(2)}, u32[]{:S(2)}) collective-permute-start(bf16[14,168,128]{2,1,0:T(8,128)(2,1)S(1)} %copy-done.80), channel_id=1, source_target_pairs={{0,16},{8,24},{16,0},{24,8},{1,17},{9,25},{17,1},{25,9},{2,18},{10... | collective-permute-start | bytes 1806344 | tf_op jit(solution)/shard_map/ppermute | solution.py:600
  234.0 10.6 %project.12 = (bf16[2,3,392,128]{3,2,1,0:T(8,128)(2,1)}, bf16[2,3,392,128]{3,2,1,0:T(8,128)(2,1)}, bf16[2,3,392,128]{3,2,1,0:T(8,128)(2,1)}, bf16[2,3,392,128]{3...) custom-call(s32[12]{0:T(128)} %stack.150.scalars, ...), custom_call_target="tpu_custom_call" | custom-call | tf_op jit(solution)/shard_map/project/pallas_call | solution.py:201
  251.6 14.9 %collective-permute-start.38 = (bf16[14,168,128]{2,1,0:T(8,128)(2,1)S(1)}, bf16[14,168,128]{2,1,0:T(8,128)(2,1)S(1)}, u32[]{:S(2)}, u32[]{:S(2)}) collective-permute-start(bf16[14,168,128]{2,1,0:T(8,128)(2,1)S(1)} %copy-done.83), channel_id=1, source_target_pairs={{0,16},{8,24},{16,0},{24,8},{1,17},{9,25},{17,1},{25,9},{2,18},{10... | collective-permute-start | bytes 1806344 | tf_op jit(solution)/shard_map/ppermute | solution.py:600
  285.5 10.5 %project.13 = (bf16[2,3,392,128]{3,2,1,0:T(8,128)(2,1)}, bf16[2,3,392,128]{3,2,1,0:T(8,128)(2,1)}, bf16[2,3,392,128]{3,2,1,0:T(8,128)(2,1)}, bf16[2,3,392,128]{3...) custom-call(s32[12]{0:T(128)} %stack.150.scalars, ...), custom_call_target="tpu_custom_call" | custom-call | tf_op jit(solution)/shard_map/project/pallas_call | solution.py:201
  304.0 12.2 %collective-permute-start.47 = (bf16[14,168,128]{2,1,0:T(8,128)(2,1)}, bf16[14,168,128]{2,1,0:T(8,128)(2,1)}, u32[]{:S(2)}, u32[]{:S(2)}) collective-permute-start(bf16[14,168,128]{2,1,0:T(8,128)(2,1)} %get-tuple-element.851), channel_id=1, source_target_pairs={{0,16},{8,24},{16,0},{24,8},{1,17},{9,25},{17,1},{25,9},{2,18},{10... | collective-permute-start | bytes 1806344 | tf_op jit(solution)/shard_map/ppermute | solution.py:600
  324.7 14.1 %collective-permute-start.50 = (bf16[2,3,392,128]{3,2,1,0:T(8,128)(2,1)}, bf16[2,3,392,128]{3,2,1,0:T(8,128)(2,1)S(1)}, u32[]{:S(2)}, u32[]{:S(2)}) collective-permute-start(bf16[2,3,392,128]{3,2,1,0:T(8,128)(2,1)} %get-tuple-element.873), channel_id=1, source_target_pairs={{0,4},{1,5},{2,6},{3,7},{4,0},{5,1},{6,2},{7,3},{8,12},{9,13},{10,... | collective-permute-start | bytes 1806344 | tf_op jit(solution)/shard_map/ppermute | solution.py:600
  338.9 12.2 %gram.3.rest_18_ = f32[1536,256]{1,0:T(8,128)} custom-call(s32[8]{0:T(128)} %stack.137.sources, bf16[2,3,392,128]{3,2,1,0:T(8,128)(2,1)} %get-tuple-element.621.rest_0_, bf16[2,3,392,128]{3,2,1,0:T(8,128)(2,1)} %copy-done.22, bf16[2,3,392,128]{3,2,1,0:T(8,128)(2,1)} %copy-done.24, bf16[2,3,392,128]{3,2,1,0:T(8,128)(2,1)} %copy-done.23, ...), custom_call_target="tpu_custom_call" | custom-call | tf_op jit(solution)/shard_map/gram/pallas_call | solution.py:301
  351.4 10.7 %project.14 = (bf16[2,3,392,128]{3,2,1,0:T(8,128)(2,1)}, bf16[2,3,392,128]{3,2,1,0:T(8,128)(2,1)}, bf16[2,3,392,128]{3,2,1,0:T(8,128)(2,1)}, bf16[2,3,392,128]{3...) custom-call(s32[12]{0:T(128)} %stack.150.scalars, ...), custom_call_target="tpu_custom_call" | custom-call | tf_op jit(solution)/shard_map/project/pallas_call | solution.py:201
  370.2 8.4 %collective-permute-done.53.rest_3_ = bf16[14,168,128]{2,1,0:T(8,128)(2,1)S(1)} collective-permute-done((bf16[14,168,128]{2,1,0:T(8,128)(2,1)}, bf16[14,168,128]{2,1,0:T(8,128)(2,1)S(1)}, u32[]{:S(2)}, u32[]{:S(2)}) %collective-permute-start.53) | collective-permute-done | bytes 602144 | tf_op jit(solution)/shard_map/ppermute | solution.py:600
  382.6 10.2 %collective-permute-done.56.rest_0_ = bf16[14,168,128]{2,1,0:T(8,128)(2,1)S(1)} collective-permute-done((bf16[14,168,128]{2,1,0:T(8,128)(2,1)S(1)}, bf16[14,168,128]{2,1,0:T(8,128)(2,1)S(1)}, u32[]{:S(2)}, u32[]{:S(2)}) %collective-permute-start.56) | collective-permute-done | bytes 602144 | tf_op jit(solution)/shard_map/ppermute | solution.py:600
  394.2 10.4 %project.15 = (bf16[2,3,392,128]{3,2,1,0:T(8,128)(2,1)}, bf16[2,3,392,128]{3,2,1,0:T(8,128)(2,1)}, bf16[2,3,392,128]{3,2,1,0:T(8,128)(2,1)}, bf16[2,3,392,128]{3...) custom-call(s32[12]{0:T(128)} %stack.150.scalars, ...), custom_call_target="tpu_custom_call" | custom-call | tf_op jit(solution)/shard_map/project/pallas_call | solution.py:201
  406.5 25.8 %collective-permute-done.59.rest_14_ = bf16[2,3,392,128]{3,2,1,0:T(8,128)(2,1)S(1)} collective-permute-done((bf16[2,3,392,128]{3,2,1,0:T(8,128)(2,1)}, bf16[2,3,392,128]{3,2,1,0:T(8,128)(2,1)S(1)}, u32[]{:S(2)}, u32[]{:S(2)}) %collective-permute-start.59) | collective-permute-done | bytes 602144 | tf_op jit(solution)/shard_map/ppermute | solution.py:600
  435.6 12.2 %collective-permute-done.64.rest_16_ = bf16[2,3,392,128]{3,2,1,0:T(8,128)(2,1)S(1)} collective-permute-done((bf16[2,3,392,128]{3,2,1,0:T(8,128)(2,1)S(1)}, bf16[2,3,392,128]{3,2,1,0:T(8,128)(2,1)S(1)}, u32[]{:S(2)}, u32[]{:S(2)}) %collective-permute-start.64) | collective-permute-done | bytes 602144 | tf_op jit(solution)/shard_map/ppermute | solution.py:600
  451.5 10.6 %project.16 = (bf16[2,3,392,128]{3,2,1,0:T(8,128)(2,1)}, bf16[2,3,392,128]{3,2,1,0:T(8,128)(2,1)}, bf16[2,3,392,128]{3,2,1,0:T(8,128)(2,1)}, bf16[2,3,392,128]{3,2,1,0:T(8,128)(2,1)}) custom-call(s32[12]{0:T(128)} %stack.150.scalars, bf16[84,168,1536]{2,1,0:T(8,128)(2,1)} %bitcast.89, bf16[84,168,128]{2,1,0:T(8,128)(2,1)} %collective-permute-done.6.near, ...), custom_call_target="tpu_custom_call" | custom-call | tf_op jit(solution)/shard_map/project/pallas_call | solution.py:201
  465.0 9.4 %collective-permute-start.72 = (bf16[2,3,392,128]{3,2,1,0:T(8,128)(2,1)}, bf16[2,3,392,128]{3,2,1,0:T(8,128)(2,1)S(1)}, u32[]{:S(2)}, u32[]{:S(2)}) collective-permute-start(bf16[2,3,392,128]{3,2,1,0:T(8,128)(2,1)} %get-tuple-element.1024), channel_id=1, source_target_pairs={{0,2},{1,3},{2,4},{3,5},{4,6},{5,7},{6,0},{7,1},{8,10},{9,11},{10,... | collective-permute-start | bytes 1806344 | tf_op jit(solution)/shard_map/ppermute | solution.py:600
  474.5 12.0 %collective-permute-done.68.rest_2_ = bf16[2,3,392,128]{3,2,1,0:T(8,128)(2,1)S(1)} collective-permute-done((bf16[2,3,392,128]{3,2,1,0:T(8,128)(2,1)}, bf16[2,3,392,128]{3,2,1,0:T(8,128)(2,1)S(1)}, u32[]{:S(2)}, u32[]{:S(2)}) %collective-permute-start.68) | collective-permute-done | bytes 602144 | tf_op jit(solution)/shard_map/ppermute | solution.py:600
  488.1 12.9 %gram.4.rest_20_ = f32[1536,256]{1,0:T(8,128)} custom-call(s32[8]{0:T(128)} %stack.137.sources, bf16[2,3,392,128]{3,2,1,0:T(8,128)(2,1)} %get-tuple-element.794.rest_0_, bf16[2,3,392,128]{3,2,1,0:T(8,128)(2,1)} %copy-done.2, bf16[2,3,392,128]{3,2,1,0:T(8,128)(2,1)} %copy-done.4, bf16[2,3,392,128]{3,2,1,0:T(8,128)(2,1)} %copy-done.3, ...), custom_call_target="tpu_custom_call" | custom-call | tf_op jit(solution)/shard_map/gram/pallas_call | solution.py:301
  502.6 10.3 %project.17 = (bf16[1,3,392,128]{3,2,1,0:T(8,128)(2,1)}, bf16[1,3,392,128]{3,2,1,0:T(8,128)(2,1)}, bf16[1,3,392,128]{3,2,1,0:T(8,128)(2,1)}, bf16[1,3,392,128]{3...) custom-call(s32[12]{0:T(128)} %stack.150.scalars, ...), custom_call_target="tpu_custom_call" | custom-call | tf_op jit(solution)/shard_map/project/pallas_call | solution.py:201
  516.4 19.1 %collective-permute-done.75.rest_8_ = bf16[2,3,392,128]{3,2,1,0:T(8,128)(2,1)S(1)} collective-permute-done((bf16[2,3,392,128]{3,2,1,0:T(8,128)(2,1)S(1)}, bf16[2,3,392,128]{3,2,1,0:T(8,128)(2,1)S(1)}, u32[]{:S(2)}, u32[]{:S(2)}) %collective-permute-start.75) | collective-permute-done | bytes 602144 | tf_op jit(solution)/shard_map/ppermute | solution.py:600
  553.2 19.8 %collective-permute-done.83.rest_17_ = bf16[1,3,392,128]{3,2,1,0:T(8,128)(2,1)} collective-permute-done((bf16[1,3,392,128]{3,2,1,0:T(8,128)(2,1)}, bf16[1,3,392,128]{3,2,1,0:T(8,128)(2,1)}, u32[]{:S(2)}, u32[]{:S(2)}) %collective-permute-start.83) | collective-permute-done | bytes 301088 | tf_op jit(solution)/shard_map/ppermute | solution.py:600
  582.6 12.8 %gram.5 = f32[1536,256]{1,0:T(8,128)} custom-call(s32[8]{0:T(128)} %stack.137.sources, bf16[2,3,392,128]{3,2,1,0:T(8,128)(2,1)} %get-tuple-element.920.rest_0_, bf16[2,3,392,128]{3,2,1,0:T(8,128)(2,1)} %copy-done.10, bf16[2,3,392,128]{3,2,1,0:T(8,128)(2,1)} %copy-done.12, bf16[2,3,392,128]{3,2,1,0:T(8,128)(2,1)} %copy-done.11, ...), custom_call_target="tpu_custom_call" | custom-call | tf_op jit(solution)/shard_map/gram/pallas_call | solution.py:301
  601.2 10.2 %collective-permute-done.87 = f32[384,256]{1,0:T(8,128)S(1)} collective-permute-done((f32[384,256]{1,0:T(8,128)S(1)}, f32[384,256]{1,0:T(8,128)S(1)}, u32[]{:S(2)}, u32[]{:S(2)}) %collective-permute-start.87) | collective-permute-done | bytes 393248 | tf_op jit(solution)/shard_map/ppermute | solution.py:501
  652.3 39.9 %cholesky.1 = f32[96,768]{1,0:T(8,128)} custom-call(s32[1]{0:T(128)} %bitcast.place, f32[1536,256]{1,0:T(8,128)} %maximum_select_fusion.gram_sum, f32[768,768]{1,0:T(8,128)} %select_add_fusion.rest_1_.before), custom_call_target="tpu_custom_call" | custom-call | tf_op jit(solution)/shard_map/cholesky/pallas_call | solution.py:443
  (436 shorter events, 276.3 us)
Async XLA Ops:
  12.0 53.7 %collective-permute-start.4 = (bf16[84,168,128]{2,1,0:T(8,128)(2,1)}, bf16[84,168,128]{2,1,0:T(8,128)(2,1)}, u32[]{:S(2)}, u32[]{:S(2)}) collective-permute-start(bf16[84,168,128]{2,1,0:T(8,128)(2,1)} %pack.9), channel_id=1, source_target_pairs={{0,8},{8,0},{16,24},{24,16},{1,9},{9,1},{17,25},{25,17},{2,10},{10... | collective-permute-start | bytes 10838024 | tf_op jit(solution)/shard_map/ppermute | solution.py:600
  22.1 43.8 %collective-permute-start.5 = (bf16[84,168,128]{2,1,0:T(8,128)(2,1)}, bf16[84,168,128]{2,1,0:T(8,128)(2,1)}, u32[]{:S(2)}, u32[]{:S(2)}) collective-permute-start(bf16[84,168,128]{2,1,0:T(8,128)(2,1)} %pack.7), channel_id=1, source_target_pairs={{0,8},{8,0},{16,24},{24,16},{1,9},{9,1},{17,25},{25,17},{2,10},{10... | collective-permute-start | bytes 10838024 | tf_op jit(solution)/shard_map/ppermute | solution.py:600
  34.4 41.9 %collective-permute-start.6 = (bf16[84,168,128]{2,1,0:T(8,128)(2,1)}, bf16[84,168,128]{2,1,0:T(8,128)(2,1)}, u32[]{:S(2)}, u32[]{:S(2)}) collective-permute-start(bf16[84,168,128]{2,1,0:T(8,128)(2,1)} %pack.6), channel_id=1, source_target_pairs={{0,8},{8,0},{16,24},{24,16},{1,9},{9,1},{17,25},{25,17},{2,10},{10... | collective-permute-start | bytes 10838024 | tf_op jit(solution)/shard_map/ppermute | solution.py:600
  65.7 37.4 %collective-permute-start.9 = (bf16[14,168,128]{2,1,0:T(8,128)(2,1)}, bf16[14,168,128]{2,1,0:T(8,128)(2,1)S(1)}, u32[]{:S(2)}, u32[]{:S(2)}) collective-permute-start(bf16[14,168,128]{2,1,0:T(8,128)(2,1)} %get-tuple-element.592), channel_id=1, source_target_pairs={{0,16},{8,24},{16,0},{24,8},{1,17},{9,25},{17,1},{25,9},{2,18},{10... | collective-permute-start | bytes 1806344 | tf_op jit(solution)/shard_map/ppermute | solution.py:600
  66.0 49.4 %collective-permute-start.10 = (bf16[14,168,128]{2,1,0:T(8,128)(2,1)}, bf16[14,168,128]{2,1,0:T(8,128)(2,1)S(1)}, u32[]{:S(2)}, u32[]{:S(2)}) collective-permute-start(bf16[14,168,128]{2,1,0:T(8,128)(2,1)} %get-tuple-element.597), channel_id=1, source_target_pairs={{0,24},{8,16},{16,8},{24,0},{1,25},{9,17},{17,9},{25,1},{2,26},{10... | collective-permute-start | bytes 1806344 | tf_op jit(solution)/shard_map/ppermute | solution.py:600
  76.3 41.2 %collective-permute-start.11 = (bf16[2,3,392,128]{3,2,1,0:T(8,128)(2,1)}, bf16[2,3,392,128]{3,2,1,0:T(8,128)(2,1)S(1)}, u32[]{:S(2)}, u32[]{:S(2)}) collective-permute-start(bf16[2,3,392,128]{3,2,1,0:T(8,128)(2,1)} %get-tuple-element.606), channel_id=1, source_target_pairs={{0,2},{1,3},{2,4},{3,5},{4,6},{5,7},{6,0},{7,1},{8,10},{9,11},{10,... | collective-permute-start | bytes 1806344 | tf_op jit(solution)/shard_map/ppermute | solution.py:600
  78.2 39.6 %collective-permute-start.12 = (bf16[2,3,392,128]{3,2,1,0:T(8,128)(2,1)}, bf16[2,3,392,128]{3,2,1,0:T(8,128)(2,1)S(1)}, u32[]{:S(2)}, u32[]{:S(2)}) collective-permute-start(bf16[2,3,392,128]{3,2,1,0:T(8,128)(2,1)} %get-tuple-element.613), channel_id=1, source_target_pairs={{0,6},{1,7},{2,0},{3,1},{4,2},{5,3},{6,4},{7,5},{8,14},{9,15},{10,... | collective-permute-start | bytes 1806344 | tf_op jit(solution)/shard_map/ppermute | solution.py:600
  89.6 44.0 %collective-permute-start.13 = (bf16[2,3,392,128]{3,2,1,0:T(8,128)(2,1)}, bf16[2,3,392,128]{3,2,1,0:T(8,128)(2,1)S(1)}, u32[]{:S(2)}, u32[]{:S(2)}) collective-permute-start(bf16[2,3,392,128]{3,2,1,0:T(8,128)(2,1)} %get-tuple-element.625), channel_id=1, source_target_pairs={{0,4},{1,5},{2,6},{3,7},{4,0},{5,1},{6,2},{7,3},{8,12},{9,13},{10,... | collective-permute-start | bytes 1806344 | tf_op jit(solution)/shard_map/ppermute | solution.py:600
  117.5 37.2 %collective-permute-start.16 = (bf16[14,168,128]{2,1,0:T(8,128)(2,1)}, bf16[14,168,128]{2,1,0:T(8,128)(2,1)S(1)}, u32[]{:S(2)}, u32[]{:S(2)}) collective-permute-start(bf16[14,168,128]{2,1,0:T(8,128)(2,1)} %get-tuple-element.639), channel_id=1, source_target_pairs={{0,16},{8,24},{16,0},{24,8},{1,17},{9,25},{17,1},{25,9},{2,18},{10... | collective-permute-start | bytes 1806344 | tf_op jit(solution)/shard_map/ppermute | solution.py:600
  117.8 49.2 %collective-permute-start.17 = (bf16[14,168,128]{2,1,0:T(8,128)(2,1)}, bf16[14,168,128]{2,1,0:T(8,128)(2,1)S(1)}, u32[]{:S(2)}, u32[]{:S(2)}) collective-permute-start(bf16[14,168,128]{2,1,0:T(8,128)(2,1)} %get-tuple-element.644), channel_id=1, source_target_pairs={{0,24},{8,16},{16,8},{24,0},{1,25},{9,17},{17,9},{25,1},{2,26},{10... | collective-permute-start | bytes 1806344 | tf_op jit(solution)/shard_map/ppermute | solution.py:600
  133.6 36.4 %collective-permute-start.18 = (bf16[2,3,392,128]{3,2,1,0:T(8,128)(2,1)}, bf16[2,3,392,128]{3,2,1,0:T(8,128)(2,1)S(1)}, u32[]{:S(2)}, u32[]{:S(2)}) collective-permute-start(bf16[2,3,392,128]{3,2,1,0:T(8,128)(2,1)} %get-tuple-element.649), channel_id=1, source_target_pairs={{0,2},{1,3},{2,4},{3,5},{4,6},{5,7},{6,0},{7,1},{8,10},{9,11},{10,... | collective-permute-start | bytes 1806344 | tf_op jit(solution)/shard_map/ppermute | solution.py:600
  133.7 39.0 %collective-permute-start.19 = (bf16[2,3,392,128]{3,2,1,0:T(8,128)(2,1)S(1)}, bf16[2,3,392,128]{3,2,1,0:T(8,128)(2,1)S(1)}, u32[]{:S(2)}, u32[]{:S(2)}) collective-permute-start(bf16[2,3,392,128]{3,2,1,0:T(8,128)(2,1)S(1)} %pad_maximum_fusion.1), channel_id=1, source_target_pairs={{0,1},{1,0},{2,3},{3,2},{4,5},{5,4},{6,7},{7,6},{8,9},{9,8},{10,11... | collective-permute-start | bytes 1806344 | tf_op jit(solution)/shard_map/ppermute | solution.py:600
  141.2 39.3 %collective-permute-start.20 = (bf16[14,168,128]{2,1,0:T(8,128)(2,1)S(1)}, bf16[14,168,128]{2,1,0:T(8,128)(2,1)S(1)}, u32[]{:S(2)}, u32[]{:S(2)}) collective-permute-start(bf16[14,168,128]{2,1,0:T(8,128)(2,1)S(1)} %copy-done.82), channel_id=1, source_target_pairs={{0,16},{8,24},{16,0},{24,8},{1,17},{9,25},{17,1},{25,9},{2,18},{10... | collective-permute-start | bytes 1806344 | tf_op jit(solution)/shard_map/ppermute | solution.py:600
  182.3 36.3 %collective-permute-start.26 = (bf16[14,168,128]{2,1,0:T(8,128)(2,1)}, bf16[14,168,128]{2,1,0:T(8,128)(2,1)}, u32[]{:S(2)}, u32[]{:S(2)}) collective-permute-start(bf16[14,168,128]{2,1,0:T(8,128)(2,1)} %get-tuple-element.704), channel_id=1, source_target_pairs={{0,24},{8,16},{16,8},{24,0},{1,25},{9,17},{17,9},{25,1},{2,26},{10... | collective-permute-start | bytes 1806344 | tf_op jit(solution)/shard_map/ppermute | solution.py:600
  233.9 36.3 %collective-permute-start.35 = (bf16[14,168,128]{2,1,0:T(8,128)(2,1)}, bf16[14,168,128]{2,1,0:T(8,128)(2,1)}, u32[]{:S(2)}, u32[]{:S(2)}) collective-permute-start(bf16[14,168,128]{2,1,0:T(8,128)(2,1)} %get-tuple-element.764), channel_id=1, source_target_pairs={{0,24},{8,16},{16,8},{24,0},{1,25},{9,17},{17,9},{25,1},{2,26},{10... | collective-permute-start | bytes 1806344 | tf_op jit(solution)/shard_map/ppermute | solution.py:600
  285.5 36.3 %collective-permute-start.44 = (bf16[14,168,128]{2,1,0:T(8,128)(2,1)}, bf16[14,168,128]{2,1,0:T(8,128)(2,1)}, u32[]{:S(2)}, u32[]{:S(2)}) collective-permute-start(bf16[14,168,128]{2,1,0:T(8,128)(2,1)} %get-tuple-element.824), channel_id=1, source_target_pairs={{0,24},{8,16},{16,8},{24,0},{1,25},{9,17},{17,9},{25,1},{2,26},{10... | collective-permute-start | bytes 1806344 | tf_op jit(solution)/shard_map/ppermute | solution.py:600
  302.5 48.6 %collective-permute-start.46 = (bf16[2,3,392,128]{3,2,1,0:T(8,128)(2,1)}, bf16[2,3,392,128]{3,2,1,0:T(8,128)(2,1)}, u32[]{:S(2)}, u32[]{:S(2)}) collective-permute-start(bf16[2,3,392,128]{3,2,1,0:T(8,128)(2,1)} %pad_maximum_fusion.7), channel_id=1, source_target_pairs={{0,1},{1,0},{2,3},{3,2},{4,5},{5,4},{6,7},{7,6},{8,9},{9,8},{10,11... | collective-permute-start | bytes 1806344 | tf_op jit(solution)/shard_map/ppermute | solution.py:600
  304.0 47.2 %collective-permute-start.47 = (bf16[14,168,128]{2,1,0:T(8,128)(2,1)}, bf16[14,168,128]{2,1,0:T(8,128)(2,1)}, u32[]{:S(2)}, u32[]{:S(2)}) collective-permute-start(bf16[14,168,128]{2,1,0:T(8,128)(2,1)} %get-tuple-element.851), channel_id=1, source_target_pairs={{0,16},{8,24},{16,0},{24,8},{1,17},{9,25},{17,1},{25,9},{2,18},{10... | collective-permute-start | bytes 1806344 | tf_op jit(solution)/shard_map/ppermute | solution.py:600
  321.8 40.3 %collective-permute-start.49 = (bf16[14,168,128]{2,1,0:T(8,128)(2,1)}, bf16[14,168,128]{2,1,0:T(8,128)(2,1)}, u32[]{:S(2)}, u32[]{:S(2)}) collective-permute-start(bf16[14,168,128]{2,1,0:T(8,128)(2,1)} %get-tuple-element.867), channel_id=1, source_target_pairs={{0,24},{8,16},{16,8},{24,0},{1,25},{9,17},{17,9},{25,1},{2,26},{10... | collective-permute-start | bytes 1806344 | tf_op jit(solution)/shard_map/ppermute | solution.py:600
  324.7 37.6 %collective-permute-start.50 = (bf16[2,3,392,128]{3,2,1,0:T(8,128)(2,1)}, bf16[2,3,392,128]{3,2,1,0:T(8,128)(2,1)S(1)}, u32[]{:S(2)}, u32[]{:S(2)}) collective-permute-start(bf16[2,3,392,128]{3,2,1,0:T(8,128)(2,1)} %get-tuple-element.873), channel_id=1, source_target_pairs={{0,4},{1,5},{2,6},{3,7},{4,0},{5,1},{6,2},{7,3},{8,12},{9,13},{10,... | collective-permute-start | bytes 1806344 | tf_op jit(solution)/shard_map/ppermute | solution.py:600
  380.7 51.6 %collective-permute-start.59 = (bf16[2,3,392,128]{3,2,1,0:T(8,128)(2,1)}, bf16[2,3,392,128]{3,2,1,0:T(8,128)(2,1)S(1)}, u32[]{:S(2)}, u32[]{:S(2)}) collective-permute-start(bf16[2,3,392,128]{3,2,1,0:T(8,128)(2,1)} %get-tuple-element.934), channel_id=1, source_target_pairs={{0,4},{1,5},{2,6},{3,7},{4,0},{5,1},{6,2},{7,3},{8,12},{9,13},{10,... | collective-permute-start | bytes 1806344 | tf_op jit(solution)/shard_map/ppermute | solution.py:600
  380.9 52.3 %collective-permute-start.60 = (bf16[2,3,392,128]{3,2,1,0:T(8,128)(2,1)S(1)}, bf16[2,3,392,128]{3,2,1,0:T(8,128)(2,1)S(1)}, u32[]{:S(2)}, u32[]{:S(2)}) collective-permute-start(bf16[2,3,392,128]{3,2,1,0:T(8,128)(2,1)S(1)} %pad_maximum_fusion.10), channel_id=1, source_target_pairs={{0,1},{1,0},{2,3},{3,2},{4,5},{5,4},{6,7},{7,6},{8,9},{9,8},{10,11... | collective-permute-start | bytes 1806344 | tf_op jit(solution)/shard_map/ppermute | solution.py:600
  392.9 42.1 %collective-permute-start.61 = (bf16[14,168,128]{2,1,0:T(8,128)(2,1)}, bf16[14,168,128]{2,1,0:T(8,128)(2,1)}, u32[]{:S(2)}, u32[]{:S(2)}) collective-permute-start(bf16[14,168,128]{2,1,0:T(8,128)(2,1)} %get-tuple-element.947), channel_id=1, source_target_pairs={{0,16},{8,24},{16,0},{24,8},{1,17},{9,25},{17,1},{25,9},{2,18},{10... | collective-permute-start | bytes 1806344 | tf_op jit(solution)/shard_map/ppermute | solution.py:600
  393.6 41.6 %collective-permute-start.62 = (bf16[14,168,128]{2,1,0:T(8,128)(2,1)}, bf16[14,168,128]{2,1,0:T(8,128)(2,1)}, u32[]{:S(2)}, u32[]{:S(2)}) collective-permute-start(bf16[14,168,128]{2,1,0:T(8,128)(2,1)} %get-tuple-element.952), channel_id=1, source_target_pairs={{0,24},{8,16},{16,8},{24,0},{1,25},{9,17},{17,9},{25,1},{2,26},{10... | collective-permute-start | bytes 1806344 | tf_op jit(solution)/shard_map/ppermute | solution.py:600
  435.4 51.2 %collective-permute-start.68 = (bf16[2,3,392,128]{3,2,1,0:T(8,128)(2,1)}, bf16[2,3,392,128]{3,2,1,0:T(8,128)(2,1)S(1)}, u32[]{:S(2)}, u32[]{:S(2)}) collective-permute-start(bf16[2,3,392,128]{3,2,1,0:T(8,128)(2,1)} %get-tuple-element.993), channel_id=1, source_target_pairs={{0,4},{1,5},{2,6},{3,7},{4,0},{5,1},{6,2},{7,3},{8,12},{9,13},{10,... | collective-permute-start | bytes 1806344 | tf_op jit(solution)/shard_map/ppermute | solution.py:600
  447.8 39.4 %collective-permute-start.69 = (bf16[2,3,392,128]{3,2,1,0:T(8,128)(2,1)S(1)}, bf16[2,3,392,128]{3,2,1,0:T(8,128)(2,1)S(1)}, u32[]{:S(2)}, u32[]{:S(2)}) collective-permute-start(bf16[2,3,392,128]{3,2,1,0:T(8,128)(2,1)S(1)} %pad_maximum_fusion.12), channel_id=1, source_target_pairs={{0,1},{1,0},{2,3},{3,2},{4,5},{5,4},{6,7},{7,6},{8,9},{9,8},{10,11... | collective-permute-start | bytes 1806344 | tf_op jit(solution)/shard_map/ppermute | solution.py:600
  449.8 37.5 %collective-permute-start.70 = (bf16[14,168,128]{2,1,0:T(8,128)(2,1)}, bf16[14,168,128]{2,1,0:T(8,128)(2,1)}, u32[]{:S(2)}, u32[]{:S(2)}) collective-permute-start(bf16[14,168,128]{2,1,0:T(8,128)(2,1)} %get-tuple-element.1005), channel_id=1, source_target_pairs={{0,16},{8,24},{16,0},{24,8},{1,17},{9,25},{17,1},{25,9},{2,18},{10... | collective-permute-start | bytes 1806344 | tf_op jit(solution)/shard_map/ppermute | solution.py:600
  463.0 38.1 %collective-permute-start.71 = (bf16[14,168,128]{2,1,0:T(8,128)(2,1)}, bf16[14,168,128]{2,1,0:T(8,128)(2,1)}, u32[]{:S(2)}, u32[]{:S(2)}) collective-permute-start(bf16[14,168,128]{2,1,0:T(8,128)(2,1)} %get-tuple-element.1018), channel_id=1, source_target_pairs={{0,24},{8,16},{16,8},{24,0},{1,25},{9,17},{17,9},{25,1},{2,26},{10... | collective-permute-start | bytes 1806344 | tf_op jit(solution)/shard_map/ppermute | solution.py:600
  465.0 47.8 %collective-permute-start.72 = (bf16[2,3,392,128]{3,2,1,0:T(8,128)(2,1)}, bf16[2,3,392,128]{3,2,1,0:T(8,128)(2,1)S(1)}, u32[]{:S(2)}, u32[]{:S(2)}) collective-permute-start(bf16[2,3,392,128]{3,2,1,0:T(8,128)(2,1)} %get-tuple-element.1024), channel_id=1, source_target_pairs={{0,2},{1,3},{2,4},{3,5},{4,6},{5,7},{6,0},{7,1},{8,10},{9,11},{10,... | collective-permute-start | bytes 1806344 | tf_op jit(solution)/shard_map/ppermute | solution.py:600
  501.0 34.5 %collective-permute-start.75 = (bf16[2,3,392,128]{3,2,1,0:T(8,128)(2,1)S(1)}, bf16[2,3,392,128]{3,2,1,0:T(8,128)(2,1)S(1)}, u32[]{:S(2)}, u32[]{:S(2)}) collective-permute-start(bf16[2,3,392,128]{3,2,1,0:T(8,128)(2,1)S(1)} %copy-done.74), channel_id=1, source_target_pairs={{0,4},{1,5},{2,6},{3,7},{4,0},{5,1},{6,2},{7,3},{8,12},{9,13},{10,... | collective-permute-start | bytes 1806344 | tf_op jit(solution)/shard_map/ppermute | solution.py:600
  537.2 41.8 %collective-permute-start.81 = (bf16[2,3,392,128]{3,2,1,0:T(8,128)(2,1)}, bf16[2,3,392,128]{3,2,1,0:T(8,128)(2,1)S(1)}, u32[]{:S(2)}, u32[]{:S(2)}) collective-permute-start(bf16[2,3,392,128]{3,2,1,0:T(8,128)(2,1)} %pad_maximum_fusion.16), channel_id=1, source_target_pairs={{0,1},{1,0},{2,3},{3,2},{4,5},{5,4},{6,7},{7,6},{8,9},{9,8},{10,11... | collective-permute-start | bytes 1806344 | tf_op jit(solution)/shard_map/ppermute | solution.py:600
  542.3 36.7 %collective-permute-start.82 = (bf16[1,3,392,128]{3,2,1,0:T(8,128)(2,1)}, bf16[1,3,392,128]{3,2,1,0:T(8,128)(2,1)}, u32[]{:S(2)}, u32[]{:S(2)}) collective-permute-start(bf16[1,3,392,128]{3,2,1,0:T(8,128)(2,1)} %get-tuple-element.1078), channel_id=1, source_target_pairs={{0,4},{1,5},{2,6},{3,7},{4,0},{5,1},{6,2},{7,3},{8,12},{9,13},{10,... | collective-permute-start | bytes 903176 | tf_op jit(solution)/shard_map/ppermute | solution.py:600
  (153 other events, 3362.0 us)
